TPU v7x, 32 devices: a whole 2x2x4 slice. The times are simulated.
32 devices in a mesh: ctx: 8 (over z, x), head: 4 (over y, core).
Axes of the slice: x: 2, y: 2, z: 4, core: 2. Of those that a mesh axis runs over, the one named last changes fastest.
Arguments:
- queries: bfloat16 [16384, 4096], P('ctx', 'head'), may hold values from -28 to 28
- keys: bfloat16 [16384, 1024], P('ctx', 'head'), may hold values from -13 to 13
- values: bfloat16 [16384, 1024], P('ctx', 'head'), may hold values from -6 to 6
- vertical: int32 [8, 16], P('head'), may hold values from 0 to 255, as said below
- slash: int32 [8, 8], P('head'), may hold values from 0 to 63, as said below
Outputs:
- attention: bfloat16 [16384, 4096], P(('ctx', 'head'))
Inputs may be any that keep to these rules, and one draw needn't show every extreme that they name: `vertical`: each row lists 16 different blocks; at most 4 of one row lie within one index of ctx (2048 tokens), and exactly 4 do in some index. `slash`: each row lists 8 different offsets, 0 and 2 * 32 - 1 among them.
All inputs are finite; a program needn't handle non-finite values.
Results may differ from a plain program's by a relative error of at most 0.0043.
Values may be sent and summed in bfloat16 or wider, within the bound.
No kernel may reach another device: no remote copies, remote signals or barrier semaphores. Data moves between devices by JAX's collectives and lax.ppermute only.
A program may use at most 64 MiB of HBM per device.

v0:
```python
import math

import jax
import jax.numpy as jnp
from jax import lax
from jax.sharding import PartitionSpec as P

HD = 128
BLK = 64
NV = 16
NS = 8
MOWN = 4
LOOK = 2


def shifted(array, axis, by):
    count = lax.axis_size(axis)
    pairs = [(i, i + by) for i in range(count) if 0 <= i + by < count]
    return lax.ppermute(array, axis, pairs)


def local(queries, keys, values, vertical, slash):
    shard_count = lax.axis_size("ctx")
    shard_index = lax.axis_index("ctx")
    tok_rows = queries.shape[0]
    kv_local = keys.shape[1] // HD
    group_heads = queries.shape[1] // (kv_local * HD)
    blocks_dev = tok_rows // BLK
    score_scale = 1.0 / math.sqrt(HD)
    offsets = jnp.arange(BLK, dtype=jnp.int32)
    key_value = jnp.stack([keys, values])
    pieces = [key_value]
    current = key_value
    for distance in range(LOOK):
        current = shifted(current, "ctx", 1)
        pieces = [current] + pieces
    window = jnp.concatenate(pieces, axis=1).reshape(2, (LOOK + 1) * blocks_dev, BLK, kv_local, HD)
    owners = vertical // blocks_dev
    local_block = vertical % blocks_dev
    owned_here = owners == shard_index
    local_pairs = key_value.reshape(2, blocks_dev, BLK, kv_local, HD)
    block_hot = (local_block[:, :, None] == jnp.arange(blocks_dev, dtype=jnp.int32)).astype(
        jnp.bfloat16
    )
    list_index = jnp.arange(NV, dtype=jnp.int32)
    same_owner = owners[:, :, None] == owners[:, None, :]
    earlier = list_index[None, :] < list_index[:, None]
    slot_rank = jnp.sum((same_owner & earlier[None]).astype(jnp.int32), axis=2)
    slot_hot = (
        (slot_rank[:, :, None] == jnp.arange(MOWN, dtype=jnp.int32)) & owned_here[:, :, None]
    ).astype(jnp.bfloat16)
    slot_picker = jnp.einsum(
        "jnm,jnb->jmb", slot_hot, block_hot, preferred_element_type=jnp.float32
    ).astype(jnp.bfloat16)
    slots = jnp.einsum(
        "jmb,xbtjd->xjmtd", slot_picker, local_pairs, preferred_element_type=jnp.float32
    ).astype(jnp.bfloat16)
    gathered = lax.all_gather(slots, "ctx", axis=2, tiled=True)
    slot_index = owners * MOWN + slot_rank
    chooser = (slot_index[:, :, None] == jnp.arange(shard_count * MOWN, dtype=jnp.int32)).astype(
        jnp.bfloat16
    )
    vert_pairs = jnp.einsum(
        "jns,xjstd->xjntd", chooser, gathered, preferred_element_type=jnp.float32
    ).astype(jnp.bfloat16)
    vert_keys = vert_pairs[0].reshape(kv_local, NV * BLK, HD)
    vert_values = vert_pairs[1].reshape(kv_local, NV * BLK, HD)
    vert_pos = (vertical[:, :, None] * BLK + offsets).reshape(kv_local, NV * BLK)
    query_blocks = queries.reshape(blocks_dev, BLK, kv_local, group_heads, HD)

    def take_head(window_head, indices):
        return jnp.take(window_head, indices.reshape(-1), axis=1).reshape(2, NS, 2, BLK, HD)

    def attend_group(group_index):
        group_blocks = group_index * 2 + jnp.arange(2, dtype=jnp.int32)
        window_index = group_blocks[None, None, :] + LOOK * blocks_dev - slash[:, :, None]
        slash_pairs = jax.vmap(take_head, in_axes=(3, 0))(window, window_index)
        slash_keys = slash_pairs[:, 0]
        slash_values = slash_pairs[:, 1]
        query_group = lax.dynamic_slice_in_dim(query_blocks, group_index * 2, 2, 0)
        global_blocks = shard_index * blocks_dev + group_blocks
        query_pos = global_blocks[:, None] * BLK + offsets[None, :]
        vert_scores = (
            jnp.einsum(
                "grjhd,jkd->jhgrk", query_group, vert_keys, preferred_element_type=jnp.float32
            )
            * score_scale
        )
        vert_allowed = vert_pos[:, None, None, :] <= query_pos[None, :, :, None]
        vert_scores = jnp.where(vert_allowed[:, None], vert_scores, -1e30)
        slash_blocks = global_blocks[None, None, :] - slash[:, :, None]
        in_vertical = jnp.any(slash_blocks[:, :, :, None] == vertical[:, None, None, :], axis=3)
        slash_valid = jnp.transpose((slash_blocks >= 0) & jnp.logical_not(in_vertical), (0, 2, 1))
        slash_pos = jnp.transpose(slash_blocks, (0, 2, 1))[:, :, :, None] * BLK + offsets
        slash_allowed = slash_valid[:, :, None, :, None] & (
            slash_pos[:, :, None, :, :] <= query_pos[None, :, :, None, None]
        )
        slash_scores = (
            jnp.einsum(
                "grjhd,jngtd->jhgrnt", query_group, slash_keys, preferred_element_type=jnp.float32
            )
            * score_scale
        )
        slash_scores = jnp.where(slash_allowed[:, None], slash_scores, -1e30)
        row_max = jnp.maximum(jnp.max(vert_scores, axis=4), jnp.max(slash_scores, axis=(4, 5)))
        vert_weights = jnp.exp(vert_scores - row_max[..., None])
        slash_weights = jnp.exp(slash_scores - row_max[..., None, None])
        denominator = jnp.sum(vert_weights, axis=4) + jnp.sum(slash_weights, axis=(4, 5))
        weighted = jnp.einsum(
            "jhgrk,jkd->grjhd",
            vert_weights.astype(jnp.bfloat16),
            vert_values,
            preferred_element_type=jnp.float32,
        )
        weighted = weighted + jnp.einsum(
            "jhgrnt,jngtd->grjhd",
            slash_weights.astype(jnp.bfloat16),
            slash_values,
            preferred_element_type=jnp.float32,
        )
        return (weighted / jnp.transpose(denominator, (2, 3, 0, 1))[..., None]).astype(jnp.bfloat16)

    attended = lax.map(attend_group, jnp.arange(blocks_dev // 2, dtype=jnp.int32))
    attended = attended.reshape(tok_rows, kv_local * group_heads * HD)
    return lax.all_to_all(attended, "head", split_axis=0, concat_axis=1, tiled=True)


def solution(mesh):
    in_specs = (
        P("ctx", "head"),
        P("ctx", "head"),
        P("ctx", "head"),
        P("head", None),
        P("head", None),
    )
    out_specs = P(("ctx", "head"), None)
    return jax.shard_map(local, mesh=mesh, in_specs=in_specs, out_specs=out_specs, check_vma=False)
```

profile of v0, /device:TPU:0, one launch (start us, length us, event | category | flops | bytes accessed | tf_op | source)
XLA Modules:
  0.0 541.5 jit_solution(9632939695698876780)
XLA Ops:
  12.2 2.9 copy.90
  15.2 2.1 fusion.59
  18.3 6.2 %collective-permute-start = (bf16[2,2048,256]{2,1,0:T(8,128)(2,1)S(1)}, bf16[2,2048,256]{2,1,0:T(8,128)(2,1)}, u32[]{:S(2)}, u32[]{:S(2)}) collective-permute-start(bf16[2,2048,256]{2,1,0:T(8,128)(2,1)S(1)} %pad_maximum_fusion), channel_id=1, source_target_pairs={{0,4},{4,8},{8,12},{12,16},{16,20},{20,24},{24,28},{1,5},{5,9},{9,... | collective-permute-start | bytes 6291464 | tf_op jit(solution)/shard_map/ppermute | solution.py:19
  24.5 57.6 %collective-permute-done = bf16[2,2048,256]{2,1,0:T(8,128)(2,1)} collective-permute-done((bf16[2,2048,256]{2,1,0:T(8,128)(2,1)S(1)}, bf16[2,2048,256]{2,1,0:T(8,128)(2,1)}, u32[]{:S(2)}, u32[]{:S(2)}) %collective-permute-start) | collective-permute-done | bytes 2097184 | tf_op jit(solution)/shard_map/ppermute | solution.py:19
  82.1 16.1 %collective-permute-start.1 = (bf16[2,2048,256]{2,1,0:T(8,128)(2,1)}, bf16[2,2048,256]{2,1,0:T(8,128)(2,1)}, u32[]{:S(2)}, u32[]{:S(2)}) collective-permute-start(bf16[2,2048,256]{2,1,0:T(8,128)(2,1)} %collective-permute-done), channel_id=1, source_target_pairs={{0,4},{4,8},{8,12},{12,16},{16,20},{20,24},{24,28},{1,5},{5,9},{9,... | collective-permute-start | bytes 6291464 | tf_op jit(solution)/shard_map/ppermute | solution.py:19
  98.2 7.8 %reshape.222 = bf16[32,64,2,4,128]{4,3,2,1,0:T(4,128)(2,1)} reshape(bf16[2048,1024]{1,0:T(8,128)(2,1)} %param.7) | data formatting | bytes 8388608 | tf_op jit(solution)/shard_map/reshape | solution.py:69
  105.9 2.9 fusion.53
  109.3 31.8 %collective-permute-done.1 = bf16[2,2048,256]{2,1,0:T(8,128)(2,1)} collective-permute-done((bf16[2,2048,256]{2,1,0:T(8,128)(2,1)}, bf16[2,2048,256]{2,1,0:T(8,128)(2,1)}, u32[]{:S(2)}, u32[]{:S(2)}) %collective-permute-start.1) | collective-permute-done | bytes 2097184 | tf_op jit(solution)/shard_map/ppermute | solution.py:19
  141.1 17.8 %maximum_maximum_fusion = bf16[2,6144,256]{2,1,0:T(8,128)(2,1)} fusion(bf16[1,2048,256]{2,1,0:T(8,128)(2,1)S(1)} %bitcast.141, bf16[1,2048,256]{2,1,0:T(8,128)(2,1)S(1)} %bitcast.143, bf16[2,2048,256]{2,1,0:T(8,128)(2,1)} %collective-permute-done, bf16[2,2048,256]{2,1,0:T(8,128)(2,1)} %collective-permute-done.1), kind=kLoop, calls=%fused_computation.56 | loop fusion | flops 25165824 | bytes 12582912 | tf_op jit(solution)/shard_map/concatenate | solution.py:37
  158.9 9.8 %reshape.223 = bf16[2,96,64,2,128]{4,3,2,1,0:T(2,128)(2,1)} reshape(bf16[2,6144,256]{2,1,0:T(8,128)(2,1)} %maximum_maximum_fusion) | data formatting | bytes 12582912 | tf_op jit(solution)/shard_map/reshape | solution.py:37
  168.6 7.2 %copy.96 = bf16[2,96,64,2,128]{4,2,1,0,3:T(8,128)(2,1)} copy(bf16[2,96,64,2,128]{4,3,2,1,0:T(2,128)(2,1)} %reshape.223) | data formatting | bytes 12582912
  175.8 284.8 %while.14 = (s32[]{:T(128)}, bf16[16,2,64,2,4,128]{5,4,3,2,1,0:T(4,128)(2,1)}, s32[]{:T(128)}, s32[16]{0:T(128)S(1)}, bf16[32,64,2,4,128]{4,3,2,1,0:T(4,128)(2,1...) while((s32[]{:T(128)}, ...), condition=%wide.region_7.8_spmd.clone.clone, body=%wide.region_1.7_spmd.clone.clone.sunk | while | flops 819334976 | bytes 38912952 | solution.py:123
  178.7 3.5 gather_fusion
  183.5 2.9 fusion.91
  196.5 3.5 gather_fusion
  201.3 2.9 fusion.91
  214.3 3.5 gather_fusion
  219.1 2.9 fusion.91
  232.0 3.5 gather_fusion
  236.9 2.9 fusion.91
  249.8 3.5 gather_fusion
  254.7 2.9 fusion.91
  267.6 3.5 gather_fusion
  272.5 2.9 fusion.91
  285.4 3.5 gather_fusion
  290.3 2.9 fusion.91
  303.2 3.5 gather_fusion
  308.0 2.9 fusion.91
  321.0 3.5 gather_fusion
  325.8 2.9 fusion.91
  338.8 3.5 gather_fusion
  343.6 2.9 fusion.91
  356.5 3.5 gather_fusion
  361.4 2.9 fusion.91
  374.3 3.5 gather_fusion
  379.2 2.9 fusion.91
  392.1 3.5 gather_fusion
  397.0 2.9 fusion.91
  409.9 3.5 gather_fusion
  414.8 2.9 fusion.91
  427.7 3.5 gather_fusion
  432.5 2.9 fusion.91
  445.5 3.5 gather_fusion
  450.3 2.9 fusion.91
  460.5 7.7 %all_to_all.14 = bf16[4,512,1024]{2,1,0:T(8,128)(2,1)} reshape(bf16[16,2,64,2,4,128]{5,4,3,2,1,0:T(4,128)(2,1)} %get-tuple-element.146) | data formatting | bytes 8388608 | tf_op jit(solution)/shard_map/all_to_all | solution.py:125
  468.3 53.8 %all_to_all.19 = bf16[4,512,1024]{2,1,0:T(8,128)(2,1)} all-to-all(bf16[4,512,1024]{2,1,0:T(8,128)(2,1)} %all_to_all.14), channel_id=1, replica_groups=mesh['ctx'=8,'head'=4] {'head'}, dimensions={0} | all-to-all | bytes 8388608 | tf_op jit(solution)/shard_map/all_to_all | solution.py:125
  522.1 6.2 %copy.98 = bf16[512,4,1024]{0,2,1:T(8,128)(2,1)} copy(bf16[512,4,1024]{2,0,1:T(8,128)(2,1)} %bitcast.138) | data formatting | bytes 8388608 | tf_op jit(solution)/shard_map/all_to_all | solution.py:125
  528.3 6.3 %copy.99 = bf16[512,4096]{1,0:T(8,128)(2,1)} copy(bf16[512,4096]{0,1:T(8,128)(2,1)} %bitcast.139) | data formatting | bytes 8388608 | tf_op jit(solution)/shard_map/all_to_all | solution.py:125
  (538 shorter events, 176.3 us)
Async XLA Ops:
  6.5 4.5 copy-start.1
  6.5 99.4 %all-gather.2.cloned.1.call-start = ((), (), s32[]{:S(2)}) async-start(), calls=%async_computation.1 | async-start | bytes 2359296 | tf_op jit(solution)/shard_map/all_gather | solution.py:58
  11.1 7.0 %copy-start.2 = (bf16[2048,256]{1,0:T(8,128)(2,1)S(1)}, bf16[2048,256]{1,0:T(8,128)(2,1)}, u32[]{:S(2)}) copy-start(bf16[2048,256]{1,0:T(8,128)(2,1)} %param.8) | copy-start | bytes 3145732
  18.3 63.8 %collective-permute-start = (bf16[2,2048,256]{2,1,0:T(8,128)(2,1)S(1)}, bf16[2,2048,256]{2,1,0:T(8,128)(2,1)}, u32[]{:S(2)}, u32[]{:S(2)}) collective-permute-start(bf16[2,2048,256]{2,1,0:T(8,128)(2,1)S(1)} %pad_maximum_fusion), channel_id=1, source_target_pairs={{0,4},{4,8},{8,12},{12,16},{16,20},{20,24},{24,28},{1,5},{5,9},{9,... | collective-permute-start | bytes 6291464 | tf_op jit(solution)/shard_map/ppermute | solution.py:19
  82.1 59.0 %collective-permute-start.1 = (bf16[2,2048,256]{2,1,0:T(8,128)(2,1)}, bf16[2,2048,256]{2,1,0:T(8,128)(2,1)}, u32[]{:S(2)}, u32[]{:S(2)}) collective-permute-start(bf16[2,2048,256]{2,1,0:T(8,128)(2,1)} %collective-permute-done), channel_id=1, source_target_pairs={{0,4},{4,8},{8,12},{12,16},{16,20},{20,24},{24,28},{1,5},{5,9},{9,... | collective-permute-start | bytes 6291464 | tf_op jit(solution)/shard_map/ppermute | solution.py:19
  168.6 7.2 %copy-start.3 = (s32[2,8]{1,0:T(2,128)S(1)}, s32[2,8]{1,0:T(2,128)}, u32[]{:S(2)}) copy-start(s32[2,8]{1,0:T(2,128)} %param.11) | copy-start | bytes 196
  168.6 7.2 %copy-start.4 = (s32[2,16]{1,0:T(2,128)S(1)}, s32[2,16]{1,0:T(2,128)}, u32[]{:S(2)}) copy-start(s32[2,16]{1,0:T(2,128)} %param.10) | copy-start | bytes 388
  187.8 2.2 copy-start
  205.6 2.2 copy-start
  223.4 2.2 copy-start
  241.2 2.2 copy-start
  258.9 2.2 copy-start
  276.7 2.2 copy-start
  294.5 2.2 copy-start
  312.3 2.2 copy-start
  330.1 2.2 copy-start
  347.9 2.2 copy-start
  365.7 2.2 copy-start
  383.5 2.2 copy-start
  401.2 2.2 copy-start
  419.0 2.2 copy-start
  436.8 2.2 copy-start
  454.6 2.2 copy-start
Sparse Core Ops, SparseCore 0:
  18.2 67.6 all-gather.1
where the time goes:
time: 547 us; the launch traced here: 541 us
  local copies, waits for them, and re-layouts  173 us (32%)
  matrix products  90.4 us (17%)
  waiting for transfers between devices  89.4 us (16%)
  other arithmetic  86.7 us (16%)
  blocking collectives  53.8 us (10%)
  starting transfers between devices  22.2 us (4%)
  between operations  13.5 us (2%)
  loops' own time  12.3 us (2%)
    ppermute x2, waiting for transfers between devices, shifted(): return lax.ppermute(array, axis, pairs)  89.4 us
    gather x32, local copies, waits for them, and re-layouts, take_head(): jnp.take(window_head, indices.reshape(-1), axis=1)  57.9 us
    all_to_all x1, blocking collectives, local(): lax.all_to_all(attended, 'head', split_axis=0, concat_axis=1, tiled=True)  53.8 us
    dot_general x16, matrix products, attend_group(): jnp.einsum('grjhd,jngtd->jhgrnt', query_group, slash_keys, preferred_elem...  46.9 us
    ppermute x2, starting transfers between devices, shifted(): return lax.ppermute(array, axis, pairs)  22.2 us
    reduce_sum x16, other arithmetic, attend_group(): jnp.sum(slash_weights, axis=(4, 5))  21.7 us
    all_to_all x3, local copies, waits for them, and re-layouts, local(): lax.all_to_all(attended, 'head', split_axis=0, concat_axis=1, tiled=True)  20.2 us
    reduce_sum x16, other arithmetic, attend_group(): jnp.sum(vert_weights, axis=4) + jnp.sum(slash_weights, axis=(4, 5))  19.5 us
  transfers between devices with their start and end apart: 3, of which 2 were waited for; matrix products, arithmetic and copies ran while one was open for 2% of the time, Pallas kernels for 0%

commit v1 on v0

v1 whole, which is shorter than its diff:
```python
import functools
import math

import jax
import jax.numpy as jnp
from jax import lax
from jax.experimental import pallas as pl
from jax.experimental.pallas import tpu as pltpu
from jax.sharding import PartitionSpec as P

HD = 128
BLK = 64
NV = 16
NS = 8
MOWN = 4
LOOK = 2
NEG = -1e30
STEP_BLOCKS = 2
CHUNKS = 2


def slots_kernel(local_ref, keys_ref, values_ref, out_ref, sem):
    copies = []
    for head in range(out_ref.shape[0]):
        for slot in range(MOWN):
            rows = pl.ds(pl.multiple_of(local_ref[head, slot] * BLK, BLK), BLK)
            for side, source in enumerate((keys_ref, values_ref)):
                copies.append(
                    pltpu.make_async_copy(
                        source.at[rows, pl.ds(head * HD, HD)],
                        out_ref.at[head, pl.ds(slot * BLK, BLK), pl.ds(side * HD, HD)],
                        sem.at[len(copies)],
                    )
                )
    for copy in copies:
        copy.start()
    for copy in copies:
        copy.wait()


def owned_slots(local_block, keys, values):
    heads = local_block.shape[0]
    return pl.pallas_call(
        slots_kernel,
        out_shape=jax.ShapeDtypeStruct((heads, MOWN * BLK, 2 * HD), keys.dtype),
        in_specs=[
            pl.BlockSpec(memory_space=pltpu.SMEM),
            pl.BlockSpec(memory_space=pl.ANY),
            pl.BlockSpec(memory_space=pl.ANY),
        ],
        out_specs=pl.BlockSpec(memory_space=pl.ANY),
        scratch_shapes=[pltpu.SemaphoreType.DMA((heads * MOWN * 2,))],
        compiler_params=pltpu.CompilerParams(vmem_limit_bytes=1 << 20),
        cost_estimate=pl.CostEstimate(
            flops=0, bytes_accessed=4 * heads * MOWN * BLK * 2 * HD, transcendentals=0
        ),
    )(local_block, keys, values)


def attend_kernel(
    head,
    steps,
    group_heads,
    chunk_blocks,
    part_ref,
    parity_ref,
    slot_ref,
    slash_ref,
    query_ref,
    bias_ref,
    own_ref,
    *rest,
):
    two_back = rest[:CHUNKS]
    even_back = rest[CHUNKS : 2 * CHUNKS]
    odd_back, gathered_ref, out_ref, vert, slash, vert_sem, slash_sem = rest[2 * CHUNKS :]
    blocks_dev = own_ref.shape[0] // BLK
    step = pl.program_id(0)
    part = part_ref[0]
    parity = parity_ref[0]

    def block_index(at_step, at):
        return (part * steps + at_step) * STEP_BLOCKS + at

    def fetch(at_step):
        buffer = lax.rem(at_step, 2)
        for at in range(STEP_BLOCKS):
            for entry in range(NS):
                source = block_index(at_step, at) - slash_ref[head, entry]
                target = slash.at[buffer, at, pl.ds(entry * BLK, BLK)]
                sem = slash_sem.at[buffer]

                def rows(first):
                    return pl.ds(pl.multiple_of(first * BLK, BLK), BLK)

                @pl.when(source >= 0)
                def _():
                    pltpu.make_async_copy(own_ref.at[rows(source)], target, sem).start()

                @pl.when((source < 0) & (source >= -blocks_dev) & (parity == 1))
                def _():
                    pltpu.make_async_copy(
                        odd_back.at[rows(source + blocks_dev)], target, sem
                    ).start()

                for chunk in range(CHUNKS):
                    low = chunk * chunk_blocks
                    first = source + blocks_dev - low

                    @pl.when((first >= 0) & (first < chunk_blocks) & (source < 0) & (parity == 0))
                    def _():
                        pltpu.make_async_copy(
                            even_back[chunk].at[rows(first)], target, sem
                        ).start()

                    second = source + 2 * blocks_dev - low

                    @pl.when((second >= 0) & (second < chunk_blocks))
                    def _():
                        pltpu.make_async_copy(
                            two_back[chunk].at[rows(second)], target, sem
                        ).start()

    @pl.when(step == 0)
    def _():
        fetch(0)
        for entry in range(NV):
            pltpu.make_async_copy(
                gathered_ref.at[
                    slot_ref[head, entry] // MOWN,
                    head,
                    pl.ds(pl.multiple_of(lax.rem(slot_ref[head, entry], MOWN) * BLK, BLK), BLK),
                ],
                vert.at[pl.ds(entry * BLK, BLK)],
                vert_sem,
            ).start()
        pltpu.make_async_copy(vert, vert, vert_sem).wait()

    @pl.when(step + 1 < steps)
    def _():
        fetch(step + 1)

    buffer = lax.rem(step, 2)
    here = slash.at[buffer]
    pltpu.make_async_copy(here, here, slash_sem.at[buffer]).wait()

    rate = math.log2(math.e) / math.sqrt(HD)
    rows = group_heads * BLK
    row_token = lax.broadcasted_iota(jnp.int32, (rows, 2 * BLK), 0) % BLK
    column = lax.broadcasted_iota(jnp.int32, (rows, 2 * BLK), 1)
    diagonal = jnp.where((column < BLK) & (column > row_token), NEG, 0.0).astype(jnp.float32)
    ones_vert = jnp.ones((NV * BLK, HD), jnp.bfloat16)
    ones_slash = jnp.ones((NS * BLK, HD), jnp.bfloat16)
    contract = (((1,), (1,)), ((), ()))
    for at in range(STEP_BLOCKS):
        query = jnp.concatenate(
            [
                query_ref[at * BLK : (at + 1) * BLK, h * HD : (h + 1) * HD]
                for h in range(group_heads)
            ],
            axis=0,
        )
        bias = bias_ref[pl.ds(block_index(step, at), 1), :]
        vert_scores = lax.dot_general(
            query, vert[:, :HD], contract, preferred_element_type=jnp.float32
        )
        slash_scores = lax.dot_general(
            query, slash[buffer, at, :, :HD], contract, preferred_element_type=jnp.float32
        )
        vert_scores = vert_scores + bias[:, : NV * BLK]
        slash_scores = slash_scores + bias[:, NV * BLK :]
        slash_scores = jnp.concatenate(
            [slash_scores[:, : 2 * BLK] + diagonal, slash_scores[:, 2 * BLK :]], axis=1
        )
        row_max = jnp.maximum(
            jnp.max(vert_scores, axis=1, keepdims=True),
            jnp.max(slash_scores, axis=1, keepdims=True),
        )
        vert_weights = jnp.exp2((vert_scores - row_max) * rate).astype(jnp.bfloat16)
        slash_weights = jnp.exp2((slash_scores - row_max) * rate).astype(jnp.bfloat16)
        total = jnp.dot(
            vert_weights,
            jnp.concatenate([vert[:, HD:], ones_vert], axis=1),
            preferred_element_type=jnp.float32,
        ) + jnp.dot(
            slash_weights,
            jnp.concatenate([slash[buffer, at, :, HD:], ones_slash], axis=1),
            preferred_element_type=jnp.float32,
        )
        result = (total[:, :HD] / total[:, HD:]).astype(jnp.bfloat16)
        for h in range(group_heads):
            out_ref[at * BLK : (at + 1) * BLK, h * HD : (h + 1) * HD] = result[
                h * BLK : (h + 1) * BLK
            ]


def attend(head, part, parity, slot_index, slash, queries, bias, own, two_back, even_back, odd_back,
           gathered, part_rows):
    group_cols = queries.shape[1] // slash.shape[0]
    group_heads = group_cols // HD
    step_rows = STEP_BLOCKS * BLK
    steps = part_rows // step_rows
    any_spec = pl.BlockSpec(memory_space=pl.ANY)
    keys_seen = (NV + NS) * BLK
    return pl.pallas_call(
        functools.partial(
            attend_kernel, head, steps, group_heads, two_back[0].shape[0] // BLK
        ),
        out_shape=jax.ShapeDtypeStruct((part_rows, group_cols), jnp.bfloat16),
        grid_spec=pltpu.PrefetchScalarGridSpec(
            num_scalar_prefetch=4,
            grid=(steps,),
            in_specs=[
                pl.BlockSpec(
                    (step_rows, group_cols), lambda s, part, *_: (part[0] * steps + s, head)
                ),
                pl.BlockSpec(bias.shape, lambda s, *_: (0, 0)),
            ]
            + [any_spec] * (3 + 2 * CHUNKS),
            out_specs=pl.BlockSpec((step_rows, group_cols), lambda s, *_: (s, 0)),
            scratch_shapes=[
                pltpu.VMEM((NV * BLK, 2 * HD), jnp.bfloat16),
                pltpu.VMEM((2, STEP_BLOCKS, NS * BLK, 2 * HD), jnp.bfloat16),
                pltpu.SemaphoreType.DMA,
                pltpu.SemaphoreType.DMA((2,)),
            ],
        ),
        compiler_params=pltpu.CompilerParams(
            dimension_semantics=("arbitrary",), vmem_limit_bytes=32 << 20
        ),
        cost_estimate=pl.CostEstimate(
            flops=4 * part_rows * group_heads * keys_seen * HD,
            bytes_accessed=4 * part_rows * group_cols + 16 * keys_seen * HD,
            transcendentals=part_rows * group_heads * keys_seen,
        ),
    )(part, parity, slot_index, slash, queries, bias, own, *two_back, *even_back, odd_back, gathered)


def local(queries, keys, values, vertical, slash):
    shard_count = lax.axis_size("ctx")
    shard_index = lax.axis_index("ctx")
    head_count = lax.axis_size("head")
    head_index = lax.axis_index("head")
    tok_rows = queries.shape[0]
    kv_local = keys.shape[1] // HD
    group_cols = queries.shape[1] // kv_local
    blocks_dev = tok_rows // BLK
    part_rows = tok_rows // head_count

    owners = vertical // blocks_dev
    order = jnp.arange(NV, dtype=jnp.int32)
    same_owner = owners[:, :, None] == owners[:, None, :]
    earlier = order[None, :] < order[:, None]
    slot_rank = jnp.sum((same_owner & earlier[None]).astype(jnp.int32), axis=2)
    slot_index = owners * MOWN + slot_rank
    in_slot = (owners == shard_index)[:, :, None] & (
        slot_rank[:, :, None] == jnp.arange(MOWN, dtype=jnp.int32)
    )
    local_block = jnp.sum(in_slot * (vertical % blocks_dev)[:, :, None], axis=1)
    gathered = lax.all_gather(owned_slots(local_block, keys, values), "ctx")

    slash_rank = jnp.sum((slash[:, None, :] < slash[:, :, None]).astype(jnp.int32), axis=2)
    place = slash_rank[:, :, None] == jnp.arange(NS, dtype=jnp.int32)
    slash = jnp.sum(place * slash[:, :, None], axis=1)

    global_blocks = shard_index * blocks_dev + jnp.arange(blocks_dev, dtype=jnp.int32)
    vert_valid = vertical[:, None, :] < global_blocks[None, :, None]
    slash_blocks = global_blocks[None, :, None] - slash[:, None, :]
    in_vertical = jnp.any(slash_blocks[:, :, :, None] == vertical[:, None, None, :], axis=3)
    slash_valid = (slash[:, None, :] == 0) | ((slash_blocks >= 0) & jnp.logical_not(in_vertical))
    valid = jnp.concatenate([vert_valid, slash_valid], axis=2)
    bias = jnp.repeat(jnp.where(valid, 0.0, NEG).astype(jnp.float32), BLK, axis=2)

    two_pairs = [(i, i + 2) for i in range(shard_count - 2)]
    even_to_odd = [(i, i + 1) for i in range(0, shard_count - 1, 2)]
    odd_to_even = [(i, i - 1) for i in range(1, shard_count, 2)]
    chunk_rows = tok_rows // CHUNKS
    windows = []
    for head in range(kv_local):
        columns = slice(head * HD, (head + 1) * HD)
        own = jnp.concatenate([keys[:, columns], values[:, columns]], axis=1)
        two_back = [
            lax.ppermute(own[c * chunk_rows : (c + 1) * chunk_rows], "ctx", two_pairs)
            for c in range(CHUNKS)
        ]
        odd_back = lax.ppermute(own, "ctx", even_to_odd)
        even_back = [lax.ppermute(piece, "ctx", odd_to_even) for piece in two_back]
        windows.append((own, two_back, even_back, odd_back))

    parity = (shard_index % 2).reshape(1).astype(jnp.int32)
    out = jnp.zeros((part_rows, head_count * kv_local * group_cols), jnp.bfloat16)
    for head in range(kv_local):
        own, two_back, even_back, odd_back = windows[head]
        for flip in range(head_count - 1, -1, -1):
            other = head_index ^ flip
            piece = attend(
                head, other.reshape(1).astype(jnp.int32), parity, slot_index, slash, queries,
                bias[head], own, two_back, even_back, odd_back, gathered, part_rows,
            )
            if flip:
                piece = lax.ppermute(piece, "head", [(i, i ^ flip) for i in range(head_count)])
            out = lax.dynamic_update_slice(
                out, piece, (0, other * kv_local * group_cols + head * group_cols)
            )
    return out


def solution(mesh):
    in_specs = (
        P("ctx", "head"),
        P("ctx", "head"),
        P("ctx", "head"),
        P("head", None),
        P("head", None),
    )
    out_specs = P(("ctx", "head"), None)
    return jax.shard_map(local, mesh=mesh, in_specs=in_specs, out_specs=out_specs, check_vma=False)
```

time: 547 us -> 214 us (0.39)
  the two profiles are of different devices: /device:TPU:0 before, /device:TPU:31 now
where the time goes in v1:
time: 214 us; the launch traced here: 215 us
  Pallas kernels  90.2 us (42%)
  waiting for transfers between devices  55.9 us (26%)
  starting transfers between devices  33.8 us (16%)
  local copies, waits for them, and re-layouts  14.6 us (7%)
  between operations  13.8 us (6%)
  other arithmetic  6.27 us (3%)
    pallas_call x8, Pallas kernels, attend(): pl.pallas_call(functools.partial(attend_kernel, head, steps, group_heads,...  88.8 us
    ppermute x4, waiting for transfers between devices, local(): lax.ppermute(own[c * chunk_rows:(c + 1) * chunk_rows], 'ctx', two_pairs)  54.3 us
    ppermute x4, starting transfers between devices, local(): even_back = [lax.ppermute(piece, 'ctx', odd_to_even) for piece in two_back]  15.7 us
    ppermute x6, starting transfers between devices, local(): lax.ppermute(piece, 'head', [(i, i ^ flip) for i in range(head_count)])  10.3 us
    unnamed x22, local copies, waits for them, and re-layouts  8.27 us
    ppermute x4, starting transfers between devices, local(): lax.ppermute(own[c * chunk_rows:(c + 1) * chunk_rows], 'ctx', two_pairs)  5.14 us
  transfers between devices with their start and end apart: 17, of which 5 were waited for; matrix products, arithmetic and copies ran while one was open for 5% of the time, Pallas kernels for 41%

profile of v1, /device:TPU:31, one launch (start us, length us, event | category | flops | bytes accessed | tf_op | source)
XLA Modules:
  0.0 214.6 jit_solution(8788551262973492392)
XLA Ops:
  6.5 0.7 and_select_fusion
  7.2 0.7 broadcast_compare_fusion.1
  7.9 0.2 convert_reduce_fusion
  8.1 0.2 select_reduce_fusion.1.local_ref
  8.3 1.2 copy-done.4
  9.5 1.2 copy-done.5
  10.7 1.4 shard_map.55
  12.1 0.4 fusion.5
  12.5 1.3 fusion.1
  13.8 1.3 collective-permute-start.9
  15.1 1.3 collective-permute-start.8
  16.4 1.1 fusion.3
  17.5 1.3 collective-permute-start.1
  18.8 1.3 collective-permute-start
  20.2 1.3 collective-permute-start.4
  21.5 0.2 convert_reduce_fusion.1
  22.1 1.4 pad_maximum_fusion.1.own_ref
  23.5 13.3 %collective-permute-done.9.rest_1_ = bf16[1024,256]{1,0:T(8,128)(2,1)} collective-permute-done((bf16[1024,256]{1,0:T(8,128)(2,1)}, bf16[1024,256]{1,0:T(8,128)(2,1)}, u32[]{:S(2)}, u32[]{:S(2)}) %collective-permute-start.9) | collective-permute-done | bytes 524320 | tf_op jit(solution)/shard_map/ppermute | solution.py:283
  36.8 1.3 collective-permute-start.12
  38.1 32.9 %collective-permute-done.1.rest_1_ = bf16[1024,256]{1,0:T(8,128)(2,1)} collective-permute-done((bf16[1024,256]{1,0:T(8,128)(2,1)}, bf16[1024,256]{1,0:T(8,128)(2,1)}, u32[]{:S(2)}, u32[]{:S(2)}) %collective-permute-start.1) | collective-permute-done | bytes 524320 | tf_op jit(solution)/shard_map/ppermute | solution.py:283
  70.9 8.6 %collective-permute-start.3 = (bf16[1024,256]{1,0:T(8,128)(2,1)}, bf16[1024,256]{1,0:T(8,128)(2,1)}, u32[]{:S(2)}, u32[]{:S(2)}) collective-permute-start(bf16[1024,256]{1,0:T(8,128)(2,1)} %collective-permute-done.1.rest_1_), channel_id=1, source_target_pairs={{4,0},{12,8},{20,16},{28,24},{5,1},{13,9},{21,17},{29,25},{6,2},{1... | collective-permute-start | bytes 1572872 | tf_op jit(solution)/shard_map/ppermute | solution.py:287
  79.7 8.1 %collective-permute-done.rest_0_ = bf16[1024,256]{1,0:T(8,128)(2,1)} collective-permute-done((bf16[1024,256]{1,0:T(8,128)(2,1)}, bf16[1024,256]{1,0:T(8,128)(2,1)}, u32[]{:S(2)}, u32[]{:S(2)}) %collective-permute-start) | collective-permute-done | bytes 524320 | tf_op jit(solution)/shard_map/ppermute | solution.py:283
  87.8 3.0 %collective-permute-start.2 = (bf16[1024,256]{1,0:T(8,128)(2,1)}, bf16[1024,256]{1,0:T(8,128)(2,1)}, u32[]{:S(2)}, u32[]{:S(2)}) collective-permute-start(bf16[1024,256]{1,0:T(8,128)(2,1)} %collective-permute-done.rest_0_), channel_id=1, source_target_pairs={{4,0},{12,8},{20,16},{28,24},{5,1},{13,9},{21,17},{29,25},{6,2},{1... | collective-permute-start | bytes 1572872 | tf_op jit(solution)/shard_map/ppermute | solution.py:287
  90.8 2.1 collective-permute-start.11
  92.9 2.1 collective-permute-start.10
  95.1 0.9 broadcast_in_dim.21
  96.0 1.1 broadcast_in_dim.22.bias_ref
  97.1 0.9 broadcast_in_dim.19
  98.0 1.1 broadcast_in_dim.20.bias_ref
  99.2 0.7 collective-permute-done.2.rest_2_
  99.9 2.2 %copy-done = bf16[2048,1024]{1,0:T(8,128)(2,1)S(1)} copy-done((bf16[2048,1024]{1,0:T(8,128)(2,1)S(1)}, bf16[2048,1024]{1,0:T(8,128)(2,1)}, u32[]{:S(2)}) %copy-start) | copy-done | bytes 4194328
  102.1 1.6 copy-done.2
  103.7 10.9 %shard_map.56 = bf16[512,512]{1,0:T(8,128)(2,1)S(1)} custom-call(s32[1]{0:T(128)} %bitcast.part_ref, s32[1]{0:T(128)} %bitcast.1.parity_ref, s32[2,16]{1,0:T(2,128)S(1)} %multiply_add_fusion.slot_ref, s32[2,8]{1,0:T(2,128)S(1)} %select_reduce_fusion.slash_ref, bf16[2048,1024]{1,0:T(8,128)(2,1)S(1)} %copy-done, f32[32,1536]{1,0:T(8,128)S(1)} %broadcast_in_dim.20.bias_ref, ...), custom_call_target="tpu_custom_call" | custom-call | flops 1610612736 | bytes 4194304 | tf_op jit(solution)/shard_map/pallas_call | solution.py:205
  114.6 5.9 %collective-permute-start.5 = (bf16[512,512]{1,0:T(8,128)(2,1)S(1)}, bf16[512,512]{1,0:T(8,128)(2,1)S(1)}, u32[]{:S(2)}, u32[]{:S(2)}) collective-permute-start(bf16[512,512]{1,0:T(8,128)(2,1)S(1)} %shard_map.56), channel_id=1, source_target_pairs={{0,3},{1,2},{2,1},{3,0},{4,7},{5,6},{6,5},{7,4},{8,11},{9,10},{10,... | collective-permute-start | bytes 1572872 | tf_op jit(solution)/shard_map/ppermute | solution.py:301
  120.4 11.4 %shard_map.57 = bf16[512,512]{1,0:T(8,128)(2,1)S(1)} custom-call(s32[1]{0:T(128)} %bitcast.4.part_ref, s32[1]{0:T(128)} %bitcast.1.parity_ref, s32[2,16]{1,0:T(2,128)S(1)} %multiply_add_fusion.slot_ref, s32[2,8]{1,0:T(2,128)S(1)} %select_reduce_fusion.slash_ref, bf16[2048,1024]{1,0:T(8,128)(2,1)S(1)} %copy-done.1, f32[32,1536]{1,0:T(8,128)S(1)} %broadcast_in_dim.20.bias_ref, ...), custom_call_target="tpu_custom_call" | custom-call | flops 1610612736 | bytes 4194304 | tf_op jit(solution)/shard_map/pallas_call | solution.py:205
  131.9 1.7 collective-permute-start.6
  133.5 12.0 %shard_map.58 = bf16[512,512]{1,0:T(8,128)(2,1)S(1)} custom-call(s32[1]{0:T(128)} %bitcast.5.part_ref, s32[1]{0:T(128)} %bitcast.1.parity_ref, s32[2,16]{1,0:T(2,128)S(1)} %multiply_add_fusion.slot_ref, s32[2,8]{1,0:T(2,128)S(1)} %select_reduce_fusion.slash_ref, bf16[2048,1024]{1,0:T(8,128)(2,1)S(1)} %copy-done.1, f32[32,1536]{1,0:T(8,128)S(1)} %broadcast_in_dim.20.bias_ref, ...), custom_call_target="tpu_custom_call" | custom-call | flops 1610612736 | bytes 4194304 | tf_op jit(solution)/shard_map/pallas_call | solution.py:205
  145.7 10.0 %shard_map.60 = bf16[512,512]{1,0:T(8,128)(2,1)S(1)} custom-call(s32[1]{0:T(128)} %bitcast.part_ref, s32[1]{0:T(128)} %bitcast.1.parity_ref, s32[2,16]{1,0:T(2,128)S(1)} %multiply_add_fusion.slot_ref, s32[2,8]{1,0:T(2,128)S(1)} %select_reduce_fusion.slash_ref, bf16[2048,1024]{1,0:T(8,128)(2,1)S(1)} %copy-done.1, f32[32,1536]{1,0:T(8,128)S(1)} %broadcast_in_dim.22.bias_ref, ...), custom_call_target="tpu_custom_call" | custom-call | flops 1610612736 | bytes 4194304 | tf_op jit(solution)/shard_map/pallas_call | solution.py:205
  155.7 1.2 collective-permute-start.13
  156.8 10.5 %shard_map.61 = bf16[512,512]{1,0:T(8,128)(2,1)S(1)} custom-call(s32[1]{0:T(128)} %bitcast.4.part_ref, s32[1]{0:T(128)} %bitcast.1.parity_ref, s32[2,16]{1,0:T(2,128)S(1)} %multiply_add_fusion.slot_ref, s32[2,8]{1,0:T(2,128)S(1)} %select_reduce_fusion.slash_ref, bf16[2048,1024]{1,0:T(8,128)(2,1)S(1)} %copy-done.1, f32[32,1536]{1,0:T(8,128)S(1)} %broadcast_in_dim.22.bias_ref, ...), custom_call_target="tpu_custom_call" | custom-call | flops 1610612736 | bytes 4194304 | tf_op jit(solution)/shard_map/pallas_call | solution.py:205
  167.4 1.5 collective-permute-start.14
  168.9 12.0 %shard_map.59 = bf16[512,512]{1,0:T(8,128)(2,1)S(1)} custom-call(s32[1]{0:T(128)} %bitcast.6.part_ref, s32[1]{0:T(128)} %bitcast.1.parity_ref, s32[2,16]{1,0:T(2,128)S(1)} %multiply_add_fusion.slot_ref, s32[2,8]{1,0:T(2,128)S(1)} %select_reduce_fusion.slash_ref, bf16[2048,1024]{1,0:T(8,128)(2,1)S(1)} %copy-done.1, f32[32,1536]{1,0:T(8,128)S(1)} %broadcast_in_dim.20.bias_ref, ...), custom_call_target="tpu_custom_call" | custom-call | flops 1610612736 | bytes 4194304 | tf_op jit(solution)/shard_map/pallas_call | solution.py:205
  180.9 11.1 %shard_map.63 = bf16[512,512]{1,0:T(8,128)(2,1)S(1)} custom-call(s32[1]{0:T(128)} %bitcast.6.part_ref, s32[1]{0:T(128)} %bitcast.1.parity_ref, s32[2,16]{1,0:T(2,128)S(1)} %multiply_add_fusion.slot_ref, s32[2,8]{1,0:T(2,128)S(1)} %select_reduce_fusion.slash_ref, bf16[2048,1024]{1,0:T(8,128)(2,1)S(1)} %copy-done.1, f32[32,1536]{1,0:T(8,128)S(1)} %broadcast_in_dim.22.bias_ref, ...), custom_call_target="tpu_custom_call" | custom-call | flops 1610612736 | bytes 4194304 | tf_op jit(solution)/shard_map/pallas_call | solution.py:205
  192.1 10.8 %shard_map.62 = bf16[512,512]{1,0:T(8,128)(2,1)S(1)} custom-call(s32[1]{0:T(128)} %bitcast.5.part_ref, s32[1]{0:T(128)} %bitcast.1.parity_ref, s32[2,16]{1,0:T(2,128)S(1)} %multiply_add_fusion.slot_ref, s32[2,8]{1,0:T(2,128)S(1)} %select_reduce_fusion.slash_ref, bf16[2048,1024]{1,0:T(8,128)(2,1)S(1)} %copy-done.1, f32[32,1536]{1,0:T(8,128)S(1)} %broadcast_in_dim.22.bias_ref, ...), custom_call_target="tpu_custom_call" | custom-call | flops 1610612736 | bytes 4194304 | tf_op jit(solution)/shard_map/pallas_call | solution.py:205
  202.9 0.5 broadcast_in_dim.16
  203.9 0.9 collective-permute-done.15
  204.9 2.0 copy-done.8
  206.9 0.8 constant_dynamic-update-slice_fusion.7
  (53 shorter events, 1.4 us)
Async XLA Ops:
  6.5 93.4 %all-gather.3.cloned.1.call-start = ((), (), s32[]{:S(2)}) async-start(), calls=%async_computation | async-start | bytes 2359296 | tf_op jit(solution)/shard_map/all_gather | solution.py:260
  8.3 1.2 copy-start.4
  9.5 1.2 copy-start.5
  12.5 9.0 %copy-start.6 = (bf16[2048,128]{1,0:T(8,128)(2,1)}, bf16[2048,128]{1,0:T(8,128)(2,1)S(1)}, u32[]{:S(2)}) copy-start(bf16[2048,128]{1,0:T(8,128)(2,1)S(1)} %get-tuple-element.9) | copy-start | bytes 1572868
  12.5 9.5 %copy-start.7 = (bf16[2048,128]{1,0:T(8,128)(2,1)}, bf16[2048,128]{1,0:T(8,128)(2,1)S(1)}, u32[]{:S(2)}) copy-start(bf16[2048,128]{1,0:T(8,128)(2,1)S(1)} %get-tuple-element.18) | copy-start | bytes 1572868
  12.5 9.0 %copy-start.10 = (s32[2,8]{1,0:T(2,128)S(1)}, s32[2,8]{1,0:T(2,128)}, u32[]{:S(2)}) copy-start(s32[2,8]{1,0:T(2,128)} %param.9) | copy-start | bytes 196
  12.5 9.3 %copy-start.9 = (s32[2,16]{1,0:T(2,128)S(1)}, s32[2,16]{1,0:T(2,128)}, u32[]{:S(2)}) copy-start(s32[2,16]{1,0:T(2,128)} %param.8) | copy-start | bytes 388
  13.8 23.0 %collective-permute-start.9 = (bf16[1024,256]{1,0:T(8,128)(2,1)}, bf16[1024,256]{1,0:T(8,128)(2,1)}, u32[]{:S(2)}, u32[]{:S(2)}) collective-permute-start(bf16[1024,256]{1,0:T(8,128)(2,1)} %get-tuple-element.7), channel_id=1, source_target_pairs={{0,8},{4,12},{8,16},{12,20},{16,24},{20,28},{1,9},{5,13},{9,17},{1... | collective-permute-start | bytes 1572872 | tf_op jit(solution)/shard_map/ppermute | solution.py:283
  15.1 75.7 %collective-permute-start.8 = (bf16[1024,256]{1,0:T(8,128)(2,1)}, bf16[1024,256]{1,0:T(8,128)(2,1)}, u32[]{:S(2)}, u32[]{:S(2)}) collective-permute-start(bf16[1024,256]{1,0:T(8,128)(2,1)} %get-tuple-element.8), channel_id=1, source_target_pairs={{0,8},{4,12},{8,16},{12,20},{16,24},{20,28},{1,9},{5,13},{9,17},{1... | collective-permute-start | bytes 1572872 | tf_op jit(solution)/shard_map/ppermute | solution.py:283
  17.5 53.4 %collective-permute-start.1 = (bf16[1024,256]{1,0:T(8,128)(2,1)}, bf16[1024,256]{1,0:T(8,128)(2,1)}, u32[]{:S(2)}, u32[]{:S(2)}) collective-permute-start(bf16[1024,256]{1,0:T(8,128)(2,1)} %get-tuple-element.13), channel_id=1, source_target_pairs={{0,8},{4,12},{8,16},{12,20},{16,24},{20,28},{1,9},{5,13},{9,17},{1... | collective-permute-start | bytes 1572872 | tf_op jit(solution)/shard_map/ppermute | solution.py:283
  18.8 69.0 %collective-permute-start = (bf16[1024,256]{1,0:T(8,128)(2,1)}, bf16[1024,256]{1,0:T(8,128)(2,1)}, u32[]{:S(2)}, u32[]{:S(2)}) collective-permute-start(bf16[1024,256]{1,0:T(8,128)(2,1)} %get-tuple-element.14), channel_id=1, source_target_pairs={{0,8},{4,12},{8,16},{12,20},{16,24},{20,28},{1,9},{5,13},{9,17},{1... | collective-permute-start | bytes 1572872 | tf_op jit(solution)/shard_map/ppermute | solution.py:283
  20.2 79.7 %collective-permute-start.4 = (bf16[2048,256]{1,0:T(8,128)(2,1)S(1)}, bf16[2048,256]{1,0:T(8,128)(2,1)S(1)}, u32[]{:S(2)}, u32[]{:S(2)}) collective-permute-start(bf16[2048,256]{1,0:T(8,128)(2,1)S(1)} %pad_maximum_fusion.own_ref), channel_id=1, source_target_pairs={{0,4},{8,12},{16,20},{24,28},{1,5},{9,13},{17,21},{25,29},{2,6},{1... | collective-permute-start | bytes 3145736 | tf_op jit(solution)/shard_map/ppermute | solution.py:286
  36.8 108.9 %collective-permute-start.12 = (bf16[2048,256]{1,0:T(8,128)(2,1)S(1)}, bf16[2048,256]{1,0:T(8,128)(2,1)}, u32[]{:S(2)}, u32[]{:S(2)}) collective-permute-start(bf16[2048,256]{1,0:T(8,128)(2,1)S(1)} %pad_maximum_fusion.1.own_ref), channel_id=1, source_target_pairs={{0,4},{8,12},{16,20},{24,28},{1,5},{9,13},{17,21},{25,29},{2,6},{1... | collective-permute-start | bytes 3145736 | tf_op jit(solution)/shard_map/ppermute | solution.py:286
  70.9 22.0 %collective-permute-start.3 = (bf16[1024,256]{1,0:T(8,128)(2,1)}, bf16[1024,256]{1,0:T(8,128)(2,1)}, u32[]{:S(2)}, u32[]{:S(2)}) collective-permute-start(bf16[1024,256]{1,0:T(8,128)(2,1)} %collective-permute-done.1.rest_1_), channel_id=1, source_target_pairs={{4,0},{12,8},{20,16},{28,24},{5,1},{13,9},{21,17},{29,25},{6,2},{1... | collective-permute-start | bytes 1572872 | tf_op jit(solution)/shard_map/ppermute | solution.py:287
  87.8 12.1 %collective-permute-start.2 = (bf16[1024,256]{1,0:T(8,128)(2,1)}, bf16[1024,256]{1,0:T(8,128)(2,1)}, u32[]{:S(2)}, u32[]{:S(2)}) collective-permute-start(bf16[1024,256]{1,0:T(8,128)(2,1)} %collective-permute-done.rest_0_), channel_id=1, source_target_pairs={{4,0},{12,8},{20,16},{28,24},{5,1},{13,9},{21,17},{29,25},{6,2},{1... | collective-permute-start | bytes 1572872 | tf_op jit(solution)/shard_map/ppermute | solution.py:287
  90.8 54.7 %collective-permute-start.11 = (bf16[1024,256]{1,0:T(8,128)(2,1)}, bf16[1024,256]{1,0:T(8,128)(2,1)}, u32[]{:S(2)}, u32[]{:S(2)}) collective-permute-start(bf16[1024,256]{1,0:T(8,128)(2,1)} %collective-permute-done.9.rest_1_), channel_id=1, source_target_pairs={{4,0},{12,8},{20,16},{28,24},{5,1},{13,9},{21,17},{29,25},{6,2},{1... | collective-permute-start | bytes 1572872 | tf_op jit(solution)/shard_map/ppermute | solution.py:287
  92.9 52.7 %collective-permute-start.10 = (bf16[1024,256]{1,0:T(8,128)(2,1)}, bf16[1024,256]{1,0:T(8,128)(2,1)}, u32[]{:S(2)}, u32[]{:S(2)}) collective-permute-start(bf16[1024,256]{1,0:T(8,128)(2,1)} %collective-permute-done.8.rest_0_), channel_id=1, source_target_pairs={{4,0},{12,8},{20,16},{28,24},{5,1},{13,9},{21,17},{29,25},{6,2},{1... | collective-permute-start | bytes 1572872 | tf_op jit(solution)/shard_map/ppermute | solution.py:287
  99.9 2.2 %copy-start = (bf16[2048,1024]{1,0:T(8,128)(2,1)S(1)}, bf16[2048,1024]{1,0:T(8,128)(2,1)}, u32[]{:S(2)}) copy-start(bf16[2048,1024]{1,0:T(8,128)(2,1)} %query_ref.15) | copy-start | bytes 12582916
  102.1 1.6 copy-start.2
  103.7 16.8 %copy-start.1 = (bf16[2048,1024]{1,0:T(8,128)(2,1)S(1)}, bf16[2048,1024]{1,0:T(8,128)(2,1)}, u32[]{:S(2)}) copy-start(bf16[2048,1024]{1,0:T(8,128)(2,1)} %query_ref.15) | copy-start | bytes 12582916
  103.7 16.8 %copy-start.3 = (bf16[16,256,256]{2,1,0:T(8,128)(2,1)S(1)}, bf16[16,256,256]{2,1,0:T(8,128)(2,1)}, u32[]{:S(2)}) copy-start(bf16[16,256,256]{2,1,0:T(8,128)(2,1)} %all-gather.3.cloned.1.call-done) | copy-start | bytes 6291460
  114.6 88.3 %collective-permute-start.5 = (bf16[512,512]{1,0:T(8,128)(2,1)S(1)}, bf16[512,512]{1,0:T(8,128)(2,1)S(1)}, u32[]{:S(2)}, u32[]{:S(2)}) collective-permute-start(bf16[512,512]{1,0:T(8,128)(2,1)S(1)} %shard_map.56), channel_id=1, source_target_pairs={{0,3},{1,2},{2,1},{3,0},{4,7},{5,6},{6,5},{7,4},{8,11},{9,10},{10,... | collective-permute-start | bytes 1572872 | tf_op jit(solution)/shard_map/ppermute | solution.py:301
  131.9 71.6 %collective-permute-start.6 = (bf16[512,512]{1,0:T(8,128)(2,1)S(1)}, bf16[512,512]{1,0:T(8,128)(2,1)S(1)}, u32[]{:S(2)}, u32[]{:S(2)}) collective-permute-start(bf16[512,512]{1,0:T(8,128)(2,1)S(1)} %shard_map.57), channel_id=1, source_target_pairs={{0,2},{1,3},{2,0},{3,1},{4,6},{5,7},{6,4},{7,5},{8,10},{9,11},{10,... | collective-permute-start | bytes 1572872 | tf_op jit(solution)/shard_map/ppermute | solution.py:301
  145.6 58.0 %collective-permute-start.7 = (bf16[512,512]{1,0:T(8,128)(2,1)S(1)}, bf16[512,512]{1,0:T(8,128)(2,1)S(1)}, u32[]{:S(2)}, u32[]{:S(2)}) collective-permute-start(bf16[512,512]{1,0:T(8,128)(2,1)S(1)} %shard_map.58), channel_id=1, source_target_pairs={{0,1},{1,0},{2,3},{3,2},{4,5},{5,4},{6,7},{7,6},{8,9},{9,8},{10,11... | collective-permute-start | bytes 1572872 | tf_op jit(solution)/shard_map/ppermute | solution.py:301
  155.7 48.1 %collective-permute-start.13 = (bf16[512,512]{1,0:T(8,128)(2,1)S(1)}, bf16[512,512]{1,0:T(8,128)(2,1)S(1)}, u32[]{:S(2)}, u32[]{:S(2)}) collective-permute-start(bf16[512,512]{1,0:T(8,128)(2,1)S(1)} %shard_map.60), channel_id=1, source_target_pairs={{0,3},{1,2},{2,1},{3,0},{4,7},{5,6},{6,5},{7,4},{8,11},{9,10},{10,... | collective-permute-start | bytes 1572872 | tf_op jit(solution)/shard_map/ppermute | solution.py:301
  167.4 36.4 %collective-permute-start.14 = (bf16[512,512]{1,0:T(8,128)(2,1)S(1)}, bf16[512,512]{1,0:T(8,128)(2,1)S(1)}, u32[]{:S(2)}, u32[]{:S(2)}) collective-permute-start(bf16[512,512]{1,0:T(8,128)(2,1)S(1)} %shard_map.61), channel_id=1, source_target_pairs={{0,2},{1,3},{2,0},{3,1},{4,6},{5,7},{6,4},{7,5},{8,10},{9,11},{10,... | collective-permute-start | bytes 1572872 | tf_op jit(solution)/shard_map/ppermute | solution.py:301
  202.8 2.0 collective-permute-start.15
  204.9 2.0 copy-start.8
Sparse Core Ops, SparseCore 0:
  12.3 67.7 all-gather.2

commit v2 on v1

--- a/solution.py
+++ b/solution.py
@@ -17,6 +17,8 @@
 NEG = -1e30
 STEP_BLOCKS = 2
 CHUNKS = 2
+BUFFERS = 4
+TILE = 256
 
 
 def slots_kernel(local_ref, keys_ref, values_ref, out_ref, sem):
@@ -73,20 +75,24 @@
 ):
     two_back = rest[:CHUNKS]
     even_back = rest[CHUNKS : 2 * CHUNKS]
-    odd_back, gathered_ref, out_ref, vert, slash, vert_sem, slash_sem = rest[2 * CHUNKS :]
+    (
+        odd_back, gathered_ref, out_ref, vert, slash, scores_a, scores_b, weights_a, weights_b,
+        max_a, max_b, diagonal_ref, vert_sem, slash_sem,
+    ) = rest[2 * CHUNKS :]
+    scores, weights, maxima = (scores_a, scores_b), (weights_a, weights_b), (max_a, max_b)
     blocks_dev = own_ref.shape[0] // BLK
     step = pl.program_id(0)
     part = part_ref[0]
     parity = parity_ref[0]
-
-    def block_index(at_step, at):
-        return (part * steps + at_step) * STEP_BLOCKS + at
-
-    def fetch(at_step):
-        buffer = lax.rem(at_step, 2)
+    part_blocks = steps * STEP_BLOCKS
+    rate = math.log2(math.e) / math.sqrt(HD)
+    contract = (((1,), (1,)), ((), ()))
+
+    def fetch(pair):
+        buffer = lax.rem(pair, BUFFERS)
         for at in range(STEP_BLOCKS):
             for entry in range(NS):
-                source = block_index(at_step, at) - slash_ref[head, entry]
+                source = part * part_blocks + pair * STEP_BLOCKS + at - slash_ref[head, entry]
                 target = slash.at[buffer, at, pl.ds(entry * BLK, BLK)]
                 sem = slash_sem.at[buffer]
 
@@ -120,6 +126,90 @@
                         pltpu.make_async_copy(
                             two_back[chunk].at[rows(second)], target, sem
                         ).start()
+
+    def arrived(pair):
+        here = slash.at[lax.rem(pair, BUFFERS)]
+        pltpu.make_async_copy(here, here, slash_sem.at[lax.rem(pair, BUFFERS)]).wait()
+
+    def slash_of(pair, at):
+        return slash.at[lax.rem(pair + BUFFERS, BUFFERS), at]
+
+    def query_of(block):
+        start = pl.multiple_of(jnp.minimum(block, part_blocks - 1) * BLK, BLK)
+        return jnp.concatenate(
+            [query_ref[pl.ds(start, BLK), h * HD : (h + 1) * HD] for h in range(group_heads)],
+            axis=0,
+        )
+
+    def score_tile(query, bias, here, tile):
+        low = tile * TILE
+        if low < NV * BLK:
+            keys = vert[low : low + TILE, :HD]
+        else:
+            keys = here[low - NV * BLK : low - NV * BLK + TILE, :HD]
+        found = lax.dot_general(query, keys, contract, preferred_element_type=jnp.float32)
+        found = found + bias[:, low : low + TILE]
+        if low == NV * BLK:
+            diagonal = jnp.concatenate([diagonal_ref[...]] * group_heads, axis=0)
+            found = jnp.concatenate(
+                [found[:, : 2 * BLK] + diagonal, found[:, 2 * BLK :]], axis=1
+            )
+        return found
+
+    def weighted_values(here, at):
+        ones = jnp.ones((TILE, HD), jnp.bfloat16)
+        values = [
+            jnp.concatenate([vert[low : low + TILE, HD:], ones], axis=1)
+            for low in range(0, NV * BLK, TILE)
+        ] + [
+            jnp.concatenate([here[low : low + TILE, HD:], ones], axis=1)
+            for low in range(0, NS * BLK, TILE)
+        ]
+        return jnp.dot(
+            weights[at][...], jnp.concatenate(values, axis=0), preferred_element_type=jnp.float32
+        )
+
+    def store(total, block):
+        result = (total[:, :HD] / total[:, HD:]).astype(jnp.bfloat16)
+        start = pl.multiple_of(block * BLK, BLK)
+        for h in range(group_heads):
+            out_ref[pl.ds(start, BLK), h * HD : (h + 1) * HD] = result[h * BLK : (h + 1) * BLK]
+
+    def stage(block, pair, at, before_pair, score, weigh, combine):
+        other = 1 - at
+        here = slash_of(pair, at)
+        if score:
+            query = query_of(block)
+            row = part * part_blocks + jnp.minimum(block, part_blocks - 1)
+            bias = bias_ref[pl.ds(row, 1), :]
+        if combine:
+            total = weighted_values(slash_of(before_pair, at), at)
+        if weigh:
+            row_max = maxima[other][...]
+            row_max = jnp.concatenate([row_max] * (TILE // HD), axis=1)
+        highest = None
+        fresh = []
+        for tile in range((NV + NS) * BLK // TILE):
+            low = tile * TILE
+            if score:
+                found = score_tile(query, bias, here, tile)
+                scores[at][:, low : low + TILE] = found
+                for part_low in range(0, TILE, HD):
+                    piece = found[:, part_low : part_low + HD]
+                    highest = piece if highest is None else jnp.maximum(highest, piece)
+            if weigh:
+                fresh.append(
+                    jnp.exp2((scores[other][:, low : low + TILE] - row_max) * rate).astype(
+                        jnp.bfloat16
+                    )
+                )
+                weights[other][:, low : low + TILE] = fresh[-1]
+        if score:
+            maxima[at][...] = jnp.broadcast_to(
+                jnp.max(highest, axis=1, keepdims=True), highest.shape
+            )
+        if combine:
+            store(total, jnp.maximum(block - 2, 0))
 
     @pl.when(step == 0)
     def _():
@@ -134,64 +224,35 @@
                 vert.at[pl.ds(entry * BLK, BLK)],
                 vert_sem,
             ).start()
+
+        @pl.when(steps > 1)
+        def _():
+            fetch(1)
+
+        column = lax.broadcasted_iota(jnp.int32, (BLK, 2 * BLK), 1)
+        row = lax.broadcasted_iota(jnp.int32, (BLK, 2 * BLK), 0)
+        diagonal_ref[...] = jnp.where((column < BLK) & (column > row), NEG, 0.0).astype(jnp.float32)
+        weights_b[...] = jnp.zeros_like(weights_b)
+        slash[BUFFERS - 1, 1] = jnp.zeros(slash.shape[2:], slash.dtype)
         pltpu.make_async_copy(vert, vert, vert_sem).wait()
+        arrived(0)
+        stage(0, 0, 0, 0, True, False, False)
 
     @pl.when(step + 1 < steps)
     def _():
-        fetch(step + 1)
-
-    buffer = lax.rem(step, 2)
-    here = slash.at[buffer]
-    pltpu.make_async_copy(here, here, slash_sem.at[buffer]).wait()
-
-    rate = math.log2(math.e) / math.sqrt(HD)
-    rows = group_heads * BLK
-    row_token = lax.broadcasted_iota(jnp.int32, (rows, 2 * BLK), 0) % BLK
-    column = lax.broadcasted_iota(jnp.int32, (rows, 2 * BLK), 1)
-    diagonal = jnp.where((column < BLK) & (column > row_token), NEG, 0.0).astype(jnp.float32)
-    ones_vert = jnp.ones((NV * BLK, HD), jnp.bfloat16)
-    ones_slash = jnp.ones((NS * BLK, HD), jnp.bfloat16)
-    contract = (((1,), (1,)), ((), ()))
-    for at in range(STEP_BLOCKS):
-        query = jnp.concatenate(
-            [
-                query_ref[at * BLK : (at + 1) * BLK, h * HD : (h + 1) * HD]
-                for h in range(group_heads)
-            ],
-            axis=0,
-        )
-        bias = bias_ref[pl.ds(block_index(step, at), 1), :]
-        vert_scores = lax.dot_general(
-            query, vert[:, :HD], contract, preferred_element_type=jnp.float32
-        )
-        slash_scores = lax.dot_general(
-            query, slash[buffer, at, :, :HD], contract, preferred_element_type=jnp.float32
-        )
-        vert_scores = vert_scores + bias[:, : NV * BLK]
-        slash_scores = slash_scores + bias[:, NV * BLK :]
-        slash_scores = jnp.concatenate(
-            [slash_scores[:, : 2 * BLK] + diagonal, slash_scores[:, 2 * BLK :]], axis=1
-        )
-        row_max = jnp.maximum(
-            jnp.max(vert_scores, axis=1, keepdims=True),
-            jnp.max(slash_scores, axis=1, keepdims=True),
-        )
-        vert_weights = jnp.exp2((vert_scores - row_max) * rate).astype(jnp.bfloat16)
-        slash_weights = jnp.exp2((slash_scores - row_max) * rate).astype(jnp.bfloat16)
-        total = jnp.dot(
-            vert_weights,
-            jnp.concatenate([vert[:, HD:], ones_vert], axis=1),
-            preferred_element_type=jnp.float32,
-        ) + jnp.dot(
-            slash_weights,
-            jnp.concatenate([slash[buffer, at, :, HD:], ones_slash], axis=1),
-            preferred_element_type=jnp.float32,
-        )
-        result = (total[:, :HD] / total[:, HD:]).astype(jnp.bfloat16)
-        for h in range(group_heads):
-            out_ref[at * BLK : (at + 1) * BLK, h * HD : (h + 1) * HD] = result[
-                h * BLK : (h + 1) * BLK
-            ]
+        arrived(step + 1)
+
+    @pl.when(step + 2 < steps)
+    def _():
+        fetch(step + 2)
+
+    first = step * STEP_BLOCKS
+    stage(first + 1, step, 1, step - 1, True, True, True)
+    stage(first + 2, step + 1, 0, step, True, True, True)
+
+    @pl.when(step + 1 == steps)
+    def _():
+        store(weighted_values(slash_of(step, 1), 1), first + 1)
 
 
 def attend(head, part, parity, slot_index, slash, queries, bias, own, two_back, even_back, odd_back,
@@ -201,6 +262,7 @@
     step_rows = STEP_BLOCKS * BLK
     steps = part_rows // step_rows
     any_spec = pl.BlockSpec(memory_space=pl.ANY)
+    rows = group_heads * BLK
     keys_seen = (NV + NS) * BLK
     return pl.pallas_call(
         functools.partial(
@@ -211,18 +273,23 @@
             num_scalar_prefetch=4,
             grid=(steps,),
             in_specs=[
-                pl.BlockSpec(
-                    (step_rows, group_cols), lambda s, part, *_: (part[0] * steps + s, head)
-                ),
+                pl.BlockSpec((part_rows, group_cols), lambda s, part, *_: (part[0], head)),
                 pl.BlockSpec(bias.shape, lambda s, *_: (0, 0)),
             ]
             + [any_spec] * (3 + 2 * CHUNKS),
-            out_specs=pl.BlockSpec((step_rows, group_cols), lambda s, *_: (s, 0)),
+            out_specs=pl.BlockSpec((part_rows, group_cols), lambda s, *_: (0, 0)),
             scratch_shapes=[
                 pltpu.VMEM((NV * BLK, 2 * HD), jnp.bfloat16),
-                pltpu.VMEM((2, STEP_BLOCKS, NS * BLK, 2 * HD), jnp.bfloat16),
+                pltpu.VMEM((BUFFERS, STEP_BLOCKS, NS * BLK, 2 * HD), jnp.bfloat16),
+                pltpu.VMEM((rows, keys_seen), jnp.float32),
+                pltpu.VMEM((rows, keys_seen), jnp.float32),
+                pltpu.VMEM((rows, keys_seen), jnp.bfloat16),
+                pltpu.VMEM((rows, keys_seen), jnp.bfloat16),
+                pltpu.VMEM((rows, HD), jnp.float32),
+                pltpu.VMEM((rows, HD), jnp.float32),
+                pltpu.VMEM((BLK, 2 * BLK), jnp.float32),
                 pltpu.SemaphoreType.DMA,
-                pltpu.SemaphoreType.DMA((2,)),
+                pltpu.SemaphoreType.DMA((BUFFERS,)),
             ],
         ),
         compiler_params=pltpu.CompilerParams(
@@ -276,15 +343,20 @@
     odd_to_even = [(i, i - 1) for i in range(1, shard_count, 2)]
     chunk_rows = tok_rows // CHUNKS
     windows = []
+    before = gathered
     for head in range(kv_local):
         columns = slice(head * HD, (head + 1) * HD)
         own = jnp.concatenate([keys[:, columns], values[:, columns]], axis=1)
+        own, before = lax.optimization_barrier((own, before))
+        if head == 0:
+            gathered = before
         two_back = [
             lax.ppermute(own[c * chunk_rows : (c + 1) * chunk_rows], "ctx", two_pairs)
             for c in range(CHUNKS)
         ]
         odd_back = lax.ppermute(own, "ctx", even_to_odd)
         even_back = [lax.ppermute(piece, "ctx", odd_to_even) for piece in two_back]
+        two_back[-1], before = lax.optimization_barrier((two_back[-1], two_back[-1][:8]))
         windows.append((own, two_back, even_back, odd_back))
 
     parity = (shard_index % 2).reshape(1).astype(jnp.int32)

time: 214 us -> 215 us (level)
  the two profiles are of different devices: /device:TPU:31 before, /device:TPU:15 now
where the time goes in v2:
time: 215 us; the launch traced here: 214 us
  Pallas kernels  80.7 us (38%)
  starting transfers between devices  62.3 us (29%)
  waiting for transfers between devices  37.6 us (17%)
  local copies, waits for them, and re-layouts  16.2 us (8%)
  between operations  13.8 us (6%)
  other arithmetic  3.65 us (2%)
    pallas_call x8, Pallas kernels, attend(): pl.pallas_call(functools.partial(attend_kernel, head, steps, group_heads,...  79.3 us
    ppermute x4, starting transfers between devices, local(): even_back = [lax.ppermute(piece, 'ctx', odd_to_even) for piece in two_back]  39.5 us
    all_gather x1, waiting for transfers between devices, local(): gathered = lax.all_gather(owned_slots(local_block, keys, values), 'ctx')  23.9 us
    ppermute x4, starting transfers between devices, local(): lax.ppermute(own[c * chunk_rows:(c + 1) * chunk_rows], 'ctx', two_pairs)  12.8 us
    ppermute x4, waiting for transfers between devices, local(): lax.ppermute(own[c * chunk_rows:(c + 1) * chunk_rows], 'ctx', two_pairs)  12.7 us
    ppermute x6, starting transfers between devices, local(): lax.ppermute(piece, 'head', [(i, i ^ flip) for i in range(head_count)])  7.34 us
    unnamed x18, local copies, waits for them, and re-layouts  6.67 us
  transfers between devices with their start and end apart: 17, of which 3 were waited for; matrix products, arithmetic and copies ran while one was open for 5% of the time, Pallas kernels for 37%

profile of v2, /device:TPU:15, one launch (start us, length us, event | category | flops | bytes accessed | tf_op | source)
XLA Modules:
  0.0 214.3 jit_solution(11186079209818225077)
XLA Ops:
  6.5 0.7 and_select_fusion
  7.2 0.7 broadcast_compare_fusion.1
  7.9 0.2 convert_reduce_fusion
  8.1 0.2 select_reduce_fusion.1.local_ref
  8.3 1.2 copy-done.4
  9.5 1.2 copy-done.5
  10.7 1.4 shard_map.55
  12.2 0.4 fusion.2
  12.5 0.1 pad_maximum_fusion.1.own_ref
  12.7 1.3 collective-permute-start.12
  14.0 0.9 fusion.1
  14.8 3.2 %collective-permute-start.9 = (bf16[1024,256]{1,0:T(8,128)(2,1)S(1)}, bf16[1024,256]{1,0:T(8,128)(2,1)}, u32[]{:S(2)}, u32[]{:S(2)}) collective-permute-start(bf16[1024,256]{1,0:T(8,128)(2,1)S(1)} %get-tuple-element.11), channel_id=1, source_target_pairs={{0,8},{4,12},{8,16},{12,20},{16,24},{20,28},{1,9},{5,13},{9,17},{1... | collective-permute-start | bytes 1572872 | tf_op jit(solution)/shard_map/ppermute | solution.py:354
  18.0 3.2 %collective-permute-start.8 = (bf16[1024,256]{1,0:T(8,128)(2,1)}, bf16[1024,256]{1,0:T(8,128)(2,1)}, u32[]{:S(2)}, u32[]{:S(2)}) collective-permute-start(bf16[1024,256]{1,0:T(8,128)(2,1)} %get-tuple-element.12), channel_id=1, source_target_pairs={{0,8},{4,12},{8,16},{12,20},{16,24},{20,28},{1,9},{5,13},{9,17},{1... | collective-permute-start | bytes 1572872 | tf_op jit(solution)/shard_map/ppermute | solution.py:354
  21.3 0.2 convert_reduce_fusion.1
  21.7 1.1 pad_maximum_fusion.own_ref
  22.8 12.7 %collective-permute-done.9.rest_1_ = bf16[1024,256]{1,0:T(8,128)(2,1)} collective-permute-done((bf16[1024,256]{1,0:T(8,128)(2,1)S(1)}, bf16[1024,256]{1,0:T(8,128)(2,1)}, u32[]{:S(2)}, u32[]{:S(2)}) %collective-permute-start.9) | collective-permute-done | bytes 524320 | tf_op jit(solution)/shard_map/ppermute | solution.py:354
  35.5 8.1 %collective-permute-start.11 = (bf16[1024,256]{1,0:T(8,128)(2,1)}, bf16[1024,256]{1,0:T(8,128)(2,1)}, u32[]{:S(2)}, u32[]{:S(2)}) collective-permute-start(bf16[1024,256]{1,0:T(8,128)(2,1)} %collective-permute-done.9.rest_1_), channel_id=1, source_target_pairs={{4,0},{12,8},{20,16},{28,24},{5,1},{13,9},{21,17},{29,25},{6,2},{1... | collective-permute-start | bytes 1572872 | tf_op jit(solution)/shard_map/ppermute | solution.py:358
  43.6 0.1 compare_reduce_fusion
  43.7 23.9 %all-gather.3.cloned.1.call-done = bf16[16,256,256]{2,1,0:T(8,128)(2,1)} async-done(((bf16[2,256,256]{2,1,0:T(8,128)(2,1)}), bf16[16,256,256]{2,1,0:T(8,128)(2,1)}) %all-gather.3.cloned.1.call-update) | async-done | bytes 2097168 | tf_op jit(solution)/shard_map/all_gather | solution.py:327
  67.6 1.4 collective-permute-start.4
  69.1 2.3 %fusion.4 = (bf16[1024,256]{1,0:T(8,128)(2,1)}, bf16[1024,256]{1,0:T(8,128)(2,1)}) fusion(bf16[2048,256]{1,0:T(8,128)(2,1)} %pad_maximum_fusion.own_ref), kind=kLoop, calls=%fused_computation.39 | loop fusion | bytes 2097152 | tf_op jit(solution)/shard_map/slice | solution.py:354
  71.3 2.4 %collective-permute-start.1 = (bf16[1024,256]{1,0:T(8,128)(2,1)}, bf16[1024,256]{1,0:T(8,128)(2,1)}, u32[]{:S(2)}, u32[]{:S(2)}) collective-permute-start(bf16[1024,256]{1,0:T(8,128)(2,1)} %get-tuple-element.17), channel_id=1, source_target_pairs={{0,8},{4,12},{8,16},{12,20},{16,24},{20,28},{1,9},{5,13},{9,17},{1... | collective-permute-start | bytes 1572872 | tf_op jit(solution)/shard_map/ppermute | solution.py:354
  73.7 4.0 %collective-permute-start = (bf16[1024,256]{1,0:T(8,128)(2,1)}, bf16[1024,256]{1,0:T(8,128)(2,1)}, u32[]{:S(2)}, u32[]{:S(2)}) collective-permute-start(bf16[1024,256]{1,0:T(8,128)(2,1)} %get-tuple-element.18), channel_id=1, source_target_pairs={{0,8},{4,12},{8,16},{12,20},{16,24},{20,28},{1,9},{5,13},{9,17},{1... | collective-permute-start | bytes 1572872 | tf_op jit(solution)/shard_map/ppermute | solution.py:354
  77.8 0.1 copy.6
  78.0 11.6 %collective-permute-start.10 = (bf16[1024,256]{1,0:T(8,128)(2,1)}, bf16[1024,256]{1,0:T(8,128)(2,1)}, u32[]{:S(2)}, u32[]{:S(2)}) collective-permute-start(bf16[1024,256]{1,0:T(8,128)(2,1)} %collective-permute-done.8.rest_0_), channel_id=1, source_target_pairs={{4,0},{12,8},{20,16},{28,24},{5,1},{13,9},{21,17},{29,25},{6,2},{1... | collective-permute-start | bytes 1572872 | tf_op jit(solution)/shard_map/ppermute | solution.py:358
  89.7 8.5 %collective-permute-start.3 = (bf16[1024,256]{1,0:T(8,128)(2,1)}, bf16[1024,256]{1,0:T(8,128)(2,1)}, u32[]{:S(2)}, u32[]{:S(2)}) collective-permute-start(bf16[1024,256]{1,0:T(8,128)(2,1)} %collective-permute-done.1.rest_1_), channel_id=1, source_target_pairs={{4,0},{12,8},{20,16},{28,24},{5,1},{13,9},{21,17},{29,25},{6,2},{1... | collective-permute-start | bytes 1572872 | tf_op jit(solution)/shard_map/ppermute | solution.py:358
  98.2 11.2 %collective-permute-start.2 = (bf16[1024,256]{1,0:T(8,128)(2,1)}, bf16[1024,256]{1,0:T(8,128)(2,1)}, u32[]{:S(2)}, u32[]{:S(2)}) collective-permute-start(bf16[1024,256]{1,0:T(8,128)(2,1)} %collective-permute-done.rest_0_), channel_id=1, source_target_pairs={{4,0},{12,8},{20,16},{28,24},{5,1},{13,9},{21,17},{29,25},{6,2},{1... | collective-permute-start | bytes 1572872 | tf_op jit(solution)/shard_map/ppermute | solution.py:358
  109.4 0.9 broadcast_in_dim.21
  110.4 1.1 broadcast_in_dim.22.bias_ref
  111.5 0.9 broadcast_in_dim.19
  112.5 1.1 broadcast_in_dim.20.bias_ref
  113.7 2.2 %copy-done = bf16[2048,1024]{1,0:T(8,128)(2,1)S(1)} copy-done((bf16[2048,1024]{1,0:T(8,128)(2,1)S(1)}, bf16[2048,1024]{1,0:T(8,128)(2,1)}, u32[]{:S(2)}) %copy-start) | copy-done | bytes 4194328
  115.8 9.5 %shard_map.60 = bf16[512,512]{1,0:T(8,128)(2,1)S(1)} custom-call(s32[1]{0:T(128)} %bitcast.part_ref, s32[1]{0:T(128)} %bitcast.1.parity_ref, s32[2,16]{1,0:T(2,128)S(1)} %multiply_add_fusion.slot_ref, s32[2,8]{1,0:T(2,128)S(1)} %select_reduce_fusion.slash_ref, bf16[2048,1024]{1,0:T(8,128)(2,1)S(1)} %copy-done, f32[32,1536]{1,0:T(8,128)S(1)} %broadcast_in_dim.22.bias_ref, ...), custom_call_target="tpu_custom_call" | custom-call | flops 1610612736 | bytes 4194304 | tf_op jit(solution)/shard_map/pallas_call | solution.py:267
  125.3 4.0 %collective-permute-start.13 = (bf16[512,512]{1,0:T(8,128)(2,1)S(1)}, bf16[512,512]{1,0:T(8,128)(2,1)S(1)}, u32[]{:S(2)}, u32[]{:S(2)}) collective-permute-start(bf16[512,512]{1,0:T(8,128)(2,1)S(1)} %shard_map.60), channel_id=1, source_target_pairs={{0,3},{1,2},{2,1},{3,0},{4,7},{5,6},{6,5},{7,4},{8,11},{9,10},{10,... | collective-permute-start | bytes 1572872 | tf_op jit(solution)/shard_map/ppermute | solution.py:373
  129.3 9.5 %shard_map.61 = bf16[512,512]{1,0:T(8,128)(2,1)S(1)} custom-call(s32[1]{0:T(128)} %bitcast.4.part_ref, s32[1]{0:T(128)} %bitcast.1.parity_ref, s32[2,16]{1,0:T(2,128)S(1)} %multiply_add_fusion.slot_ref, s32[2,8]{1,0:T(2,128)S(1)} %select_reduce_fusion.slash_ref, bf16[2048,1024]{1,0:T(8,128)(2,1)S(1)} %copy-done.1, f32[32,1536]{1,0:T(8,128)S(1)} %broadcast_in_dim.22.bias_ref, ...), custom_call_target="tpu_custom_call" | custom-call | flops 1610612736 | bytes 4194304 | tf_op jit(solution)/shard_map/pallas_call | solution.py:267
  138.8 0.8 collective-permute-start.14
  139.7 9.8 %shard_map.62 = bf16[512,512]{1,0:T(8,128)(2,1)S(1)} custom-call(s32[1]{0:T(128)} %bitcast.5.part_ref, s32[1]{0:T(128)} %bitcast.1.parity_ref, s32[2,16]{1,0:T(2,128)S(1)} %multiply_add_fusion.slot_ref, s32[2,8]{1,0:T(2,128)S(1)} %select_reduce_fusion.slash_ref, bf16[2048,1024]{1,0:T(8,128)(2,1)S(1)} %copy-done.1, f32[32,1536]{1,0:T(8,128)S(1)} %broadcast_in_dim.22.bias_ref, ...), custom_call_target="tpu_custom_call" | custom-call | flops 1610612736 | bytes 4194304 | tf_op jit(solution)/shard_map/pallas_call | solution.py:267
  149.5 9.8 %shard_map.56 = bf16[512,512]{1,0:T(8,128)(2,1)S(1)} custom-call(s32[1]{0:T(128)} %bitcast.part_ref, s32[1]{0:T(128)} %bitcast.1.parity_ref, s32[2,16]{1,0:T(2,128)S(1)} %multiply_add_fusion.slot_ref, s32[2,8]{1,0:T(2,128)S(1)} %select_reduce_fusion.slash_ref, bf16[2048,1024]{1,0:T(8,128)(2,1)S(1)} %copy-done.1, f32[32,1536]{1,0:T(8,128)S(1)} %broadcast_in_dim.20.bias_ref, ...), custom_call_target="tpu_custom_call" | custom-call | flops 1610612736 | bytes 4194304 | tf_op jit(solution)/shard_map/pallas_call | solution.py:267
  159.2 0.9 collective-permute-start.5
  160.2 10.0 %shard_map.57 = bf16[512,512]{1,0:T(8,128)(2,1)S(1)} custom-call(s32[1]{0:T(128)} %bitcast.4.part_ref, s32[1]{0:T(128)} %bitcast.1.parity_ref, s32[2,16]{1,0:T(2,128)S(1)} %multiply_add_fusion.slot_ref, s32[2,8]{1,0:T(2,128)S(1)} %select_reduce_fusion.slash_ref, bf16[2048,1024]{1,0:T(8,128)(2,1)S(1)} %copy-done.1, f32[32,1536]{1,0:T(8,128)S(1)} %broadcast_in_dim.20.bias_ref, ...), custom_call_target="tpu_custom_call" | custom-call | flops 1610612736 | bytes 4194304 | tf_op jit(solution)/shard_map/pallas_call | solution.py:267
  170.2 1.4 collective-permute-start.6
  171.6 10.2 %shard_map.58 = bf16[512,512]{1,0:T(8,128)(2,1)S(1)} custom-call(s32[1]{0:T(128)} %bitcast.5.part_ref, s32[1]{0:T(128)} %bitcast.1.parity_ref, s32[2,16]{1,0:T(2,128)S(1)} %multiply_add_fusion.slot_ref, s32[2,8]{1,0:T(2,128)S(1)} %select_reduce_fusion.slash_ref, bf16[2048,1024]{1,0:T(8,128)(2,1)S(1)} %copy-done.1, f32[32,1536]{1,0:T(8,128)S(1)} %broadcast_in_dim.20.bias_ref, ...), custom_call_target="tpu_custom_call" | custom-call | flops 1610612736 | bytes 4194304 | tf_op jit(solution)/shard_map/pallas_call | solution.py:267
  181.9 10.1 %shard_map.63 = bf16[512,512]{1,0:T(8,128)(2,1)S(1)} custom-call(s32[1]{0:T(128)} %bitcast.6.part_ref, s32[1]{0:T(128)} %bitcast.1.parity_ref, s32[2,16]{1,0:T(2,128)S(1)} %multiply_add_fusion.slot_ref, s32[2,8]{1,0:T(2,128)S(1)} %select_reduce_fusion.slash_ref, bf16[2048,1024]{1,0:T(8,128)(2,1)S(1)} %copy-done.1, f32[32,1536]{1,0:T(8,128)S(1)} %broadcast_in_dim.22.bias_ref, ...), custom_call_target="tpu_custom_call" | custom-call | flops 1610612736 | bytes 4194304 | tf_op jit(solution)/shard_map/pallas_call | solution.py:267
  192.0 10.5 %shard_map.59 = bf16[512,512]{1,0:T(8,128)(2,1)S(1)} custom-call(s32[1]{0:T(128)} %bitcast.6.part_ref, s32[1]{0:T(128)} %bitcast.1.parity_ref, s32[2,16]{1,0:T(2,128)S(1)} %multiply_add_fusion.slot_ref, s32[2,8]{1,0:T(2,128)S(1)} %select_reduce_fusion.slash_ref, bf16[2048,1024]{1,0:T(8,128)(2,1)S(1)} %copy-done.1, f32[32,1536]{1,0:T(8,128)S(1)} %broadcast_in_dim.20.bias_ref, ...), custom_call_target="tpu_custom_call" | custom-call | flops 1610612736 | bytes 4194304 | tf_op jit(solution)/shard_map/pallas_call | solution.py:267
  202.7 0.5 broadcast_in_dim.16
  203.7 0.9 collective-permute-done.15
  204.6 2.0 copy-done.6
  206.7 0.8 constant_dynamic-update-slice_fusion.7
  (49 shorter events, 1.1 us)
Async XLA Ops:
  6.5 61.1 %all-gather.3.cloned.1.call-start = ((), (), s32[]{:S(2)}) async-start(), calls=%async_computation | async-start | bytes 2359296 | tf_op jit(solution)/shard_map/all_gather | solution.py:327
  8.3 1.2 copy-start.4
  9.5 1.2 copy-start.5
  12.2 9.1 %copy-start.8 = (s32[2,8]{1,0:T(2,128)S(1)}, s32[2,8]{1,0:T(2,128)}, u32[]{:S(2)}) copy-start(s32[2,8]{1,0:T(2,128)} %param.9) | copy-start | bytes 196
  12.2 9.4 %copy-start.7 = (s32[2,16]{1,0:T(2,128)S(1)}, s32[2,16]{1,0:T(2,128)}, u32[]{:S(2)}) copy-start(s32[2,16]{1,0:T(2,128)} %param.8) | copy-start | bytes 388
  12.7 101.0 %collective-permute-start.12 = (bf16[2048,256]{1,0:T(8,128)(2,1)S(1)}, bf16[2048,256]{1,0:T(8,128)(2,1)}, u32[]{:S(2)}, u32[]{:S(2)}) collective-permute-start(bf16[2048,256]{1,0:T(8,128)(2,1)S(1)} %pad_maximum_fusion.1.own_ref), channel_id=1, source_target_pairs={{0,4},{8,12},{16,20},{24,28},{1,5},{9,13},{17,21},{25,29},{2,6},{1... | collective-permute-start | bytes 3145736 | tf_op jit(solution)/shard_map/ppermute | solution.py:357
  14.8 20.7 %collective-permute-start.9 = (bf16[1024,256]{1,0:T(8,128)(2,1)S(1)}, bf16[1024,256]{1,0:T(8,128)(2,1)}, u32[]{:S(2)}, u32[]{:S(2)}) collective-permute-start(bf16[1024,256]{1,0:T(8,128)(2,1)S(1)} %get-tuple-element.11), channel_id=1, source_target_pairs={{0,8},{4,12},{8,16},{12,20},{16,24},{20,28},{1,9},{5,13},{9,17},{1... | collective-permute-start | bytes 1572872 | tf_op jit(solution)/shard_map/ppermute | solution.py:354
  18.0 55.7 %collective-permute-start.8 = (bf16[1024,256]{1,0:T(8,128)(2,1)}, bf16[1024,256]{1,0:T(8,128)(2,1)}, u32[]{:S(2)}, u32[]{:S(2)}) collective-permute-start(bf16[1024,256]{1,0:T(8,128)(2,1)} %get-tuple-element.12), channel_id=1, source_target_pairs={{0,8},{4,12},{8,16},{12,20},{16,24},{20,28},{1,9},{5,13},{9,17},{1... | collective-permute-start | bytes 1572872 | tf_op jit(solution)/shard_map/ppermute | solution.py:354
  35.5 42.4 %collective-permute-start.11 = (bf16[1024,256]{1,0:T(8,128)(2,1)}, bf16[1024,256]{1,0:T(8,128)(2,1)}, u32[]{:S(2)}, u32[]{:S(2)}) collective-permute-start(bf16[1024,256]{1,0:T(8,128)(2,1)} %collective-permute-done.9.rest_1_), channel_id=1, source_target_pairs={{4,0},{12,8},{20,16},{28,24},{5,1},{13,9},{21,17},{29,25},{6,2},{1... | collective-permute-start | bytes 1572872 | tf_op jit(solution)/shard_map/ppermute | solution.py:358
  67.6 46.0 %copy-start.2 = (bf16[16,256,256]{2,1,0:T(8,128)(2,1)S(1)}, bf16[16,256,256]{2,1,0:T(8,128)(2,1)}, u32[]{:S(2)}) copy-start(bf16[16,256,256]{2,1,0:T(8,128)(2,1)} %all-gather.3.cloned.1.call-done) | copy-start | bytes 6291460
  67.6 81.8 %collective-permute-start.4 = (bf16[2048,256]{1,0:T(8,128)(2,1)}, bf16[2048,256]{1,0:T(8,128)(2,1)}, u32[]{:S(2)}, u32[]{:S(2)}) collective-permute-start(bf16[2048,256]{1,0:T(8,128)(2,1)} %pad_maximum_fusion.own_ref), channel_id=1, source_target_pairs={{0,4},{8,12},{16,20},{24,28},{1,5},{9,13},{17,21},{25,29},{2,6},{1... | collective-permute-start | bytes 3145736 | tf_op jit(solution)/shard_map/ppermute | solution.py:357
  71.3 18.4 %collective-permute-start.1 = (bf16[1024,256]{1,0:T(8,128)(2,1)}, bf16[1024,256]{1,0:T(8,128)(2,1)}, u32[]{:S(2)}, u32[]{:S(2)}) collective-permute-start(bf16[1024,256]{1,0:T(8,128)(2,1)} %get-tuple-element.17), channel_id=1, source_target_pairs={{0,8},{4,12},{8,16},{12,20},{16,24},{20,28},{1,9},{5,13},{9,17},{1... | collective-permute-start | bytes 1572872 | tf_op jit(solution)/shard_map/ppermute | solution.py:354
  73.7 24.5 %collective-permute-start = (bf16[1024,256]{1,0:T(8,128)(2,1)}, bf16[1024,256]{1,0:T(8,128)(2,1)}, u32[]{:S(2)}, u32[]{:S(2)}) collective-permute-start(bf16[1024,256]{1,0:T(8,128)(2,1)} %get-tuple-element.18), channel_id=1, source_target_pairs={{0,8},{4,12},{8,16},{12,20},{16,24},{20,28},{1,9},{5,13},{9,17},{1... | collective-permute-start | bytes 1572872 | tf_op jit(solution)/shard_map/ppermute | solution.py:354
  78.0 35.7 %collective-permute-start.10 = (bf16[1024,256]{1,0:T(8,128)(2,1)}, bf16[1024,256]{1,0:T(8,128)(2,1)}, u32[]{:S(2)}, u32[]{:S(2)}) collective-permute-start(bf16[1024,256]{1,0:T(8,128)(2,1)} %collective-permute-done.8.rest_0_), channel_id=1, source_target_pairs={{4,0},{12,8},{20,16},{28,24},{5,1},{13,9},{21,17},{29,25},{6,2},{1... | collective-permute-start | bytes 1572872 | tf_op jit(solution)/shard_map/ppermute | solution.py:358
  89.7 59.7 %collective-permute-start.3 = (bf16[1024,256]{1,0:T(8,128)(2,1)}, bf16[1024,256]{1,0:T(8,128)(2,1)}, u32[]{:S(2)}, u32[]{:S(2)}) collective-permute-start(bf16[1024,256]{1,0:T(8,128)(2,1)} %collective-permute-done.1.rest_1_), channel_id=1, source_target_pairs={{4,0},{12,8},{20,16},{28,24},{5,1},{13,9},{21,17},{29,25},{6,2},{1... | collective-permute-start | bytes 1572872 | tf_op jit(solution)/shard_map/ppermute | solution.py:358
  98.2 51.2 %collective-permute-start.2 = (bf16[1024,256]{1,0:T(8,128)(2,1)}, bf16[1024,256]{1,0:T(8,128)(2,1)}, u32[]{:S(2)}, u32[]{:S(2)}) collective-permute-start(bf16[1024,256]{1,0:T(8,128)(2,1)} %collective-permute-done.rest_0_), channel_id=1, source_target_pairs={{4,0},{12,8},{20,16},{28,24},{5,1},{13,9},{21,17},{29,25},{6,2},{1... | collective-permute-start | bytes 1572872 | tf_op jit(solution)/shard_map/ppermute | solution.py:358
  113.7 2.2 %copy-start = (bf16[2048,1024]{1,0:T(8,128)(2,1)S(1)}, bf16[2048,1024]{1,0:T(8,128)(2,1)}, u32[]{:S(2)}) copy-start(bf16[2048,1024]{1,0:T(8,128)(2,1)} %query_ref.15) | copy-start | bytes 12582916
  115.8 13.5 %copy-start.1 = (bf16[2048,1024]{1,0:T(8,128)(2,1)S(1)}, bf16[2048,1024]{1,0:T(8,128)(2,1)}, u32[]{:S(2)}) copy-start(bf16[2048,1024]{1,0:T(8,128)(2,1)} %query_ref.15) | copy-start | bytes 12582916
  125.3 78.2 %collective-permute-start.13 = (bf16[512,512]{1,0:T(8,128)(2,1)S(1)}, bf16[512,512]{1,0:T(8,128)(2,1)S(1)}, u32[]{:S(2)}, u32[]{:S(2)}) collective-permute-start(bf16[512,512]{1,0:T(8,128)(2,1)S(1)} %shard_map.60), channel_id=1, source_target_pairs={{0,3},{1,2},{2,1},{3,0},{4,7},{5,6},{6,5},{7,4},{8,11},{9,10},{10,... | collective-permute-start | bytes 1572872 | tf_op jit(solution)/shard_map/ppermute | solution.py:373
  138.8 64.8 %collective-permute-start.14 = (bf16[512,512]{1,0:T(8,128)(2,1)S(1)}, bf16[512,512]{1,0:T(8,128)(2,1)S(1)}, u32[]{:S(2)}, u32[]{:S(2)}) collective-permute-start(bf16[512,512]{1,0:T(8,128)(2,1)S(1)} %shard_map.61), channel_id=1, source_target_pairs={{0,2},{1,3},{2,0},{3,1},{4,6},{5,7},{6,4},{7,5},{8,10},{9,11},{10,... | collective-permute-start | bytes 1572872 | tf_op jit(solution)/shard_map/ppermute | solution.py:373
  139.7 9.8 %copy-start.3 = (bf16[2048,256]{1,0:T(8,128)(2,1)S(1)}, bf16[2048,256]{1,0:T(8,128)(2,1)}, u32[]{:S(2)}) copy-start(bf16[2048,256]{1,0:T(8,128)(2,1)} %pad_maximum_fusion.own_ref) | copy-start | bytes 3145732
  159.2 43.3 %collective-permute-start.5 = (bf16[512,512]{1,0:T(8,128)(2,1)S(1)}, bf16[512,512]{1,0:T(8,128)(2,1)S(1)}, u32[]{:S(2)}, u32[]{:S(2)}) collective-permute-start(bf16[512,512]{1,0:T(8,128)(2,1)S(1)} %shard_map.56), channel_id=1, source_target_pairs={{0,3},{1,2},{2,1},{3,0},{4,7},{5,6},{6,5},{7,4},{8,11},{9,10},{10,... | collective-permute-start | bytes 1572872 | tf_op jit(solution)/shard_map/ppermute | solution.py:373
  170.2 33.0 %collective-permute-start.6 = (bf16[512,512]{1,0:T(8,128)(2,1)S(1)}, bf16[512,512]{1,0:T(8,128)(2,1)S(1)}, u32[]{:S(2)}, u32[]{:S(2)}) collective-permute-start(bf16[512,512]{1,0:T(8,128)(2,1)S(1)} %shard_map.57), channel_id=1, source_target_pairs={{0,2},{1,3},{2,0},{3,1},{4,6},{5,7},{6,4},{7,5},{8,10},{9,11},{10,... | collective-permute-start | bytes 1572872 | tf_op jit(solution)/shard_map/ppermute | solution.py:373
  181.9 21.5 %collective-permute-start.7 = (bf16[512,512]{1,0:T(8,128)(2,1)S(1)}, bf16[512,512]{1,0:T(8,128)(2,1)S(1)}, u32[]{:S(2)}, u32[]{:S(2)}) collective-permute-start(bf16[512,512]{1,0:T(8,128)(2,1)S(1)} %shard_map.58), channel_id=1, source_target_pairs={{0,1},{1,0},{2,3},{3,2},{4,5},{5,4},{6,7},{7,6},{8,9},{9,8},{10,11... | collective-permute-start | bytes 1572872 | tf_op jit(solution)/shard_map/ppermute | solution.py:373
  202.6 2.0 collective-permute-start.15
  204.6 2.0 copy-start.6
Sparse Core Ops, SparseCore 0:
  12.3 55.3 all-gather.2

commit v3 on v2

v3 whole, which is shorter than its diff:
```python
import functools
import math

import jax
import jax.numpy as jnp
from jax import lax
from jax.experimental import pallas as pl
from jax.experimental.pallas import tpu as pltpu
from jax.sharding import PartitionSpec as P

HD = 128
BLK = 64
NV = 16
NS = 8
MOWN = 4
LOOK = 2
NEG = -1e30
STEP_BLOCKS = 2
CHUNKS = 2
TILE = 256
ANY = pl.BlockSpec(memory_space=pl.ANY)
SMEM = pl.BlockSpec(memory_space=pltpu.SMEM)


def blocks_at(index, count=1):
    return pl.ds(pl.multiple_of(index * BLK, BLK), count * BLK)


def slots_kernel(local_ref, keys_ref, values_ref, out_ref, sem):
    copies = []
    for head in range(out_ref.shape[0]):
        for slot in range(MOWN):
            for side, source in enumerate((keys_ref, values_ref)):
                copies.append(
                    pltpu.make_async_copy(
                        source.at[blocks_at(local_ref[head, slot]), pl.ds(head * HD, HD)],
                        out_ref.at[head, pl.ds(slot * BLK, BLK), pl.ds(side * HD, HD)],
                        sem.at[len(copies)],
                    )
                )
    for copy in copies:
        copy.start()
    for copy in copies:
        copy.wait()


def owned_slots(local_block, keys, values):
    heads = local_block.shape[0]
    return pl.pallas_call(
        slots_kernel,
        out_shape=jax.ShapeDtypeStruct((heads, MOWN * BLK, 2 * HD), keys.dtype),
        in_specs=[SMEM, ANY, ANY],
        out_specs=ANY,
        scratch_shapes=[pltpu.SemaphoreType.DMA((heads * MOWN * 2,))],
        compiler_params=pltpu.CompilerParams(vmem_limit_bytes=1 << 20),
        cost_estimate=pl.CostEstimate(
            flops=0, bytes_accessed=4 * heads * MOWN * BLK * 2 * HD, transcendentals=0
        ),
    )(local_block, keys, values)


def pair_kernel(head, keys_ref, values_ref, *rest):
    out_ref, sem = rest[-2:]
    copies = [
        pltpu.make_async_copy(
            source.at[:, pl.ds(head * HD, HD)], out_ref.at[:, pl.ds(side * HD, HD)], sem.at[side]
        )
        for side, source in enumerate((keys_ref, values_ref))
    ]
    for copy in copies:
        copy.start()
    for copy in copies:
        copy.wait()


def pair_of(head, keys, values, after):
    return pl.pallas_call(
        functools.partial(pair_kernel, head),
        out_shape=jax.ShapeDtypeStruct((keys.shape[0], 2 * HD), keys.dtype),
        in_specs=[ANY] * (2 + len(after)),
        out_specs=ANY,
        scratch_shapes=[pltpu.SemaphoreType.DMA((2,))],
        compiler_params=pltpu.CompilerParams(vmem_limit_bytes=1 << 20),
        cost_estimate=pl.CostEstimate(
            flops=0, bytes_accessed=8 * keys.shape[0] * HD, transcendentals=0
        ),
    )(keys, values, *after)


def listed_kernel(place_ref, source_ref, *rest):
    arrays, out_ref, sem = rest[:-2], rest[-2], rest[-1]
    heads = out_ref.shape[0]
    for head in range(heads):
        for index, array in enumerate(arrays):
            for slot in range(MOWN):
                place = place_ref[index, head, slot]

                @pl.when(place >= 0)
                def _():
                    pltpu.make_async_copy(
                        array.at[head, pl.ds(slot * BLK, BLK)],
                        out_ref.at[head, blocks_at(place)],
                        sem,
                    ).start()

        for entry in range(NV):

            @pl.when(source_ref[head, entry] < 0)
            def _():
                pltpu.make_async_copy(
                    arrays[0].at[head, pl.ds(0, BLK)],
                    out_ref.at[head, pl.ds(entry * BLK, BLK)],
                    sem,
                ).start()

    pltpu.make_async_copy(out_ref, out_ref, sem).wait()


def listed_blocks(place, source, arrays):
    heads = source.shape[0]
    return pl.pallas_call(
        listed_kernel,
        out_shape=jax.ShapeDtypeStruct((heads, NV * BLK, 2 * HD), arrays[0].dtype),
        in_specs=[SMEM, SMEM] + [ANY] * len(arrays),
        out_specs=ANY,
        scratch_shapes=[pltpu.SemaphoreType.DMA],
        compiler_params=pltpu.CompilerParams(vmem_limit_bytes=1 << 20),
        cost_estimate=pl.CostEstimate(
            flops=0, bytes_accessed=8 * heads * NV * BLK * HD, transcendentals=0
        ),
    )(place, source, *arrays)


def attend_kernel(
    head, parts, part_blocks, group_heads, part_ref, parity_ref, slash_ref, bias_ref, query_ref,
    vert_ref, own_ref, *rest,
):
    two_back = rest[:CHUNKS]
    even_back = rest[CHUNKS : 2 * CHUNKS]
    odd_back = rest[2 * CHUNKS]
    rest = rest[2 * CHUNKS + 1 :]
    out_refs = rest[:parts]
    (
        queries, out, vert, vert_keys, window, scores_a, scores_b, weights_a, weights_b, max_a,
        max_b, diagonal_ref, query_sem, vert_sem, window_sem, out_sem,
    ) = rest[parts:]
    scores, weights, maxima = (scores_a, scores_b), (weights_a, weights_b), (max_a, max_b)
    tok_rows = own_ref.shape[0]
    blocks_dev = tok_rows // BLK
    part_rows = part_blocks * BLK
    group_cols = group_heads * HD
    chunk_rows = tok_rows // CHUNKS
    last = parts * part_blocks - 1
    step = pl.program_id(0)
    scale = 1.0 / math.sqrt(HD)
    contract = (((1,), (1,)), ((), ()))

    def shard_block(block):
        return part_ref[block // part_blocks] * part_blocks + lax.rem(block, part_blocks)

    def slash_rows(block):
        first = LOOK * blocks_dev + shard_block(block)
        return [blocks_at(first - slash_ref[head, entry]) for entry in range(NS)]

    def query_of(block):
        rows = blocks_at(block)
        return jnp.concatenate(
            [queries[rows, h * HD : (h + 1) * HD] for h in range(group_heads)], axis=0
        )

    def score_tile(query, bias, rows, tile):
        low = tile * TILE
        if low < NV * BLK:
            found = jnp.dot(
                query, vert_keys[:, low : low + TILE], preferred_element_type=jnp.float32
            )
        else:
            entry = (low - NV * BLK) // BLK
            keys = jnp.concatenate(
                [window[r, :HD] for r in rows[entry : entry + TILE // BLK]], axis=0
            )
            found = lax.dot_general(query, keys, contract, preferred_element_type=jnp.float32)
        found = found + bias[:, low : low + TILE]
        if low == NV * BLK:
            diagonal = jnp.concatenate([diagonal_ref[...]] * group_heads, axis=0)
            found = jnp.concatenate(
                [found[:, : 2 * BLK] + diagonal, found[:, 2 * BLK :]], axis=1
            )
        return found

    def weighted_values(block, at):
        ones = jnp.ones(((NV + NS) * BLK, HD), jnp.bfloat16)
        values = jnp.concatenate([vert[:, HD:]] + [window[r, HD:] for r in slash_rows(block)], axis=0)
        return jnp.dot(
            weights[at][...],
            jnp.concatenate([values, ones], axis=1),
            preferred_element_type=jnp.float32,
        )

    def store(total, block):
        result = (total[:, :HD] / total[:, HD:]).astype(jnp.bfloat16)
        rows = blocks_at(block)
        for h in range(group_heads):
            out[rows, h * HD : (h + 1) * HD] = result[h * BLK : (h + 1) * BLK]

    def stage(block, at, score, weigh, combine):
        other = 1 - at
        if score:
            fresh = jnp.minimum(block, last)
            query = query_of(fresh)
            rows = slash_rows(fresh)
            bias = bias_ref[pl.ds(shard_block(fresh), 1), :]
        if combine:
            done = jnp.maximum(block - 2, 0)
            total = weighted_values(done, at)
        if weigh:
            row_max = maxima[other][...]
            row_max = jnp.concatenate([row_max] * (TILE // HD), axis=1)
        highest = None
        for tile in range((NV + NS) * BLK // TILE):
            low = tile * TILE
            if score:
                found = score_tile(query, bias, rows, tile)
                scores[at][:, low : low + TILE] = found
                for piece_low in range(0, TILE, HD):
                    piece = found[:, piece_low : piece_low + HD]
                    highest = piece if highest is None else jnp.maximum(highest, piece)
            if weigh:
                weights[other][:, low : low + TILE] = jnp.exp(
                    (scores[other][:, low : low + TILE] - row_max) * scale
                ).astype(jnp.bfloat16)
        if score:
            maxima[at][...] = jnp.broadcast_to(
                jnp.max(highest, axis=1, keepdims=True), highest.shape
            )
        if combine:
            store(total, done)

    @pl.when(step == 0)
    def _():
        for k in range(parts):
            pltpu.make_async_copy(
                query_ref.at[
                    pl.ds(pl.multiple_of(part_ref[k] * part_rows, part_rows), part_rows),
                    pl.ds(head * group_cols, group_cols),
                ],
                queries.at[pl.ds(k * part_rows, part_rows)],
                query_sem,
            ).start()
        pltpu.make_async_copy(vert_ref.at[head], vert, vert_sem).start()
        for chunk in range(CHUNKS):
            pltpu.make_async_copy(
                two_back[chunk], window.at[pl.ds(chunk * chunk_rows, chunk_rows)], window_sem
            ).start()

        @pl.when(parity_ref[0] == 1)
        def _():
            pltpu.make_async_copy(
                odd_back, window.at[pl.ds(tok_rows, tok_rows)], window_sem
            ).start()

        @pl.when(parity_ref[0] == 0)
        def _():
            for chunk in range(CHUNKS):
                pltpu.make_async_copy(
                    even_back[chunk],
                    window.at[pl.ds(tok_rows + chunk * chunk_rows, chunk_rows)],
                    window_sem,
                ).start()

        pltpu.make_async_copy(
            own_ref, window.at[pl.ds(LOOK * tok_rows, tok_rows)], window_sem
        ).start()
        column = lax.broadcasted_iota(jnp.int32, (BLK, 2 * BLK), 1)
        row = lax.broadcasted_iota(jnp.int32, (BLK, 2 * BLK), 0)
        diagonal_ref[...] = jnp.where((column < BLK) & (column > row), NEG, 0.0).astype(jnp.float32)
        weights_b[...] = jnp.zeros_like(weights_b)
        pltpu.make_async_copy(vert, vert, vert_sem).wait()
        vert_keys[...] = vert[:, :HD].T
        pltpu.make_async_copy(queries, queries, query_sem).wait()
        pltpu.make_async_copy(window, window, window_sem).wait()
        stage(0, 0, True, False, False)

    first = step * STEP_BLOCKS
    stage(first + 1, 1, True, True, True)
    stage(first + 2, 0, True, True, True)

    @pl.when(first + STEP_BLOCKS > last)
    def _():
        store(weighted_values(last, 1), last)
        for k in range(parts):
            pltpu.make_async_copy(
                out.at[pl.ds(k * part_rows, part_rows)], out_refs[k], out_sem.at[k]
            ).start()
        for k in range(parts):
            pltpu.make_async_copy(
                out.at[pl.ds(k * part_rows, part_rows)], out_refs[k], out_sem.at[k]
            ).wait()


def attend(head, part, parity, slash, bias, queries, vert, own, two_back, even_back, odd_back,
           part_rows):
    parts = part.shape[0]
    group_cols = queries.shape[1] // slash.shape[0]
    group_heads = group_cols // HD
    part_blocks = part_rows // BLK
    tok_rows = own.shape[0]
    rows = group_heads * BLK
    keys_seen = (NV + NS) * BLK
    return pl.pallas_call(
        functools.partial(attend_kernel, head, parts, part_blocks, group_heads),
        out_shape=[jax.ShapeDtypeStruct((part_rows, group_cols), jnp.bfloat16)] * parts,
        grid_spec=pltpu.PrefetchScalarGridSpec(
            num_scalar_prefetch=3,
            grid=(parts * part_blocks // STEP_BLOCKS,),
            in_specs=[pl.BlockSpec(bias.shape, lambda s, *_: (0, 0))] + [ANY] * (4 + 2 * CHUNKS),
            out_specs=[ANY] * parts,
            scratch_shapes=[
                pltpu.VMEM((parts * part_rows, group_cols), jnp.bfloat16),
                pltpu.VMEM((parts * part_rows, group_cols), jnp.bfloat16),
                pltpu.VMEM((NV * BLK, 2 * HD), jnp.bfloat16),
                pltpu.VMEM((HD, NV * BLK), jnp.bfloat16),
                pltpu.VMEM(((LOOK + 1) * tok_rows, 2 * HD), jnp.bfloat16),
                pltpu.VMEM((rows, keys_seen), jnp.float32),
                pltpu.VMEM((rows, keys_seen), jnp.float32),
                pltpu.VMEM((rows, keys_seen), jnp.bfloat16),
                pltpu.VMEM((rows, keys_seen), jnp.bfloat16),
                pltpu.VMEM((rows, HD), jnp.float32),
                pltpu.VMEM((rows, HD), jnp.float32),
                pltpu.VMEM((BLK, 2 * BLK), jnp.float32),
                pltpu.SemaphoreType.DMA,
                pltpu.SemaphoreType.DMA,
                pltpu.SemaphoreType.DMA,
                pltpu.SemaphoreType.DMA((parts,)),
            ],
        ),
        compiler_params=pltpu.CompilerParams(
            dimension_semantics=("arbitrary",), vmem_limit_bytes=32 << 20
        ),
        cost_estimate=pl.CostEstimate(
            flops=4 * parts * part_rows * group_heads * keys_seen * HD,
            bytes_accessed=4 * parts * part_rows * group_cols + 12 * tok_rows * HD,
            transcendentals=parts * part_rows * group_heads * keys_seen,
        ),
    )(part, parity, slash, bias, queries, vert, own, *two_back, *even_back, odd_back)


def local(queries, keys, values, vertical, slash):
    shard_count = lax.axis_size("ctx")
    shard_index = lax.axis_index("ctx")
    head_count = lax.axis_size("head")
    head_index = lax.axis_index("head")
    tok_rows = queries.shape[0]
    kv_local = keys.shape[1] // HD
    group_cols = queries.shape[1] // kv_local
    blocks_dev = tok_rows // BLK
    part_rows = tok_rows // head_count
    partner = shard_index ^ 1
    two_pairs = [(i, i + 2) for i in range(shard_count - 2)]
    even_to_odd = [(i, i + 1) for i in range(0, shard_count - 1, 2)]
    odd_to_even = [(i, i - 1) for i in range(1, shard_count, 2)]
    chunk_rows = tok_rows // CHUNKS

    owners = vertical // blocks_dev
    order = jnp.arange(NV, dtype=jnp.int32)
    same_owner = owners[:, :, None] == owners[:, None, :]
    earlier = order[None, :] < order[:, None]
    slot_rank = jnp.sum((same_owner & earlier[None]).astype(jnp.int32), axis=2)
    slots = jnp.arange(MOWN, dtype=jnp.int32)
    in_slot = slot_rank[:, :, None] == slots
    local_block = jnp.sum(
        ((owners == shard_index)[:, :, None] & in_slot) * (vertical % blocks_dev)[:, :, None],
        axis=1,
    )
    behind = [owned_slots(local_block, keys, values)]
    for _ in range(1, shard_count // 2):
        behind.append(lax.ppermute(behind[-1], "ctx", two_pairs))
    across = [
        lax.ppermute(array, "ctx", even_to_odd + (odd_to_even if k else []))
        for k, array in enumerate(behind)
    ]
    steps = 2 * jnp.arange(shard_count // 2, dtype=jnp.int32)
    array_owner = jnp.concatenate([shard_index - steps, partner - steps])
    array_owner = jnp.where(array_owner <= shard_index, array_owner, -1)
    here = (array_owner[:, None, None] == owners)[:, :, :, None] & in_slot[None]
    place = jnp.sum(here * (order + 1)[None, None, :, None], axis=2) - 1
    source = jnp.where(owners <= shard_index, 0, -1).astype(jnp.int32)

    slash_rank = jnp.sum((slash[:, None, :] < slash[:, :, None]).astype(jnp.int32), axis=2)
    at_rank = slash_rank[:, :, None] == jnp.arange(NS, dtype=jnp.int32)
    slash = jnp.sum(at_rank * slash[:, :, None], axis=1)

    global_blocks = shard_index * blocks_dev + jnp.arange(blocks_dev, dtype=jnp.int32)
    vert_valid = vertical[:, None, :] < global_blocks[None, :, None]
    slash_blocks = global_blocks[None, :, None] - slash[:, None, :]
    in_vertical = jnp.any(slash_blocks[:, :, :, None] == vertical[:, None, None, :], axis=3)
    slash_valid = (slash[:, None, :] == 0) | ((slash_blocks >= 0) & jnp.logical_not(in_vertical))
    valid = jnp.concatenate([vert_valid, slash_valid], axis=2)
    bias = jnp.repeat(jnp.where(valid, 0.0, NEG).astype(jnp.float32), BLK, axis=2)

    windows = []
    after = []
    for head in range(kv_local):
        own = pair_of(head, keys, values, after)
        two_back = [
            lax.ppermute(own[c * chunk_rows : (c + 1) * chunk_rows], "ctx", two_pairs)
            for c in range(CHUNKS)
        ]
        odd_back = lax.ppermute(own, "ctx", even_to_odd)
        even_back = [lax.ppermute(piece, "ctx", odd_to_even) for piece in two_back]
        windows.append((own, two_back, even_back, odd_back))
        after = [two_back[0]]
    vert = listed_blocks(place, source, behind + across)

    parity = (shard_index % 2).reshape(1).astype(jnp.int32)
    out = jnp.zeros((part_rows, head_count * kv_local * group_cols), jnp.bfloat16)
    half = head_count // 2
    for head in range(kv_local):
        own, two_back, even_back, odd_back = windows[head]
        for flips in (range(head_count - 1, half - 1, -1), range(half - 1, -1, -1)):
            others = [head_index ^ flip for flip in flips]
            pieces = attend(
                head, jnp.stack(others).astype(jnp.int32), parity, slash, bias[head], queries,
                vert, own, two_back, even_back, odd_back, part_rows,
            )
            for flip, other, piece in zip(flips, others, pieces):
                if flip:
                    piece = lax.ppermute(piece, "head", [(i, i ^ flip) for i in range(head_count)])
                out = lax.dynamic_update_slice(
                    out, piece, (0, other * kv_local * group_cols + head * group_cols)
                )
    return out


def solution(mesh):
    in_specs = (
        P("ctx", "head"),
        P("ctx", "head"),
        P("ctx", "head"),
        P("head", None),
        P("head", None),
    )
    out_specs = P(("ctx", "head"), None)
    return jax.shard_map(local, mesh=mesh, in_specs=in_specs, out_specs=out_specs, check_vma=False)
```

time: 215 us -> 184 us (0.86)
  the two profiles are of different devices: /device:TPU:15 before, /device:TPU:0 now
where the time goes in v3:
time: 184 us; the launch traced here: 183 us
  Pallas kernels  58.7 us (32%)
  waiting for transfers between devices  54 us (29%)
  starting transfers between devices  51.9 us (28%)
  local copies, waits for them, and re-layouts  15.5 us (8%)
  other arithmetic  2.98 us (2%)
    pallas_call x4, Pallas kernels, attend(): pl.pallas_call(functools.partial(attend_kernel, head, parts, part_blocks,...  54.9 us
    ppermute x3, waiting for transfers between devices, local(): behind.append(lax.ppermute(behind[-1], 'ctx', two_pairs))  20.3 us
    ppermute x6, waiting for transfers between devices, local(): lax.ppermute(piece, 'head', [(i, i ^ flip) for i in range(head_count)])  16.1 us
    ppermute x4, starting transfers between devices, local(): lax.ppermute(own[c * chunk_rows:(c + 1) * chunk_rows], 'ctx', two_pairs)  12.7 us
    ppermute x4, waiting for transfers between devices, local(): lax.ppermute(array, 'ctx', even_to_odd + (odd_to_even if k else []))  12.6 us
    ppermute x3, starting transfers between devices, local(): behind.append(lax.ppermute(behind[-1], 'ctx', two_pairs))  11.3 us
    ppermute x4, starting transfers between devices, local(): lax.ppermute(array, 'ctx', even_to_odd + (odd_to_even if k else []))  11.1 us
    ppermute x2, starting transfers between devices, local(): odd_back = lax.ppermute(own, 'ctx', even_to_odd)  6.94 us
  transfers between devices with their start and end apart: 23, of which 7 were waited for; matrix products, arithmetic and copies ran while one was open for 5% of the time, Pallas kernels for 32%

profile of v3, /device:TPU:0, one launch (start us, length us, event | category | flops | bytes accessed | tf_op | source)
XLA Modules:
  0.0 183.4 jit_solution(16676642331168631565)
XLA Ops:
  0.0 0.7 and_select_fusion
  0.8 0.7 broadcast_compare_fusion.2
  1.8 1.2 copy-done
  3.0 1.2 copy-done.3
  4.3 0.8 shard_map.55.rest_0_
  5.0 5.6 %collective-permute-start.3 = (bf16[2,256,256]{2,1,0:T(8,128)(2,1)S(1)}, bf16[2,256,256]{2,1,0:T(8,128)(2,1)}, u32[]{:S(2)}, u32[]{:S(2)}) collective-permute-start(bf16[2,256,256]{2,1,0:T(8,128)(2,1)S(1)} %shard_map.55.rest_0_), channel_id=1, source_target_pairs={{0,4},{8,12},{16,20},{24,28},{1,5},{9,13},{17,21},{25,29},{2,6},{1... | collective-permute-start | bytes 786440 | tf_op jit(solution)/shard_map/ppermute | solution.py:379
  10.6 4.2 %collective-permute-start = (bf16[2,256,256]{2,1,0:T(8,128)(2,1)S(1)}, bf16[2,256,256]{2,1,0:T(8,128)(2,1)}, u32[]{:S(2)}, u32[]{:S(2)}) collective-permute-start(bf16[2,256,256]{2,1,0:T(8,128)(2,1)S(1)} %shard_map.55.rest_0_), channel_id=1, source_target_pairs={{0,8},{4,12},{8,16},{12,20},{16,24},{20,28},{1,9},{5,13},{9,17},{1... | collective-permute-start | bytes 786440 | tf_op jit(solution)/shard_map/ppermute | solution.py:377
  14.8 1.2 copy-done.1
  16.0 1.2 copy-done.4
  17.5 2.3 %collective-permute-start.11 = (bf16[2048,256]{1,0:T(8,128)(2,1)S(1)}, bf16[2048,256]{1,0:T(8,128)(2,1)}, u32[]{:S(2)}, u32[]{:S(2)}) collective-permute-start(bf16[2048,256]{1,0:T(8,128)(2,1)S(1)} %shard_map.57.own_ref), channel_id=1, source_target_pairs={{0,4},{8,12},{16,20},{24,28},{1,5},{9,13},{17,21},{25,29},{2,6},{1... | collective-permute-start | bytes 3145736 | tf_op jit(solution)/shard_map/ppermute | solution.py:409
  19.8 1.0 fusion.3
  20.8 3.6 %collective-permute-start.8 = (bf16[1024,256]{1,0:T(8,128)(2,1)}, bf16[1024,256]{1,0:T(8,128)(2,1)}, u32[]{:S(2)}, u32[]{:S(2)}) collective-permute-start(bf16[1024,256]{1,0:T(8,128)(2,1)} %get-tuple-element.25), channel_id=1, source_target_pairs={{0,8},{4,12},{8,16},{12,20},{16,24},{20,28},{1,9},{5,13},{9,17},{1... | collective-permute-start | bytes 1572872 | tf_op jit(solution)/shard_map/ppermute | solution.py:406
  24.4 3.5 %collective-permute-start.7 = (bf16[1024,256]{1,0:T(8,128)(2,1)}, bf16[1024,256]{1,0:T(8,128)(2,1)}, u32[]{:S(2)}, u32[]{:S(2)}) collective-permute-start(bf16[1024,256]{1,0:T(8,128)(2,1)} %get-tuple-element.26), channel_id=1, source_target_pairs={{0,8},{4,12},{8,16},{12,20},{16,24},{20,28},{1,9},{5,13},{9,17},{1... | collective-permute-start | bytes 1572872 | tf_op jit(solution)/shard_map/ppermute | solution.py:406
  28.6 2.0 %collective-permute-start.1 = (bf16[2,256,256]{2,1,0:T(8,128)(2,1)}, bf16[2,256,256]{2,1,0:T(8,128)(2,1)}, u32[]{:S(2)}, u32[]{:S(2)}) collective-permute-start(bf16[2,256,256]{2,1,0:T(8,128)(2,1)} %collective-permute-done.rest_1_), channel_id=1, source_target_pairs={{0,8},{4,12},{8,16},{12,20},{16,24},{20,28},{1,9},{5,13},{9,17},{1... | collective-permute-start | bytes 786440 | tf_op jit(solution)/shard_map/ppermute | solution.py:377
  31.0 20.3 %collective-permute-done.1.rest_2_ = bf16[2,256,256]{2,1,0:T(8,128)(2,1)} collective-permute-done((bf16[2,256,256]{2,1,0:T(8,128)(2,1)}, bf16[2,256,256]{2,1,0:T(8,128)(2,1)}, u32[]{:S(2)}, u32[]{:S(2)}) %collective-permute-start.1) | collective-permute-done | bytes 262176 | tf_op jit(solution)/shard_map/ppermute | solution.py:377
  51.3 5.1 %collective-permute-start.2 = (bf16[2,256,256]{2,1,0:T(8,128)(2,1)}, bf16[2,256,256]{2,1,0:T(8,128)(2,1)}, u32[]{:S(2)}, u32[]{:S(2)}) collective-permute-start(bf16[2,256,256]{2,1,0:T(8,128)(2,1)} %collective-permute-done.1.rest_2_), channel_id=1, source_target_pairs={{0,8},{4,12},{8,16},{12,20},{16,24},{20,28},{1,9},{5,13},{9,17},{1... | collective-permute-start | bytes 786440 | tf_op jit(solution)/shard_map/ppermute | solution.py:377
  56.6 1.3 collective-permute-start.10
  57.9 0.9 broadcast_in_dim.30
  58.8 1.8 broadcast_in_dim.31.bias_ref
  60.6 0.9 broadcast_in_dim.27
  61.6 1.8 broadcast_in_dim.28.bias_ref
  63.4 3.5 %collective-permute-start.4 = (bf16[2,256,256]{2,1,0:T(8,128)(2,1)}, bf16[2,256,256]{2,1,0:T(8,128)(2,1)S(1)}, u32[]{:S(2)}, u32[]{:S(2)}) collective-permute-start(bf16[2,256,256]{2,1,0:T(8,128)(2,1)} %collective-permute-done.rest_1_), channel_id=1, source_target_pairs={{0,4},{8,12},{16,20},{24,28},{4,0},{12,8},{20,16},{28,24},{1,5},{9... | collective-permute-start | bytes 786440 | tf_op jit(solution)/shard_map/ppermute | solution.py:379
  67.2 2.0 %collective-permute-start.6 = (bf16[2,256,256]{2,1,0:T(8,128)(2,1)}, bf16[2,256,256]{2,1,0:T(8,128)(2,1)S(1)}, u32[]{:S(2)}, u32[]{:S(2)}) collective-permute-start(bf16[2,256,256]{2,1,0:T(8,128)(2,1)} %collective-permute-done.2.rest_3_), channel_id=1, source_target_pairs={{0,4},{8,12},{16,20},{24,28},{4,0},{12,8},{20,16},{28,24},{1,5},{9... | collective-permute-start | bytes 786440 | tf_op jit(solution)/shard_map/ppermute | solution.py:379
  69.3 9.9 %collective-permute-done.4.rest_5_ = bf16[2,256,256]{2,1,0:T(8,128)(2,1)S(1)} collective-permute-done((bf16[2,256,256]{2,1,0:T(8,128)(2,1)}, bf16[2,256,256]{2,1,0:T(8,128)(2,1)S(1)}, u32[]{:S(2)}, u32[]{:S(2)}) %collective-permute-start.4) | collective-permute-done | bytes 262176 | tf_op jit(solution)/shard_map/ppermute | solution.py:379
  79.2 2.8 %collective-permute-start.16 = (bf16[1024,256]{1,0:T(8,128)(2,1)S(1)}, bf16[1024,256]{1,0:T(8,128)(2,1)S(1)}, u32[]{:S(2)}, u32[]{:S(2)}) collective-permute-start(bf16[1024,256]{1,0:T(8,128)(2,1)S(1)} %get-tuple-element.23), channel_id=1, source_target_pairs={{0,8},{4,12},{8,16},{12,20},{16,24},{20,28},{1,9},{5,13},{9,17},{1... | collective-permute-start | bytes 1572872 | tf_op jit(solution)/shard_map/ppermute | solution.py:406
  82.0 2.7 %collective-permute-done.5.rest_6_ = bf16[2,256,256]{2,1,0:T(8,128)(2,1)S(1)} collective-permute-done((bf16[2,256,256]{2,1,0:T(8,128)(2,1)}, bf16[2,256,256]{2,1,0:T(8,128)(2,1)S(1)}, u32[]{:S(2)}, u32[]{:S(2)}) %collective-permute-start.5) | collective-permute-done | bytes 262176 | tf_op jit(solution)/shard_map/ppermute | solution.py:379
  84.6 2.8 %collective-permute-start.15 = (bf16[1024,256]{1,0:T(8,128)(2,1)S(1)}, bf16[1024,256]{1,0:T(8,128)(2,1)S(1)}, u32[]{:S(2)}, u32[]{:S(2)}) collective-permute-start(bf16[1024,256]{1,0:T(8,128)(2,1)S(1)} %get-tuple-element.24), channel_id=1, source_target_pairs={{0,8},{4,12},{8,16},{12,20},{16,24},{20,28},{1,9},{5,13},{9,17},{1... | collective-permute-start | bytes 1572872 | tf_op jit(solution)/shard_map/ppermute | solution.py:406
  87.5 1.3 collective-permute-start.9
  88.8 4.6 %collective-permute-start.19 = (bf16[2048,256]{1,0:T(8,128)(2,1)S(1)}, bf16[2048,256]{1,0:T(8,128)(2,1)S(1)}, u32[]{:S(2)}, u32[]{:S(2)}) collective-permute-start(bf16[2048,256]{1,0:T(8,128)(2,1)S(1)} %shard_map.60.own_ref), channel_id=1, source_target_pairs={{0,4},{8,12},{16,20},{24,28},{1,5},{9,13},{17,21},{25,29},{2,6},{1... | collective-permute-start | bytes 3145736 | tf_op jit(solution)/shard_map/ppermute | solution.py:409
  93.5 2.6 %shard_map.56.vert_ref = bf16[2,1024,256]{2,1,0:T(8,128)(2,1)S(1)} custom-call(s32[8,2,4]{2,1,0:T(2,128)S(1)} %broadcast_add_fusion.place_ref, s32[2,16]{1,0:T(2,128)S(1)} %compare_select_fusion.1.source_ref, bf16[2,256,256]{2,1,0:T(8,128)(2,1)S(1)} %shard_map.55.rest_0_, bf16[2,256,256]{2,1,0:T(8,128)(2,1)} %collective-permute-done.rest_1_, ...), custom_call_target="tpu_custom_call" | custom-call | bytes 2097152 | tf_op jit(solution)/shard_map/pallas_call | solution.py:121
  96.1 1.3 collective-permute-start.18
  97.4 1.4 collective-permute-done.15.rest_0_
  98.8 1.5 collective-permute-start.17
  100.3 3.5 %collective-permute-done.9.rest_2_ = bf16[1024,256]{1,0:T(8,128)(2,1)S(1)} collective-permute-done((bf16[1024,256]{1,0:T(8,128)(2,1)}, bf16[1024,256]{1,0:T(8,128)(2,1)S(1)}, u32[]{:S(2)}, u32[]{:S(2)}) %collective-permute-start.9) | collective-permute-done | bytes 524320 | tf_op jit(solution)/shard_map/ppermute | solution.py:410
  103.8 14.2 %shard_map.59 = (bf16[512,512]{1,0:T(8,128)(2,1)S(1)}, bf16[512,512]{1,0:T(8,128)(2,1)S(1)}) custom-call(s32[2]{0:T(128)S(1)} %get-tuple-element.30.part_ref, s32[1]{0:T(128)} %bitcast.2.parity_ref, s32[2,8]{1,0:T(2,128)S(1)} %select_reduce_fusion.1.slash_ref, f32[32,1536]{1,0:T(8,128)S(1)} %copy-done.7, bf16[2048,1024]{1,0:T(8,128)(2,1)S(1)} %copy-done.8, ...), custom_call_target="tpu_custom_call" | custom-call | flops 3221225472 | bytes 5242880 | tf_op jit(solution)/shard_map/pallas_call | solution.py:310
  118.1 14.2 %shard_map.58 = (bf16[512,512]{1,0:T(8,128)(2,1)S(1)}, bf16[512,512]{1,0:T(8,128)(2,1)S(1)}) custom-call(s32[2]{0:T(128)S(1)} %get-tuple-element.29.part_ref, s32[1]{0:T(128)} %bitcast.2.parity_ref, s32[2,8]{1,0:T(2,128)S(1)} %select_reduce_fusion.1.slash_ref, f32[32,1536]{1,0:T(8,128)S(1)} %copy-done.7, bf16[2048,1024]{1,0:T(8,128)(2,1)S(1)} %copy-done.8, ...), custom_call_target="tpu_custom_call" | custom-call | flops 3221225472 | bytes 5242880 | tf_op jit(solution)/shard_map/pallas_call | solution.py:310
  132.4 1.7 collective-permute-start.12
  134.0 0.5 collective-permute-start.13
  134.5 13.2 %shard_map.61 = (bf16[512,512]{1,0:T(8,128)(2,1)S(1)}, bf16[512,512]{1,0:T(8,128)(2,1)S(1)}) custom-call(s32[2]{0:T(128)S(1)} %get-tuple-element.29.part_ref, s32[1]{0:T(128)} %bitcast.2.parity_ref, s32[2,8]{1,0:T(2,128)S(1)} %select_reduce_fusion.1.slash_ref, f32[32,1536]{1,0:T(8,128)S(1)} %copy-done.6, bf16[2048,1024]{1,0:T(8,128)(2,1)S(1)} %copy-done.8, ...), custom_call_target="tpu_custom_call" | custom-call | flops 3221225472 | bytes 5242880 | tf_op jit(solution)/shard_map/pallas_call | solution.py:310
  147.8 0.9 collective-permute-start.20
  148.7 13.2 %shard_map.62 = (bf16[512,512]{1,0:T(8,128)(2,1)S(1)}, bf16[512,512]{1,0:T(8,128)(2,1)S(1)}) custom-call(s32[2]{0:T(128)S(1)} %get-tuple-element.30.part_ref, s32[1]{0:T(128)} %bitcast.2.parity_ref, s32[2,8]{1,0:T(2,128)S(1)} %select_reduce_fusion.1.slash_ref, f32[32,1536]{1,0:T(8,128)S(1)} %copy-done.6, bf16[2048,1024]{1,0:T(8,128)(2,1)S(1)} %copy-done.8, ...), custom_call_target="tpu_custom_call" | custom-call | flops 3221225472 | bytes 5242880 | tf_op jit(solution)/shard_map/pallas_call | solution.py:310
  162.0 0.8 collective-permute-start.22
  162.8 0.5 collective-permute-start.21
  163.3 0.5 broadcast_in_dim.24
  164.2 4.6 %collective-permute-done.20 = bf16[512,512]{1,0:T(8,128)(2,1)S(1)} collective-permute-done((bf16[512,512]{1,0:T(8,128)(2,1)S(1)}, bf16[512,512]{1,0:T(8,128)(2,1)S(1)}, u32[]{:S(2)}, u32[]{:S(2)}) %collective-permute-start.20) | collective-permute-done | bytes 524320 | tf_op jit(solution)/shard_map/ppermute | solution.py:428
  168.8 11.5 %collective-permute-done.21 = bf16[512,512]{1,0:T(8,128)(2,1)S(1)} collective-permute-done((bf16[512,512]{1,0:T(8,128)(2,1)S(1)}, bf16[512,512]{1,0:T(8,128)(2,1)S(1)}, u32[]{:S(2)}, u32[]{:S(2)}) %collective-permute-start.21) | collective-permute-done | bytes 524320 | tf_op jit(solution)/shard_map/ppermute | solution.py:428
  180.5 2.0 %copy-done.9 = bf16[512,4096]{1,0:T(8,128)(2,1)} copy-done((bf16[512,4096]{1,0:T(8,128)(2,1)}, bf16[512,4096]{1,0:T(8,128)(2,1)S(1)}, u32[]{:S(2)}) %copy-start.9) | copy-done | bytes 4194328
  182.5 0.8 constant_dynamic-update-slice_fusion
  (71 shorter events, 2.9 us)
Async XLA Ops:
  0.0 28.4 %copy-start.10 = (s32[2,16]{1,0:T(2,128)S(1)}, s32[2,16]{1,0:T(2,128)}, u32[]{:S(2)}) copy-start(s32[2,16]{1,0:T(2,128)} %param.8) | copy-start | bytes 388
  0.0 27.9 %copy-start.11 = (s32[2,8]{1,0:T(2,128)S(1)}, s32[2,8]{1,0:T(2,128)}, u32[]{:S(2)}) copy-start(s32[2,8]{1,0:T(2,128)} %param.9) | copy-start | bytes 196
  1.8 1.2 copy-start
  3.0 1.2 copy-start.3
  4.2 62.6 %copy-start.2 = (bf16[2048,256]{1,0:T(8,128)(2,1)S(1)}, bf16[2048,256]{1,0:T(8,128)(2,1)}, u32[]{:S(2)}) copy-start(bf16[2048,256]{1,0:T(8,128)(2,1)} %keys_ref.5) | copy-start | bytes 3145732
  4.2 62.6 %copy-start.5 = (bf16[2048,256]{1,0:T(8,128)(2,1)S(1)}, bf16[2048,256]{1,0:T(8,128)(2,1)}, u32[]{:S(2)}) copy-start(bf16[2048,256]{1,0:T(8,128)(2,1)} %values_ref.5) | copy-start | bytes 3145732
  5.0 62.1 %collective-permute-start.3 = (bf16[2,256,256]{2,1,0:T(8,128)(2,1)S(1)}, bf16[2,256,256]{2,1,0:T(8,128)(2,1)}, u32[]{:S(2)}, u32[]{:S(2)}) collective-permute-start(bf16[2,256,256]{2,1,0:T(8,128)(2,1)S(1)} %shard_map.55.rest_0_), channel_id=1, source_target_pairs={{0,4},{8,12},{16,20},{24,28},{1,5},{9,13},{17,21},{25,29},{2,6},{1... | collective-permute-start | bytes 786440 | tf_op jit(solution)/shard_map/ppermute | solution.py:379
  10.6 18.0 %collective-permute-start = (bf16[2,256,256]{2,1,0:T(8,128)(2,1)S(1)}, bf16[2,256,256]{2,1,0:T(8,128)(2,1)}, u32[]{:S(2)}, u32[]{:S(2)}) collective-permute-start(bf16[2,256,256]{2,1,0:T(8,128)(2,1)S(1)} %shard_map.55.rest_0_), channel_id=1, source_target_pairs={{0,8},{4,12},{8,16},{12,20},{16,24},{20,28},{1,9},{5,13},{9,17},{1... | collective-permute-start | bytes 786440 | tf_op jit(solution)/shard_map/ppermute | solution.py:377
  14.8 1.2 copy-start.1
  16.0 1.2 copy-start.4
  17.5 86.4 %collective-permute-start.11 = (bf16[2048,256]{1,0:T(8,128)(2,1)S(1)}, bf16[2048,256]{1,0:T(8,128)(2,1)}, u32[]{:S(2)}, u32[]{:S(2)}) collective-permute-start(bf16[2048,256]{1,0:T(8,128)(2,1)S(1)} %shard_map.57.own_ref), channel_id=1, source_target_pairs={{0,4},{8,12},{16,20},{24,28},{1,5},{9,13},{17,21},{25,29},{2,6},{1... | collective-permute-start | bytes 3145736 | tf_op jit(solution)/shard_map/ppermute | solution.py:409
  20.8 35.8 %collective-permute-start.8 = (bf16[1024,256]{1,0:T(8,128)(2,1)}, bf16[1024,256]{1,0:T(8,128)(2,1)}, u32[]{:S(2)}, u32[]{:S(2)}) collective-permute-start(bf16[1024,256]{1,0:T(8,128)(2,1)} %get-tuple-element.25), channel_id=1, source_target_pairs={{0,8},{4,12},{8,16},{12,20},{16,24},{20,28},{1,9},{5,13},{9,17},{1... | collective-permute-start | bytes 1572872 | tf_op jit(solution)/shard_map/ppermute | solution.py:406
  24.4 39.0 %collective-permute-start.7 = (bf16[1024,256]{1,0:T(8,128)(2,1)}, bf16[1024,256]{1,0:T(8,128)(2,1)}, u32[]{:S(2)}, u32[]{:S(2)}) collective-permute-start(bf16[1024,256]{1,0:T(8,128)(2,1)} %get-tuple-element.26), channel_id=1, source_target_pairs={{0,8},{4,12},{8,16},{12,20},{16,24},{20,28},{1,9},{5,13},{9,17},{1... | collective-permute-start | bytes 1572872 | tf_op jit(solution)/shard_map/ppermute | solution.py:406
  28.6 22.7 %collective-permute-start.1 = (bf16[2,256,256]{2,1,0:T(8,128)(2,1)}, bf16[2,256,256]{2,1,0:T(8,128)(2,1)}, u32[]{:S(2)}, u32[]{:S(2)}) collective-permute-start(bf16[2,256,256]{2,1,0:T(8,128)(2,1)} %collective-permute-done.rest_1_), channel_id=1, source_target_pairs={{0,8},{4,12},{8,16},{12,20},{16,24},{20,28},{1,9},{5,13},{9,17},{1... | collective-permute-start | bytes 786440 | tf_op jit(solution)/shard_map/ppermute | solution.py:377
  51.3 15.9 %collective-permute-start.2 = (bf16[2,256,256]{2,1,0:T(8,128)(2,1)}, bf16[2,256,256]{2,1,0:T(8,128)(2,1)}, u32[]{:S(2)}, u32[]{:S(2)}) collective-permute-start(bf16[2,256,256]{2,1,0:T(8,128)(2,1)} %collective-permute-done.1.rest_2_), channel_id=1, source_target_pairs={{0,8},{4,12},{8,16},{12,20},{16,24},{20,28},{1,9},{5,13},{9,17},{1... | collective-permute-start | bytes 786440 | tf_op jit(solution)/shard_map/ppermute | solution.py:377
  56.6 32.2 %collective-permute-start.10 = (bf16[1024,256]{1,0:T(8,128)(2,1)}, bf16[1024,256]{1,0:T(8,128)(2,1)}, u32[]{:S(2)}, u32[]{:S(2)}) collective-permute-start(bf16[1024,256]{1,0:T(8,128)(2,1)} %collective-permute-done.8.rest_1_), channel_id=1, source_target_pairs={{4,0},{12,8},{20,16},{28,24},{5,1},{13,9},{21,17},{29,25},{6,2},{1... | collective-permute-start | bytes 1572872 | tf_op jit(solution)/shard_map/ppermute | solution.py:410
  63.4 40.4 %copy-start.7 = (f32[32,1536]{1,0:T(8,128)S(1)}, f32[32,1536]{1,0:T(8,128)}, u32[]{:S(2)}) copy-start(f32[32,1536]{1,0:T(8,128)} %broadcast_in_dim.28.bias_ref) | copy-start | bytes 589828
  63.4 40.4 %copy-start.8 = (bf16[2048,1024]{1,0:T(8,128)(2,1)S(1)}, bf16[2048,1024]{1,0:T(8,128)(2,1)}, u32[]{:S(2)}) copy-start(bf16[2048,1024]{1,0:T(8,128)(2,1)} %query_ref.7) | copy-start | bytes 12582916
  63.4 15.8 %collective-permute-start.4 = (bf16[2,256,256]{2,1,0:T(8,128)(2,1)}, bf16[2,256,256]{2,1,0:T(8,128)(2,1)S(1)}, u32[]{:S(2)}, u32[]{:S(2)}) collective-permute-start(bf16[2,256,256]{2,1,0:T(8,128)(2,1)} %collective-permute-done.rest_1_), channel_id=1, source_target_pairs={{0,4},{8,12},{16,20},{24,28},{4,0},{12,8},{20,16},{28,24},{1,5},{9... | collective-permute-start | bytes 786440 | tf_op jit(solution)/shard_map/ppermute | solution.py:379
  67.1 17.5 %collective-permute-start.5 = (bf16[2,256,256]{2,1,0:T(8,128)(2,1)}, bf16[2,256,256]{2,1,0:T(8,128)(2,1)S(1)}, u32[]{:S(2)}, u32[]{:S(2)}) collective-permute-start(bf16[2,256,256]{2,1,0:T(8,128)(2,1)} %collective-permute-done.1.rest_2_), channel_id=1, source_target_pairs={{0,4},{8,12},{16,20},{24,28},{4,0},{12,8},{20,16},{28,24},{1,5},{9... | collective-permute-start | bytes 786440 | tf_op jit(solution)/shard_map/ppermute | solution.py:379
  67.2 20.3 %collective-permute-start.6 = (bf16[2,256,256]{2,1,0:T(8,128)(2,1)}, bf16[2,256,256]{2,1,0:T(8,128)(2,1)S(1)}, u32[]{:S(2)}, u32[]{:S(2)}) collective-permute-start(bf16[2,256,256]{2,1,0:T(8,128)(2,1)} %collective-permute-done.2.rest_3_), channel_id=1, source_target_pairs={{0,4},{8,12},{16,20},{24,28},{4,0},{12,8},{20,16},{28,24},{1,5},{9... | collective-permute-start | bytes 786440 | tf_op jit(solution)/shard_map/ppermute | solution.py:379
  79.2 16.9 %collective-permute-start.16 = (bf16[1024,256]{1,0:T(8,128)(2,1)S(1)}, bf16[1024,256]{1,0:T(8,128)(2,1)S(1)}, u32[]{:S(2)}, u32[]{:S(2)}) collective-permute-start(bf16[1024,256]{1,0:T(8,128)(2,1)S(1)} %get-tuple-element.23), channel_id=1, source_target_pairs={{0,8},{4,12},{8,16},{12,20},{16,24},{20,28},{1,9},{5,13},{9,17},{1... | collective-permute-start | bytes 1572872 | tf_op jit(solution)/shard_map/ppermute | solution.py:406
  84.6 14.2 %collective-permute-start.15 = (bf16[1024,256]{1,0:T(8,128)(2,1)S(1)}, bf16[1024,256]{1,0:T(8,128)(2,1)S(1)}, u32[]{:S(2)}, u32[]{:S(2)}) collective-permute-start(bf16[1024,256]{1,0:T(8,128)(2,1)S(1)} %get-tuple-element.24), channel_id=1, source_target_pairs={{0,8},{4,12},{8,16},{12,20},{16,24},{20,28},{1,9},{5,13},{9,17},{1... | collective-permute-start | bytes 1572872 | tf_op jit(solution)/shard_map/ppermute | solution.py:406
  87.5 16.4 %collective-permute-start.9 = (bf16[1024,256]{1,0:T(8,128)(2,1)}, bf16[1024,256]{1,0:T(8,128)(2,1)S(1)}, u32[]{:S(2)}, u32[]{:S(2)}) collective-permute-start(bf16[1024,256]{1,0:T(8,128)(2,1)} %collective-permute-done.7.rest_0_), channel_id=1, source_target_pairs={{4,0},{12,8},{20,16},{28,24},{5,1},{13,9},{21,17},{29,25},{6,2},{1... | collective-permute-start | bytes 1572872 | tf_op jit(solution)/shard_map/ppermute | solution.py:410
  88.8 45.7 %collective-permute-start.19 = (bf16[2048,256]{1,0:T(8,128)(2,1)S(1)}, bf16[2048,256]{1,0:T(8,128)(2,1)S(1)}, u32[]{:S(2)}, u32[]{:S(2)}) collective-permute-start(bf16[2048,256]{1,0:T(8,128)(2,1)S(1)} %shard_map.60.own_ref), channel_id=1, source_target_pairs={{0,4},{8,12},{16,20},{24,28},{1,5},{9,13},{17,21},{25,29},{2,6},{1... | collective-permute-start | bytes 3145736 | tf_op jit(solution)/shard_map/ppermute | solution.py:409
  96.1 37.9 %collective-permute-start.18 = (bf16[1024,256]{1,0:T(8,128)(2,1)S(1)}, bf16[1024,256]{1,0:T(8,128)(2,1)S(1)}, u32[]{:S(2)}, u32[]{:S(2)}) collective-permute-start(bf16[1024,256]{1,0:T(8,128)(2,1)S(1)} %collective-permute-done.16.rest_1_), channel_id=1, source_target_pairs={{4,0},{12,8},{20,16},{28,24},{5,1},{13,9},{21,17},{29,25},{6,2},{1... | collective-permute-start | bytes 1572872 | tf_op jit(solution)/shard_map/ppermute | solution.py:410
  98.8 35.7 %collective-permute-start.17 = (bf16[1024,256]{1,0:T(8,128)(2,1)S(1)}, bf16[1024,256]{1,0:T(8,128)(2,1)S(1)}, u32[]{:S(2)}, u32[]{:S(2)}) collective-permute-start(bf16[1024,256]{1,0:T(8,128)(2,1)S(1)} %collective-permute-done.15.rest_0_), channel_id=1, source_target_pairs={{4,0},{12,8},{20,16},{28,24},{5,1},{13,9},{21,17},{29,25},{6,2},{1... | collective-permute-start | bytes 1572872 | tf_op jit(solution)/shard_map/ppermute | solution.py:410
  118.0 45.9 %collective-permute-start.14 = (bf16[512,512]{1,0:T(8,128)(2,1)S(1)}, bf16[512,512]{1,0:T(8,128)(2,1)S(1)}, u32[]{:S(2)}, u32[]{:S(2)}) collective-permute-start(bf16[512,512]{1,0:T(8,128)(2,1)S(1)} %get-tuple-element.15), channel_id=1, source_target_pairs={{0,1},{1,0},{2,3},{3,2},{4,5},{5,4},{6,7},{7,6},{8,9},{9,8},{10,11... | collective-permute-start | bytes 1572872 | tf_op jit(solution)/shard_map/ppermute | solution.py:428
  118.1 16.4 %copy-start.6 = (f32[32,1536]{1,0:T(8,128)S(1)}, f32[32,1536]{1,0:T(8,128)}, u32[]{:S(2)}) copy-start(f32[32,1536]{1,0:T(8,128)} %broadcast_in_dim.31.bias_ref) | copy-start | bytes 589828
  132.4 30.5 %collective-permute-start.12 = (bf16[512,512]{1,0:T(8,128)(2,1)S(1)}, bf16[512,512]{1,0:T(8,128)(2,1)S(1)}, u32[]{:S(2)}, u32[]{:S(2)}) collective-permute-start(bf16[512,512]{1,0:T(8,128)(2,1)S(1)} %get-tuple-element.13), channel_id=1, source_target_pairs={{0,3},{1,2},{2,1},{3,0},{4,7},{5,6},{6,5},{7,4},{8,11},{9,10},{10,... | collective-permute-start | bytes 1572872 | tf_op jit(solution)/shard_map/ppermute | solution.py:428
  134.0 29.9 %collective-permute-start.13 = (bf16[512,512]{1,0:T(8,128)(2,1)S(1)}, bf16[512,512]{1,0:T(8,128)(2,1)S(1)}, u32[]{:S(2)}, u32[]{:S(2)}) collective-permute-start(bf16[512,512]{1,0:T(8,128)(2,1)S(1)} %get-tuple-element.14), channel_id=1, source_target_pairs={{0,2},{1,3},{2,0},{3,1},{4,6},{5,7},{6,4},{7,5},{8,10},{9,11},{10,... | collective-permute-start | bytes 1572872 | tf_op jit(solution)/shard_map/ppermute | solution.py:428
  147.8 21.0 %collective-permute-start.20 = (bf16[512,512]{1,0:T(8,128)(2,1)S(1)}, bf16[512,512]{1,0:T(8,128)(2,1)S(1)}, u32[]{:S(2)}, u32[]{:S(2)}) collective-permute-start(bf16[512,512]{1,0:T(8,128)(2,1)S(1)} %get-tuple-element.17), channel_id=1, source_target_pairs={{0,3},{1,2},{2,1},{3,0},{4,7},{5,6},{6,5},{7,4},{8,11},{9,10},{10,... | collective-permute-start | bytes 1572872 | tf_op jit(solution)/shard_map/ppermute | solution.py:428
  162.0 18.4 %collective-permute-start.22 = (bf16[512,512]{1,0:T(8,128)(2,1)S(1)}, bf16[512,512]{1,0:T(8,128)(2,1)S(1)}, u32[]{:S(2)}, u32[]{:S(2)}) collective-permute-start(bf16[512,512]{1,0:T(8,128)(2,1)S(1)} %get-tuple-element.19), channel_id=1, source_target_pairs={{0,1},{1,0},{2,3},{3,2},{4,5},{5,4},{6,7},{7,6},{8,9},{9,8},{10,11... | collective-permute-start | bytes 1572872 | tf_op jit(solution)/shard_map/ppermute | solution.py:428
  162.8 17.5 %collective-permute-start.21 = (bf16[512,512]{1,0:T(8,128)(2,1)S(1)}, bf16[512,512]{1,0:T(8,128)(2,1)S(1)}, u32[]{:S(2)}, u32[]{:S(2)}) collective-permute-start(bf16[512,512]{1,0:T(8,128)(2,1)S(1)} %get-tuple-element.18), channel_id=1, source_target_pairs={{0,2},{1,3},{2,0},{3,1},{4,6},{5,7},{6,4},{7,5},{8,10},{9,11},{10,... | collective-permute-start | bytes 1572872 | tf_op jit(solution)/shard_map/ppermute | solution.py:428
  180.5 2.0 %copy-start.9 = (bf16[512,4096]{1,0:T(8,128)(2,1)}, bf16[512,4096]{1,0:T(8,128)(2,1)S(1)}, u32[]{:S(2)}) copy-start(bf16[512,4096]{1,0:T(8,128)(2,1)S(1)} %constant_dynamic-update-slice_fusion.1) | copy-start | bytes 12582916

commit v4 on v3

--- a/solution.py
+++ b/solution.py
@@ -26,47 +26,49 @@
     return pl.ds(pl.multiple_of(index * BLK, BLK), count * BLK)
 
 
-def slots_kernel(local_ref, keys_ref, values_ref, out_ref, sem):
+def slots_kernel(head, local_ref, keys_ref, values_ref, *rest):
+    out_ref, sem = rest[-2:]
     copies = []
-    for head in range(out_ref.shape[0]):
-        for slot in range(MOWN):
-            for side, source in enumerate((keys_ref, values_ref)):
-                copies.append(
-                    pltpu.make_async_copy(
-                        source.at[blocks_at(local_ref[head, slot]), pl.ds(head * HD, HD)],
-                        out_ref.at[head, pl.ds(slot * BLK, BLK), pl.ds(side * HD, HD)],
-                        sem.at[len(copies)],
-                    )
+    for slot in range(MOWN):
+        for side, source in enumerate((keys_ref, values_ref)):
+            copies.append(
+                pltpu.make_async_copy(
+                    source.at[blocks_at(local_ref[head, slot]), pl.ds(head * HD, HD)],
+                    out_ref.at[pl.ds(slot * BLK, BLK), pl.ds(side * HD, HD)],
+                    sem.at[len(copies)],
                 )
+            )
     for copy in copies:
         copy.start()
     for copy in copies:
         copy.wait()
 
 
-def owned_slots(local_block, keys, values):
-    heads = local_block.shape[0]
+def owned_slots(head, local_block, keys, values, after):
     return pl.pallas_call(
-        slots_kernel,
-        out_shape=jax.ShapeDtypeStruct((heads, MOWN * BLK, 2 * HD), keys.dtype),
-        in_specs=[SMEM, ANY, ANY],
+        functools.partial(slots_kernel, head),
+        out_shape=jax.ShapeDtypeStruct((MOWN * BLK, 2 * HD), keys.dtype),
+        in_specs=[SMEM] + [ANY] * (2 + len(after)),
         out_specs=ANY,
-        scratch_shapes=[pltpu.SemaphoreType.DMA((heads * MOWN * 2,))],
+        scratch_shapes=[pltpu.SemaphoreType.DMA((MOWN * 2,))],
         compiler_params=pltpu.CompilerParams(vmem_limit_bytes=1 << 20),
         cost_estimate=pl.CostEstimate(
-            flops=0, bytes_accessed=4 * heads * MOWN * BLK * 2 * HD, transcendentals=0
+            flops=0, bytes_accessed=8 * MOWN * BLK * HD, transcendentals=0
         ),
-    )(local_block, keys, values)
+    )(local_block, keys, values, *after)
 
 
 def pair_kernel(head, keys_ref, values_ref, *rest):
-    out_ref, sem = rest[-2:]
-    copies = [
-        pltpu.make_async_copy(
-            source.at[:, pl.ds(head * HD, HD)], out_ref.at[:, pl.ds(side * HD, HD)], sem.at[side]
-        )
-        for side, source in enumerate((keys_ref, values_ref))
-    ]
+    out_refs, sem = rest[-2 - CHUNKS : -1], rest[-1]
+    whole, chunks = out_refs[0], out_refs[1:]
+    copies = []
+    for side, source in enumerate((keys_ref, values_ref)):
+        columns, to = pl.ds(head * HD, HD), pl.ds(side * HD, HD)
+        for index, chunk in enumerate(chunks):
+            rows = pl.ds(index * chunk.shape[0], chunk.shape[0])
+            copies.append((source.at[rows, columns], chunk.at[:, to]))
+        copies.append((source.at[:, columns], whole.at[:, to]))
+    copies = [pltpu.make_async_copy(*ends, sem.at[k]) for k, ends in enumerate(copies)]
     for copy in copies:
         copy.start()
     for copy in copies:
@@ -74,71 +76,65 @@
 
 
 def pair_of(head, keys, values, after):
+    rows = keys.shape[0]
+    whole, *chunks = pl.pallas_call(
+        functools.partial(pair_kernel, head),
+        out_shape=[jax.ShapeDtypeStruct((rows, 2 * HD), keys.dtype)]
+        + [jax.ShapeDtypeStruct((rows // CHUNKS, 2 * HD), keys.dtype)] * CHUNKS,
+        in_specs=[ANY] * (2 + len(after)),
+        out_specs=[ANY] * (1 + CHUNKS),
+        scratch_shapes=[pltpu.SemaphoreType.DMA((2 + 2 * CHUNKS,))],
+        compiler_params=pltpu.CompilerParams(vmem_limit_bytes=1 << 20),
+        cost_estimate=pl.CostEstimate(flops=0, bytes_accessed=16 * rows * HD, transcendentals=0),
+    )(keys, values, *after)
+    return whole, chunks
+
+
+def listed_kernel(head, place_ref, source_ref, behind_refs, across_ref, out_ref, sem):
+    count = len(behind_refs)
+    for index in range(2 * count):
+        for slot in range(MOWN):
+            place = place_ref[index, head, slot]
+            if index < count:
+                found = behind_refs[index].at[pl.ds(slot * BLK, BLK)]
+            else:
+                found = across_ref.at[pl.ds(((index - count) * MOWN + slot) * BLK, BLK)]
+
+            @pl.when(place >= 0)
+            def _():
+                pltpu.make_async_copy(found, out_ref.at[blocks_at(place)], sem).start()
+
+    for entry in range(NV):
+
+        @pl.when(source_ref[head, entry] < 0)
+        def _():
+            pltpu.make_async_copy(
+                behind_refs[0].at[pl.ds(0, BLK)], out_ref.at[pl.ds(entry * BLK, BLK)], sem
+            ).start()
+
+    pltpu.make_async_copy(out_ref, out_ref, sem).wait()
+
+
+def listed_blocks(head, place, source, behind, across):
     return pl.pallas_call(
-        functools.partial(pair_kernel, head),
-        out_shape=jax.ShapeDtypeStruct((keys.shape[0], 2 * HD), keys.dtype),
-        in_specs=[ANY] * (2 + len(after)),
-        out_specs=ANY,
-        scratch_shapes=[pltpu.SemaphoreType.DMA((2,))],
-        compiler_params=pltpu.CompilerParams(vmem_limit_bytes=1 << 20),
-        cost_estimate=pl.CostEstimate(
-            flops=0, bytes_accessed=8 * keys.shape[0] * HD, transcendentals=0
-        ),
-    )(keys, values, *after)
-
-
-def listed_kernel(place_ref, source_ref, *rest):
-    arrays, out_ref, sem = rest[:-2], rest[-2], rest[-1]
-    heads = out_ref.shape[0]
-    for head in range(heads):
-        for index, array in enumerate(arrays):
-            for slot in range(MOWN):
-                place = place_ref[index, head, slot]
-
-                @pl.when(place >= 0)
-                def _():
-                    pltpu.make_async_copy(
-                        array.at[head, pl.ds(slot * BLK, BLK)],
-                        out_ref.at[head, blocks_at(place)],
-                        sem,
-                    ).start()
-
-        for entry in range(NV):
-
-            @pl.when(source_ref[head, entry] < 0)
-            def _():
-                pltpu.make_async_copy(
-                    arrays[0].at[head, pl.ds(0, BLK)],
-                    out_ref.at[head, pl.ds(entry * BLK, BLK)],
-                    sem,
-                ).start()
-
-    pltpu.make_async_copy(out_ref, out_ref, sem).wait()
-
-
-def listed_blocks(place, source, arrays):
-    heads = source.shape[0]
-    return pl.pallas_call(
-        listed_kernel,
-        out_shape=jax.ShapeDtypeStruct((heads, NV * BLK, 2 * HD), arrays[0].dtype),
-        in_specs=[SMEM, SMEM] + [ANY] * len(arrays),
+        functools.partial(listed_kernel, head),
+        out_shape=jax.ShapeDtypeStruct((NV * BLK, 2 * HD), across.dtype),
+        in_specs=[SMEM, SMEM, [ANY] * len(behind), ANY],
         out_specs=ANY,
         scratch_shapes=[pltpu.SemaphoreType.DMA],
         compiler_params=pltpu.CompilerParams(vmem_limit_bytes=1 << 20),
-        cost_estimate=pl.CostEstimate(
-            flops=0, bytes_accessed=8 * heads * NV * BLK * HD, transcendentals=0
-        ),
-    )(place, source, *arrays)
+        cost_estimate=pl.CostEstimate(flops=0, bytes_accessed=8 * NV * BLK * HD, transcendentals=0),
+    )(place, source, behind, across)
 
 
 def attend_kernel(
-    head, parts, part_blocks, group_heads, part_ref, parity_ref, slash_ref, bias_ref, query_ref,
+    head, parts, waits, part_blocks, group_heads, part_ref, parity_ref, slash_ref, bias_ref, query_ref,
     vert_ref, own_ref, *rest,
 ):
     two_back = rest[:CHUNKS]
     even_back = rest[CHUNKS : 2 * CHUNKS]
     odd_back = rest[2 * CHUNKS]
-    rest = rest[2 * CHUNKS + 1 :]
+    rest = rest[2 * CHUNKS + 1 + waits :]
     out_refs = rest[:parts]
     (
         queries, out, vert, vert_keys, window, scores_a, scores_b, weights_a, weights_b, max_a,
@@ -247,7 +243,7 @@
                 queries.at[pl.ds(k * part_rows, part_rows)],
                 query_sem,
             ).start()
-        pltpu.make_async_copy(vert_ref.at[head], vert, vert_sem).start()
+        pltpu.make_async_copy(vert_ref, vert, vert_sem).start()
         for chunk in range(CHUNKS):
             pltpu.make_async_copy(
                 two_back[chunk], window.at[pl.ds(chunk * chunk_rows, chunk_rows)], window_sem
@@ -299,7 +295,7 @@
 
 
 def attend(head, part, parity, slash, bias, queries, vert, own, two_back, even_back, odd_back,
-           part_rows):
+           part_rows, after):
     parts = part.shape[0]
     group_cols = queries.shape[1] // slash.shape[0]
     group_heads = group_cols // HD
@@ -308,12 +304,12 @@
     rows = group_heads * BLK
     keys_seen = (NV + NS) * BLK
     return pl.pallas_call(
-        functools.partial(attend_kernel, head, parts, part_blocks, group_heads),
+        functools.partial(attend_kernel, head, parts, len(after), part_blocks, group_heads),
         out_shape=[jax.ShapeDtypeStruct((part_rows, group_cols), jnp.bfloat16)] * parts,
         grid_spec=pltpu.PrefetchScalarGridSpec(
             num_scalar_prefetch=3,
             grid=(parts * part_blocks // STEP_BLOCKS,),
-            in_specs=[pl.BlockSpec(bias.shape, lambda s, *_: (0, 0))] + [ANY] * (4 + 2 * CHUNKS),
+            in_specs=[pl.BlockSpec(bias.shape, lambda s, *_: (0, 0))] + [ANY] * (4 + 2 * CHUNKS + len(after)),
             out_specs=[ANY] * parts,
             scratch_shapes=[
                 pltpu.VMEM((parts * part_rows, group_cols), jnp.bfloat16),
@@ -342,7 +338,7 @@
             bytes_accessed=4 * parts * part_rows * group_cols + 12 * tok_rows * HD,
             transcendentals=parts * part_rows * group_heads * keys_seen,
         ),
-    )(part, parity, slash, bias, queries, vert, own, *two_back, *even_back, odd_back)
+    )(part, parity, slash, bias, queries, vert, own, *two_back, *even_back, odd_back, *after)
 
 
 def local(queries, keys, values, vertical, slash):
@@ -359,7 +355,6 @@
     two_pairs = [(i, i + 2) for i in range(shard_count - 2)]
     even_to_odd = [(i, i + 1) for i in range(0, shard_count - 1, 2)]
     odd_to_even = [(i, i - 1) for i in range(1, shard_count, 2)]
-    chunk_rows = tok_rows // CHUNKS
 
     owners = vertical // blocks_dev
     order = jnp.arange(NV, dtype=jnp.int32)
@@ -372,13 +367,6 @@
         ((owners == shard_index)[:, :, None] & in_slot) * (vertical % blocks_dev)[:, :, None],
         axis=1,
     )
-    behind = [owned_slots(local_block, keys, values)]
-    for _ in range(1, shard_count // 2):
-        behind.append(lax.ppermute(behind[-1], "ctx", two_pairs))
-    across = [
-        lax.ppermute(array, "ctx", even_to_odd + (odd_to_even if k else []))
-        for k, array in enumerate(behind)
-    ]
     steps = 2 * jnp.arange(shard_count // 2, dtype=jnp.int32)
     array_owner = jnp.concatenate([shard_index - steps, partner - steps])
     array_owner = jnp.where(array_owner <= shard_index, array_owner, -1)
@@ -401,28 +389,35 @@
     windows = []
     after = []
     for head in range(kv_local):
-        own = pair_of(head, keys, values, after)
-        two_back = [
-            lax.ppermute(own[c * chunk_rows : (c + 1) * chunk_rows], "ctx", two_pairs)
-            for c in range(CHUNKS)
-        ]
+        behind = [owned_slots(head, local_block, keys, values, after)]
+        own, chunks = pair_of(head, keys, values, behind)
+        for distance in range(2, shard_count, 2):
+            pairs = [(i, i + distance) for i in range(shard_count - distance)]
+            behind.append(lax.ppermute(behind[0], "ctx", pairs))
+        two_back = [lax.ppermute(chunk, "ctx", two_pairs) for chunk in chunks]
         odd_back = lax.ppermute(own, "ctx", even_to_odd)
+        across = lax.ppermute(jnp.concatenate(behind), "ctx", even_to_odd + odd_to_even)
         even_back = [lax.ppermute(piece, "ctx", odd_to_even) for piece in two_back]
-        windows.append((own, two_back, even_back, odd_back))
-        after = [two_back[0]]
-    vert = listed_blocks(place, source, behind + across)
+        vert = listed_blocks(head, place, source, behind, across)
+        windows.append((vert, own, two_back, even_back, odd_back))
+        after = two_back + even_back[:-1]
 
     parity = (shard_index % 2).reshape(1).astype(jnp.int32)
     out = jnp.zeros((part_rows, head_count * kv_local * group_cols), jnp.bfloat16)
     half = head_count // 2
+    after = []
     for head in range(kv_local):
-        own, two_back, even_back, odd_back = windows[head]
-        for flips in (range(head_count - 1, half - 1, -1), range(half - 1, -1, -1)):
+        vert, own, two_back, even_back, odd_back = windows[head]
+        calls = [range(head_count - 1, half - 1, -1), range(half - 1, -1, -1)]
+        if head + 1 == kv_local:
+            calls = [range(f, f - 1, -1) for f in calls[0]] + calls[1:]
+        for flips in calls:
             others = [head_index ^ flip for flip in flips]
             pieces = attend(
                 head, jnp.stack(others).astype(jnp.int32), parity, slash, bias[head], queries,
-                vert, own, two_back, even_back, odd_back, part_rows,
-            )
+                vert, own, two_back, even_back, odd_back, part_rows, after,
+            )
+            after = [pieces[-1]]
             for flip, other, piece in zip(flips, others, pieces):
                 if flip:
                     piece = lax.ppermute(piece, "head", [(i, i ^ flip) for i in range(head_count)])

time: 184 us -> 173 us (0.940)
  waiting for transfers between devices: 54 us -> 34.7 us
  Pallas kernels: 58.7 us -> 64.2 us
  local copies, waits for them, and re-layouts: 15.5 us -> 17.7 us
    ppermute x11 -> x12, waiting for transfers between devices: 34.3 us -> 13.6 us  [the longest x6 11 us: local(): behind.append(lax.ppermute(behind[0], 'ctx', pairs))]
    ppermute x4, waiting for transfers between devices: 3.55 us -> 18.8 us  [local(): even_back = [lax.ppermute(piece, 'ctx', odd_to_even) for piece in two_back]]
    ppermute x6, waiting for transfers between devices: 16.1 us -> 2.22 us  [local(): lax.ppermute(piece, 'head', [(i, i ^ flip) for i in range(head_count)])]
    pallas_call x8 -> x11, Pallas kernels: 58.7 us -> 64.2 us  [the longest x5 57.5 us: attend(): pl.pallas_call(functools.partial(attend_kernel, head, parts, len(after),...]
    unnamed x24 -> x30, local copies, waits for them, and re-layouts: 6.94 us -> 10.9 us
    ppermute x11 -> x12, starting transfers between devices: 35.1 us -> 35.5 us  [the longest x6 23.1 us: local(): behind.append(lax.ppermute(behind[0], 'ctx', pairs))]
  transfers between devices with their start and end apart: 23 -> 24, of which waited for: 7 -> 6; matrix products, arithmetic and copies ran while one was open for 5% -> 5% of each run, Pallas kernels for 32% -> 37%
where the time goes in v4:
time: 173 us; the launch traced here: 172 us
  Pallas kernels  64.2 us (37%)
  starting transfers between devices  50.9 us (29%)
  waiting for transfers between devices  34.7 us (20%)
  local copies, waits for them, and re-layouts  17.7 us (10%)
  other arithmetic  3.94 us (2%)
    pallas_call x5, Pallas kernels, attend(): pl.pallas_call(functools.partial(attend_kernel, head, parts, len(after),...  57.5 us
    ppermute x6, starting transfers between devices, local(): behind.append(lax.ppermute(behind[0], 'ctx', pairs))  23.1 us
    ppermute x4, waiting for transfers between devices, local(): even_back = [lax.ppermute(piece, 'ctx', odd_to_even) for piece in two_back]  18.8 us
    ppermute x6, waiting for transfers between devices, local(): behind.append(lax.ppermute(behind[0], 'ctx', pairs))  11 us
    unnamed x30, local copies, waits for them, and re-layouts  10.9 us
    ppermute x4, starting transfers between devices, local(): two_back = [lax.ppermute(chunk, 'ctx', two_pairs) for chunk in chunks]  10.8 us
    ppermute x2, starting transfers between devices, local(): odd_back = lax.ppermute(own, 'ctx', even_to_odd)  5.89 us
    ppermute x4, starting transfers between devices, local(): even_back = [lax.ppermute(piece, 'ctx', odd_to_even) for piece in two_back]  5.15 us
  transfers between devices with their start and end apart: 24, of which 6 were waited for; matrix products, arithmetic and copies ran while one was open for 5% of the time, Pallas kernels for 37%

profile of v4, /device:TPU:0, one launch (start us, length us, event | category | flops | bytes accessed | tf_op | source)
XLA Modules:
  0.0 172.0 jit_solution(2156468581678503372)
XLA Ops:
  1.8 1.2 copy-done.2
  3.0 1.2 copy-done.5
  4.9 4.9 %collective-permute-start = (bf16[256,256]{1,0:T(8,128)(2,1)S(1)}, bf16[256,256]{1,0:T(8,128)(2,1)S(1)}, u32[]{:S(2)}, u32[]{:S(2)}) collective-permute-start(bf16[256,256]{1,0:T(8,128)(2,1)S(1)} %shard_map.55.behind_refs_0_.rest_0_), channel_id=1, source_target_pairs={{0,8},{4,12},{8,16},{12,20},{16,24},{20,28},{1,9},{5,13},{9,17},{1... | collective-permute-start | bytes 393224 | tf_op jit(solution)/shard_map/ppermute | solution.py:396
  9.9 4.5 %collective-permute-start.1 = (bf16[256,256]{1,0:T(8,128)(2,1)S(1)}, bf16[256,256]{1,0:T(8,128)(2,1)S(1)}, u32[]{:S(2)}, u32[]{:S(2)}) collective-permute-start(bf16[256,256]{1,0:T(8,128)(2,1)S(1)} %shard_map.55.behind_refs_0_.rest_0_), channel_id=1, source_target_pairs={{0,16},{4,20},{8,24},{12,28},{1,17},{5,21},{9,25},{13,29},{2,18},{... | collective-permute-start | bytes 393224 | tf_op jit(solution)/shard_map/ppermute | solution.py:396
  14.4 1.2 copy-done.3
  15.6 1.2 copy-done.6
  16.8 1.4 shard_map.57
  18.2 1.3 collective-permute-start.4
  19.5 3.2 %collective-permute-start.5 = (bf16[1024,256]{1,0:T(8,128)(2,1)}, bf16[1024,256]{1,0:T(8,128)(2,1)}, u32[]{:S(2)}, u32[]{:S(2)}) collective-permute-start(bf16[1024,256]{1,0:T(8,128)(2,1)} %get-tuple-element.19), channel_id=1, source_target_pairs={{0,8},{4,12},{8,16},{12,20},{16,24},{20,28},{1,9},{5,13},{9,17},{1... | collective-permute-start | bytes 1572872 | tf_op jit(solution)/shard_map/ppermute | solution.py:397
  22.8 4.4 %collective-permute-start.8 = (bf16[2048,256]{1,0:T(8,128)(2,1)}, bf16[2048,256]{1,0:T(8,128)(2,1)}, u32[]{:S(2)}, u32[]{:S(2)}) collective-permute-start(bf16[2048,256]{1,0:T(8,128)(2,1)} %get-tuple-element.17.own_ref), channel_id=1, source_target_pairs={{0,4},{8,12},{16,20},{24,28},{1,5},{9,13},{17,21},{25,29},{2,6},{1... | collective-permute-start | bytes 3145736 | tf_op jit(solution)/shard_map/ppermute | solution.py:398
  28.3 1.3 collective-permute-start.2
  29.6 2.6 %collective-permute-done.4.rest_0_ = bf16[1024,256]{1,0:T(8,128)(2,1)S(1)} collective-permute-done((bf16[1024,256]{1,0:T(8,128)(2,1)}, bf16[1024,256]{1,0:T(8,128)(2,1)S(1)}, u32[]{:S(2)}, u32[]{:S(2)}) %collective-permute-start.4) | collective-permute-done | bytes 524320 | tf_op jit(solution)/shard_map/ppermute | solution.py:397
  32.2 1.3 collective-permute-start.6
  33.6 11.0 %collective-permute-done.2.behind_refs_3_ = bf16[256,256]{1,0:T(8,128)(2,1)S(1)} collective-permute-done((bf16[256,256]{1,0:T(8,128)(2,1)S(1)}, bf16[256,256]{1,0:T(8,128)(2,1)S(1)}, u32[]{:S(2)}, u32[]{:S(2)}) %collective-permute-start.2) | collective-permute-done | bytes 131104 | tf_op jit(solution)/shard_map/ppermute | solution.py:396
  44.6 0.8 pad_maximum_fusion
  45.5 1.5 collective-permute-start.3
  47.0 1.3 collective-permute-start.7
  49.1 4.9 %collective-permute-start.12 = (bf16[256,256]{1,0:T(8,128)(2,1)S(1)}, bf16[256,256]{1,0:T(8,128)(2,1)S(1)}, u32[]{:S(2)}, u32[]{:S(2)}) collective-permute-start(bf16[256,256]{1,0:T(8,128)(2,1)S(1)} %shard_map.60.behind_refs_0_.rest_0_), channel_id=1, source_target_pairs={{0,8},{4,12},{8,16},{12,20},{16,24},{20,28},{1,9},{5,13},{9,17},{1... | collective-permute-start | bytes 393224 | tf_op jit(solution)/shard_map/ppermute | solution.py:396
  54.0 0.9 broadcast_in_dim.27
  54.9 1.8 %broadcast_in_dim.28.bias_ref = f32[32,1536]{1,0:T(8,128)} reshape(f32[32,24,64]{2,1,0:T(8,128)} %broadcast_in_dim.27) | data formatting | bytes 393216 | tf_op jit(solution)/shard_map/broadcast_in_dim | solution.py:387
  56.8 0.9 broadcast_in_dim.30
  57.7 1.1 broadcast_in_dim.31.bias_ref
  59.3 2.5 %collective-permute-start.16 = (bf16[1024,256]{1,0:T(8,128)(2,1)S(1)}, bf16[1024,256]{1,0:T(8,128)(2,1)S(1)}, u32[]{:S(2)}, u32[]{:S(2)}) collective-permute-start(bf16[1024,256]{1,0:T(8,128)(2,1)S(1)} %get-tuple-element.25), channel_id=1, source_target_pairs={{0,8},{4,12},{8,16},{12,20},{16,24},{20,28},{1,9},{5,13},{9,17},{1... | collective-permute-start | bytes 1572872 | tf_op jit(solution)/shard_map/ppermute | solution.py:397
  61.8 3.8 %collective-permute-start.17 = (bf16[1024,256]{1,0:T(8,128)(2,1)S(1)}, bf16[1024,256]{1,0:T(8,128)(2,1)S(1)}, u32[]{:S(2)}, u32[]{:S(2)}) collective-permute-start(bf16[1024,256]{1,0:T(8,128)(2,1)S(1)} %get-tuple-element.26), channel_id=1, source_target_pairs={{0,8},{4,12},{8,16},{12,20},{16,24},{20,28},{1,9},{5,13},{9,17},{1... | collective-permute-start | bytes 1572872 | tf_op jit(solution)/shard_map/ppermute | solution.py:397
  65.6 4.0 %collective-permute-done.7.rest_3_ = bf16[1024,256]{1,0:T(8,128)(2,1)} collective-permute-done((bf16[1024,256]{1,0:T(8,128)(2,1)}, bf16[1024,256]{1,0:T(8,128)(2,1)}, u32[]{:S(2)}, u32[]{:S(2)}) %collective-permute-start.7) | collective-permute-done | bytes 524320 | tf_op jit(solution)/shard_map/ppermute | solution.py:400
  69.5 1.5 collective-permute-start.20
  71.1 0.9 copy-done.9
  72.0 1.6 shard_map.56.vert_ref
  73.6 3.0 %collective-permute-start.13 = (bf16[256,256]{1,0:T(8,128)(2,1)S(1)}, bf16[256,256]{1,0:T(8,128)(2,1)S(1)}, u32[]{:S(2)}, u32[]{:S(2)}) collective-permute-start(bf16[256,256]{1,0:T(8,128)(2,1)S(1)} %shard_map.60.behind_refs_0_.rest_0_), channel_id=1, source_target_pairs={{0,16},{4,20},{8,24},{12,28},{1,17},{5,21},{9,25},{13,29},{2,18},{... | collective-permute-start | bytes 393224 | tf_op jit(solution)/shard_map/ppermute | solution.py:396
  76.6 4.5 %collective-permute-start.14 = (bf16[256,256]{1,0:T(8,128)(2,1)S(1)}, bf16[256,256]{1,0:T(8,128)(2,1)S(1)}, u32[]{:S(2)}, u32[]{:S(2)}) collective-permute-start(bf16[256,256]{1,0:T(8,128)(2,1)S(1)} %shard_map.60.behind_refs_0_.rest_0_), channel_id=1, source_target_pairs={{0,24},{4,28},{1,25},{5,29},{2,26},{6,30},{3,27},{7,31}} | collective-permute-start | bytes 393224 | tf_op jit(solution)/shard_map/ppermute | solution.py:396
  81.2 2.2 %copy-done = bf16[2048,1024]{1,0:T(8,128)(2,1)S(1)} copy-done((bf16[2048,1024]{1,0:T(8,128)(2,1)S(1)}, bf16[2048,1024]{1,0:T(8,128)(2,1)}, u32[]{:S(2)}) %copy-start) | copy-done | bytes 4194328
  83.3 0.9 copy-done.10
  84.3 14.9 %shard_map.58 = (bf16[512,512]{1,0:T(8,128)(2,1)S(1)}, bf16[512,512]{1,0:T(8,128)(2,1)S(1)}) custom-call(s32[2]{0:T(128)S(1)} %pad_add_fusion.part_ref, s32[1]{0:T(128)} %bitcast.2.parity_ref, s32[2,8]{1,0:T(2,128)S(1)} %select_reduce_fusion.1.slash_ref, f32[32,1536]{1,0:T(8,128)S(1)} %copy-done.10, bf16[2048,1024]{1,0:T(8,128)(2,1)S(1)} %copy-done, ...), custom_call_target="tpu_custom_call" | custom-call | flops 3221225472 | bytes 5242880 | tf_op jit(solution)/shard_map/pallas_call | solution.py:306
  99.4 1.3 collective-permute-start.18
  100.7 1.3 collective-permute-start.19
  102.1 14.5 %shard_map.59 = (bf16[512,512]{1,0:T(8,128)(2,1)S(1)}, bf16[512,512]{1,0:T(8,128)(2,1)S(1)}) custom-call(s32[2]{0:T(128)S(1)} %pad_add_fusion.1.part_ref, s32[1]{0:T(128)} %bitcast.2.parity_ref, s32[2,8]{1,0:T(2,128)S(1)} %select_reduce_fusion.1.slash_ref, f32[32,1536]{1,0:T(8,128)S(1)} %copy-done.11, bf16[2048,1024]{1,0:T(8,128)(2,1)S(1)} %copy-done.1, ...), custom_call_target="tpu_custom_call" | custom-call | flops 3221225472 | bytes 5242880 | tf_op jit(solution)/shard_map/pallas_call | solution.py:306
  116.6 1.7 collective-permute-start.10
  119.2 1.9 %shard_map.61.vert_ref = bf16[1024,256]{1,0:T(8,128)(2,1)S(1)} custom-call(s32[8,2,4]{2,1,0:T(2,128)S(1)} %broadcast_add_fusion.place_ref, s32[2,16]{1,0:T(2,128)S(1)} %compare_select_fusion.1.source_ref, bf16[256,256]{1,0:T(8,128)(2,1)S(1)} %shard_map.60.behind_refs_0_.rest_0_, bf16[256,256]{1,0:T(8,128)(2,1)S(1)} %collective-permute-done.12.behind_refs_1_, ...), custom_call_target="tpu_custom_call" | custom-call | bytes 1048576 | tf_op jit(solution)/shard_map/pallas_call | solution.py:119
  121.1 3.6 %collective-permute-done.18.rest_2_ = bf16[1024,256]{1,0:T(8,128)(2,1)S(1)} collective-permute-done((bf16[1024,256]{1,0:T(8,128)(2,1)S(1)}, bf16[1024,256]{1,0:T(8,128)(2,1)S(1)}, u32[]{:S(2)}, u32[]{:S(2)}) %collective-permute-start.18) | collective-permute-done | bytes 524320 | tf_op jit(solution)/shard_map/ppermute | solution.py:400
  124.7 11.2 %collective-permute-done.19.rest_3_ = bf16[1024,256]{1,0:T(8,128)(2,1)S(1)} collective-permute-done((bf16[1024,256]{1,0:T(8,128)(2,1)S(1)}, bf16[1024,256]{1,0:T(8,128)(2,1)S(1)}, u32[]{:S(2)}, u32[]{:S(2)}) %collective-permute-start.19) | collective-permute-done | bytes 524320 | tf_op jit(solution)/shard_map/ppermute | solution.py:400
  136.0 7.5 %shard_map.63.rest_5_ = bf16[512,512]{1,0:T(8,128)(2,1)S(1)} custom-call(s32[1]{0:T(128)} %bitcast.part_ref, s32[1]{0:T(128)} %bitcast.2.parity_ref, s32[2,8]{1,0:T(2,128)S(1)} %select_reduce_fusion.1.slash_ref, f32[32,1536]{1,0:T(8,128)S(1)} %broadcast_in_dim.31.bias_ref, bf16[2048,1024]{1,0:T(8,128)(2,1)S(1)} %copy-done.1, ...), custom_call_target="tpu_custom_call" | custom-call | flops 1610612736 | bytes 4194304 | tf_op jit(solution)/shard_map/pallas_call | solution.py:306
  143.5 1.2 collective-permute-start.21
  144.7 7.5 %shard_map.64.rest_5_ = bf16[512,512]{1,0:T(8,128)(2,1)S(1)} custom-call(s32[1]{0:T(128)} %bitcast.1.part_ref, s32[1]{0:T(128)} %bitcast.2.parity_ref, s32[2,8]{1,0:T(2,128)S(1)} %select_reduce_fusion.1.slash_ref, f32[32,1536]{1,0:T(8,128)S(1)} %broadcast_in_dim.31.bias_ref, bf16[2048,1024]{1,0:T(8,128)(2,1)S(1)} %copy-done.1, ...), custom_call_target="tpu_custom_call" | custom-call | flops 1610612736 | bytes 4194304 | tf_op jit(solution)/shard_map/pallas_call | solution.py:306
  152.2 1.0 collective-permute-start.22
  153.2 13.2 %shard_map.65 = (bf16[512,512]{1,0:T(8,128)(2,1)S(1)}, bf16[512,512]{1,0:T(8,128)(2,1)S(1)}) custom-call(s32[2]{0:T(128)S(1)} %pad_add_fusion.1.part_ref, s32[1]{0:T(128)} %bitcast.2.parity_ref, s32[2,8]{1,0:T(2,128)S(1)} %select_reduce_fusion.1.slash_ref, f32[32,1536]{1,0:T(8,128)S(1)} %broadcast_in_dim.31.bias_ref, bf16[2048,1024]{1,0:T(8,128)(2,1)S(1)} %copy-done.1, ...), custom_call_target="tpu_custom_call" | custom-call | flops 3221225472 | bytes 5242880 | tf_op jit(solution)/shard_map/pallas_call | solution.py:306
  166.8 2.2 %collective-permute-done.22 = bf16[512,512]{1,0:T(8,128)(2,1)S(1)} collective-permute-done((bf16[512,512]{1,0:T(8,128)(2,1)S(1)}, bf16[512,512]{1,0:T(8,128)(2,1)S(1)}, u32[]{:S(2)}, u32[]{:S(2)}) %collective-permute-start.22) | collective-permute-done | bytes 524320 | tf_op jit(solution)/shard_map/ppermute | solution.py:423
  169.2 2.0 %copy-done.12 = bf16[512,4096]{1,0:T(8,128)(2,1)} copy-done((bf16[512,4096]{1,0:T(8,128)(2,1)}, bf16[512,4096]{1,0:T(8,128)(2,1)S(1)}, u32[]{:S(2)}) %copy-start.12) | copy-done | bytes 4194328
  171.2 0.8 constant_dynamic-update-slice_fusion
  (83 shorter events, 6.6 us)
Async XLA Ops:
  0.0 28.0 %copy-start.13 = (s32[2,16]{1,0:T(2,128)S(1)}, s32[2,16]{1,0:T(2,128)}, u32[]{:S(2)}) copy-start(s32[2,16]{1,0:T(2,128)} %param.8) | copy-start | bytes 388
  0.0 27.7 %copy-start.14 = (s32[2,8]{1,0:T(2,128)S(1)}, s32[2,8]{1,0:T(2,128)}, u32[]{:S(2)}) copy-start(s32[2,8]{1,0:T(2,128)} %param.9) | copy-start | bytes 196
  1.8 1.2 copy-start.2
  3.0 1.2 copy-start.5
  4.2 44.1 %copy-start.4 = (bf16[2048,256]{1,0:T(8,128)(2,1)S(1)}, bf16[2048,256]{1,0:T(8,128)(2,1)}, u32[]{:S(2)}) copy-start(bf16[2048,256]{1,0:T(8,128)(2,1)} %keys_ref.7) | copy-start | bytes 3145732
  4.2 44.1 %copy-start.7 = (bf16[2048,256]{1,0:T(8,128)(2,1)S(1)}, bf16[2048,256]{1,0:T(8,128)(2,1)}, u32[]{:S(2)}) copy-start(bf16[2048,256]{1,0:T(8,128)(2,1)} %values_ref.7) | copy-start | bytes 3145732
  4.9 23.3 %collective-permute-start = (bf16[256,256]{1,0:T(8,128)(2,1)S(1)}, bf16[256,256]{1,0:T(8,128)(2,1)S(1)}, u32[]{:S(2)}, u32[]{:S(2)}) collective-permute-start(bf16[256,256]{1,0:T(8,128)(2,1)S(1)} %shard_map.55.behind_refs_0_.rest_0_), channel_id=1, source_target_pairs={{0,8},{4,12},{8,16},{12,20},{16,24},{20,28},{1,9},{5,13},{9,17},{1... | collective-permute-start | bytes 393224 | tf_op jit(solution)/shard_map/ppermute | solution.py:396
  9.9 23.8 %collective-permute-start.1 = (bf16[256,256]{1,0:T(8,128)(2,1)S(1)}, bf16[256,256]{1,0:T(8,128)(2,1)S(1)}, u32[]{:S(2)}, u32[]{:S(2)}) collective-permute-start(bf16[256,256]{1,0:T(8,128)(2,1)S(1)} %shard_map.55.behind_refs_0_.rest_0_), channel_id=1, source_target_pairs={{0,16},{4,20},{8,24},{12,28},{1,17},{5,21},{9,25},{13,29},{2,18},{... | collective-permute-start | bytes 393224 | tf_op jit(solution)/shard_map/ppermute | solution.py:396
  14.4 1.2 copy-start.3
  15.6 1.2 copy-start.6
  18.2 14.0 %collective-permute-start.4 = (bf16[1024,256]{1,0:T(8,128)(2,1)}, bf16[1024,256]{1,0:T(8,128)(2,1)S(1)}, u32[]{:S(2)}, u32[]{:S(2)}) collective-permute-start(bf16[1024,256]{1,0:T(8,128)(2,1)} %get-tuple-element.18), channel_id=1, source_target_pairs={{0,8},{4,12},{8,16},{12,20},{16,24},{20,28},{1,9},{5,13},{9,17},{1... | collective-permute-start | bytes 1572872 | tf_op jit(solution)/shard_map/ppermute | solution.py:397
  19.5 27.5 %collective-permute-start.5 = (bf16[1024,256]{1,0:T(8,128)(2,1)}, bf16[1024,256]{1,0:T(8,128)(2,1)}, u32[]{:S(2)}, u32[]{:S(2)}) collective-permute-start(bf16[1024,256]{1,0:T(8,128)(2,1)} %get-tuple-element.19), channel_id=1, source_target_pairs={{0,8},{4,12},{8,16},{12,20},{16,24},{20,28},{1,9},{5,13},{9,17},{1... | collective-permute-start | bytes 1572872 | tf_op jit(solution)/shard_map/ppermute | solution.py:397
  22.8 50.9 %collective-permute-start.8 = (bf16[2048,256]{1,0:T(8,128)(2,1)}, bf16[2048,256]{1,0:T(8,128)(2,1)}, u32[]{:S(2)}, u32[]{:S(2)}) collective-permute-start(bf16[2048,256]{1,0:T(8,128)(2,1)} %get-tuple-element.17.own_ref), channel_id=1, source_target_pairs={{0,4},{8,12},{16,20},{24,28},{1,5},{9,13},{17,21},{25,29},{2,6},{1... | collective-permute-start | bytes 3145736 | tf_op jit(solution)/shard_map/ppermute | solution.py:398
  28.3 16.4 %collective-permute-start.2 = (bf16[256,256]{1,0:T(8,128)(2,1)S(1)}, bf16[256,256]{1,0:T(8,128)(2,1)S(1)}, u32[]{:S(2)}, u32[]{:S(2)}) collective-permute-start(bf16[256,256]{1,0:T(8,128)(2,1)S(1)} %shard_map.55.behind_refs_0_.rest_0_), channel_id=1, source_target_pairs={{0,24},{4,28},{1,25},{5,29},{2,26},{6,30},{3,27},{7,31}} | collective-permute-start | bytes 393224 | tf_op jit(solution)/shard_map/ppermute | solution.py:396
  32.2 16.2 %collective-permute-start.6 = (bf16[1024,256]{1,0:T(8,128)(2,1)S(1)}, bf16[1024,256]{1,0:T(8,128)(2,1)}, u32[]{:S(2)}, u32[]{:S(2)}) collective-permute-start(bf16[1024,256]{1,0:T(8,128)(2,1)S(1)} %collective-permute-done.4.rest_0_), channel_id=1, source_target_pairs={{4,0},{12,8},{20,16},{28,24},{5,1},{13,9},{21,17},{29,25},{6,2},{1... | collective-permute-start | bytes 1572872 | tf_op jit(solution)/shard_map/ppermute | solution.py:400
  44.6 3.7 %copy-start.8 = (bf16[256,256]{1,0:T(8,128)(2,1)}, bf16[256,256]{1,0:T(8,128)(2,1)S(1)}, u32[]{:S(2)}) copy-start(bf16[256,256]{1,0:T(8,128)(2,1)S(1)} %collective-permute-done.2.behind_refs_3_) | copy-start | bytes 393220
  45.5 16.3 %collective-permute-start.3 = (bf16[1024,256]{1,0:T(8,128)(2,1)}, bf16[1024,256]{1,0:T(8,128)(2,1)}, u32[]{:S(2)}, u32[]{:S(2)}) collective-permute-start(bf16[1024,256]{1,0:T(8,128)(2,1)} %pad_maximum_fusion), channel_id=1, source_target_pairs={{0,4},{8,12},{16,20},{24,28},{4,0},{12,8},{20,16},{28,24},{1,5},{9... | collective-permute-start | bytes 1572872 | tf_op jit(solution)/shard_map/ppermute | solution.py:399
  47.0 22.5 %collective-permute-start.7 = (bf16[1024,256]{1,0:T(8,128)(2,1)}, bf16[1024,256]{1,0:T(8,128)(2,1)}, u32[]{:S(2)}, u32[]{:S(2)}) collective-permute-start(bf16[1024,256]{1,0:T(8,128)(2,1)} %collective-permute-done.5.rest_1_), channel_id=1, source_target_pairs={{4,0},{12,8},{20,16},{28,24},{5,1},{13,9},{21,17},{29,25},{6,2},{1... | collective-permute-start | bytes 1572872 | tf_op jit(solution)/shard_map/ppermute | solution.py:400
  49.1 27.5 %collective-permute-start.12 = (bf16[256,256]{1,0:T(8,128)(2,1)S(1)}, bf16[256,256]{1,0:T(8,128)(2,1)S(1)}, u32[]{:S(2)}, u32[]{:S(2)}) collective-permute-start(bf16[256,256]{1,0:T(8,128)(2,1)S(1)} %shard_map.60.behind_refs_0_.rest_0_), channel_id=1, source_target_pairs={{0,8},{4,12},{8,16},{12,20},{16,24},{20,28},{1,9},{5,13},{9,17},{1... | collective-permute-start | bytes 393224 | tf_op jit(solution)/shard_map/ppermute | solution.py:396
  59.3 40.1 %collective-permute-start.16 = (bf16[1024,256]{1,0:T(8,128)(2,1)S(1)}, bf16[1024,256]{1,0:T(8,128)(2,1)S(1)}, u32[]{:S(2)}, u32[]{:S(2)}) collective-permute-start(bf16[1024,256]{1,0:T(8,128)(2,1)S(1)} %get-tuple-element.25), channel_id=1, source_target_pairs={{0,8},{4,12},{8,16},{12,20},{16,24},{20,28},{1,9},{5,13},{9,17},{1... | collective-permute-start | bytes 1572872 | tf_op jit(solution)/shard_map/ppermute | solution.py:397
  61.8 38.9 %collective-permute-start.17 = (bf16[1024,256]{1,0:T(8,128)(2,1)S(1)}, bf16[1024,256]{1,0:T(8,128)(2,1)S(1)}, u32[]{:S(2)}, u32[]{:S(2)}) collective-permute-start(bf16[1024,256]{1,0:T(8,128)(2,1)S(1)} %get-tuple-element.26), channel_id=1, source_target_pairs={{0,8},{4,12},{8,16},{12,20},{16,24},{20,28},{1,9},{5,13},{9,17},{1... | collective-permute-start | bytes 1572872 | tf_op jit(solution)/shard_map/ppermute | solution.py:397
  69.5 66.5 %collective-permute-start.20 = (bf16[2048,256]{1,0:T(8,128)(2,1)S(1)}, bf16[2048,256]{1,0:T(8,128)(2,1)S(1)}, u32[]{:S(2)}, u32[]{:S(2)}) collective-permute-start(bf16[2048,256]{1,0:T(8,128)(2,1)S(1)} %get-tuple-element.24.own_ref), channel_id=1, source_target_pairs={{0,4},{8,12},{16,20},{24,28},{1,5},{9,13},{17,21},{25,29},{2,6},{1... | collective-permute-start | bytes 3145736 | tf_op jit(solution)/shard_map/ppermute | solution.py:398
  71.1 0.9 copy-start.9
  73.6 25.5 %collective-permute-start.13 = (bf16[256,256]{1,0:T(8,128)(2,1)S(1)}, bf16[256,256]{1,0:T(8,128)(2,1)S(1)}, u32[]{:S(2)}, u32[]{:S(2)}) collective-permute-start(bf16[256,256]{1,0:T(8,128)(2,1)S(1)} %shard_map.60.behind_refs_0_.rest_0_), channel_id=1, source_target_pairs={{0,16},{4,20},{8,24},{12,28},{1,17},{5,21},{9,25},{13,29},{2,18},{... | collective-permute-start | bytes 393224 | tf_op jit(solution)/shard_map/ppermute | solution.py:396
  76.6 22.6 %collective-permute-start.14 = (bf16[256,256]{1,0:T(8,128)(2,1)S(1)}, bf16[256,256]{1,0:T(8,128)(2,1)S(1)}, u32[]{:S(2)}, u32[]{:S(2)}) collective-permute-start(bf16[256,256]{1,0:T(8,128)(2,1)S(1)} %shard_map.60.behind_refs_0_.rest_0_), channel_id=1, source_target_pairs={{0,24},{4,28},{1,25},{5,29},{2,26},{6,30},{3,27},{7,31}} | collective-permute-start | bytes 393224 | tf_op jit(solution)/shard_map/ppermute | solution.py:396
  81.1 2.2 %copy-start = (bf16[2048,1024]{1,0:T(8,128)(2,1)S(1)}, bf16[2048,1024]{1,0:T(8,128)(2,1)}, u32[]{:S(2)}) copy-start(bf16[2048,1024]{1,0:T(8,128)(2,1)} %query_ref.9) | copy-start | bytes 12582916
  83.3 0.9 copy-start.10
  84.3 17.8 %copy-start.1 = (bf16[2048,1024]{1,0:T(8,128)(2,1)S(1)}, bf16[2048,1024]{1,0:T(8,128)(2,1)}, u32[]{:S(2)}) copy-start(bf16[2048,1024]{1,0:T(8,128)(2,1)} %query_ref.9) | copy-start | bytes 12582916
  84.3 17.8 %copy-start.11 = (f32[32,1536]{1,0:T(8,128)S(1)}, f32[32,1536]{1,0:T(8,128)}, u32[]{:S(2)}) copy-start(f32[32,1536]{1,0:T(8,128)} %broadcast_in_dim.28.bias_ref) | copy-start | bytes 589828
  99.2 17.5 %collective-permute-start.9 = (bf16[512,512]{1,0:T(8,128)(2,1)S(1)}, bf16[512,512]{1,0:T(8,128)(2,1)S(1)}, u32[]{:S(2)}, u32[]{:S(2)}) collective-permute-start(bf16[512,512]{1,0:T(8,128)(2,1)S(1)} %get-tuple-element.20), channel_id=1, source_target_pairs={{0,3},{1,2},{2,1},{3,0},{4,7},{5,6},{6,5},{7,4},{8,11},{9,10},{10,... | collective-permute-start | bytes 1572872 | tf_op jit(solution)/shard_map/ppermute | solution.py:423
  99.3 19.6 %collective-permute-start.15 = (bf16[1024,256]{1,0:T(8,128)(2,1)S(1)}, bf16[1024,256]{1,0:T(8,128)(2,1)S(1)}, u32[]{:S(2)}, u32[]{:S(2)}) collective-permute-start(bf16[1024,256]{1,0:T(8,128)(2,1)S(1)} %pad_maximum_fusion.1), channel_id=1, source_target_pairs={{0,4},{8,12},{16,20},{24,28},{4,0},{12,8},{20,16},{28,24},{1,5},{9... | collective-permute-start | bytes 1572872 | tf_op jit(solution)/shard_map/ppermute | solution.py:399
  99.4 25.3 %collective-permute-start.18 = (bf16[1024,256]{1,0:T(8,128)(2,1)S(1)}, bf16[1024,256]{1,0:T(8,128)(2,1)S(1)}, u32[]{:S(2)}, u32[]{:S(2)}) collective-permute-start(bf16[1024,256]{1,0:T(8,128)(2,1)S(1)} %collective-permute-done.16.rest_0_), channel_id=1, source_target_pairs={{4,0},{12,8},{20,16},{28,24},{5,1},{13,9},{21,17},{29,25},{6,2},{1... | collective-permute-start | bytes 1572872 | tf_op jit(solution)/shard_map/ppermute | solution.py:400
  100.7 35.3 %collective-permute-start.19 = (bf16[1024,256]{1,0:T(8,128)(2,1)S(1)}, bf16[1024,256]{1,0:T(8,128)(2,1)S(1)}, u32[]{:S(2)}, u32[]{:S(2)}) collective-permute-start(bf16[1024,256]{1,0:T(8,128)(2,1)S(1)} %collective-permute-done.17.rest_1_), channel_id=1, source_target_pairs={{4,0},{12,8},{20,16},{28,24},{5,1},{13,9},{21,17},{29,25},{6,2},{1... | collective-permute-start | bytes 1572872 | tf_op jit(solution)/shard_map/ppermute | solution.py:400
  116.6 49.8 %collective-permute-start.10 = (bf16[512,512]{1,0:T(8,128)(2,1)S(1)}, bf16[512,512]{1,0:T(8,128)(2,1)S(1)}, u32[]{:S(2)}, u32[]{:S(2)}) collective-permute-start(bf16[512,512]{1,0:T(8,128)(2,1)S(1)} %get-tuple-element.21.rest_5_), channel_id=1, source_target_pairs={{0,2},{1,3},{2,0},{3,1},{4,6},{5,7},{6,4},{7,5},{8,10},{9,11},{10,... | collective-permute-start | bytes 1572872 | tf_op jit(solution)/shard_map/ppermute | solution.py:423
  118.9 47.7 %collective-permute-start.11 = (bf16[512,512]{1,0:T(8,128)(2,1)S(1)}, bf16[512,512]{1,0:T(8,128)(2,1)S(1)}, u32[]{:S(2)}, u32[]{:S(2)}) collective-permute-start(bf16[512,512]{1,0:T(8,128)(2,1)S(1)} %get-tuple-element.22), channel_id=1, source_target_pairs={{0,1},{1,0},{2,3},{3,2},{4,5},{5,4},{6,7},{7,6},{8,9},{9,8},{10,11... | collective-permute-start | bytes 1572872 | tf_op jit(solution)/shard_map/ppermute | solution.py:423
  143.5 23.2 %collective-permute-start.21 = (bf16[512,512]{1,0:T(8,128)(2,1)S(1)}, bf16[512,512]{1,0:T(8,128)(2,1)S(1)}, u32[]{:S(2)}, u32[]{:S(2)}) collective-permute-start(bf16[512,512]{1,0:T(8,128)(2,1)S(1)} %shard_map.63.rest_5_), channel_id=1, source_target_pairs={{0,3},{1,2},{2,1},{3,0},{4,7},{5,6},{6,5},{7,4},{8,11},{9,10},{10,... | collective-permute-start | bytes 1572872 | tf_op jit(solution)/shard_map/ppermute | solution.py:423
  152.2 16.8 %collective-permute-start.22 = (bf16[512,512]{1,0:T(8,128)(2,1)S(1)}, bf16[512,512]{1,0:T(8,128)(2,1)S(1)}, u32[]{:S(2)}, u32[]{:S(2)}) collective-permute-start(bf16[512,512]{1,0:T(8,128)(2,1)S(1)} %shard_map.64.rest_5_), channel_id=1, source_target_pairs={{0,2},{1,3},{2,0},{3,1},{4,6},{5,7},{6,4},{7,5},{8,10},{9,11},{10,... | collective-permute-start | bytes 1572872 | tf_op jit(solution)/shard_map/ppermute | solution.py:423
  166.4 2.7 %collective-permute-start.23 = (bf16[512,512]{1,0:T(8,128)(2,1)S(1)}, bf16[512,512]{1,0:T(8,128)(2,1)S(1)}, u32[]{:S(2)}, u32[]{:S(2)}) collective-permute-start(bf16[512,512]{1,0:T(8,128)(2,1)S(1)} %get-tuple-element.27), channel_id=1, source_target_pairs={{0,1},{1,0},{2,3},{3,2},{4,5},{5,4},{6,7},{7,6},{8,9},{9,8},{10,11... | collective-permute-start | bytes 1572872 | tf_op jit(solution)/shard_map/ppermute | solution.py:423
  169.1 2.0 %copy-start.12 = (bf16[512,4096]{1,0:T(8,128)(2,1)}, bf16[512,4096]{1,0:T(8,128)(2,1)S(1)}, u32[]{:S(2)}) copy-start(bf16[512,4096]{1,0:T(8,128)(2,1)S(1)} %constant_dynamic-update-slice_fusion.1) | copy-start | bytes 12582916

commit v5 on v4

--- a/solution.py
+++ b/solution.py
@@ -26,40 +26,43 @@
     return pl.ds(pl.multiple_of(index * BLK, BLK), count * BLK)
 
 
-def slots_kernel(head, local_ref, keys_ref, values_ref, *rest):
-    out_ref, sem = rest[-2:]
+def slots_kernel(local_ref, keys_ref, values_ref, out_ref, sem):
     copies = []
-    for slot in range(MOWN):
-        for side, source in enumerate((keys_ref, values_ref)):
-            copies.append(
-                pltpu.make_async_copy(
-                    source.at[blocks_at(local_ref[head, slot]), pl.ds(head * HD, HD)],
-                    out_ref.at[pl.ds(slot * BLK, BLK), pl.ds(side * HD, HD)],
-                    sem.at[len(copies)],
+    for head in range(local_ref.shape[0]):
+        for slot in range(MOWN):
+            for side, source in enumerate((keys_ref, values_ref)):
+                copies.append(
+                    pltpu.make_async_copy(
+                        source.at[blocks_at(local_ref[head, slot]), pl.ds(head * HD, HD)],
+                        out_ref.at[
+                            pl.ds((head * MOWN + slot) * BLK, BLK), pl.ds(side * HD, HD)
+                        ],
+                        sem.at[len(copies)],
+                    )
                 )
-            )
     for copy in copies:
         copy.start()
     for copy in copies:
         copy.wait()
 
 
-def owned_slots(head, local_block, keys, values, after):
+def owned_slots(local_block, keys, values):
+    heads = local_block.shape[0]
     return pl.pallas_call(
-        functools.partial(slots_kernel, head),
-        out_shape=jax.ShapeDtypeStruct((MOWN * BLK, 2 * HD), keys.dtype),
-        in_specs=[SMEM] + [ANY] * (2 + len(after)),
+        slots_kernel,
+        out_shape=jax.ShapeDtypeStruct((heads * MOWN * BLK, 2 * HD), keys.dtype),
+        in_specs=[SMEM, ANY, ANY],
         out_specs=ANY,
-        scratch_shapes=[pltpu.SemaphoreType.DMA((MOWN * 2,))],
+        scratch_shapes=[pltpu.SemaphoreType.DMA((heads * MOWN * 2,))],
         compiler_params=pltpu.CompilerParams(vmem_limit_bytes=1 << 20),
         cost_estimate=pl.CostEstimate(
-            flops=0, bytes_accessed=8 * MOWN * BLK * HD, transcendentals=0
+            flops=0, bytes_accessed=8 * heads * MOWN * BLK * HD, transcendentals=0
         ),
-    )(local_block, keys, values, *after)
-
-
-def pair_kernel(head, keys_ref, values_ref, *rest):
-    out_refs, sem = rest[-2 - CHUNKS : -1], rest[-1]
+    )(local_block, keys, values)
+
+
+def pair_kernel(head, count, keys_ref, values_ref, *rest):
+    out_refs, sem = rest[-2 - count : -1], rest[-1]
     whole, chunks = out_refs[0], out_refs[1:]
     copies = []
     for side, source in enumerate((keys_ref, values_ref)):
@@ -75,15 +78,15 @@
         copy.wait()
 
 
-def pair_of(head, keys, values, after):
+def pair_of(head, count, keys, values, after):
     rows = keys.shape[0]
     whole, *chunks = pl.pallas_call(
-        functools.partial(pair_kernel, head),
+        functools.partial(pair_kernel, head, count),
         out_shape=[jax.ShapeDtypeStruct((rows, 2 * HD), keys.dtype)]
-        + [jax.ShapeDtypeStruct((rows // CHUNKS, 2 * HD), keys.dtype)] * CHUNKS,
+        + [jax.ShapeDtypeStruct((rows // count, 2 * HD), keys.dtype)] * count,
         in_specs=[ANY] * (2 + len(after)),
-        out_specs=[ANY] * (1 + CHUNKS),
-        scratch_shapes=[pltpu.SemaphoreType.DMA((2 + 2 * CHUNKS,))],
+        out_specs=[ANY] * (1 + count),
+        scratch_shapes=[pltpu.SemaphoreType.DMA((2 + 2 * count,))],
         compiler_params=pltpu.CompilerParams(vmem_limit_bytes=1 << 20),
         cost_estimate=pl.CostEstimate(flops=0, bytes_accessed=16 * rows * HD, transcendentals=0),
     )(keys, values, *after)
@@ -92,13 +95,15 @@
 
 def listed_kernel(head, place_ref, source_ref, behind_refs, across_ref, out_ref, sem):
     count = len(behind_refs)
+    heads = place_ref.shape[1]
     for index in range(2 * count):
         for slot in range(MOWN):
             place = place_ref[index, head, slot]
             if index < count:
-                found = behind_refs[index].at[pl.ds(slot * BLK, BLK)]
+                found = behind_refs[index].at[pl.ds((head * MOWN + slot) * BLK, BLK)]
             else:
-                found = across_ref.at[pl.ds(((index - count) * MOWN + slot) * BLK, BLK)]
+                first = ((index - count) * heads + head) * MOWN + slot
+                found = across_ref.at[pl.ds(first * BLK, BLK)]
 
             @pl.when(place >= 0)
             def _():
@@ -128,13 +133,13 @@
 
 
 def attend_kernel(
-    head, parts, waits, part_blocks, group_heads, part_ref, parity_ref, slash_ref, bias_ref, query_ref,
+    head, parts, chunks, waits, part_blocks, group_heads, part_ref, parity_ref, slash_ref, bias_ref, query_ref,
     vert_ref, own_ref, *rest,
 ):
-    two_back = rest[:CHUNKS]
-    even_back = rest[CHUNKS : 2 * CHUNKS]
-    odd_back = rest[2 * CHUNKS]
-    rest = rest[2 * CHUNKS + 1 + waits :]
+    two_back = rest[:chunks]
+    even_back = rest[chunks : 2 * chunks]
+    odd_back = rest[2 * chunks]
+    rest = rest[2 * chunks + 1 + waits :]
     out_refs = rest[:parts]
     (
         queries, out, vert, vert_keys, window, scores_a, scores_b, weights_a, weights_b, max_a,
@@ -145,7 +150,7 @@
     blocks_dev = tok_rows // BLK
     part_rows = part_blocks * BLK
     group_cols = group_heads * HD
-    chunk_rows = tok_rows // CHUNKS
+    chunk_rows = tok_rows // chunks
     last = parts * part_blocks - 1
     step = pl.program_id(0)
     scale = 1.0 / math.sqrt(HD)
@@ -244,7 +249,7 @@
                 query_sem,
             ).start()
         pltpu.make_async_copy(vert_ref, vert, vert_sem).start()
-        for chunk in range(CHUNKS):
+        for chunk in range(chunks):
             pltpu.make_async_copy(
                 two_back[chunk], window.at[pl.ds(chunk * chunk_rows, chunk_rows)], window_sem
             ).start()
@@ -257,7 +262,7 @@
 
         @pl.when(parity_ref[0] == 0)
         def _():
-            for chunk in range(CHUNKS):
+            for chunk in range(chunks):
                 pltpu.make_async_copy(
                     even_back[chunk],
                     window.at[pl.ds(tok_rows + chunk * chunk_rows, chunk_rows)],
@@ -304,12 +309,14 @@
     rows = group_heads * BLK
     keys_seen = (NV + NS) * BLK
     return pl.pallas_call(
-        functools.partial(attend_kernel, head, parts, len(after), part_blocks, group_heads),
+        functools.partial(
+            attend_kernel, head, parts, len(two_back), len(after), part_blocks, group_heads
+        ),
         out_shape=[jax.ShapeDtypeStruct((part_rows, group_cols), jnp.bfloat16)] * parts,
         grid_spec=pltpu.PrefetchScalarGridSpec(
             num_scalar_prefetch=3,
             grid=(parts * part_blocks // STEP_BLOCKS,),
-            in_specs=[pl.BlockSpec(bias.shape, lambda s, *_: (0, 0))] + [ANY] * (4 + 2 * CHUNKS + len(after)),
+            in_specs=[pl.BlockSpec(bias.shape, lambda s, *_: (0, 0))] + [ANY] * (4 + 2 * len(two_back) + len(after)),
             out_specs=[ANY] * parts,
             scratch_shapes=[
                 pltpu.VMEM((parts * part_rows, group_cols), jnp.bfloat16),
@@ -386,32 +393,30 @@
     valid = jnp.concatenate([vert_valid, slash_valid], axis=2)
     bias = jnp.repeat(jnp.where(valid, 0.0, NEG).astype(jnp.float32), BLK, axis=2)
 
+    behind = [owned_slots(local_block, keys, values)]
+    for distance in range(2, shard_count, 2):
+        pairs = [(i, i + distance) for i in range(shard_count - distance)]
+        behind.append(lax.ppermute(behind[0], "ctx", pairs))
+    across = lax.ppermute(jnp.concatenate(behind), "ctx", even_to_odd + odd_to_even)
+
     windows = []
-    after = []
+    after = [behind[1]]
     for head in range(kv_local):
-        behind = [owned_slots(head, local_block, keys, values, after)]
-        own, chunks = pair_of(head, keys, values, behind)
-        for distance in range(2, shard_count, 2):
-            pairs = [(i, i + distance) for i in range(shard_count - distance)]
-            behind.append(lax.ppermute(behind[0], "ctx", pairs))
+        own, chunks = pair_of(head, CHUNKS if head == 0 else 1, keys, values, after)
         two_back = [lax.ppermute(chunk, "ctx", two_pairs) for chunk in chunks]
         odd_back = lax.ppermute(own, "ctx", even_to_odd)
-        across = lax.ppermute(jnp.concatenate(behind), "ctx", even_to_odd + odd_to_even)
         even_back = [lax.ppermute(piece, "ctx", odd_to_even) for piece in two_back]
         vert = listed_blocks(head, place, source, behind, across)
         windows.append((vert, own, two_back, even_back, odd_back))
-        after = two_back + even_back[:-1]
+        after = two_back[-1:]
 
     parity = (shard_index % 2).reshape(1).astype(jnp.int32)
     out = jnp.zeros((part_rows, head_count * kv_local * group_cols), jnp.bfloat16)
-    half = head_count // 2
     after = []
     for head in range(kv_local):
         vert, own, two_back, even_back, odd_back = windows[head]
-        calls = [range(head_count - 1, half - 1, -1), range(half - 1, -1, -1)]
-        if head + 1 == kv_local:
-            calls = [range(f, f - 1, -1) for f in calls[0]] + calls[1:]
-        for flips in calls:
+        for flip in range(head_count - 1, -1, -1):
+            flips = [flip]
             others = [head_index ^ flip for flip in flips]
             pieces = attend(
                 head, jnp.stack(others).astype(jnp.int32), parity, slash, bias[head], queries,

time: 173 us -> 182 us (1.052); the launches traced: 172 us -> 178 us
  waiting for transfers between devices: 34.7 us -> 16.3 us
  Pallas kernels: 64.2 us -> 76.2 us
  local copies, waits for them, and re-layouts: 17.7 us -> 27.1 us
  other arithmetic: 3.94 us -> 7.79 us
    ppermute x4 -> x3, waiting for transfers between devices: 18.8 us -> 0.59 us  [local(): even_back = [lax.ppermute(piece, 'ctx', odd_to_even) for piece in two_back]]
    pallas_call x9 -> x11, Pallas kernels: 60.7 us -> 72.9 us  [the longest x8 70.1 us: attend(): pl.pallas_call(functools.partial(attend_kernel, head, parts, len(two_back...]
    ppermute x6 -> x3, waiting for transfers between devices: 11 us -> 0.01 us  [local(): behind.append(lax.ppermute(behind[0], 'ctx', pairs))]
    ppermute x6 -> x3, starting transfers between devices: 23.1 us -> 12.2 us  [local(): behind.append(lax.ppermute(behind[0], 'ctx', pairs))]
    ppermute x4 -> x3, starting transfers between devices: 10.8 us -> 20.2 us  [local(): two_back = [lax.ppermute(chunk, 'ctx', two_pairs) for chunk in chunks]]
    ppermute x2, waiting for transfers between devices: 0.01 us -> 7.64 us  [local(): odd_back = lax.ppermute(own, 'ctx', even_to_odd)]
    unnamed x30 -> x40, local copies, waits for them, and re-layouts: 10.9 us -> 17.6 us
    dynamic_update_slice x8, local copies, waits for them, and re-layouts: 1.29 us -> 4.67 us  [local(): lax.dynamic_update_slice(out, piece, (0, other * kv_local * group_cols +...]
  transfers between devices with their start and end apart: 24 -> 18, of which waited for: 6 -> 5; matrix products, arithmetic and copies ran while one was open for 5% -> 8% of each run, Pallas kernels for 37% -> 38%
where the time goes in v5:
time: 182 us; the launch traced here: 178 us
  Pallas kernels  76.2 us (42%)
  starting transfers between devices  50.6 us (28%)
  local copies, waits for them, and re-layouts  27.1 us (15%)
  waiting for transfers between devices  16.3 us (9%)
  other arithmetic  7.79 us (4%)
    pallas_call x8, Pallas kernels, attend(): pl.pallas_call(functools.partial(attend_kernel, head, parts, len(two_back...  70.1 us
    ppermute x3, starting transfers between devices, local(): two_back = [lax.ppermute(chunk, 'ctx', two_pairs) for chunk in chunks]  20.2 us
    unnamed x40, local copies, waits for them, and re-layouts  17.6 us
    ppermute x3, starting transfers between devices, local(): behind.append(lax.ppermute(behind[0], 'ctx', pairs))  12.2 us
    ppermute x2, starting transfers between devices, local(): odd_back = lax.ppermute(own, 'ctx', even_to_odd)  8.79 us
    ppermute x2, waiting for transfers between devices, local(): odd_back = lax.ppermute(own, 'ctx', even_to_odd)  7.64 us
    ppermute x3, waiting for transfers between devices, local(): two_back = [lax.ppermute(chunk, 'ctx', two_pairs) for chunk in chunks]  5.32 us
    dynamic_update_slice x8, local copies, waits for them, and re-layouts, local(): lax.dynamic_update_slice(out, piece, (0, other * kv_local * group_cols +...  4.67 us
  transfers between devices with their start and end apart: 18, of which 5 were waited for; matrix products, arithmetic and copies ran while one was open for 8% of the time, Pallas kernels for 38%

profile of v5, /device:TPU:0, one launch (start us, length us, event | category | flops | bytes accessed | tf_op | source)
XLA Modules:
  0.0 178.5 jit_solution(15319762151860047214)
XLA Ops:
  1.7 1.2 copy-done.9
  3.0 1.2 copy-done.11
  5.0 5.0 %collective-permute-start = (bf16[512,256]{1,0:T(8,128)(2,1)S(1)}, bf16[512,256]{1,0:T(8,128)(2,1)S(1)}, u32[]{:S(2)}, u32[]{:S(2)}) collective-permute-start(bf16[512,256]{1,0:T(8,128)(2,1)S(1)} %shard_map.55.behind_refs_0_), channel_id=1, source_target_pairs={{0,8},{4,12},{8,16},{12,20},{16,24},{20,28},{1,9},{5,13},{9,17},{1... | collective-permute-start | bytes 786440 | tf_op jit(solution)/shard_map/ppermute | solution.py:399
  9.9 5.2 %collective-permute-start.1 = (bf16[512,256]{1,0:T(8,128)(2,1)S(1)}, bf16[512,256]{1,0:T(8,128)(2,1)}, u32[]{:S(2)}, u32[]{:S(2)}) collective-permute-start(bf16[512,256]{1,0:T(8,128)(2,1)S(1)} %shard_map.55.behind_refs_0_), channel_id=1, source_target_pairs={{0,16},{4,20},{8,24},{12,28},{1,17},{5,21},{9,25},{13,29},{2,18},{... | collective-permute-start | bytes 786440 | tf_op jit(solution)/shard_map/ppermute | solution.py:399
  15.1 2.0 %collective-permute-start.2 = (bf16[512,256]{1,0:T(8,128)(2,1)S(1)}, bf16[512,256]{1,0:T(8,128)(2,1)}, u32[]{:S(2)}, u32[]{:S(2)}) collective-permute-start(bf16[512,256]{1,0:T(8,128)(2,1)S(1)} %shard_map.55.behind_refs_0_), channel_id=1, source_target_pairs={{0,24},{4,28},{1,25},{5,29},{2,26},{6,30},{3,27},{7,31}} | collective-permute-start | bytes 786440 | tf_op jit(solution)/shard_map/ppermute | solution.py:399
  17.1 1.0 convert_reduce_fusion.1
  21.5 0.9 copy-done.16
  23.4 10.2 %collective-permute-start.5 = (bf16[1024,256]{1,0:T(8,128)(2,1)S(1)}, bf16[1024,256]{1,0:T(8,128)(2,1)S(1)}, u32[]{:S(2)}, u32[]{:S(2)}) collective-permute-start(bf16[1024,256]{1,0:T(8,128)(2,1)S(1)} %get-tuple-element.12), channel_id=1, source_target_pairs={{0,8},{4,12},{8,16},{12,20},{16,24},{20,28},{1,9},{5,13},{9,17},{1... | collective-permute-start | bytes 1572872 | tf_op jit(solution)/shard_map/ppermute | solution.py:406
  33.6 2.1 %pad_maximum_fusion = bf16[2048,256]{1,0:T(8,128)(2,1)} fusion(bf16[512,256]{1,0:T(8,128)(2,1)} %collective-permute-done.2.behind_refs_3_, bf16[512,256]{1,0:T(8,128)(2,1)} %collective-permute-done.1.behind_refs_2_, bf16[512,256]{1,0:T(8,128)(2,1)} %copy-done.15, bf16[512,256]{1,0:T(8,128)(2,1)S(1)} %shard_map.55.behind_refs_0_), kind=kLoop, calls=%fused_computation | loop fusion | flops 4194304 | bytes 2097152 | tf_op jit(solution)/shard_map/concatenate | solution.py:400
  35.8 1.5 collective-permute-start.3
  37.2 5.6 %collective-permute-start.4 = (bf16[1024,256]{1,0:T(8,128)(2,1)}, bf16[1024,256]{1,0:T(8,128)(2,1)}, u32[]{:S(2)}, u32[]{:S(2)}) collective-permute-start(bf16[1024,256]{1,0:T(8,128)(2,1)} %get-tuple-element.11), channel_id=1, source_target_pairs={{0,8},{4,12},{8,16},{12,20},{16,24},{20,28},{1,9},{5,13},{9,17},{1... | collective-permute-start | bytes 1572872 | tf_op jit(solution)/shard_map/ppermute | solution.py:406
  42.8 3.4 %collective-permute-start.8 = (bf16[2048,256]{1,0:T(8,128)(2,1)S(1)}, bf16[2048,256]{1,0:T(8,128)(2,1)}, u32[]{:S(2)}, u32[]{:S(2)}) collective-permute-start(bf16[2048,256]{1,0:T(8,128)(2,1)S(1)} %get-tuple-element.10.own_ref), channel_id=1, source_target_pairs={{0,4},{8,12},{16,20},{24,28},{1,5},{9,13},{17,21},{25,29},{2,6},{1... | collective-permute-start | bytes 3145736 | tf_op jit(solution)/shard_map/ppermute | solution.py:407
  46.3 1.0 shard_map.63
  47.5 4.5 %collective-permute-start.12 = (bf16[2048,256]{1,0:T(8,128)(2,1)}, bf16[2048,256]{1,0:T(8,128)(2,1)S(1)}, u32[]{:S(2)}, u32[]{:S(2)}) collective-permute-start(bf16[2048,256]{1,0:T(8,128)(2,1)} %get-tuple-element.14), channel_id=1, source_target_pairs={{0,8},{4,12},{8,16},{12,20},{16,24},{20,28},{1,9},{5,13},{9,17},{1... | collective-permute-start | bytes 3145736 | tf_op jit(solution)/shard_map/ppermute | solution.py:406
  52.1 1.3 collective-permute-start.7
  53.4 1.3 collective-permute-done.4.rest_0_
  54.7 1.3 collective-permute-start.6
  57.2 1.1 broadcast_in_dim.28.bias_ref
  58.4 2.8 %collective-permute-done.3.across_ref = bf16[2048,256]{1,0:T(8,128)(2,1)} collective-permute-done((bf16[2048,256]{1,0:T(8,128)(2,1)}, bf16[2048,256]{1,0:T(8,128)(2,1)}, u32[]{:S(2)}, u32[]{:S(2)}) %collective-permute-start.3) | collective-permute-done | bytes 1048608 | tf_op jit(solution)/shard_map/ppermute | solution.py:400
  61.2 5.3 %collective-permute-start.14 = (bf16[2048,256]{1,0:T(8,128)(2,1)S(1)}, bf16[2048,256]{1,0:T(8,128)(2,1)}, u32[]{:S(2)}, u32[]{:S(2)}) collective-permute-start(bf16[2048,256]{1,0:T(8,128)(2,1)S(1)} %get-tuple-element.13.own_ref), channel_id=1, source_target_pairs={{0,4},{8,12},{16,20},{24,28},{1,5},{9,13},{17,21},{25,29},{2,6},{1... | collective-permute-start | bytes 3145736 | tf_op jit(solution)/shard_map/ppermute | solution.py:407
  66.5 0.9 copy-done.13
  67.5 0.9 copy-done.17
  68.4 1.6 shard_map.56.vert_ref
  70.0 4.0 %collective-permute-done.12.rest_0_ = bf16[2048,256]{1,0:T(8,128)(2,1)S(1)} collective-permute-done((bf16[2048,256]{1,0:T(8,128)(2,1)}, bf16[2048,256]{1,0:T(8,128)(2,1)S(1)}, u32[]{:S(2)}, u32[]{:S(2)}) %collective-permute-start.12) | collective-permute-done | bytes 1048608 | tf_op jit(solution)/shard_map/ppermute | solution.py:406
  74.0 1.3 collective-permute-start.13
  75.9 7.6 %collective-permute-done.8.rest_4_ = bf16[2048,256]{1,0:T(8,128)(2,1)} collective-permute-done((bf16[2048,256]{1,0:T(8,128)(2,1)S(1)}, bf16[2048,256]{1,0:T(8,128)(2,1)}, u32[]{:S(2)}, u32[]{:S(2)}) %collective-permute-start.8) | collective-permute-done | bytes 1048608 | tf_op jit(solution)/shard_map/ppermute | solution.py:407
  83.5 2.2 %copy-done = bf16[2048,1024]{1,0:T(8,128)(2,1)S(1)} copy-done((bf16[2048,1024]{1,0:T(8,128)(2,1)S(1)}, bf16[2048,1024]{1,0:T(8,128)(2,1)}, u32[]{:S(2)}) %copy-start) | copy-done | bytes 4194328
  85.7 1.0 copy-done.5
  86.8 9.5 %shard_map.58.rest_5_ = bf16[512,512]{1,0:T(8,128)(2,1)} custom-call(s32[1]{0:T(128)} %bitcast.part_ref, s32[1]{0:T(128)} %bitcast.1.parity_ref, s32[2,8]{1,0:T(2,128)S(1)} %select_reduce_fusion.1.slash_ref, f32[32,1536]{1,0:T(8,128)S(1)} %broadcast_in_dim.28.bias_ref, bf16[2048,1024]{1,0:T(8,128)(2,1)S(1)} %copy-done, ...), custom_call_target="tpu_custom_call" | custom-call | flops 1610612736 | bytes 4194304 | tf_op jit(solution)/shard_map/pallas_call | solution.py:311
  96.4 9.2 %shard_map.59.rest_5_ = bf16[512,512]{1,0:T(8,128)(2,1)} custom-call(s32[1]{0:T(128)} %bitcast.3.part_ref, s32[1]{0:T(128)} %bitcast.1.parity_ref, s32[2,8]{1,0:T(2,128)S(1)} %select_reduce_fusion.1.slash_ref, f32[32,1536]{1,0:T(8,128)S(1)} %broadcast_in_dim.28.bias_ref, bf16[2048,1024]{1,0:T(8,128)(2,1)S(1)} %copy-done.1, ...), custom_call_target="tpu_custom_call" | custom-call | flops 1610612736 | bytes 4194304 | tf_op jit(solution)/shard_map/pallas_call | solution.py:311
  105.7 1.6 collective-permute-start.10
  107.3 9.3 %shard_map.60.rest_5_ = bf16[512,512]{1,0:T(8,128)(2,1)} custom-call(s32[1]{0:T(128)} %bitcast.4.part_ref, s32[1]{0:T(128)} %bitcast.1.parity_ref, s32[2,8]{1,0:T(2,128)S(1)} %select_reduce_fusion.1.slash_ref, f32[32,1536]{1,0:T(8,128)S(1)} %broadcast_in_dim.28.bias_ref, bf16[2048,1024]{1,0:T(8,128)(2,1)S(1)} %copy-done.1, ...), custom_call_target="tpu_custom_call" | custom-call | flops 1610612736 | bytes 4194304 | tf_op jit(solution)/shard_map/pallas_call | solution.py:311
  117.9 1.1 broadcast_in_dim.31.bias_ref
  120.0 0.9 copy-done.18
  120.9 1.7 shard_map.62.vert_ref
  122.7 2.2 %copy-done.2 = bf16[2048,1024]{1,0:T(8,128)(2,1)S(1)} copy-done((bf16[2048,1024]{1,0:T(8,128)(2,1)S(1)}, bf16[2048,1024]{1,0:T(8,128)(2,1)}, u32[]{:S(2)}) %copy-start.2) | copy-done | bytes 4194328
  124.9 1.0 copy-done.6
  125.9 1.0 copy-done.8
  127.0 8.5 %shard_map.61.rest_3_ = bf16[512,512]{1,0:T(8,128)(2,1)S(1)} custom-call(s32[1]{0:T(128)} %bitcast.5.part_ref, s32[1]{0:T(128)} %bitcast.1.parity_ref, s32[2,8]{1,0:T(2,128)S(1)} %select_reduce_fusion.1.slash_ref, f32[32,1536]{1,0:T(8,128)S(1)} %broadcast_in_dim.28.bias_ref, bf16[2048,1024]{1,0:T(8,128)(2,1)S(1)} %copy-done.2, ...), custom_call_target="tpu_custom_call" | custom-call | flops 1610612736 | bytes 4194304 | tf_op jit(solution)/shard_map/pallas_call | solution.py:311
  136.0 1.4 constant_dynamic-update-slice_fusion.6
  137.4 1.1 constant_dynamic-update-slice_fusion.5
  138.5 1.1 constant_dynamic-update-slice_fusion.4
  139.6 8.4 %shard_map.64.rest_3_ = bf16[512,512]{1,0:T(8,128)(2,1)S(1)} custom-call(s32[1]{0:T(128)} %bitcast.part_ref, s32[1]{0:T(128)} %bitcast.1.parity_ref, s32[2,8]{1,0:T(2,128)S(1)} %select_reduce_fusion.1.slash_ref, f32[32,1536]{1,0:T(8,128)S(1)} %broadcast_in_dim.31.bias_ref, bf16[2048,1024]{1,0:T(8,128)(2,1)S(1)} %copy-done.3, ...), custom_call_target="tpu_custom_call" | custom-call | flops 1610612736 | bytes 4194304 | tf_op jit(solution)/shard_map/pallas_call | solution.py:311
  148.0 1.2 collective-permute-start.15
  149.3 8.4 %shard_map.65.rest_3_ = bf16[512,512]{1,0:T(8,128)(2,1)S(1)} custom-call(s32[1]{0:T(128)} %bitcast.3.part_ref, s32[1]{0:T(128)} %bitcast.1.parity_ref, s32[2,8]{1,0:T(2,128)S(1)} %select_reduce_fusion.1.slash_ref, f32[32,1536]{1,0:T(8,128)S(1)} %broadcast_in_dim.31.bias_ref, bf16[2048,1024]{1,0:T(8,128)(2,1)S(1)} %copy-done.3, ...), custom_call_target="tpu_custom_call" | custom-call | flops 1610612736 | bytes 4194304 | tf_op jit(solution)/shard_map/pallas_call | solution.py:311
  158.4 8.4 %shard_map.66.rest_3_ = bf16[512,512]{1,0:T(8,128)(2,1)S(1)} custom-call(s32[1]{0:T(128)} %bitcast.4.part_ref, s32[1]{0:T(128)} %bitcast.1.parity_ref, s32[2,8]{1,0:T(2,128)S(1)} %select_reduce_fusion.1.slash_ref, f32[32,1536]{1,0:T(8,128)S(1)} %broadcast_in_dim.31.bias_ref, bf16[2048,1024]{1,0:T(8,128)(2,1)S(1)} %copy-done.3, ...), custom_call_target="tpu_custom_call" | custom-call | flops 1610612736 | bytes 4194304 | tf_op jit(solution)/shard_map/pallas_call | solution.py:311
  167.0 8.4 %shard_map.67 = bf16[512,512]{1,0:T(8,128)(2,1)S(1)} custom-call(s32[1]{0:T(128)} %bitcast.5.part_ref, s32[1]{0:T(128)} %bitcast.1.parity_ref, s32[2,8]{1,0:T(2,128)S(1)} %select_reduce_fusion.1.slash_ref, f32[32,1536]{1,0:T(8,128)S(1)} %broadcast_in_dim.31.bias_ref, bf16[2048,1024]{1,0:T(8,128)(2,1)S(1)} %copy-done.3, ...), custom_call_target="tpu_custom_call" | custom-call | flops 1610612736 | bytes 4194304 | tf_op jit(solution)/shard_map/pallas_call | solution.py:311
  175.6 2.0 %copy-done.19 = bf16[512,4096]{1,0:T(8,128)(2,1)} copy-done((bf16[512,4096]{1,0:T(8,128)(2,1)}, bf16[512,4096]{1,0:T(8,128)(2,1)S(1)}, u32[]{:S(2)}) %copy-start.19) | copy-done | bytes 4194328
  (80 shorter events, 13.7 us)
Async XLA Ops:
  1.7 1.2 copy-start.9
  3.0 1.2 copy-start.11
  5.0 51.4 %copy-start.12 = (bf16[512,256]{1,0:T(8,128)(2,1)}, bf16[512,256]{1,0:T(8,128)(2,1)S(1)}, u32[]{:S(2)}) copy-start(bf16[512,256]{1,0:T(8,128)(2,1)S(1)} %shard_map.55.behind_refs_0_) | copy-start | bytes 786436
  5.0 15.8 %collective-permute-start = (bf16[512,256]{1,0:T(8,128)(2,1)S(1)}, bf16[512,256]{1,0:T(8,128)(2,1)S(1)}, u32[]{:S(2)}, u32[]{:S(2)}) collective-permute-start(bf16[512,256]{1,0:T(8,128)(2,1)S(1)} %shard_map.55.behind_refs_0_), channel_id=1, source_target_pairs={{0,8},{4,12},{8,16},{12,20},{16,24},{20,28},{1,9},{5,13},{9,17},{1... | collective-permute-start | bytes 786440 | tf_op jit(solution)/shard_map/ppermute | solution.py:399
  9.9 23.6 %collective-permute-start.1 = (bf16[512,256]{1,0:T(8,128)(2,1)S(1)}, bf16[512,256]{1,0:T(8,128)(2,1)}, u32[]{:S(2)}, u32[]{:S(2)}) collective-permute-start(bf16[512,256]{1,0:T(8,128)(2,1)S(1)} %shard_map.55.behind_refs_0_), channel_id=1, source_target_pairs={{0,16},{4,20},{8,24},{12,28},{1,17},{5,21},{9,25},{13,29},{2,18},{... | collective-permute-start | bytes 786440 | tf_op jit(solution)/shard_map/ppermute | solution.py:399
  15.1 18.5 %collective-permute-start.2 = (bf16[512,256]{1,0:T(8,128)(2,1)S(1)}, bf16[512,256]{1,0:T(8,128)(2,1)}, u32[]{:S(2)}, u32[]{:S(2)}) collective-permute-start(bf16[512,256]{1,0:T(8,128)(2,1)S(1)} %shard_map.55.behind_refs_0_), channel_id=1, source_target_pairs={{0,24},{4,28},{1,25},{5,29},{2,26},{6,30},{3,27},{7,31}} | collective-permute-start | bytes 786440 | tf_op jit(solution)/shard_map/ppermute | solution.py:399
  20.7 25.6 %copy-start.10 = (bf16[2048,256]{1,0:T(8,128)(2,1)S(1)}, bf16[2048,256]{1,0:T(8,128)(2,1)}, u32[]{:S(2)}) copy-start(bf16[2048,256]{1,0:T(8,128)(2,1)} %keys_ref.5) | copy-start | bytes 3145732
  20.8 0.7 copy-start.15
  21.5 0.9 copy-start.16
  23.4 22.9 %collective-permute-start.5 = (bf16[1024,256]{1,0:T(8,128)(2,1)S(1)}, bf16[1024,256]{1,0:T(8,128)(2,1)S(1)}, u32[]{:S(2)}, u32[]{:S(2)}) collective-permute-start(bf16[1024,256]{1,0:T(8,128)(2,1)S(1)} %get-tuple-element.12), channel_id=1, source_target_pairs={{0,8},{4,12},{8,16},{12,20},{16,24},{20,28},{1,9},{5,13},{9,17},{1... | collective-permute-start | bytes 1572872 | tf_op jit(solution)/shard_map/ppermute | solution.py:406
  35.8 25.4 %collective-permute-start.3 = (bf16[2048,256]{1,0:T(8,128)(2,1)}, bf16[2048,256]{1,0:T(8,128)(2,1)}, u32[]{:S(2)}, u32[]{:S(2)}) collective-permute-start(bf16[2048,256]{1,0:T(8,128)(2,1)} %pad_maximum_fusion), channel_id=1, source_target_pairs={{0,4},{8,12},{16,20},{24,28},{4,0},{12,8},{20,16},{28,24},{1,5},{9... | collective-permute-start | bytes 3145736 | tf_op jit(solution)/shard_map/ppermute | solution.py:400
  37.2 17.5 %collective-permute-start.4 = (bf16[1024,256]{1,0:T(8,128)(2,1)}, bf16[1024,256]{1,0:T(8,128)(2,1)}, u32[]{:S(2)}, u32[]{:S(2)}) collective-permute-start(bf16[1024,256]{1,0:T(8,128)(2,1)} %get-tuple-element.11), channel_id=1, source_target_pairs={{0,8},{4,12},{8,16},{12,20},{16,24},{20,28},{1,9},{5,13},{9,17},{1... | collective-permute-start | bytes 1572872 | tf_op jit(solution)/shard_map/ppermute | solution.py:406
  42.8 40.7 %collective-permute-start.8 = (bf16[2048,256]{1,0:T(8,128)(2,1)S(1)}, bf16[2048,256]{1,0:T(8,128)(2,1)}, u32[]{:S(2)}, u32[]{:S(2)}) collective-permute-start(bf16[2048,256]{1,0:T(8,128)(2,1)S(1)} %get-tuple-element.10.own_ref), channel_id=1, source_target_pairs={{0,4},{8,12},{16,20},{24,28},{1,5},{9,13},{17,21},{25,29},{2,6},{1... | collective-permute-start | bytes 3145736 | tf_op jit(solution)/shard_map/ppermute | solution.py:407
  46.3 1.2 copy-start.4
  47.5 26.6 %collective-permute-start.12 = (bf16[2048,256]{1,0:T(8,128)(2,1)}, bf16[2048,256]{1,0:T(8,128)(2,1)S(1)}, u32[]{:S(2)}, u32[]{:S(2)}) collective-permute-start(bf16[2048,256]{1,0:T(8,128)(2,1)} %get-tuple-element.14), channel_id=1, source_target_pairs={{0,8},{4,12},{8,16},{12,20},{16,24},{20,28},{1,9},{5,13},{9,17},{1... | collective-permute-start | bytes 3145736 | tf_op jit(solution)/shard_map/ppermute | solution.py:406
  52.1 23.2 %collective-permute-start.7 = (bf16[1024,256]{1,0:T(8,128)(2,1)}, bf16[1024,256]{1,0:T(8,128)(2,1)}, u32[]{:S(2)}, u32[]{:S(2)}) collective-permute-start(bf16[1024,256]{1,0:T(8,128)(2,1)} %copy-done.4), channel_id=1, source_target_pairs={{4,0},{12,8},{20,16},{28,24},{5,1},{13,9},{21,17},{29,25},{6,2},{1... | collective-permute-start | bytes 1572872 | tf_op jit(solution)/shard_map/ppermute | solution.py:408
  54.7 21.2 %collective-permute-start.6 = (bf16[1024,256]{1,0:T(8,128)(2,1)}, bf16[1024,256]{1,0:T(8,128)(2,1)}, u32[]{:S(2)}, u32[]{:S(2)}) collective-permute-start(bf16[1024,256]{1,0:T(8,128)(2,1)} %collective-permute-done.4.rest_0_), channel_id=1, source_target_pairs={{4,0},{12,8},{20,16},{28,24},{5,1},{13,9},{21,17},{29,25},{6,2},{1... | collective-permute-start | bytes 1572872 | tf_op jit(solution)/shard_map/ppermute | solution.py:408
  61.2 78.4 %collective-permute-start.14 = (bf16[2048,256]{1,0:T(8,128)(2,1)S(1)}, bf16[2048,256]{1,0:T(8,128)(2,1)}, u32[]{:S(2)}, u32[]{:S(2)}) collective-permute-start(bf16[2048,256]{1,0:T(8,128)(2,1)S(1)} %get-tuple-element.13.own_ref), channel_id=1, source_target_pairs={{0,4},{8,12},{16,20},{24,28},{1,5},{9,13},{17,21},{25,29},{2,6},{1... | collective-permute-start | bytes 3145736 | tf_op jit(solution)/shard_map/ppermute | solution.py:407
  66.5 0.9 copy-start.13
  67.5 0.9 copy-start.17
  70.0 37.2 %copy-start.7 = (bf16[1024,256]{1,0:T(8,128)(2,1)}, bf16[1024,256]{1,0:T(8,128)(2,1)S(1)}, u32[]{:S(2)}) copy-start(bf16[1024,256]{1,0:T(8,128)(2,1)S(1)} %shard_map.56.vert_ref) | copy-start | bytes 1572868
  74.0 65.6 %collective-permute-start.13 = (bf16[2048,256]{1,0:T(8,128)(2,1)S(1)}, bf16[2048,256]{1,0:T(8,128)(2,1)}, u32[]{:S(2)}, u32[]{:S(2)}) collective-permute-start(bf16[2048,256]{1,0:T(8,128)(2,1)S(1)} %collective-permute-done.12.rest_0_), channel_id=1, source_target_pairs={{4,0},{12,8},{20,16},{28,24},{5,1},{13,9},{21,17},{29,25},{6,2},{1... | collective-permute-start | bytes 3145736 | tf_op jit(solution)/shard_map/ppermute | solution.py:408
  83.5 2.2 %copy-start = (bf16[2048,1024]{1,0:T(8,128)(2,1)S(1)}, bf16[2048,1024]{1,0:T(8,128)(2,1)}, u32[]{:S(2)}) copy-start(bf16[2048,1024]{1,0:T(8,128)(2,1)} %query_ref.15) | copy-start | bytes 12582916
  85.7 1.0 copy-start.5
  86.8 9.6 %copy-start.1 = (bf16[2048,1024]{1,0:T(8,128)(2,1)S(1)}, bf16[2048,1024]{1,0:T(8,128)(2,1)}, u32[]{:S(2)}) copy-start(bf16[2048,1024]{1,0:T(8,128)(2,1)} %query_ref.15) | copy-start | bytes 12582916
  96.3 39.1 %collective-permute-start.9 = (bf16[512,512]{1,0:T(8,128)(2,1)}, bf16[512,512]{1,0:T(8,128)(2,1)}, u32[]{:S(2)}, u32[]{:S(2)}) collective-permute-start(bf16[512,512]{1,0:T(8,128)(2,1)} %shard_map.58.rest_5_), channel_id=1, source_target_pairs={{0,3},{1,2},{2,1},{3,0},{4,7},{5,6},{6,5},{7,4},{8,11},{9,10},{10,... | collective-permute-start | bytes 1572872 | tf_op jit(solution)/shard_map/ppermute | solution.py:428
  105.7 31.7 %collective-permute-start.10 = (bf16[512,512]{1,0:T(8,128)(2,1)}, bf16[512,512]{1,0:T(8,128)(2,1)}, u32[]{:S(2)}, u32[]{:S(2)}) collective-permute-start(bf16[512,512]{1,0:T(8,128)(2,1)} %shard_map.59.rest_5_), channel_id=1, source_target_pairs={{0,2},{1,3},{2,0},{3,1},{4,6},{5,7},{6,4},{7,5},{8,10},{9,11},{10,... | collective-permute-start | bytes 1572872 | tf_op jit(solution)/shard_map/ppermute | solution.py:428
  116.5 21.9 %collective-permute-start.11 = (bf16[512,512]{1,0:T(8,128)(2,1)}, bf16[512,512]{1,0:T(8,128)(2,1)}, u32[]{:S(2)}, u32[]{:S(2)}) collective-permute-start(bf16[512,512]{1,0:T(8,128)(2,1)} %shard_map.60.rest_5_), channel_id=1, source_target_pairs={{0,1},{1,0},{2,3},{3,2},{4,5},{5,4},{6,7},{7,6},{8,9},{9,8},{10,11... | collective-permute-start | bytes 1572872 | tf_op jit(solution)/shard_map/ppermute | solution.py:428
  119.0 1.0 copy-start.14
  120.0 0.9 copy-start.18
  122.7 2.2 %copy-start.2 = (bf16[2048,1024]{1,0:T(8,128)(2,1)S(1)}, bf16[2048,1024]{1,0:T(8,128)(2,1)}, u32[]{:S(2)}) copy-start(bf16[2048,1024]{1,0:T(8,128)(2,1)} %query_ref.15) | copy-start | bytes 12582916
  124.9 1.0 copy-start.6
  125.9 1.0 copy-start.8
  135.4 4.2 %copy-start.3 = (bf16[2048,1024]{1,0:T(8,128)(2,1)S(1)}, bf16[2048,1024]{1,0:T(8,128)(2,1)}, u32[]{:S(2)}) copy-start(bf16[2048,1024]{1,0:T(8,128)(2,1)} %query_ref.15) | copy-start | bytes 12582916
  148.0 27.3 %collective-permute-start.15 = (bf16[512,512]{1,0:T(8,128)(2,1)S(1)}, bf16[512,512]{1,0:T(8,128)(2,1)S(1)}, u32[]{:S(2)}, u32[]{:S(2)}) collective-permute-start(bf16[512,512]{1,0:T(8,128)(2,1)S(1)} %shard_map.64.rest_3_), channel_id=1, source_target_pairs={{0,3},{1,2},{2,1},{3,0},{4,7},{5,6},{6,5},{7,4},{8,11},{9,10},{10,... | collective-permute-start | bytes 1572872 | tf_op jit(solution)/shard_map/ppermute | solution.py:428
  157.7 17.8 %collective-permute-start.16 = (bf16[512,512]{1,0:T(8,128)(2,1)S(1)}, bf16[512,512]{1,0:T(8,128)(2,1)S(1)}, u32[]{:S(2)}, u32[]{:S(2)}) collective-permute-start(bf16[512,512]{1,0:T(8,128)(2,1)S(1)} %shard_map.65.rest_3_), channel_id=1, source_target_pairs={{0,2},{1,3},{2,0},{3,1},{4,6},{5,7},{6,4},{7,5},{8,10},{9,11},{10,... | collective-permute-start | bytes 1572872 | tf_op jit(solution)/shard_map/ppermute | solution.py:428
  166.8 8.8 %collective-permute-start.17 = (bf16[512,512]{1,0:T(8,128)(2,1)S(1)}, bf16[512,512]{1,0:T(8,128)(2,1)S(1)}, u32[]{:S(2)}, u32[]{:S(2)}) collective-permute-start(bf16[512,512]{1,0:T(8,128)(2,1)S(1)} %shard_map.66.rest_3_), channel_id=1, source_target_pairs={{0,1},{1,0},{2,3},{3,2},{4,5},{5,4},{6,7},{7,6},{8,9},{9,8},{10,11... | collective-permute-start | bytes 1572872 | tf_op jit(solution)/shard_map/ppermute | solution.py:428
  175.6 2.0 %copy-start.19 = (bf16[512,4096]{1,0:T(8,128)(2,1)}, bf16[512,4096]{1,0:T(8,128)(2,1)S(1)}, u32[]{:S(2)}) copy-start(bf16[512,4096]{1,0:T(8,128)(2,1)S(1)} %constant_dynamic-update-slice_fusion) | copy-start | bytes 12582916

commit v6 on v4

--- a/solution.py
+++ b/solution.py
@@ -16,7 +16,6 @@
 LOOK = 2
 NEG = -1e30
 STEP_BLOCKS = 2
-CHUNKS = 2
 TILE = 256
 ANY = pl.BlockSpec(memory_space=pl.ANY)
 SMEM = pl.BlockSpec(memory_space=pltpu.SMEM)
@@ -26,48 +25,7 @@
     return pl.ds(pl.multiple_of(index * BLK, BLK), count * BLK)
 
 
-def slots_kernel(head, local_ref, keys_ref, values_ref, *rest):
-    out_ref, sem = rest[-2:]
-    copies = []
-    for slot in range(MOWN):
-        for side, source in enumerate((keys_ref, values_ref)):
-            copies.append(
-                pltpu.make_async_copy(
-                    source.at[blocks_at(local_ref[head, slot]), pl.ds(head * HD, HD)],
-                    out_ref.at[pl.ds(slot * BLK, BLK), pl.ds(side * HD, HD)],
-                    sem.at[len(copies)],
-                )
-            )
-    for copy in copies:
-        copy.start()
-    for copy in copies:
-        copy.wait()
-
-
-def owned_slots(head, local_block, keys, values, after):
-    return pl.pallas_call(
-        functools.partial(slots_kernel, head),
-        out_shape=jax.ShapeDtypeStruct((MOWN * BLK, 2 * HD), keys.dtype),
-        in_specs=[SMEM] + [ANY] * (2 + len(after)),
-        out_specs=ANY,
-        scratch_shapes=[pltpu.SemaphoreType.DMA((MOWN * 2,))],
-        compiler_params=pltpu.CompilerParams(vmem_limit_bytes=1 << 20),
-        cost_estimate=pl.CostEstimate(
-            flops=0, bytes_accessed=8 * MOWN * BLK * HD, transcendentals=0
-        ),
-    )(local_block, keys, values, *after)
-
-
-def pair_kernel(head, keys_ref, values_ref, *rest):
-    out_refs, sem = rest[-2 - CHUNKS : -1], rest[-1]
-    whole, chunks = out_refs[0], out_refs[1:]
-    copies = []
-    for side, source in enumerate((keys_ref, values_ref)):
-        columns, to = pl.ds(head * HD, HD), pl.ds(side * HD, HD)
-        for index, chunk in enumerate(chunks):
-            rows = pl.ds(index * chunk.shape[0], chunk.shape[0])
-            copies.append((source.at[rows, columns], chunk.at[:, to]))
-        copies.append((source.at[:, columns], whole.at[:, to]))
+def run_all(copies, sem):
     copies = [pltpu.make_async_copy(*ends, sem.at[k]) for k, ends in enumerate(copies)]
     for copy in copies:
         copy.start()
@@ -75,66 +33,151 @@
         copy.wait()
 
 
+def first_kernel(local_ref, keys_ref, values_ref, own_ref, send_ref, slots_ref, sem):
+    chunk_rows = send_ref.shape[0] - slots_ref.shape[0]
+    copies = []
+    for side, source in enumerate((keys_ref, values_ref)):
+        to = pl.ds(side * HD, HD)
+        for head in range(local_ref.shape[0]):
+            for slot in range(MOWN):
+                found = source.at[blocks_at(local_ref[head, slot]), pl.ds(head * HD, HD)]
+                low = (head * MOWN + slot) * BLK
+                copies.append((found, send_ref.at[pl.ds(chunk_rows + low, BLK), to]))
+                copies.append((found, slots_ref.at[pl.ds(low, BLK), to]))
+        rows = pl.ds(0, chunk_rows)
+        copies.append((source.at[rows, pl.ds(0, HD)], send_ref.at[rows, to]))
+        copies.append((source.at[:, pl.ds(0, HD)], own_ref.at[:, to]))
+    run_all(copies, sem)
+
+
+def first_of(chunk_rows, local_block, keys, values):
+    heads = local_block.shape[0]
+    rows = keys.shape[0]
+    slot_rows = heads * MOWN * BLK
+    return pl.pallas_call(
+        first_kernel,
+        out_shape=[
+            jax.ShapeDtypeStruct((rows, 2 * HD), keys.dtype),
+            jax.ShapeDtypeStruct((chunk_rows + slot_rows, 2 * HD), keys.dtype),
+            jax.ShapeDtypeStruct((slot_rows, 2 * HD), keys.dtype),
+        ],
+        in_specs=[SMEM, ANY, ANY],
+        out_specs=[ANY] * 3,
+        scratch_shapes=[pltpu.SemaphoreType.DMA((4 * heads * MOWN + 4,))],
+        compiler_params=pltpu.CompilerParams(vmem_limit_bytes=1 << 20),
+        cost_estimate=pl.CostEstimate(flops=0, bytes_accessed=16 * rows * HD, transcendentals=0),
+    )(local_block, keys, values)
+
+
+def pair_kernel(head, keys_ref, values_ref, *rest):
+    out_ref, sem = rest[-2:]
+    run_all(
+        [
+            (source.at[:, pl.ds(head * HD, HD)], out_ref.at[:, pl.ds(side * HD, HD)])
+            for side, source in enumerate((keys_ref, values_ref))
+        ],
+        sem,
+    )
+
+
 def pair_of(head, keys, values, after):
     rows = keys.shape[0]
-    whole, *chunks = pl.pallas_call(
+    return pl.pallas_call(
         functools.partial(pair_kernel, head),
-        out_shape=[jax.ShapeDtypeStruct((rows, 2 * HD), keys.dtype)]
-        + [jax.ShapeDtypeStruct((rows // CHUNKS, 2 * HD), keys.dtype)] * CHUNKS,
+        out_shape=jax.ShapeDtypeStruct((rows, 2 * HD), keys.dtype),
         in_specs=[ANY] * (2 + len(after)),
-        out_specs=[ANY] * (1 + CHUNKS),
-        scratch_shapes=[pltpu.SemaphoreType.DMA((2 + 2 * CHUNKS,))],
+        out_specs=ANY,
+        scratch_shapes=[pltpu.SemaphoreType.DMA((2,))],
         compiler_params=pltpu.CompilerParams(vmem_limit_bytes=1 << 20),
-        cost_estimate=pl.CostEstimate(flops=0, bytes_accessed=16 * rows * HD, transcendentals=0),
+        cost_estimate=pl.CostEstimate(flops=0, bytes_accessed=8 * rows * HD, transcendentals=0),
     )(keys, values, *after)
-    return whole, chunks
-
-
-def listed_kernel(head, place_ref, source_ref, behind_refs, across_ref, out_ref, sem):
-    count = len(behind_refs)
-    for index in range(2 * count):
+
+
+def joined_kernel(pieces, parity_ref, *rest):
+    refs, out_ref, sem = rest[:-2], rest[-2], rest[-1]
+    to = 0
+    for rows, even, odd in pieces:
+        for value, (index, low) in enumerate((even, odd)):
+
+            @pl.when(parity_ref[0] == value)
+            def _():
+                pltpu.make_async_copy(
+                    refs[index].at[pl.ds(low, rows)], out_ref.at[pl.ds(to, rows)], sem
+                ).start()
+
+        to += rows
+    pltpu.make_async_copy(out_ref, out_ref, sem).wait()
+
+
+def joined(parity, pieces, after=()):
+    arrays = []
+    plan = []
+    for rows, *sources in pieces:
+        found = []
+        for array, low in sources:
+            at = [k for k, known in enumerate(arrays) if known is array]
+            if not at:
+                at = [len(arrays)]
+                arrays.append(array)
+            found.append((at[0], low))
+        plan.append((rows, *found))
+    total = sum(rows for rows, *_ in plan)
+    return pl.pallas_call(
+        functools.partial(joined_kernel, plan),
+        out_shape=jax.ShapeDtypeStruct((total, 2 * HD), jnp.bfloat16),
+        in_specs=[SMEM] + [ANY] * (len(arrays) + len(after)),
+        out_specs=ANY,
+        scratch_shapes=[pltpu.SemaphoreType.DMA],
+        compiler_params=pltpu.CompilerParams(vmem_limit_bytes=1 << 20),
+        cost_estimate=pl.CostEstimate(flops=0, bytes_accessed=8 * total * HD, transcendentals=0),
+    )(parity, *arrays, *after)
+
+
+def listed_kernel(head, lows, place_ref, source_ref, *rest):
+    refs, out_ref, sem = rest[:-2], rest[-2], rest[-1]
+
+    def block(index, slot):
+        return refs[index].at[pl.ds(lows[index] + (head * MOWN + slot) * BLK, BLK)]
+
+    for index in range(len(refs)):
         for slot in range(MOWN):
             place = place_ref[index, head, slot]
-            if index < count:
-                found = behind_refs[index].at[pl.ds(slot * BLK, BLK)]
-            else:
-                found = across_ref.at[pl.ds(((index - count) * MOWN + slot) * BLK, BLK)]
 
             @pl.when(place >= 0)
             def _():
-                pltpu.make_async_copy(found, out_ref.at[blocks_at(place)], sem).start()
+                pltpu.make_async_copy(block(index, slot), out_ref.at[blocks_at(place)], sem).start()
 
     for entry in range(NV):
 
         @pl.when(source_ref[head, entry] < 0)
         def _():
             pltpu.make_async_copy(
-                behind_refs[0].at[pl.ds(0, BLK)], out_ref.at[pl.ds(entry * BLK, BLK)], sem
+                block(0, 0), out_ref.at[pl.ds(entry * BLK, BLK)], sem
             ).start()
 
     pltpu.make_async_copy(out_ref, out_ref, sem).wait()
 
 
-def listed_blocks(head, place, source, behind, across):
+def listed_blocks(head, place, source, slots):
     return pl.pallas_call(
-        functools.partial(listed_kernel, head),
-        out_shape=jax.ShapeDtypeStruct((NV * BLK, 2 * HD), across.dtype),
-        in_specs=[SMEM, SMEM, [ANY] * len(behind), ANY],
+        functools.partial(listed_kernel, head, [low for _, low in slots]),
+        out_shape=jax.ShapeDtypeStruct((NV * BLK, 2 * HD), jnp.bfloat16),
+        in_specs=[SMEM, SMEM] + [ANY] * len(slots),
         out_specs=ANY,
         scratch_shapes=[pltpu.SemaphoreType.DMA],
         compiler_params=pltpu.CompilerParams(vmem_limit_bytes=1 << 20),
         cost_estimate=pl.CostEstimate(flops=0, bytes_accessed=8 * NV * BLK * HD, transcendentals=0),
-    )(place, source, behind, across)
+    )(place, source, *[array for array, _ in slots])
 
 
 def attend_kernel(
-    head, parts, waits, part_blocks, group_heads, part_ref, parity_ref, slash_ref, bias_ref, query_ref,
+    head, parts, bounds, waits, part_blocks, group_heads, part_ref, slash_ref, bias_ref, query_ref,
     vert_ref, own_ref, *rest,
 ):
-    two_back = rest[:CHUNKS]
-    even_back = rest[CHUNKS : 2 * CHUNKS]
-    odd_back = rest[2 * CHUNKS]
-    rest = rest[2 * CHUNKS + 1 + waits :]
+    chunks = len(bounds) - 1
+    two_back = rest[:chunks]
+    one_back = rest[chunks : 2 * chunks]
+    rest = rest[2 * chunks + waits :]
     out_refs = rest[:parts]
     (
         queries, out, vert, vert_keys, window, scores_a, scores_b, weights_a, weights_b, max_a,
@@ -145,7 +188,6 @@
     blocks_dev = tok_rows // BLK
     part_rows = part_blocks * BLK
     group_cols = group_heads * HD
-    chunk_rows = tok_rows // CHUNKS
     last = parts * part_blocks - 1
     step = pl.program_id(0)
     scale = 1.0 / math.sqrt(HD)
@@ -244,26 +286,14 @@
                 query_sem,
             ).start()
         pltpu.make_async_copy(vert_ref, vert, vert_sem).start()
-        for chunk in range(CHUNKS):
-            pltpu.make_async_copy(
-                two_back[chunk], window.at[pl.ds(chunk * chunk_rows, chunk_rows)], window_sem
-            ).start()
-
-        @pl.when(parity_ref[0] == 1)
-        def _():
-            pltpu.make_async_copy(
-                odd_back, window.at[pl.ds(tok_rows, tok_rows)], window_sem
-            ).start()
-
-        @pl.when(parity_ref[0] == 0)
-        def _():
-            for chunk in range(CHUNKS):
+        for back, sources in enumerate((two_back, one_back)):
+            for chunk, source in enumerate(sources):
+                rows = bounds[chunk + 1] - bounds[chunk]
                 pltpu.make_async_copy(
-                    even_back[chunk],
-                    window.at[pl.ds(tok_rows + chunk * chunk_rows, chunk_rows)],
+                    source.at[pl.ds(0, rows)],
+                    window.at[pl.ds(back * tok_rows + bounds[chunk], rows)],
                     window_sem,
                 ).start()
-
         pltpu.make_async_copy(
             own_ref, window.at[pl.ds(LOOK * tok_rows, tok_rows)], window_sem
         ).start()
@@ -294,8 +324,7 @@
             ).wait()
 
 
-def attend(head, part, parity, slash, bias, queries, vert, own, two_back, even_back, odd_back,
-           part_rows, after):
+def attend(head, part, bounds, slash, bias, queries, vert, own, two_back, one_back, part_rows, after):
     parts = part.shape[0]
     group_cols = queries.shape[1] // slash.shape[0]
     group_heads = group_cols // HD
@@ -304,12 +333,14 @@
     rows = group_heads * BLK
     keys_seen = (NV + NS) * BLK
     return pl.pallas_call(
-        functools.partial(attend_kernel, head, parts, len(after), part_blocks, group_heads),
+        functools.partial(
+            attend_kernel, head, parts, bounds, len(after), part_blocks, group_heads
+        ),
         out_shape=[jax.ShapeDtypeStruct((part_rows, group_cols), jnp.bfloat16)] * parts,
         grid_spec=pltpu.PrefetchScalarGridSpec(
-            num_scalar_prefetch=3,
+            num_scalar_prefetch=2,
             grid=(parts * part_blocks // STEP_BLOCKS,),
-            in_specs=[pl.BlockSpec(bias.shape, lambda s, *_: (0, 0))] + [ANY] * (4 + 2 * CHUNKS + len(after)),
+            in_specs=[pl.BlockSpec(bias.shape, lambda s, *_: (0, 0))] + [ANY] * (3 + 2 * len(two_back) + len(after)),
             out_specs=[ANY] * parts,
             scratch_shapes=[
                 pltpu.VMEM((parts * part_rows, group_cols), jnp.bfloat16),
@@ -331,14 +362,14 @@
             ],
         ),
         compiler_params=pltpu.CompilerParams(
-            dimension_semantics=("arbitrary",), vmem_limit_bytes=32 << 20
+            dimension_semantics=("arbitrary",), vmem_limit_bytes=24 << 20
         ),
         cost_estimate=pl.CostEstimate(
             flops=4 * parts * part_rows * group_heads * keys_seen * HD,
             bytes_accessed=4 * parts * part_rows * group_cols + 12 * tok_rows * HD,
             transcendentals=parts * part_rows * group_heads * keys_seen,
         ),
-    )(part, parity, slash, bias, queries, vert, own, *two_back, *even_back, odd_back, *after)
+    )(part, slash, bias, queries, vert, own, *two_back, *one_back, *after)
 
 
 def local(queries, keys, values, vertical, slash):
@@ -353,8 +384,8 @@
     part_rows = tok_rows // head_count
     partner = shard_index ^ 1
     two_pairs = [(i, i + 2) for i in range(shard_count - 2)]
-    even_to_odd = [(i, i + 1) for i in range(0, shard_count - 1, 2)]
-    odd_to_even = [(i, i - 1) for i in range(1, shard_count, 2)]
+    across_pairs = [(i, i ^ 1) for i in range(shard_count)]
+    parity = (shard_index % 2).reshape(1).astype(jnp.int32)
 
     owners = vertical // blocks_dev
     order = jnp.arange(NV, dtype=jnp.int32)
@@ -367,8 +398,8 @@
         ((owners == shard_index)[:, :, None] & in_slot) * (vertical % blocks_dev)[:, :, None],
         axis=1,
     )
-    steps = 2 * jnp.arange(shard_count // 2, dtype=jnp.int32)
-    array_owner = jnp.concatenate([shard_index - steps, partner - steps])
+    distances = 2 * jnp.arange(shard_count // 2, dtype=jnp.int32)
+    array_owner = jnp.concatenate([shard_index - distances, partner - distances])
     array_owner = jnp.where(array_owner <= shard_index, array_owner, -1)
     here = (array_owner[:, None, None] == owners)[:, :, :, None] & in_slot[None]
     place = jnp.sum(here * (order + 1)[None, None, :, None], axis=2) - 1
@@ -386,38 +417,60 @@
     valid = jnp.concatenate([vert_valid, slash_valid], axis=2)
     bias = jnp.repeat(jnp.where(valid, 0.0, NEG).astype(jnp.float32), BLK, axis=2)
 
-    windows = []
+    steps = shard_count // 2 - 1
+    bounds = [k * blocks_dev // steps * BLK for k in range(steps + 1)]
+    slot_rows = kv_local * MOWN * BLK
+    own, send, slots_own = first_of(bounds[1], local_block, keys, values)
+    behind = [(slots_own, 0)]
+    across = []
+    two_back = []
+    one_back = []
+    for step in range(steps):
+        rows = bounds[step + 1] - bounds[step]
+        here = (own, bounds[step])
+        if step:
+            send = joined(
+                parity, [(rows, here, here), (slot_rows, behind[-1], behind[-1])],
+                [cross] + one_back[-2:-1],
+            )
+        come = lax.ppermute(send, "ctx", two_pairs)
+        if step == 0:
+            pairs = [(i, i + 1) for i in range(0, shard_count, 2)]
+            across.append((lax.ppermute(slots_own, "ctx", pairs), 0))
+        two_back.append(come)
+        behind.append((come, rows))
+        cross = joined(parity, [(rows, here, (come, 0)), (slot_rows, behind[-1], behind[-1])])
+        one_back.append(lax.ppermute(cross, "ctx", across_pairs))
+        across.append((one_back[-1], rows))
+    slots = behind + across
+    windows = [(bounds, own, two_back, one_back)]
+    after = two_back[-1:] + one_back[-2:-1]
+    for head in range(1, kv_local):
+        own = pair_of(head, keys, values, after)
+        come = lax.ppermute(own, "ctx", two_pairs)
+        windows.append(([0, tok_rows], own, [come], None))
+        after = [come]
+
+    out = jnp.zeros((part_rows, head_count * kv_local * group_cols), jnp.bfloat16)
     after = []
+    half = head_count // 2
+    calls = [[flip] for flip in range(head_count - 1, half - 1, -1)]
+    calls.append(list(range(half - 1, -1, -1)))
     for head in range(kv_local):
-        behind = [owned_slots(head, local_block, keys, values, after)]
-        own, chunks = pair_of(head, keys, values, behind)
-        for distance in range(2, shard_count, 2):
-            pairs = [(i, i + distance) for i in range(shard_count - distance)]
-            behind.append(lax.ppermute(behind[0], "ctx", pairs))
-        two_back = [lax.ppermute(chunk, "ctx", two_pairs) for chunk in chunks]
-        odd_back = lax.ppermute(own, "ctx", even_to_odd)
-        across = lax.ppermute(jnp.concatenate(behind), "ctx", even_to_odd + odd_to_even)
-        even_back = [lax.ppermute(piece, "ctx", odd_to_even) for piece in two_back]
-        vert = listed_blocks(head, place, source, behind, across)
-        windows.append((vert, own, two_back, even_back, odd_back))
-        after = two_back + even_back[:-1]
-
-    parity = (shard_index % 2).reshape(1).astype(jnp.int32)
-    out = jnp.zeros((part_rows, head_count * kv_local * group_cols), jnp.bfloat16)
-    half = head_count // 2
-    after = []
-    for head in range(kv_local):
-        vert, own, two_back, even_back, odd_back = windows[head]
-        calls = [range(head_count - 1, half - 1, -1), range(half - 1, -1, -1)]
-        if head + 1 == kv_local:
-            calls = [range(f, f - 1, -1) for f in calls[0]] + calls[1:]
+        bounds, own, two_back, one_back = windows[head]
+        vert = listed_blocks(head, place, source, slots)
         for flips in calls:
             others = [head_index ^ flip for flip in flips]
             pieces = attend(
-                head, jnp.stack(others).astype(jnp.int32), parity, slash, bias[head], queries,
-                vert, own, two_back, even_back, odd_back, part_rows, after,
+                head, jnp.stack(others).astype(jnp.int32), bounds, slash, bias[head], queries, vert, own,
+                two_back, one_back, part_rows, after,
             )
             after = [pieces[-1]]
+            if flips == calls[0] and head + 1 < kv_local:
+                near, own_next, (come,), _ = windows[head + 1]
+                cross = joined(parity, [(tok_rows, (own_next, 0), (come, 0))], after)
+                crossed = lax.ppermute(cross, "ctx", across_pairs)
+                windows[head + 1] = (near, own_next, [come], [crossed])
             for flip, other, piece in zip(flips, others, pieces):
                 if flip:
                     piece = lax.ppermute(piece, "head", [(i, i ^ flip) for i in range(head_count)])

time: 173 us -> 205 us (1.18)
  Pallas kernels: 64.2 us -> 106 us
  starting transfers between devices: 50.9 us -> 32.4 us
  local copies, waits for them, and re-layouts: 17.7 us -> 22.7 us
  waiting for transfers between devices: 34.7 us -> 37.2 us
    pallas_call x11 -> x16, Pallas kernels: 64.2 us -> 106 us  [the longest x6 63.3 us: attend(): pl.pallas_call(functools.partial(attend_kernel, head, parts, bounds, len(...]
    ppermute x18 -> x9, starting transfers between devices: 46.5 us -> 28.3 us  [the longest x3 13.7 us: local(): come = lax.ppermute(send, 'ctx', two_pairs)]
    unnamed x30 -> x40, local copies, waits for them, and re-layouts: 10.9 us -> 14.7 us
    ppermute x18 -> x9, waiting for transfers between devices: 32.5 us -> 35.7 us  [the longest x3 29.2 us: local(): come = lax.ppermute(send, 'ctx', two_pairs)]
  transfers between devices with their start and end apart: 24 -> 15, of which waited for: 6 -> 5; matrix products, arithmetic and copies ran while one was open for 5% -> 5% of each run, Pallas kernels for 37% -> 35%
where the time goes in v6:
time: 205 us; the launch traced here: 204 us
  Pallas kernels  106 us (52%)
  waiting for transfers between devices  37.2 us (18%)
  starting transfers between devices  32.4 us (16%)
  local copies, waits for them, and re-layouts  22.7 us (11%)
  other arithmetic  5.26 us (3%)
    pallas_call x6, Pallas kernels, attend(): pl.pallas_call(functools.partial(attend_kernel, head, parts, bounds, len(...  63.3 us
    pallas_call x6, Pallas kernels, joined(): pl.pallas_call(functools.partial(joined_kernel, plan), out_shape=jax.Shap...  35.8 us
    ppermute x3, waiting for transfers between devices, local(): come = lax.ppermute(send, 'ctx', two_pairs)  29.2 us
    unnamed x40, local copies, waits for them, and re-layouts  14.7 us
    ppermute x3, starting transfers between devices, local(): come = lax.ppermute(send, 'ctx', two_pairs)  13.7 us
    ppermute x3, waiting for transfers between devices, local(): one_back.append(lax.ppermute(cross, 'ctx', across_pairs))  6.51 us
    broadcast_in_dim x4, local copies, waits for them, and re-layouts, local(): jnp.repeat(jnp.where(valid, 0.0, NEG).astype(jnp.float32), BLK, axis=2)  5.51 us
    ppermute x1, starting transfers between devices, local(): come = lax.ppermute(own, 'ctx', two_pairs)  5.4 us
  transfers between devices with their start and end apart: 15, of which 5 were waited for; matrix products, arithmetic and copies ran while one was open for 5% of the time, Pallas kernels for 35%

profile of v6, /device:TPU:0, one launch (start us, length us, event | category | flops | bytes accessed | tf_op | source)
XLA Modules:
  0.0 204.3 jit_solution(12258777150370910194)
XLA Ops:
  1.8 1.2 copy-done.11
  3.0 1.2 copy-done.13
  4.2 1.7 shard_map.55
  6.0 5.0 %collective-permute-start = (bf16[1152,256]{1,0:T(8,128)(2,1)S(1)}, bf16[1152,256]{1,0:T(8,128)(2,1)S(1)}, u32[]{:S(2)}, u32[]{:S(2)}) collective-permute-start(bf16[1152,256]{1,0:T(8,128)(2,1)S(1)} %get-tuple-element.13), channel_id=1, source_target_pairs={{0,8},{4,12},{8,16},{12,20},{16,24},{20,28},{1,9},{5,13},{9,17},{1... | collective-permute-start | bytes 1769480 | tf_op jit(solution)/shard_map/ppermute | solution.py:436
  10.9 4.1 %collective-permute-start.4 = (bf16[512,256]{1,0:T(8,128)(2,1)}, bf16[512,256]{1,0:T(8,128)(2,1)}, u32[]{:S(2)}, u32[]{:S(2)}) collective-permute-start(bf16[512,256]{1,0:T(8,128)(2,1)} %get-tuple-element.12.rest_0_), channel_id=1, source_target_pairs={{0,4},{8,12},{16,20},{24,28},{1,5},{9,13},{17,21},{25,29},{2,6},{1... | collective-permute-start | bytes 786440 | tf_op jit(solution)/shard_map/ppermute | solution.py:439
  15.0 1.0 convert_reduce_fusion.1
  16.9 6.6 %collective-permute-done.rest_1_.rest_0_ = bf16[1152,256]{1,0:T(8,128)(2,1)S(1)} collective-permute-done((bf16[1152,256]{1,0:T(8,128)(2,1)S(1)}, bf16[1152,256]{1,0:T(8,128)(2,1)S(1)}, u32[]{:S(2)}, u32[]{:S(2)}) %collective-permute-start) | collective-permute-done | bytes 589856 | tf_op jit(solution)/shard_map/ppermute | solution.py:436
  23.5 0.8 shard_map.56.rest_2_
  24.3 1.6 collective-permute-start.2
  25.9 0.8 shard_map.57
  26.7 4.4 %collective-permute-start.1 = (bf16[1216,256]{1,0:T(8,128)(2,1)}, bf16[1216,256]{1,0:T(8,128)(2,1)S(1)}, u32[]{:S(2)}, u32[]{:S(2)}) collective-permute-start(bf16[1216,256]{1,0:T(8,128)(2,1)} %shard_map.57), channel_id=1, source_target_pairs={{0,8},{4,12},{8,16},{12,20},{16,24},{20,28},{1,9},{5,13},{9,17},{1... | collective-permute-start | bytes 1867784 | tf_op jit(solution)/shard_map/ppermute | solution.py:436
  31.6 12.0 %collective-permute-done.1.rest_1_.rest_2_ = bf16[1216,256]{1,0:T(8,128)(2,1)S(1)} collective-permute-done((bf16[1216,256]{1,0:T(8,128)(2,1)}, bf16[1216,256]{1,0:T(8,128)(2,1)S(1)}, u32[]{:S(2)}, u32[]{:S(2)}) %collective-permute-start.1) | collective-permute-done | bytes 622624 | tf_op jit(solution)/shard_map/ppermute | solution.py:436
  44.5 0.8 copy-done.3
  45.3 4.3 %collective-permute-start.3 = (bf16[1216,256]{1,0:T(8,128)(2,1)S(1)}, bf16[1216,256]{1,0:T(8,128)(2,1)S(1)}, u32[]{:S(2)}, u32[]{:S(2)}) collective-permute-start(bf16[1216,256]{1,0:T(8,128)(2,1)S(1)} %shard_map.59), channel_id=1, source_target_pairs={{0,8},{4,12},{8,16},{12,20},{16,24},{20,28},{1,9},{5,13},{9,17},{1... | collective-permute-start | bytes 1867784 | tf_op jit(solution)/shard_map/ppermute | solution.py:436
  49.9 10.6 %collective-permute-done.3.rest_1_.rest_3_.rest_2_.rest_0_ = bf16[1216,256]{1,0:T(8,128)(2,1)S(1)} collective-permute-done((bf16[1216,256]{1,0:T(8,128)(2,1)S(1)}, bf16[1216,256]{1,0:T(8,128)(2,1)S(1)}, u32[]{:S(2)}, u32[]{:S(2)}) %collective-permute-start.3) | collective-permute-done | bytes 622624 | tf_op jit(solution)/shard_map/ppermute | solution.py:436
  60.5 1.0 shard_map.66.rest_0_.own_ref
  61.5 5.4 %collective-permute-start.10 = (bf16[2048,256]{1,0:T(8,128)(2,1)}, bf16[2048,256]{1,0:T(8,128)(2,1)}, u32[]{:S(2)}, u32[]{:S(2)}) collective-permute-start(bf16[2048,256]{1,0:T(8,128)(2,1)} %shard_map.66.rest_0_.own_ref), channel_id=1, source_target_pairs={{0,8},{4,12},{8,16},{12,20},{16,24},{20,28},{1,9},{5,13},{9,17},{1... | collective-permute-start | bytes 3145736 | tf_op jit(solution)/shard_map/ppermute | solution.py:450
  66.9 0.9 shard_map.60
  67.8 1.6 collective-permute-start.6
  70.3 0.9 broadcast_in_dim.27
  71.2 1.8 broadcast_in_dim.28.bias_ref
  73.0 0.9 broadcast_add_fusion.place_ref
  73.9 6.5 %collective-permute-done.6.rest_7_.rest_5_ = bf16[1216,256]{1,0:T(8,128)(2,1)} collective-permute-done((bf16[1216,256]{1,0:T(8,128)(2,1)}, bf16[1216,256]{1,0:T(8,128)(2,1)}, u32[]{:S(2)}, u32[]{:S(2)}) %collective-permute-start.6) | collective-permute-done | bytes 622624 | tf_op jit(solution)/shard_map/ppermute | solution.py:443
  80.4 1.1 copy-done.4
  81.5 2.1 %shard_map.61.vert_ref = bf16[1024,256]{1,0:T(8,128)(2,1)S(1)} custom-call(s32[8,2,4]{2,1,0:T(2,128)S(1)} %broadcast_add_fusion.place_ref, s32[2,16]{1,0:T(2,128)S(1)} %compare_select_fusion.1.source_ref, bf16[512,256]{1,0:T(8,128)(2,1)} %get-tuple-element.12.rest_0_, bf16[1152,256]{1,0:T(8,128)(2,1)S(1)} %collective-permute-done.rest_1_.rest_0_, ...), custom_call_target="tpu_custom_call" | custom-call | bytes 1048576 | tf_op jit(solution)/shard_map/pallas_call | solution.py:162
  83.7 1.2 copy-done.5
  84.9 8.6 %shard_map.62.rest_6_.rest_2_ = bf16[512,512]{1,0:T(8,128)(2,1)S(1)} custom-call(s32[1]{0:T(128)} %bitcast.part_ref, s32[2,8]{1,0:T(2,128)S(1)} %select_reduce_fusion.1.slash_ref, f32[32,1536]{1,0:T(8,128)S(1)} %copy-done.15, bf16[2048,1024]{1,0:T(8,128)(2,1)S(1)} %copy-done, bf16[1024,256]{1,0:T(8,128)(2,1)S(1)} %shard_map.61.vert_ref, ...), custom_call_target="tpu_custom_call" | custom-call | flops 1610612736 | bytes 4194304 | tf_op jit(solution)/shard_map/pallas_call | solution.py:335
  93.5 32.9 %shard_map.67 = bf16[2048,256]{1,0:T(8,128)(2,1)} custom-call(s32[1]{0:T(128)} %bitcast.2.parity_ref, bf16[2048,256]{1,0:T(8,128)(2,1)} %shard_map.66.rest_0_.own_ref, bf16[2048,256]{1,0:T(8,128)(2,1)} %collective-permute-done.10.rest_1_.rest_0_, bf16[512,512]{1,0:T(8,128)(2,1)S(1)} %shard_map.62.rest_6_.rest_2_), custom_call_target="tpu_custom_call" | custom-call | bytes 2097152 | tf_op jit(solution)/shard_map/pallas_call | solution.py:125
  126.4 0.8 copy-done.7
  127.2 1.4 collective-permute-start.11
  128.6 0.9 broadcast_in_dim.30
  129.5 1.8 broadcast_in_dim.31.bias_ref
  131.5 2.2 %copy-done.1 = bf16[2048,1024]{1,0:T(8,128)(2,1)S(1)} copy-done((bf16[2048,1024]{1,0:T(8,128)(2,1)S(1)}, bf16[2048,1024]{1,0:T(8,128)(2,1)}, u32[]{:S(2)}) %copy-start.1) | copy-done | bytes 4194328
  133.6 1.1 copy-done.6
  134.7 1.0 copy-done.8
  135.8 1.0 copy-done.10
  136.8 0.9 copy-done.16
  137.7 8.6 %shard_map.63.rest_6_ = bf16[512,512]{1,0:T(8,128)(2,1)S(1)} custom-call(s32[1]{0:T(128)} %bitcast.3.part_ref, s32[2,8]{1,0:T(2,128)S(1)} %select_reduce_fusion.1.slash_ref, f32[32,1536]{1,0:T(8,128)S(1)} %copy-done.16, bf16[2048,1024]{1,0:T(8,128)(2,1)S(1)} %copy-done.1, bf16[1024,256]{1,0:T(8,128)(2,1)S(1)} %copy-done.10, ...), custom_call_target="tpu_custom_call" | custom-call | flops 1610612736 | bytes 4194304 | tf_op jit(solution)/shard_map/pallas_call | solution.py:335
  146.3 1.6 collective-permute-start.8
  147.9 14.1 %shard_map.64 = (bf16[512,512]{1,0:T(8,128)(2,1)S(1)}, bf16[512,512]{1,0:T(8,128)(2,1)S(1)}) custom-call(s32[2]{0:T(128)S(1)} %pad_add_fusion.part_ref, s32[2,8]{1,0:T(2,128)S(1)} %select_reduce_fusion.1.slash_ref, f32[32,1536]{1,0:T(8,128)S(1)} %copy-done.16, bf16[2048,1024]{1,0:T(8,128)(2,1)S(1)} %copy-done.1, bf16[1024,256]{1,0:T(8,128)(2,1)S(1)} %copy-done.10, ...), custom_call_target="tpu_custom_call" | custom-call | flops 3221225472 | bytes 5242880 | tf_op jit(solution)/shard_map/pallas_call | solution.py:335
  162.4 2.3 %shard_map.65.vert_ref = bf16[1024,256]{1,0:T(8,128)(2,1)S(1)} custom-call(s32[8,2,4]{2,1,0:T(2,128)S(1)} %broadcast_add_fusion.place_ref, s32[2,16]{1,0:T(2,128)S(1)} %compare_select_fusion.1.source_ref, bf16[512,256]{1,0:T(8,128)(2,1)} %get-tuple-element.12.rest_0_, bf16[1152,256]{1,0:T(8,128)(2,1)S(1)} %collective-permute-done.rest_1_.rest_0_, ...), custom_call_target="tpu_custom_call" | custom-call | bytes 1048576 | tf_op jit(solution)/shard_map/pallas_call | solution.py:162
  165.4 8.8 %shard_map.68.rest_2_ = bf16[512,512]{1,0:T(8,128)(2,1)S(1)} custom-call(s32[1]{0:T(128)} %bitcast.part_ref, s32[2,8]{1,0:T(2,128)S(1)} %select_reduce_fusion.1.slash_ref, f32[32,1536]{1,0:T(8,128)S(1)} %copy-done.17, bf16[2048,1024]{1,0:T(8,128)(2,1)S(1)} %copy-done.2, bf16[1024,256]{1,0:T(8,128)(2,1)S(1)} %shard_map.65.vert_ref, ...), custom_call_target="tpu_custom_call" | custom-call | flops 1610612736 | bytes 4194304 | tf_op jit(solution)/shard_map/pallas_call | solution.py:335
  174.2 1.2 collective-permute-start.12
  175.4 8.8 %shard_map.69.rest_2_ = bf16[512,512]{1,0:T(8,128)(2,1)S(1)} custom-call(s32[1]{0:T(128)} %bitcast.3.part_ref, s32[2,8]{1,0:T(2,128)S(1)} %select_reduce_fusion.1.slash_ref, f32[32,1536]{1,0:T(8,128)S(1)} %copy-done.17, bf16[2048,1024]{1,0:T(8,128)(2,1)S(1)} %copy-done.2, bf16[1024,256]{1,0:T(8,128)(2,1)S(1)} %shard_map.65.vert_ref, ...), custom_call_target="tpu_custom_call" | custom-call | flops 1610612736 | bytes 4194304 | tf_op jit(solution)/shard_map/pallas_call | solution.py:335
  185.0 14.4 %shard_map.70 = (bf16[512,512]{1,0:T(8,128)(2,1)S(1)}, bf16[512,512]{1,0:T(8,128)(2,1)S(1)}) custom-call(s32[2]{0:T(128)S(1)} %pad_add_fusion.part_ref, s32[2,8]{1,0:T(2,128)S(1)} %select_reduce_fusion.1.slash_ref, f32[32,1536]{1,0:T(8,128)S(1)} %copy-done.17, bf16[2048,1024]{1,0:T(8,128)(2,1)S(1)} %copy-done.2, bf16[1024,256]{1,0:T(8,128)(2,1)S(1)} %shard_map.65.vert_ref, ...), custom_call_target="tpu_custom_call" | custom-call | flops 3221225472 | bytes 5242880 | tf_op jit(solution)/shard_map/pallas_call | solution.py:335
  199.9 1.5 collective-permute-done.14
  201.4 2.0 copy-done.18
  203.4 0.8 constant_dynamic-update-slice_fusion
  (77 shorter events, 7.5 us)
Async XLA Ops:
  0.0 31.1 %copy-start.19 = (s32[2,16]{1,0:T(2,128)S(1)}, s32[2,16]{1,0:T(2,128)}, u32[]{:S(2)}) copy-start(s32[2,16]{1,0:T(2,128)} %param.8) | copy-start | bytes 388
  1.8 1.2 copy-start.11
  3.0 1.2 copy-start.13
  6.0 17.5 %collective-permute-start = (bf16[1152,256]{1,0:T(8,128)(2,1)S(1)}, bf16[1152,256]{1,0:T(8,128)(2,1)S(1)}, u32[]{:S(2)}, u32[]{:S(2)}) collective-permute-start(bf16[1152,256]{1,0:T(8,128)(2,1)S(1)} %get-tuple-element.13), channel_id=1, source_target_pairs={{0,8},{4,12},{8,16},{12,20},{16,24},{20,28},{1,9},{5,13},{9,17},{1... | collective-permute-start | bytes 1769480 | tf_op jit(solution)/shard_map/ppermute | solution.py:436
  10.9 63.0 %collective-permute-start.4 = (bf16[512,256]{1,0:T(8,128)(2,1)}, bf16[512,256]{1,0:T(8,128)(2,1)}, u32[]{:S(2)}, u32[]{:S(2)}) collective-permute-start(bf16[512,256]{1,0:T(8,128)(2,1)} %get-tuple-element.12.rest_0_), channel_id=1, source_target_pairs={{0,4},{8,12},{16,20},{24,28},{1,5},{9,13},{17,21},{25,29},{2,6},{1... | collective-permute-start | bytes 786440 | tf_op jit(solution)/shard_map/ppermute | solution.py:439
  24.3 20.0 %collective-permute-start.2 = (bf16[1152,256]{1,0:T(8,128)(2,1)}, bf16[1152,256]{1,0:T(8,128)(2,1)S(1)}, u32[]{:S(2)}, u32[]{:S(2)}) collective-permute-start(bf16[1152,256]{1,0:T(8,128)(2,1)} %shard_map.56.rest_2_), channel_id=1, source_target_pairs={{0,4},{4,0},{8,12},{12,8},{16,20},{20,16},{24,28},{28,24},{1,5},{5... | collective-permute-start | bytes 1769480 | tf_op jit(solution)/shard_map/ppermute | solution.py:443
  26.7 16.8 %collective-permute-start.1 = (bf16[1216,256]{1,0:T(8,128)(2,1)}, bf16[1216,256]{1,0:T(8,128)(2,1)S(1)}, u32[]{:S(2)}, u32[]{:S(2)}) collective-permute-start(bf16[1216,256]{1,0:T(8,128)(2,1)} %shard_map.57), channel_id=1, source_target_pairs={{0,8},{4,12},{8,16},{12,20},{16,24},{20,28},{1,9},{5,13},{9,17},{1... | collective-permute-start | bytes 1867784 | tf_op jit(solution)/shard_map/ppermute | solution.py:436
  31.4 29.1 %copy-start.12 = (bf16[2048,256]{1,0:T(8,128)(2,1)S(1)}, bf16[2048,256]{1,0:T(8,128)(2,1)}, u32[]{:S(2)}) copy-start(bf16[2048,256]{1,0:T(8,128)(2,1)} %keys_ref.3) | copy-start | bytes 3145732
  31.5 29.1 %copy-start.14 = (bf16[2048,256]{1,0:T(8,128)(2,1)S(1)}, bf16[2048,256]{1,0:T(8,128)(2,1)}, u32[]{:S(2)}) copy-start(bf16[2048,256]{1,0:T(8,128)(2,1)} %values_ref.3) | copy-start | bytes 3145732
  43.7 16.8 %collective-permute-start.5 = (bf16[1216,256]{1,0:T(8,128)(2,1)S(1)}, bf16[1216,256]{1,0:T(8,128)(2,1)S(1)}, u32[]{:S(2)}, u32[]{:S(2)}) collective-permute-start(bf16[1216,256]{1,0:T(8,128)(2,1)S(1)} %shard_map.58.rest_2_), channel_id=1, source_target_pairs={{0,4},{4,0},{8,12},{12,8},{16,20},{20,16},{24,28},{28,24},{1,5},{5... | collective-permute-start | bytes 1867784 | tf_op jit(solution)/shard_map/ppermute | solution.py:443
  44.5 0.8 copy-start.3
  45.3 15.2 %collective-permute-start.3 = (bf16[1216,256]{1,0:T(8,128)(2,1)S(1)}, bf16[1216,256]{1,0:T(8,128)(2,1)S(1)}, u32[]{:S(2)}, u32[]{:S(2)}) collective-permute-start(bf16[1216,256]{1,0:T(8,128)(2,1)S(1)} %shard_map.59), channel_id=1, source_target_pairs={{0,8},{4,12},{8,16},{12,20},{16,24},{20,28},{1,9},{5,13},{9,17},{1... | collective-permute-start | bytes 1867784 | tf_op jit(solution)/shard_map/ppermute | solution.py:436
  61.5 31.9 %collective-permute-start.10 = (bf16[2048,256]{1,0:T(8,128)(2,1)}, bf16[2048,256]{1,0:T(8,128)(2,1)}, u32[]{:S(2)}, u32[]{:S(2)}) collective-permute-start(bf16[2048,256]{1,0:T(8,128)(2,1)} %shard_map.66.rest_0_.own_ref), channel_id=1, source_target_pairs={{0,8},{4,12},{8,16},{12,20},{16,24},{20,28},{1,9},{5,13},{9,17},{1... | collective-permute-start | bytes 3145736 | tf_op jit(solution)/shard_map/ppermute | solution.py:450
  67.8 12.6 %collective-permute-start.6 = (bf16[1216,256]{1,0:T(8,128)(2,1)}, bf16[1216,256]{1,0:T(8,128)(2,1)}, u32[]{:S(2)}, u32[]{:S(2)}) collective-permute-start(bf16[1216,256]{1,0:T(8,128)(2,1)} %shard_map.60), channel_id=1, source_target_pairs={{0,4},{4,0},{8,12},{12,8},{16,20},{20,16},{24,28},{28,24},{1,5},{5... | collective-permute-start | bytes 1867784 | tf_op jit(solution)/shard_map/ppermute | solution.py:443
  73.0 10.6 %copy-start = (bf16[2048,1024]{1,0:T(8,128)(2,1)S(1)}, bf16[2048,1024]{1,0:T(8,128)(2,1)}, u32[]{:S(2)}) copy-start(bf16[2048,1024]{1,0:T(8,128)(2,1)} %query_ref.11) | copy-start | bytes 12582916
  80.4 1.1 copy-start.4
  81.5 2.2 %copy-start.15 = (f32[32,1536]{1,0:T(8,128)S(1)}, f32[32,1536]{1,0:T(8,128)}, u32[]{:S(2)}) copy-start(f32[32,1536]{1,0:T(8,128)} %broadcast_in_dim.28.bias_ref) | copy-start | bytes 589828
  83.6 9.8 %copy-start.9 = (bf16[1024,256]{1,0:T(8,128)(2,1)}, bf16[1024,256]{1,0:T(8,128)(2,1)S(1)}, u32[]{:S(2)}) copy-start(bf16[1024,256]{1,0:T(8,128)(2,1)S(1)} %shard_map.61.vert_ref) | copy-start | bytes 1572868
  83.7 1.2 copy-start.5
  126.4 0.8 copy-start.7
  127.2 38.2 %collective-permute-start.11 = (bf16[2048,256]{1,0:T(8,128)(2,1)}, bf16[2048,256]{1,0:T(8,128)(2,1)}, u32[]{:S(2)}, u32[]{:S(2)}) collective-permute-start(bf16[2048,256]{1,0:T(8,128)(2,1)} %shard_map.67), channel_id=1, source_target_pairs={{0,4},{4,0},{8,12},{12,8},{16,20},{20,16},{24,28},{28,24},{1,5},{5... | collective-permute-start | bytes 3145736 | tf_op jit(solution)/shard_map/ppermute | solution.py:472
  131.4 33.4 %collective-permute-start.7 = (bf16[512,512]{1,0:T(8,128)(2,1)}, bf16[512,512]{1,0:T(8,128)(2,1)S(1)}, u32[]{:S(2)}, u32[]{:S(2)}) collective-permute-start(bf16[512,512]{1,0:T(8,128)(2,1)} %copy-done.7), channel_id=1, source_target_pairs={{0,3},{1,2},{2,1},{3,0},{4,7},{5,6},{6,5},{7,4},{8,11},{9,10},{10,... | collective-permute-start | bytes 1572872 | tf_op jit(solution)/shard_map/ppermute | solution.py:476
  131.5 2.2 %copy-start.1 = (bf16[2048,1024]{1,0:T(8,128)(2,1)S(1)}, bf16[2048,1024]{1,0:T(8,128)(2,1)}, u32[]{:S(2)}) copy-start(bf16[2048,1024]{1,0:T(8,128)(2,1)} %query_ref.11) | copy-start | bytes 12582916
  133.6 1.1 copy-start.6
  134.7 1.0 copy-start.8
  135.7 1.0 copy-start.10
  136.8 0.9 copy-start.16
  146.3 53.2 %collective-permute-start.8 = (bf16[512,512]{1,0:T(8,128)(2,1)S(1)}, bf16[512,512]{1,0:T(8,128)(2,1)S(1)}, u32[]{:S(2)}, u32[]{:S(2)}) collective-permute-start(bf16[512,512]{1,0:T(8,128)(2,1)S(1)} %shard_map.63.rest_6_), channel_id=1, source_target_pairs={{0,2},{1,3},{2,0},{3,1},{4,6},{5,7},{6,4},{7,5},{8,10},{9,11},{10,... | collective-permute-start | bytes 1572872 | tf_op jit(solution)/shard_map/ppermute | solution.py:476
  162.0 3.4 %copy-start.2 = (bf16[2048,1024]{1,0:T(8,128)(2,1)S(1)}, bf16[2048,1024]{1,0:T(8,128)(2,1)}, u32[]{:S(2)}) copy-start(bf16[2048,1024]{1,0:T(8,128)(2,1)} %query_ref.11) | copy-start | bytes 12582916
  162.0 3.3 %copy-start.17 = (f32[32,1536]{1,0:T(8,128)S(1)}, f32[32,1536]{1,0:T(8,128)}, u32[]{:S(2)}) copy-start(f32[32,1536]{1,0:T(8,128)} %broadcast_in_dim.31.bias_ref) | copy-start | bytes 589828
  162.0 37.5 %collective-permute-start.9 = (bf16[512,512]{1,0:T(8,128)(2,1)S(1)}, bf16[512,512]{1,0:T(8,128)(2,1)S(1)}, u32[]{:S(2)}, u32[]{:S(2)}) collective-permute-start(bf16[512,512]{1,0:T(8,128)(2,1)S(1)} %get-tuple-element.15), channel_id=1, source_target_pairs={{0,1},{1,0},{2,3},{3,2},{4,5},{5,4},{6,7},{7,6},{8,9},{9,8},{10,11... | collective-permute-start | bytes 1572872 | tf_op jit(solution)/shard_map/ppermute | solution.py:476
  174.2 25.5 %collective-permute-start.12 = (bf16[512,512]{1,0:T(8,128)(2,1)S(1)}, bf16[512,512]{1,0:T(8,128)(2,1)S(1)}, u32[]{:S(2)}, u32[]{:S(2)}) collective-permute-start(bf16[512,512]{1,0:T(8,128)(2,1)S(1)} %shard_map.68.rest_2_), channel_id=1, source_target_pairs={{0,3},{1,2},{2,1},{3,0},{4,7},{5,6},{6,5},{7,4},{8,11},{9,10},{10,... | collective-permute-start | bytes 1572872 | tf_op jit(solution)/shard_map/ppermute | solution.py:476
  184.2 15.6 %collective-permute-start.13 = (bf16[512,512]{1,0:T(8,128)(2,1)S(1)}, bf16[512,512]{1,0:T(8,128)(2,1)S(1)}, u32[]{:S(2)}, u32[]{:S(2)}) collective-permute-start(bf16[512,512]{1,0:T(8,128)(2,1)S(1)} %shard_map.69.rest_2_), channel_id=1, source_target_pairs={{0,2},{1,3},{2,0},{3,1},{4,6},{5,7},{6,4},{7,5},{8,10},{9,11},{10,... | collective-permute-start | bytes 1572872 | tf_op jit(solution)/shard_map/ppermute | solution.py:476
  199.4 2.0 collective-permute-start.14
  201.4 2.0 copy-start.18

commit v7 on v6

--- a/solution.py
+++ b/solution.py
@@ -17,7 +17,8 @@
 NEG = -1e30
 STEP_BLOCKS = 2
 TILE = 256
-ANY = pl.BlockSpec(memory_space=pl.ANY)
+HBM = pl.BlockSpec(memory_space=pltpu.HBM)
+VMEM = pl.BlockSpec(memory_space=pltpu.VMEM)
 SMEM = pl.BlockSpec(memory_space=pltpu.SMEM)
 
 
@@ -61,10 +62,10 @@
             jax.ShapeDtypeStruct((chunk_rows + slot_rows, 2 * HD), keys.dtype),
             jax.ShapeDtypeStruct((slot_rows, 2 * HD), keys.dtype),
         ],
-        in_specs=[SMEM, ANY, ANY],
-        out_specs=[ANY] * 3,
+        in_specs=[SMEM, HBM, HBM],
+        out_specs=[VMEM] * 3,
         scratch_shapes=[pltpu.SemaphoreType.DMA((4 * heads * MOWN + 4,))],
-        compiler_params=pltpu.CompilerParams(vmem_limit_bytes=1 << 20),
+        compiler_params=pltpu.CompilerParams(vmem_limit_bytes=8 << 20),
         cost_estimate=pl.CostEstimate(flops=0, bytes_accessed=16 * rows * HD, transcendentals=0),
     )(local_block, keys, values)
 
@@ -85,10 +86,10 @@
     return pl.pallas_call(
         functools.partial(pair_kernel, head),
         out_shape=jax.ShapeDtypeStruct((rows, 2 * HD), keys.dtype),
-        in_specs=[ANY] * (2 + len(after)),
-        out_specs=ANY,
+        in_specs=[HBM] * (2 + len(after)),
+        out_specs=VMEM,
         scratch_shapes=[pltpu.SemaphoreType.DMA((2,))],
-        compiler_params=pltpu.CompilerParams(vmem_limit_bytes=1 << 20),
+        compiler_params=pltpu.CompilerParams(vmem_limit_bytes=8 << 20),
         cost_estimate=pl.CostEstimate(flops=0, bytes_accessed=8 * rows * HD, transcendentals=0),
     )(keys, values, *after)
 
@@ -125,10 +126,10 @@
     return pl.pallas_call(
         functools.partial(joined_kernel, plan),
         out_shape=jax.ShapeDtypeStruct((total, 2 * HD), jnp.bfloat16),
-        in_specs=[SMEM] + [ANY] * (len(arrays) + len(after)),
-        out_specs=ANY,
+        in_specs=[SMEM] + [HBM] * (len(arrays) + len(after)),
+        out_specs=VMEM,
         scratch_shapes=[pltpu.SemaphoreType.DMA],
-        compiler_params=pltpu.CompilerParams(vmem_limit_bytes=1 << 20),
+        compiler_params=pltpu.CompilerParams(vmem_limit_bytes=8 << 20),
         cost_estimate=pl.CostEstimate(flops=0, bytes_accessed=8 * total * HD, transcendentals=0),
     )(parity, *arrays, *after)
 
@@ -162,10 +163,10 @@
     return pl.pallas_call(
         functools.partial(listed_kernel, head, [low for _, low in slots]),
         out_shape=jax.ShapeDtypeStruct((NV * BLK, 2 * HD), jnp.bfloat16),
-        in_specs=[SMEM, SMEM] + [ANY] * len(slots),
-        out_specs=ANY,
+        in_specs=[SMEM, SMEM] + [HBM] * len(slots),
+        out_specs=VMEM,
         scratch_shapes=[pltpu.SemaphoreType.DMA],
-        compiler_params=pltpu.CompilerParams(vmem_limit_bytes=1 << 20),
+        compiler_params=pltpu.CompilerParams(vmem_limit_bytes=8 << 20),
         cost_estimate=pl.CostEstimate(flops=0, bytes_accessed=8 * NV * BLK * HD, transcendentals=0),
     )(place, source, *[array for array, _ in slots])
 
@@ -241,13 +242,13 @@
         for h in range(group_heads):
             out[rows, h * HD : (h + 1) * HD] = result[h * BLK : (h + 1) * BLK]
 
-    def stage(block, at, score, weigh, combine):
+    def stage(block, at, score, weigh, combine, arrives=False):
         other = 1 - at
         if score:
             fresh = jnp.minimum(block, last)
             query = query_of(fresh)
             rows = slash_rows(fresh)
-            bias = bias_ref[pl.ds(shard_block(fresh), 1), :]
+            bias = bias_ref[pl.ds(head * blocks_dev + shard_block(fresh), 1), :]
         if combine:
             done = jnp.maximum(block - 2, 0)
             total = weighted_values(done, at)
@@ -257,6 +258,8 @@
         highest = None
         for tile in range((NV + NS) * BLK // TILE):
             low = tile * TILE
+            if arrives and low == NV * BLK:
+                pltpu.make_async_copy(window, window, window_sem).wait()
             if score:
                 found = score_tile(query, bias, rows, tile)
                 scores[at][:, low : low + TILE] = found
@@ -304,8 +307,7 @@
         pltpu.make_async_copy(vert, vert, vert_sem).wait()
         vert_keys[...] = vert[:, :HD].T
         pltpu.make_async_copy(queries, queries, query_sem).wait()
-        pltpu.make_async_copy(window, window, window_sem).wait()
-        stage(0, 0, True, False, False)
+        stage(0, 0, True, False, False, True)
 
     first = step * STEP_BLOCKS
     stage(first + 1, 1, True, True, True)
@@ -340,8 +342,8 @@
         grid_spec=pltpu.PrefetchScalarGridSpec(
             num_scalar_prefetch=2,
             grid=(parts * part_blocks // STEP_BLOCKS,),
-            in_specs=[pl.BlockSpec(bias.shape, lambda s, *_: (0, 0))] + [ANY] * (3 + 2 * len(two_back) + len(after)),
-            out_specs=[ANY] * parts,
+            in_specs=[pl.BlockSpec(bias.shape, lambda s, *_: (0, 0))] + [HBM] * (3 + 2 * len(two_back) + len(after)),
+            out_specs=[HBM] * parts,
             scratch_shapes=[
                 pltpu.VMEM((parts * part_rows, group_cols), jnp.bfloat16),
                 pltpu.VMEM((parts * part_rows, group_cols), jnp.bfloat16),
@@ -415,7 +417,12 @@
     in_vertical = jnp.any(slash_blocks[:, :, :, None] == vertical[:, None, None, :], axis=3)
     slash_valid = (slash[:, None, :] == 0) | ((slash_blocks >= 0) & jnp.logical_not(in_vertical))
     valid = jnp.concatenate([vert_valid, slash_valid], axis=2)
-    bias = jnp.repeat(jnp.where(valid, 0.0, NEG).astype(jnp.float32), BLK, axis=2)
+    listed = jnp.arange(NV + NS, dtype=jnp.int32)
+    spread = (jnp.arange((NV + NS) * BLK, dtype=jnp.int32) // BLK == listed[:, None])
+    barred = jnp.where(valid, 0.0, NEG).reshape(kv_local * blocks_dev, NV + NS)
+    bias = jnp.dot(
+        barred.astype(jnp.bfloat16), spread.astype(jnp.bfloat16), preferred_element_type=jnp.float32
+    )
 
     steps = shard_count // 2 - 1
     bounds = [k * blocks_dev // steps * BLK for k in range(steps + 1)]
@@ -444,7 +451,7 @@
         across.append((one_back[-1], rows))
     slots = behind + across
     windows = [(bounds, own, two_back, one_back)]
-    after = two_back[-1:] + one_back[-2:-1]
+    after = two_back[-1:] + one_back[-2:-1] + [cross]
     for head in range(1, kv_local):
         own = pair_of(head, keys, values, after)
         come = lax.ppermute(own, "ctx", two_pairs)
@@ -462,7 +469,7 @@
         for flips in calls:
             others = [head_index ^ flip for flip in flips]
             pieces = attend(
-                head, jnp.stack(others).astype(jnp.int32), bounds, slash, bias[head], queries, vert, own,
+                head, jnp.stack(others).astype(jnp.int32), bounds, slash, bias, queries, vert, own,
                 two_back, one_back, part_rows, after,
             )
             after = [pieces[-1]]

time: 205 us -> 170 us (0.83)
  Pallas kernels: 106 us -> 75.3 us
  local copies, waits for them, and re-layouts: 22.7 us -> 16.3 us
  waiting for transfers between devices: 37.2 us -> 40.2 us
    pallas_call x6, Pallas kernels: 35.8 us -> 4.79 us  [joined(): pl.pallas_call(functools.partial(joined_kernel, plan), out_shape=jax.Shap...]
    broadcast_in_dim x4 -> x0, local copies, waits for them, and re-layouts: 5.51 us -> none  [local(): jnp.repeat(jnp.where(valid, 0.0, NEG).astype(jnp.float32), BLK, axis=2)]
    ppermute x3, waiting for transfers between devices: 6.51 us -> 10.4 us  [local(): one_back.append(lax.ppermute(cross, 'ctx', across_pairs))]
    unnamed x40 -> x42, local copies, waits for them, and re-layouts: 14.7 us -> 13.7 us
  transfers between devices with their start and end apart: 15 -> 15, of which waited for: 5 -> 6; matrix products, arithmetic and copies ran while one was open for 5% -> 3% of each run, Pallas kernels for 35% -> 42%
where the time goes in v7:
time: 170 us; the launch traced here: 169 us
  Pallas kernels  75.3 us (44%)
  waiting for transfers between devices  40.2 us (24%)
  starting transfers between devices  32.4 us (19%)
  local copies, waits for them, and re-layouts  16.3 us (10%)
  other arithmetic  4.21 us (2%)
    pallas_call x6, Pallas kernels, attend(): pl.pallas_call(functools.partial(attend_kernel, head, parts, bounds, len(...  62.3 us
    ppermute x3, waiting for transfers between devices, local(): come = lax.ppermute(send, 'ctx', two_pairs)  28.3 us
    ppermute x3, starting transfers between devices, local(): come = lax.ppermute(send, 'ctx', two_pairs)  13.8 us
    unnamed x42, local copies, waits for them, and re-layouts  13.7 us
    ppermute x3, waiting for transfers between devices, local(): one_back.append(lax.ppermute(cross, 'ctx', across_pairs))  10.4 us
    ppermute x1, starting transfers between devices, local(): come = lax.ppermute(own, 'ctx', two_pairs)  5.4 us
    pallas_call x2, Pallas kernels, listed_blocks(): pl.pallas_call(functools.partial(listed_kernel, head, [low for _, low in...  5.1 us
    pallas_call x6, Pallas kernels, joined(): pl.pallas_call(functools.partial(joined_kernel, plan), out_shape=jax.Shap...  4.79 us
  transfers between devices with their start and end apart: 15, of which 6 were waited for; matrix products, arithmetic and copies ran while one was open for 3% of the time, Pallas kernels for 42%

profile of v7, /device:TPU:0, one launch (start us, length us, event | category | flops | bytes accessed | tf_op | source)
XLA Modules:
  0.0 169.2 jit_solution(3943175332171250181)
XLA Ops:
  0.0 0.8 and_select_fusion
  0.8 0.7 broadcast_compare_fusion.2
  1.8 1.2 copy-done.14
  3.0 1.2 copy-done.16
  4.2 2.0 %shard_map.55 = (bf16[2048,256]{1,0:T(8,128)(2,1)S(1)}, bf16[1152,256]{1,0:T(8,128)(2,1)S(1)}, bf16[512,256]{1,0:T(8,128)(2,1)}) custom-call(s32[2,4]{1,0:T(2,128)S(1)} %select_reduce_fusion.2.local_ref, bf16[2048,256]{1,0:T(8,128)(2,1)S(1)} %copy-done.14, bf16[2048,256]{1,0:T(8,128)(2,1)S(1)} %copy-done.16), custom_call_target="tpu_custom_call" | custom-call | bytes 4194304 | tf_op jit(solution)/shard_map/pallas_call | solution.py:58
  6.2 5.0 %collective-permute-start = (bf16[1152,256]{1,0:T(8,128)(2,1)S(1)}, bf16[1152,256]{1,0:T(8,128)(2,1)S(1)}, u32[]{:S(2)}, u32[]{:S(2)}) collective-permute-start(bf16[1152,256]{1,0:T(8,128)(2,1)S(1)} %get-tuple-element.13), channel_id=1, source_target_pairs={{0,8},{4,12},{8,16},{12,20},{16,24},{20,28},{1,9},{5,13},{9,17},{1... | collective-permute-start | bytes 1769480 | tf_op jit(solution)/shard_map/ppermute | solution.py:443
  11.2 4.1 %collective-permute-start.4 = (bf16[512,256]{1,0:T(8,128)(2,1)}, bf16[512,256]{1,0:T(8,128)(2,1)}, u32[]{:S(2)}, u32[]{:S(2)}) collective-permute-start(bf16[512,256]{1,0:T(8,128)(2,1)} %get-tuple-element.12.rest_0_), channel_id=1, source_target_pairs={{0,4},{8,12},{16,20},{24,28},{1,5},{9,13},{17,21},{25,29},{2,6},{1... | collective-permute-start | bytes 786440 | tf_op jit(solution)/shard_map/ppermute | solution.py:446
  15.3 1.0 convert_reduce_fusion.1
  16.3 0.8 select_reduce_fusion.1.slash_ref
  17.1 6.6 %collective-permute-done.rest_1_.rest_0_ = bf16[1152,256]{1,0:T(8,128)(2,1)S(1)} collective-permute-done((bf16[1152,256]{1,0:T(8,128)(2,1)S(1)}, bf16[1152,256]{1,0:T(8,128)(2,1)S(1)}, u32[]{:S(2)}, u32[]{:S(2)}) %collective-permute-start) | collective-permute-done | bytes 589856 | tf_op jit(solution)/shard_map/ppermute | solution.py:443
  23.7 1.0 shard_map.56.rest_2_
  24.7 1.5 collective-permute-start.2
  26.5 4.4 %collective-permute-start.1 = (bf16[1216,256]{1,0:T(8,128)(2,1)S(1)}, bf16[1216,256]{1,0:T(8,128)(2,1)S(1)}, u32[]{:S(2)}, u32[]{:S(2)}) collective-permute-start(bf16[1216,256]{1,0:T(8,128)(2,1)S(1)} %shard_map.57), channel_id=1, source_target_pairs={{0,8},{4,12},{8,16},{12,20},{16,24},{20,28},{1,9},{5,13},{9,17},{1... | collective-permute-start | bytes 1867784 | tf_op jit(solution)/shard_map/ppermute | solution.py:443
  32.1 10.8 %collective-permute-done.1.rest_1_.rest_2_ = bf16[1216,256]{1,0:T(8,128)(2,1)S(1)} collective-permute-done((bf16[1216,256]{1,0:T(8,128)(2,1)S(1)}, bf16[1216,256]{1,0:T(8,128)(2,1)S(1)}, u32[]{:S(2)}, u32[]{:S(2)}) %collective-permute-start.1) | collective-permute-done | bytes 622624 | tf_op jit(solution)/shard_map/ppermute | solution.py:443
  43.2 0.6 collective-permute-start.5
  44.0 0.8 copy-done.3
  44.8 4.4 %collective-permute-start.3 = (bf16[1216,256]{1,0:T(8,128)(2,1)S(1)}, bf16[1216,256]{1,0:T(8,128)(2,1)S(1)}, u32[]{:S(2)}, u32[]{:S(2)}) collective-permute-start(bf16[1216,256]{1,0:T(8,128)(2,1)S(1)} %shard_map.59), channel_id=1, source_target_pairs={{0,8},{4,12},{8,16},{12,20},{16,24},{20,28},{1,9},{5,13},{9,17},{1... | collective-permute-start | bytes 1867784 | tf_op jit(solution)/shard_map/ppermute | solution.py:443
  49.2 10.8 %collective-permute-done.3.rest_1_.rest_3_.rest_2_.rest_0_ = bf16[1216,256]{1,0:T(8,128)(2,1)S(1)} collective-permute-done((bf16[1216,256]{1,0:T(8,128)(2,1)S(1)}, bf16[1216,256]{1,0:T(8,128)(2,1)S(1)}, u32[]{:S(2)}, u32[]{:S(2)}) %collective-permute-start.3) | collective-permute-done | bytes 622624 | tf_op jit(solution)/shard_map/ppermute | solution.py:443
  60.1 1.0 shard_map.60.rest_2_
  61.1 1.2 shard_map.66.rest_0_.own_ref
  62.3 5.4 %collective-permute-start.10 = (bf16[2048,256]{1,0:T(8,128)(2,1)}, bf16[2048,256]{1,0:T(8,128)(2,1)}, u32[]{:S(2)}, u32[]{:S(2)}) collective-permute-start(bf16[2048,256]{1,0:T(8,128)(2,1)} %shard_map.66.rest_0_.own_ref), channel_id=1, source_target_pairs={{0,8},{4,12},{8,16},{12,20},{16,24},{20,28},{1,9},{5,13},{9,17},{1... | collective-permute-start | bytes 3145736 | tf_op jit(solution)/shard_map/ppermute | solution.py:457
  67.7 1.5 collective-permute-start.6
  69.8 10.4 %collective-permute-done.6.rest_7_.rest_5_ = bf16[1216,256]{1,0:T(8,128)(2,1)} collective-permute-done((bf16[1216,256]{1,0:T(8,128)(2,1)}, bf16[1216,256]{1,0:T(8,128)(2,1)}, u32[]{:S(2)}, u32[]{:S(2)}) %collective-permute-start.6) | collective-permute-done | bytes 622624 | tf_op jit(solution)/shard_map/ppermute | solution.py:450
  80.2 1.1 copy-done.4
  81.3 2.4 %shard_map.61.vert_ref = bf16[1024,256]{1,0:T(8,128)(2,1)S(1)} custom-call(s32[8,2,4]{2,1,0:T(2,128)S(1)} %broadcast_add_fusion.place_ref, s32[2,16]{1,0:T(2,128)S(1)} %compare_select_fusion.1.source_ref, bf16[512,256]{1,0:T(8,128)(2,1)} %get-tuple-element.12.rest_0_, bf16[1152,256]{1,0:T(8,128)(2,1)S(1)} %collective-permute-done.rest_1_.rest_0_, ...), custom_call_target="tpu_custom_call" | custom-call | bytes 1048576 | tf_op jit(solution)/shard_map/pallas_call | solution.py:163
  83.7 8.4 %shard_map.62.rest_6_.rest_2_ = bf16[512,512]{1,0:T(8,128)(2,1)S(1)} custom-call(s32[1]{0:T(128)} %bitcast.part_ref, s32[2,8]{1,0:T(2,128)S(1)} %select_reduce_fusion.1.slash_ref, f32[64,1536]{1,0:T(8,128)S(1)} %fusion.bias_ref, bf16[2048,1024]{1,0:T(8,128)(2,1)S(1)} %copy-done, bf16[1024,256]{1,0:T(8,128)(2,1)S(1)} %shard_map.61.vert_ref, ...), custom_call_target="tpu_custom_call" | custom-call | flops 1610612736 | bytes 4194304 | tf_op jit(solution)/shard_map/pallas_call | solution.py:337
  92.2 2.2 %shard_map.67 = bf16[2048,256]{1,0:T(8,128)(2,1)} custom-call(s32[1]{0:T(128)} %bitcast.1.parity_ref, bf16[2048,256]{1,0:T(8,128)(2,1)} %shard_map.66.rest_0_.own_ref, bf16[2048,256]{1,0:T(8,128)(2,1)} %collective-permute-done.10.rest_1_.rest_0_, bf16[512,512]{1,0:T(8,128)(2,1)S(1)} %shard_map.62.rest_6_.rest_2_), custom_call_target="tpu_custom_call" | custom-call | bytes 2097152 | tf_op jit(solution)/shard_map/pallas_call | solution.py:126
  94.5 0.8 copy-done.10
  95.3 1.3 collective-permute-start.11
  96.7 2.2 %copy-done.1 = bf16[2048,1024]{1,0:T(8,128)(2,1)S(1)} copy-done((bf16[2048,1024]{1,0:T(8,128)(2,1)S(1)}, bf16[2048,1024]{1,0:T(8,128)(2,1)}, u32[]{:S(2)}) %copy-start.1) | copy-done | bytes 4194328
  98.9 1.1 copy-done.6
  100.0 1.0 copy-done.8
  100.9 1.0 copy-done.11
  102.0 1.0 copy-done.13
  103.0 8.4 %shard_map.63.rest_6_ = bf16[512,512]{1,0:T(8,128)(2,1)S(1)} custom-call(s32[1]{0:T(128)} %bitcast.2.part_ref, s32[2,8]{1,0:T(2,128)S(1)} %select_reduce_fusion.1.slash_ref, f32[64,1536]{1,0:T(8,128)S(1)} %copy-done.8, bf16[2048,1024]{1,0:T(8,128)(2,1)S(1)} %copy-done.1, bf16[1024,256]{1,0:T(8,128)(2,1)S(1)} %copy-done.13, ...), custom_call_target="tpu_custom_call" | custom-call | flops 1610612736 | bytes 4194304 | tf_op jit(solution)/shard_map/pallas_call | solution.py:337
  111.5 1.7 %collective-permute-start.8 = (bf16[512,512]{1,0:T(8,128)(2,1)S(1)}, bf16[512,512]{1,0:T(8,128)(2,1)S(1)}, u32[]{:S(2)}, u32[]{:S(2)}) collective-permute-start(bf16[512,512]{1,0:T(8,128)(2,1)S(1)} %shard_map.63.rest_6_), channel_id=1, source_target_pairs={{0,2},{1,3},{2,0},{3,1},{4,6},{5,7},{6,4},{7,5},{8,10},{9,11},{10,... | collective-permute-start | bytes 1572872 | tf_op jit(solution)/shard_map/ppermute | solution.py:483
  113.2 14.0 %shard_map.64 = (bf16[512,512]{1,0:T(8,128)(2,1)S(1)}, bf16[512,512]{1,0:T(8,128)(2,1)S(1)}) custom-call(s32[2]{0:T(128)S(1)} %pad_add_fusion.part_ref, s32[2,8]{1,0:T(2,128)S(1)} %select_reduce_fusion.1.slash_ref, f32[64,1536]{1,0:T(8,128)S(1)} %copy-done.8, bf16[2048,1024]{1,0:T(8,128)(2,1)S(1)} %copy-done.1, bf16[1024,256]{1,0:T(8,128)(2,1)S(1)} %copy-done.13, ...), custom_call_target="tpu_custom_call" | custom-call | flops 3221225472 | bytes 5242880 | tf_op jit(solution)/shard_map/pallas_call | solution.py:337
  127.5 2.7 %shard_map.65.vert_ref = bf16[1024,256]{1,0:T(8,128)(2,1)S(1)} custom-call(s32[8,2,4]{2,1,0:T(2,128)S(1)} %broadcast_add_fusion.place_ref, s32[2,16]{1,0:T(2,128)S(1)} %compare_select_fusion.1.source_ref, bf16[512,256]{1,0:T(8,128)(2,1)} %get-tuple-element.12.rest_0_, bf16[1152,256]{1,0:T(8,128)(2,1)S(1)} %collective-permute-done.rest_1_.rest_0_, ...), custom_call_target="tpu_custom_call" | custom-call | bytes 1048576 | tf_op jit(solution)/shard_map/pallas_call | solution.py:163
  130.3 0.5 broadcast_in_dim.14
  130.9 8.6 %shard_map.68.rest_2_ = bf16[512,512]{1,0:T(8,128)(2,1)S(1)} custom-call(s32[1]{0:T(128)} %bitcast.part_ref, s32[2,8]{1,0:T(2,128)S(1)} %select_reduce_fusion.1.slash_ref, f32[64,1536]{1,0:T(8,128)S(1)} %copy-done.9, bf16[2048,1024]{1,0:T(8,128)(2,1)S(1)} %copy-done.2, bf16[1024,256]{1,0:T(8,128)(2,1)S(1)} %shard_map.65.vert_ref, ...), custom_call_target="tpu_custom_call" | custom-call | flops 1610612736 | bytes 4194304 | tf_op jit(solution)/shard_map/pallas_call | solution.py:337
  139.5 1.4 collective-permute-start.12
  140.9 8.6 %shard_map.69.rest_2_ = bf16[512,512]{1,0:T(8,128)(2,1)S(1)} custom-call(s32[1]{0:T(128)} %bitcast.2.part_ref, s32[2,8]{1,0:T(2,128)S(1)} %select_reduce_fusion.1.slash_ref, f32[64,1536]{1,0:T(8,128)S(1)} %copy-done.9, bf16[2048,1024]{1,0:T(8,128)(2,1)S(1)} %copy-done.2, bf16[1024,256]{1,0:T(8,128)(2,1)S(1)} %shard_map.65.vert_ref, ...), custom_call_target="tpu_custom_call" | custom-call | flops 1610612736 | bytes 4194304 | tf_op jit(solution)/shard_map/pallas_call | solution.py:337
  149.6 0.6 collective-permute-start.13
  150.2 14.1 %shard_map.70 = (bf16[512,512]{1,0:T(8,128)(2,1)S(1)}, bf16[512,512]{1,0:T(8,128)(2,1)S(1)}) custom-call(s32[2]{0:T(128)S(1)} %pad_add_fusion.part_ref, s32[2,8]{1,0:T(2,128)S(1)} %select_reduce_fusion.1.slash_ref, f32[64,1536]{1,0:T(8,128)S(1)} %copy-done.9, bf16[2048,1024]{1,0:T(8,128)(2,1)S(1)} %copy-done.2, bf16[1024,256]{1,0:T(8,128)(2,1)S(1)} %shard_map.65.vert_ref, ...), custom_call_target="tpu_custom_call" | custom-call | flops 3221225472 | bytes 5242880 | tf_op jit(solution)/shard_map/pallas_call | solution.py:337
  164.8 0.3 collective-permute-done.13
  165.1 1.2 collective-permute-done.14
  166.4 2.0 %copy-done.18 = bf16[512,4096]{1,0:T(8,128)(2,1)} copy-done((bf16[512,4096]{1,0:T(8,128)(2,1)}, bf16[512,4096]{1,0:T(8,128)(2,1)S(1)}, u32[]{:S(2)}) %copy-start.18) | copy-done | bytes 4194328
  168.4 0.8 constant_dynamic-update-slice_fusion
  (86 shorter events, 3.7 us)
Async XLA Ops:
  0.0 30.9 %copy-start.19 = (s32[2,16]{1,0:T(2,128)S(1)}, s32[2,16]{1,0:T(2,128)}, u32[]{:S(2)}) copy-start(s32[2,16]{1,0:T(2,128)} %param.8) | copy-start | bytes 388
  1.8 1.2 copy-start.14
  3.0 1.2 copy-start.16
  6.2 17.5 %collective-permute-start = (bf16[1152,256]{1,0:T(8,128)(2,1)S(1)}, bf16[1152,256]{1,0:T(8,128)(2,1)S(1)}, u32[]{:S(2)}, u32[]{:S(2)}) collective-permute-start(bf16[1152,256]{1,0:T(8,128)(2,1)S(1)} %get-tuple-element.13), channel_id=1, source_target_pairs={{0,8},{4,12},{8,16},{12,20},{16,24},{20,28},{1,9},{5,13},{9,17},{1... | collective-permute-start | bytes 1769480 | tf_op jit(solution)/shard_map/ppermute | solution.py:443
  11.2 58.6 %collective-permute-start.4 = (bf16[512,256]{1,0:T(8,128)(2,1)}, bf16[512,256]{1,0:T(8,128)(2,1)}, u32[]{:S(2)}, u32[]{:S(2)}) collective-permute-start(bf16[512,256]{1,0:T(8,128)(2,1)} %get-tuple-element.12.rest_0_), channel_id=1, source_target_pairs={{0,4},{8,12},{16,20},{24,28},{1,5},{9,13},{17,21},{25,29},{2,6},{1... | collective-permute-start | bytes 786440 | tf_op jit(solution)/shard_map/ppermute | solution.py:446
  24.7 19.1 %collective-permute-start.2 = (bf16[1152,256]{1,0:T(8,128)(2,1)}, bf16[1152,256]{1,0:T(8,128)(2,1)S(1)}, u32[]{:S(2)}, u32[]{:S(2)}) collective-permute-start(bf16[1152,256]{1,0:T(8,128)(2,1)} %shard_map.56.rest_2_), channel_id=1, source_target_pairs={{0,4},{4,0},{8,12},{12,8},{16,20},{20,16},{24,28},{28,24},{1,5},{5... | collective-permute-start | bytes 1769480 | tf_op jit(solution)/shard_map/ppermute | solution.py:450
  26.5 16.5 %collective-permute-start.1 = (bf16[1216,256]{1,0:T(8,128)(2,1)S(1)}, bf16[1216,256]{1,0:T(8,128)(2,1)S(1)}, u32[]{:S(2)}, u32[]{:S(2)}) collective-permute-start(bf16[1216,256]{1,0:T(8,128)(2,1)S(1)} %shard_map.57), channel_id=1, source_target_pairs={{0,8},{4,12},{8,16},{12,20},{16,24},{20,28},{1,9},{5,13},{9,17},{1... | collective-permute-start | bytes 1867784 | tf_op jit(solution)/shard_map/ppermute | solution.py:443
  31.9 29.2 %copy-start.15 = (bf16[2048,256]{1,0:T(8,128)(2,1)S(1)}, bf16[2048,256]{1,0:T(8,128)(2,1)}, u32[]{:S(2)}) copy-start(bf16[2048,256]{1,0:T(8,128)(2,1)} %keys_ref.3) | copy-start | bytes 3145732
  31.9 29.2 %copy-start.17 = (bf16[2048,256]{1,0:T(8,128)(2,1)S(1)}, bf16[2048,256]{1,0:T(8,128)(2,1)}, u32[]{:S(2)}) copy-start(bf16[2048,256]{1,0:T(8,128)(2,1)} %values_ref.3) | copy-start | bytes 3145732
  43.2 17.9 %collective-permute-start.5 = (bf16[1216,256]{1,0:T(8,128)(2,1)S(1)}, bf16[1216,256]{1,0:T(8,128)(2,1)S(1)}, u32[]{:S(2)}, u32[]{:S(2)}) collective-permute-start(bf16[1216,256]{1,0:T(8,128)(2,1)S(1)} %shard_map.58.rest_2_), channel_id=1, source_target_pairs={{0,4},{4,0},{8,12},{12,8},{16,20},{20,16},{24,28},{28,24},{1,5},{5... | collective-permute-start | bytes 1867784 | tf_op jit(solution)/shard_map/ppermute | solution.py:450
  44.0 0.8 copy-start.3
  44.8 15.3 %collective-permute-start.3 = (bf16[1216,256]{1,0:T(8,128)(2,1)S(1)}, bf16[1216,256]{1,0:T(8,128)(2,1)S(1)}, u32[]{:S(2)}, u32[]{:S(2)}) collective-permute-start(bf16[1216,256]{1,0:T(8,128)(2,1)S(1)} %shard_map.59), channel_id=1, source_target_pairs={{0,8},{4,12},{8,16},{12,20},{16,24},{20,28},{1,9},{5,13},{9,17},{1... | collective-permute-start | bytes 1867784 | tf_op jit(solution)/shard_map/ppermute | solution.py:443
  62.3 29.9 %collective-permute-start.10 = (bf16[2048,256]{1,0:T(8,128)(2,1)}, bf16[2048,256]{1,0:T(8,128)(2,1)}, u32[]{:S(2)}, u32[]{:S(2)}) collective-permute-start(bf16[2048,256]{1,0:T(8,128)(2,1)} %shard_map.66.rest_0_.own_ref), channel_id=1, source_target_pairs={{0,8},{4,12},{8,16},{12,20},{16,24},{20,28},{1,9},{5,13},{9,17},{1... | collective-permute-start | bytes 3145736 | tf_op jit(solution)/shard_map/ppermute | solution.py:457
  67.7 12.5 %collective-permute-start.6 = (bf16[1216,256]{1,0:T(8,128)(2,1)}, bf16[1216,256]{1,0:T(8,128)(2,1)}, u32[]{:S(2)}, u32[]{:S(2)}) collective-permute-start(bf16[1216,256]{1,0:T(8,128)(2,1)} %shard_map.60.rest_2_), channel_id=1, source_target_pairs={{0,4},{4,0},{8,12},{12,8},{16,20},{20,16},{24,28},{28,24},{1,5},{5... | collective-permute-start | bytes 1867784 | tf_op jit(solution)/shard_map/ppermute | solution.py:450
  69.5 14.2 %copy-start = (bf16[2048,1024]{1,0:T(8,128)(2,1)S(1)}, bf16[2048,1024]{1,0:T(8,128)(2,1)}, u32[]{:S(2)}) copy-start(bf16[2048,1024]{1,0:T(8,128)(2,1)} %query_ref.11) | copy-start | bytes 12582916
  69.8 22.4 %copy-start.7 = (f32[64,1536]{1,0:T(8,128)}, f32[64,1536]{1,0:T(8,128)S(1)}, u32[]{:S(2)}) copy-start(f32[64,1536]{1,0:T(8,128)S(1)} %fusion.bias_ref) | copy-start | bytes 1179652
  80.2 1.1 copy-start.4
  81.3 2.4 %copy-start.5 = (bf16[1152,256]{1,0:T(8,128)(2,1)S(1)}, bf16[1152,256]{1,0:T(8,128)(2,1)}, u32[]{:S(2)}) copy-start(bf16[1152,256]{1,0:T(8,128)(2,1)} %copy-done.3) | copy-start | bytes 1769476
  83.7 8.5 %copy-start.12 = (bf16[1024,256]{1,0:T(8,128)(2,1)}, bf16[1024,256]{1,0:T(8,128)(2,1)S(1)}, u32[]{:S(2)}) copy-start(bf16[1024,256]{1,0:T(8,128)(2,1)S(1)} %shard_map.61.vert_ref) | copy-start | bytes 1572868
  94.5 0.8 copy-start.10
  95.3 35.6 %collective-permute-start.11 = (bf16[2048,256]{1,0:T(8,128)(2,1)}, bf16[2048,256]{1,0:T(8,128)(2,1)}, u32[]{:S(2)}, u32[]{:S(2)}) collective-permute-start(bf16[2048,256]{1,0:T(8,128)(2,1)} %shard_map.67), channel_id=1, source_target_pairs={{0,4},{4,0},{8,12},{12,8},{16,20},{20,16},{24,28},{28,24},{1,5},{5... | collective-permute-start | bytes 3145736 | tf_op jit(solution)/shard_map/ppermute | solution.py:479
  96.6 33.6 %collective-permute-start.7 = (bf16[512,512]{1,0:T(8,128)(2,1)}, bf16[512,512]{1,0:T(8,128)(2,1)S(1)}, u32[]{:S(2)}, u32[]{:S(2)}) collective-permute-start(bf16[512,512]{1,0:T(8,128)(2,1)} %copy-done.10), channel_id=1, source_target_pairs={{0,3},{1,2},{2,1},{3,0},{4,7},{5,6},{6,5},{7,4},{8,11},{9,10},{10,... | collective-permute-start | bytes 1572872 | tf_op jit(solution)/shard_map/ppermute | solution.py:483
  96.7 2.2 %copy-start.1 = (bf16[2048,1024]{1,0:T(8,128)(2,1)S(1)}, bf16[2048,1024]{1,0:T(8,128)(2,1)}, u32[]{:S(2)}) copy-start(bf16[2048,1024]{1,0:T(8,128)(2,1)} %query_ref.11) | copy-start | bytes 12582916
  98.9 1.1 copy-start.6
  99.9 1.0 copy-start.8
  100.9 1.0 copy-start.11
  102.0 1.0 copy-start.13
  111.5 52.9 %collective-permute-start.8 = (bf16[512,512]{1,0:T(8,128)(2,1)S(1)}, bf16[512,512]{1,0:T(8,128)(2,1)S(1)}, u32[]{:S(2)}, u32[]{:S(2)}) collective-permute-start(bf16[512,512]{1,0:T(8,128)(2,1)S(1)} %shard_map.63.rest_6_), channel_id=1, source_target_pairs={{0,2},{1,3},{2,0},{3,1},{4,6},{5,7},{6,4},{7,5},{8,10},{9,11},{10,... | collective-permute-start | bytes 1572872 | tf_op jit(solution)/shard_map/ppermute | solution.py:483
  127.2 3.6 %copy-start.2 = (bf16[2048,1024]{1,0:T(8,128)(2,1)S(1)}, bf16[2048,1024]{1,0:T(8,128)(2,1)}, u32[]{:S(2)}) copy-start(bf16[2048,1024]{1,0:T(8,128)(2,1)} %query_ref.11) | copy-start | bytes 12582916
  127.3 3.6 %copy-start.9 = (f32[64,1536]{1,0:T(8,128)S(1)}, f32[64,1536]{1,0:T(8,128)}, u32[]{:S(2)}) copy-start(f32[64,1536]{1,0:T(8,128)} %copy-done.7) | copy-start | bytes 1179652
  127.3 37.3 %collective-permute-start.9 = (bf16[512,512]{1,0:T(8,128)(2,1)S(1)}, bf16[512,512]{1,0:T(8,128)(2,1)S(1)}, u32[]{:S(2)}, u32[]{:S(2)}) collective-permute-start(bf16[512,512]{1,0:T(8,128)(2,1)S(1)} %get-tuple-element.15), channel_id=1, source_target_pairs={{0,1},{1,0},{2,3},{3,2},{4,5},{5,4},{6,7},{7,6},{8,9},{9,8},{10,11... | collective-permute-start | bytes 1572872 | tf_op jit(solution)/shard_map/ppermute | solution.py:483
  139.5 25.2 %collective-permute-start.12 = (bf16[512,512]{1,0:T(8,128)(2,1)S(1)}, bf16[512,512]{1,0:T(8,128)(2,1)S(1)}, u32[]{:S(2)}, u32[]{:S(2)}) collective-permute-start(bf16[512,512]{1,0:T(8,128)(2,1)S(1)} %shard_map.68.rest_2_), channel_id=1, source_target_pairs={{0,3},{1,2},{2,1},{3,0},{4,7},{5,6},{6,5},{7,4},{8,11},{9,10},{10,... | collective-permute-start | bytes 1572872 | tf_op jit(solution)/shard_map/ppermute | solution.py:483
  149.6 15.5 %collective-permute-start.13 = (bf16[512,512]{1,0:T(8,128)(2,1)S(1)}, bf16[512,512]{1,0:T(8,128)(2,1)S(1)}, u32[]{:S(2)}, u32[]{:S(2)}) collective-permute-start(bf16[512,512]{1,0:T(8,128)(2,1)S(1)} %shard_map.69.rest_2_), channel_id=1, source_target_pairs={{0,2},{1,3},{2,0},{3,1},{4,6},{5,7},{6,4},{7,5},{8,10},{9,11},{10,... | collective-permute-start | bytes 1572872 | tf_op jit(solution)/shard_map/ppermute | solution.py:483
  164.3 2.0 %collective-permute-start.14 = (bf16[512,512]{1,0:T(8,128)(2,1)S(1)}, bf16[512,512]{1,0:T(8,128)(2,1)S(1)}, u32[]{:S(2)}, u32[]{:S(2)}) collective-permute-start(bf16[512,512]{1,0:T(8,128)(2,1)S(1)} %get-tuple-element.17), channel_id=1, source_target_pairs={{0,1},{1,0},{2,3},{3,2},{4,5},{5,4},{6,7},{7,6},{8,9},{9,8},{10,11... | collective-permute-start | bytes 1572872 | tf_op jit(solution)/shard_map/ppermute | solution.py:483
  166.4 2.0 %copy-start.18 = (bf16[512,4096]{1,0:T(8,128)(2,1)}, bf16[512,4096]{1,0:T(8,128)(2,1)S(1)}, u32[]{:S(2)}) copy-start(bf16[512,4096]{1,0:T(8,128)(2,1)S(1)} %constant_dynamic-update-slice_fusion.1) | copy-start | bytes 12582916

commit v8 on v7

--- a/solution.py
+++ b/solution.py
@@ -134,40 +134,41 @@
     )(parity, *arrays, *after)
 
 
-def listed_kernel(head, lows, place_ref, source_ref, *rest):
+def listed_kernel(lows, place_ref, source_ref, *rest):
     refs, out_ref, sem = rest[:-2], rest[-2], rest[-1]
-
-    def block(index, slot):
-        return refs[index].at[pl.ds(lows[index] + (head * MOWN + slot) * BLK, BLK)]
-
-    for index in range(len(refs)):
-        for slot in range(MOWN):
-            place = place_ref[index, head, slot]
-
-            @pl.when(place >= 0)
-            def _():
-                pltpu.make_async_copy(block(index, slot), out_ref.at[blocks_at(place)], sem).start()
-
-    for entry in range(NV):
-
-        @pl.when(source_ref[head, entry] < 0)
-        def _():
-            pltpu.make_async_copy(
-                block(0, 0), out_ref.at[pl.ds(entry * BLK, BLK)], sem
-            ).start()
-
+    for head in range(out_ref.shape[0]):
+
+        def block(index, slot):
+            return refs[index].at[pl.ds(lows[index] + (head * MOWN + slot) * BLK, BLK)]
+
+        def put(found, target):
+            pltpu.make_async_copy(found, out_ref.at[head, target], sem).start()
+
+        for index in range(len(refs)):
+            for slot in range(MOWN):
+                place = place_ref[index, head, slot]
+                pl.when(place >= 0)(
+                    functools.partial(put, block(index, slot), blocks_at(place))
+                )
+        for entry in range(NV):
+            pl.when(source_ref[head, entry] < 0)(
+                functools.partial(put, block(0, 0), pl.ds(entry * BLK, BLK))
+            )
     pltpu.make_async_copy(out_ref, out_ref, sem).wait()
 
 
-def listed_blocks(head, place, source, slots):
+def listed_blocks(place, source, slots):
+    heads = source.shape[0]
     return pl.pallas_call(
-        functools.partial(listed_kernel, head, [low for _, low in slots]),
-        out_shape=jax.ShapeDtypeStruct((NV * BLK, 2 * HD), jnp.bfloat16),
+        functools.partial(listed_kernel, [low for _, low in slots]),
+        out_shape=jax.ShapeDtypeStruct((heads, NV * BLK, 2 * HD), jnp.bfloat16),
         in_specs=[SMEM, SMEM] + [HBM] * len(slots),
         out_specs=VMEM,
         scratch_shapes=[pltpu.SemaphoreType.DMA],
         compiler_params=pltpu.CompilerParams(vmem_limit_bytes=8 << 20),
-        cost_estimate=pl.CostEstimate(flops=0, bytes_accessed=8 * NV * BLK * HD, transcendentals=0),
+        cost_estimate=pl.CostEstimate(
+            flops=0, bytes_accessed=8 * heads * NV * BLK * HD, transcendentals=0
+        ),
     )(place, source, *[array for array, _ in slots])
 
 
@@ -288,7 +289,7 @@
                 queries.at[pl.ds(k * part_rows, part_rows)],
                 query_sem,
             ).start()
-        pltpu.make_async_copy(vert_ref, vert, vert_sem).start()
+        pltpu.make_async_copy(vert_ref.at[head], vert, vert_sem).start()
         for back, sources in enumerate((two_back, one_back)):
             for chunk, source in enumerate(sources):
                 rows = bounds[chunk + 1] - bounds[chunk]
@@ -364,7 +365,7 @@
             ],
         ),
         compiler_params=pltpu.CompilerParams(
-            dimension_semantics=("arbitrary",), vmem_limit_bytes=24 << 20
+            dimension_semantics=("arbitrary",), vmem_limit_bytes=56 << 20
         ),
         cost_estimate=pl.CostEstimate(
             flops=4 * parts * part_rows * group_heads * keys_seen * HD,
@@ -451,7 +452,7 @@
         across.append((one_back[-1], rows))
     slots = behind + across
     windows = [(bounds, own, two_back, one_back)]
-    after = two_back[-1:] + one_back[-2:-1] + [cross]
+    after = two_back[-2:-1] + [send]
     for head in range(1, kv_local):
         own = pair_of(head, keys, values, after)
         come = lax.ppermute(own, "ctx", two_pairs)
@@ -461,19 +462,20 @@
     out = jnp.zeros((part_rows, head_count * kv_local * group_cols), jnp.bfloat16)
     after = []
     half = head_count // 2
-    calls = [[flip] for flip in range(head_count - 1, half - 1, -1)]
-    calls.append(list(range(half - 1, -1, -1)))
+    calls = [[[head_count - 1], list(range(head_count - 2, -1, -1))]] * (kv_local - 1)
+    calls.append([[flip] for flip in range(head_count - 1, half - 1, -1)])
+    calls[-1].append(list(range(half - 1, -1, -1)))
+    vert = listed_blocks(place, source, slots)
     for head in range(kv_local):
         bounds, own, two_back, one_back = windows[head]
-        vert = listed_blocks(head, place, source, slots)
-        for flips in calls:
+        for flips in calls[head]:
             others = [head_index ^ flip for flip in flips]
             pieces = attend(
                 head, jnp.stack(others).astype(jnp.int32), bounds, slash, bias, queries, vert, own,
                 two_back, one_back, part_rows, after,
             )
             after = [pieces[-1]]
-            if flips == calls[0] and head + 1 < kv_local:
+            if flips == calls[head][0] and head + 1 < kv_local:
                 near, own_next, (come,), _ = windows[head + 1]
                 cross = joined(parity, [(tok_rows, (own_next, 0), (come, 0))], after)
                 crossed = lax.ppermute(cross, "ctx", across_pairs)

time: 170 us -> 173 us (1.018)
  Pallas kernels: 75.3 us -> 79.9 us
  local copies, waits for them, and re-layouts: 16.3 us -> 12.4 us
  starting transfers between devices: 32.4 us -> 30.4 us
  other arithmetic: 4.21 us -> 6.03 us
    pallas_call x6 -> x5, Pallas kernels: 62.3 us -> 71.3 us  [attend(): pl.pallas_call(functools.partial(attend_kernel, head, parts, bounds, len(...]
    unnamed x42 -> x44, local copies, waits for them, and re-layouts: 13.7 us -> 9.79 us
    ppermute x3, waiting for transfers between devices: 10.4 us -> 13.9 us  [local(): one_back.append(lax.ppermute(cross, 'ctx', across_pairs))]
    pallas_call x2 -> x1, Pallas kernels: 5.1 us -> 2.61 us  [listed_blocks(): pl.pallas_call(functools.partial(listed_kernel, [low for _, low in slots]...]
    ppermute x3, waiting for transfers between devices: 28.3 us -> 25.9 us  [local(): come = lax.ppermute(send, 'ctx', two_pairs)]
  transfers between devices with their start and end apart: 15 -> 15, of which waited for: 6 -> 6; matrix products, arithmetic and copies ran while one was open for 3% -> 4% of each run, Pallas kernels for 42% -> 45%
where the time goes in v8:
time: 173 us; the launch traced here: 172 us
  Pallas kernels  79.9 us (46%)
  waiting for transfers between devices  41.6 us (24%)
  starting transfers between devices  30.4 us (18%)
  local copies, waits for them, and re-layouts  12.4 us (7%)
  other arithmetic  6.03 us (3%)
    pallas_call x5, Pallas kernels, attend(): pl.pallas_call(functools.partial(attend_kernel, head, parts, bounds, len(...  71.3 us
    ppermute x3, waiting for transfers between devices, local(): come = lax.ppermute(send, 'ctx', two_pairs)  25.9 us
    ppermute x3, waiting for transfers between devices, local(): one_back.append(lax.ppermute(cross, 'ctx', across_pairs))  13.9 us
    ppermute x3, starting transfers between devices, local(): come = lax.ppermute(send, 'ctx', two_pairs)  13.8 us
    unnamed x44, local copies, waits for them, and re-layouts  9.79 us
    ppermute x1, starting transfers between devices, local(): come = lax.ppermute(own, 'ctx', two_pairs)  4.42 us
    ppermute x1, starting transfers between devices, local(): across.append((lax.ppermute(slots_own, 'ctx', pairs), 0))  4.09 us
    ppermute x6, starting transfers between devices, local(): lax.ppermute(piece, 'head', [(i, i ^ flip) for i in range(head_count)])  4.01 us
  transfers between devices with their start and end apart: 15, of which 6 were waited for; matrix products, arithmetic and copies ran while one was open for 4% of the time, Pallas kernels for 45%

profile of v8, /device:TPU:0, one launch (start us, length us, event | category | flops | bytes accessed | tf_op | source)
XLA Modules:
  0.0 171.9 jit_solution(843895251665674188)
XLA Ops:
  0.0 0.8 and_select_fusion
  0.8 0.7 broadcast_compare_fusion.2
  1.8 1.2 copy-done.9
  3.0 1.2 copy-done.11
  4.2 2.0 %shard_map.55 = (bf16[2048,256]{1,0:T(8,128)(2,1)S(1)}, bf16[1152,256]{1,0:T(8,128)(2,1)S(1)}, bf16[512,256]{1,0:T(8,128)(2,1)}) custom-call(s32[2,4]{1,0:T(2,128)S(1)} %select_reduce_fusion.2.local_ref, bf16[2048,256]{1,0:T(8,128)(2,1)S(1)} %copy-done.9, bf16[2048,256]{1,0:T(8,128)(2,1)S(1)} %copy-done.11), custom_call_target="tpu_custom_call" | custom-call | bytes 4194304 | tf_op jit(solution)/shard_map/pallas_call | solution.py:58
  6.3 5.0 %collective-permute-start = (bf16[1152,256]{1,0:T(8,128)(2,1)S(1)}, bf16[1152,256]{1,0:T(8,128)(2,1)S(1)}, u32[]{:S(2)}, u32[]{:S(2)}) collective-permute-start(bf16[1152,256]{1,0:T(8,128)(2,1)S(1)} %get-tuple-element.14), channel_id=1, source_target_pairs={{0,8},{4,12},{8,16},{12,20},{16,24},{20,28},{1,9},{5,13},{9,17},{1... | collective-permute-start | bytes 1769480 | tf_op jit(solution)/shard_map/ppermute | solution.py:444
  11.2 4.1 %collective-permute-start.4 = (bf16[512,256]{1,0:T(8,128)(2,1)}, bf16[512,256]{1,0:T(8,128)(2,1)}, u32[]{:S(2)}, u32[]{:S(2)}) collective-permute-start(bf16[512,256]{1,0:T(8,128)(2,1)} %get-tuple-element.13.rest_0_), channel_id=1, source_target_pairs={{0,4},{8,12},{16,20},{24,28},{1,5},{9,13},{17,21},{25,29},{2,6},{1... | collective-permute-start | bytes 786440 | tf_op jit(solution)/shard_map/ppermute | solution.py:447
  15.3 1.0 convert_reduce_fusion.1
  16.3 0.8 select_reduce_fusion.1.slash_ref
  17.2 0.8 compare_reduce_fusion
  18.0 5.8 %collective-permute-done.rest_1_.rest_0_ = bf16[1152,256]{1,0:T(8,128)(2,1)S(1)} collective-permute-done((bf16[1152,256]{1,0:T(8,128)(2,1)S(1)}, bf16[1152,256]{1,0:T(8,128)(2,1)S(1)}, u32[]{:S(2)}, u32[]{:S(2)}) %collective-permute-start) | collective-permute-done | bytes 589856 | tf_op jit(solution)/shard_map/ppermute | solution.py:444
  23.8 1.0 shard_map.56.rest_2_
  24.8 1.6 collective-permute-start.2
  26.5 4.4 %collective-permute-start.1 = (bf16[1216,256]{1,0:T(8,128)(2,1)S(1)}, bf16[1216,256]{1,0:T(8,128)(2,1)S(1)}, u32[]{:S(2)}, u32[]{:S(2)}) collective-permute-start(bf16[1216,256]{1,0:T(8,128)(2,1)S(1)} %shard_map.57), channel_id=1, source_target_pairs={{0,8},{4,12},{8,16},{12,20},{16,24},{20,28},{1,9},{5,13},{9,17},{1... | collective-permute-start | bytes 1867784 | tf_op jit(solution)/shard_map/ppermute | solution.py:444
  32.1 11.0 %collective-permute-done.1.rest_1_.rest_2_.rest_0_ = bf16[1216,256]{1,0:T(8,128)(2,1)S(1)} collective-permute-done((bf16[1216,256]{1,0:T(8,128)(2,1)S(1)}, bf16[1216,256]{1,0:T(8,128)(2,1)S(1)}, u32[]{:S(2)}, u32[]{:S(2)}) %collective-permute-start.1) | collective-permute-done | bytes 622624 | tf_op jit(solution)/shard_map/ppermute | solution.py:444
  43.1 1.0 shard_map.58.rest_2_
  44.3 4.4 %collective-permute-start.3 = (bf16[1216,256]{1,0:T(8,128)(2,1)S(1)}, bf16[1216,256]{1,0:T(8,128)(2,1)S(1)}, u32[]{:S(2)}, u32[]{:S(2)}) collective-permute-start(bf16[1216,256]{1,0:T(8,128)(2,1)S(1)} %shard_map.59.rest_1_), channel_id=1, source_target_pairs={{0,8},{4,12},{8,16},{12,20},{16,24},{20,28},{1,9},{5,13},{9,17},{1... | collective-permute-start | bytes 1867784 | tf_op jit(solution)/shard_map/ppermute | solution.py:444
  49.1 4.4 %collective-permute-start.10 = (bf16[2048,256]{1,0:T(8,128)(2,1)S(1)}, bf16[2048,256]{1,0:T(8,128)(2,1)}, u32[]{:S(2)}, u32[]{:S(2)}) collective-permute-start(bf16[2048,256]{1,0:T(8,128)(2,1)S(1)} %shard_map.64.rest_0_.own_ref), channel_id=1, source_target_pairs={{0,8},{4,12},{8,16},{12,20},{16,24},{20,28},{1,9},{5,13},{9,17},{1... | collective-permute-start | bytes 3145736 | tf_op jit(solution)/shard_map/ppermute | solution.py:458
  53.5 0.5 collective-permute-start.5
  54.0 9.2 %collective-permute-done.3.rest_1_.rest_3_.rest_2_ = bf16[1216,256]{1,0:T(8,128)(2,1)S(1)} collective-permute-done((bf16[1216,256]{1,0:T(8,128)(2,1)S(1)}, bf16[1216,256]{1,0:T(8,128)(2,1)S(1)}, u32[]{:S(2)}, u32[]{:S(2)}) %collective-permute-start.3) | collective-permute-done | bytes 622624 | tf_op jit(solution)/shard_map/ppermute | solution.py:444
  63.2 1.1 shard_map.60
  64.3 0.6 collective-permute-start.6
  65.2 1.0 fusion.bias_ref
  66.2 4.5 %collective-permute-done.5.rest_6_.rest_4_ = bf16[1216,256]{1,0:T(8,128)(2,1)} collective-permute-done((bf16[1216,256]{1,0:T(8,128)(2,1)}, bf16[1216,256]{1,0:T(8,128)(2,1)}, u32[]{:S(2)}, u32[]{:S(2)}) %collective-permute-start.5) | collective-permute-done | bytes 622624 | tf_op jit(solution)/shard_map/ppermute | solution.py:451
  70.8 9.4 %collective-permute-done.6.rest_7_.rest_5_ = bf16[1216,256]{1,0:T(8,128)(2,1)S(1)} collective-permute-done((bf16[1216,256]{1,0:T(8,128)(2,1)}, bf16[1216,256]{1,0:T(8,128)(2,1)S(1)}, u32[]{:S(2)}, u32[]{:S(2)}) %collective-permute-start.6) | collective-permute-done | bytes 622624 | tf_op jit(solution)/shard_map/ppermute | solution.py:451
  80.2 1.1 copy-done.6
  81.3 1.1 copy-done.8
  82.3 2.6 %shard_map.61.vert_ref = bf16[2,1024,256]{2,1,0:T(8,128)(2,1)S(1)} custom-call(s32[8,2,4]{2,1,0:T(2,128)S(1)} %broadcast_add_fusion.place_ref, s32[2,16]{1,0:T(2,128)S(1)} %compare_select_fusion.1.source_ref, bf16[512,256]{1,0:T(8,128)(2,1)} %get-tuple-element.13.rest_0_, bf16[1152,256]{1,0:T(8,128)(2,1)S(1)} %collective-permute-done.rest_1_.rest_0_, ...), custom_call_target="tpu_custom_call" | custom-call | bytes 2097152 | tf_op jit(solution)/shard_map/pallas_call | solution.py:162
  85.0 1.0 copy-done.1
  85.9 10.8 %shard_map.62.rest_6_.rest_2_ = bf16[512,512]{1,0:T(8,128)(2,1)} custom-call(s32[1]{0:T(128)} %bitcast.part_ref, s32[2,8]{1,0:T(2,128)} %copy-done.19, f32[64,1536]{1,0:T(8,128)} %fusion.bias_ref, bf16[2048,1024]{1,0:T(8,128)(2,1)} %query_ref.9, bf16[2,1024,256]{2,1,0:T(8,128)(2,1)} %copy-done.1, bf16[2048,256]{1,0:T(8,128)(2,1)} %copy-done, ...), custom_call_target="tpu_custom_call" | custom-call | flops 1610612736 | bytes 4194304 | tf_op jit(solution)/shard_map/pallas_call | solution.py:338
  96.8 1.0 copy-done.14
  97.8 0.3 shard_map.65
  98.1 1.4 collective-permute-start.11
  99.4 0.6 pad_add_fusion.1.part_ref
  100.0 0.7 pad_add_fusion.part_ref
  100.7 22.4 %shard_map.63 = (bf16[512,512]{1,0:T(8,128)(2,1)}, bf16[512,512]{1,0:T(8,128)(2,1)}, bf16[512,512]{1,0:T(8,128)(2,1)}) custom-call(s32[3]{0:T(128)} %pad_add_fusion.part_ref, s32[2,8]{1,0:T(2,128)} %copy-done.19, f32[64,1536]{1,0:T(8,128)} %fusion.bias_ref, bf16[2048,1024]{1,0:T(8,128)(2,1)} %query_ref.9, bf16[2,1024,256]{2,1,0:T(8,128)(2,1)} %copy-done.1, ...), custom_call_target="tpu_custom_call" | custom-call | flops 4831838208 | bytes 6291456 | tf_op jit(solution)/shard_map/pallas_call | solution.py:338
  123.1 1.7 collective-permute-start.8
  124.8 0.3 collective-permute-start.9
  125.0 0.5 broadcast_in_dim.14
  125.7 1.0 copy-done.16
  126.6 10.8 %shard_map.66.rest_2_ = bf16[512,512]{1,0:T(8,128)(2,1)} custom-call(s32[1]{0:T(128)} %bitcast.part_ref, s32[2,8]{1,0:T(2,128)} %copy-done.19, f32[64,1536]{1,0:T(8,128)} %fusion.bias_ref, bf16[2048,1024]{1,0:T(8,128)(2,1)} %query_ref.9, bf16[2,1024,256]{2,1,0:T(8,128)(2,1)} %copy-done.1, bf16[2048,256]{1,0:T(8,128)(2,1)} %copy-done.2, ...), custom_call_target="tpu_custom_call" | custom-call | flops 1610612736 | bytes 4194304 | tf_op jit(solution)/shard_map/pallas_call | solution.py:338
  137.4 1.3 collective-permute-start.12
  138.7 10.8 %shard_map.67.rest_2_ = bf16[512,512]{1,0:T(8,128)(2,1)} custom-call(s32[1]{0:T(128)} %bitcast.2.part_ref, s32[2,8]{1,0:T(2,128)} %copy-done.19, f32[64,1536]{1,0:T(8,128)} %fusion.bias_ref, bf16[2048,1024]{1,0:T(8,128)(2,1)} %query_ref.9, bf16[2,1024,256]{2,1,0:T(8,128)(2,1)} %copy-done.1, bf16[2048,256]{1,0:T(8,128)(2,1)} %copy-done.2, ...), custom_call_target="tpu_custom_call" | custom-call | flops 1610612736 | bytes 4194304 | tf_op jit(solution)/shard_map/pallas_call | solution.py:338
  149.4 0.8 collective-permute-start.13
  150.2 16.5 %shard_map.68 = (bf16[512,512]{1,0:T(8,128)(2,1)}, bf16[512,512]{1,0:T(8,128)(2,1)}) custom-call(s32[2]{0:T(128)} %pad_add_fusion.1.part_ref, s32[2,8]{1,0:T(2,128)} %copy-done.19, f32[64,1536]{1,0:T(8,128)} %fusion.bias_ref, bf16[2048,1024]{1,0:T(8,128)(2,1)} %query_ref.9, bf16[2,1024,256]{2,1,0:T(8,128)(2,1)} %copy-done.1, bf16[2048,256]{1,0:T(8,128)(2,1)} %copy-done.2, ...), custom_call_target="tpu_custom_call" | custom-call | flops 3221225472 | bytes 5242880 | tf_op jit(solution)/shard_map/pallas_call | solution.py:338
  167.3 1.7 collective-permute-done.14
  169.0 2.0 %copy-done.15 = bf16[512,4096]{1,0:T(8,128)(2,1)} copy-done((bf16[512,4096]{1,0:T(8,128)(2,1)}, bf16[512,4096]{1,0:T(8,128)(2,1)S(1)}, u32[]{:S(2)}) %copy-start.15) | copy-done | bytes 4194328
  171.0 0.8 constant_dynamic-update-slice_fusion
  (87 shorter events, 3.1 us)
Async XLA Ops:
  0.0 31.1 %copy-start.20 = (s32[2,16]{1,0:T(2,128)S(1)}, s32[2,16]{1,0:T(2,128)}, u32[]{:S(2)}) copy-start(s32[2,16]{1,0:T(2,128)} %param.8) | copy-start | bytes 388
  1.8 1.2 copy-start.9
  3.0 1.2 copy-start.11
  6.2 57.0 %copy-start = (bf16[2048,256]{1,0:T(8,128)(2,1)}, bf16[2048,256]{1,0:T(8,128)(2,1)S(1)}, u32[]{:S(2)}) copy-start(bf16[2048,256]{1,0:T(8,128)(2,1)S(1)} %get-tuple-element.15.rest_0_.own_ref) | copy-start | bytes 3145732
  6.3 17.5 %collective-permute-start = (bf16[1152,256]{1,0:T(8,128)(2,1)S(1)}, bf16[1152,256]{1,0:T(8,128)(2,1)S(1)}, u32[]{:S(2)}, u32[]{:S(2)}) collective-permute-start(bf16[1152,256]{1,0:T(8,128)(2,1)S(1)} %get-tuple-element.14), channel_id=1, source_target_pairs={{0,8},{4,12},{8,16},{12,20},{16,24},{20,28},{1,9},{5,13},{9,17},{1... | collective-permute-start | bytes 1769480 | tf_op jit(solution)/shard_map/ppermute | solution.py:444
  11.2 55.0 %collective-permute-start.4 = (bf16[512,256]{1,0:T(8,128)(2,1)}, bf16[512,256]{1,0:T(8,128)(2,1)}, u32[]{:S(2)}, u32[]{:S(2)}) collective-permute-start(bf16[512,256]{1,0:T(8,128)(2,1)} %get-tuple-element.13.rest_0_), channel_id=1, source_target_pairs={{0,4},{8,12},{16,20},{24,28},{1,5},{9,13},{17,21},{25,29},{2,6},{1... | collective-permute-start | bytes 786440 | tf_op jit(solution)/shard_map/ppermute | solution.py:447
  17.1 27.3 %copy-start.19 = (s32[2,8]{1,0:T(2,128)}, s32[2,8]{1,0:T(2,128)S(1)}, u32[]{:S(2)}) copy-start(s32[2,8]{1,0:T(2,128)S(1)} %select_reduce_fusion.1.slash_ref) | copy-start | bytes 196
  23.8 56.4 %copy-start.4 = (bf16[1152,256]{1,0:T(8,128)(2,1)}, bf16[1152,256]{1,0:T(8,128)(2,1)S(1)}, u32[]{:S(2)}) copy-start(bf16[1152,256]{1,0:T(8,128)(2,1)S(1)} %collective-permute-done.rest_1_.rest_0_) | copy-start | bytes 1769476
  24.8 19.3 %collective-permute-start.2 = (bf16[1152,256]{1,0:T(8,128)(2,1)}, bf16[1152,256]{1,0:T(8,128)(2,1)S(1)}, u32[]{:S(2)}, u32[]{:S(2)}) collective-permute-start(bf16[1152,256]{1,0:T(8,128)(2,1)} %shard_map.56.rest_2_), channel_id=1, source_target_pairs={{0,4},{4,0},{8,12},{12,8},{16,20},{20,16},{24,28},{28,24},{1,5},{5... | collective-permute-start | bytes 1769480 | tf_op jit(solution)/shard_map/ppermute | solution.py:451
  26.5 16.5 %collective-permute-start.1 = (bf16[1216,256]{1,0:T(8,128)(2,1)S(1)}, bf16[1216,256]{1,0:T(8,128)(2,1)S(1)}, u32[]{:S(2)}, u32[]{:S(2)}) collective-permute-start(bf16[1216,256]{1,0:T(8,128)(2,1)S(1)} %shard_map.57), channel_id=1, source_target_pairs={{0,8},{4,12},{8,16},{12,20},{16,24},{20,28},{1,9},{5,13},{9,17},{1... | collective-permute-start | bytes 1867784 | tf_op jit(solution)/shard_map/ppermute | solution.py:444
  31.9 16.9 %copy-start.10 = (bf16[2048,256]{1,0:T(8,128)(2,1)S(1)}, bf16[2048,256]{1,0:T(8,128)(2,1)}, u32[]{:S(2)}) copy-start(bf16[2048,256]{1,0:T(8,128)(2,1)} %keys_ref.3) | copy-start | bytes 3145732
  31.9 16.9 %copy-start.12 = (bf16[2048,256]{1,0:T(8,128)(2,1)S(1)}, bf16[2048,256]{1,0:T(8,128)(2,1)}, u32[]{:S(2)}) copy-start(bf16[2048,256]{1,0:T(8,128)(2,1)} %values_ref.3) | copy-start | bytes 3145732
  43.1 37.1 %copy-start.3 = (bf16[1216,256]{1,0:T(8,128)(2,1)}, bf16[1216,256]{1,0:T(8,128)(2,1)S(1)}, u32[]{:S(2)}) copy-start(bf16[1216,256]{1,0:T(8,128)(2,1)S(1)} %collective-permute-done.1.rest_1_.rest_2_.rest_0_) | copy-start | bytes 1867780
  44.1 4.7 %copy-start.7 = (bf16[1152,256]{1,0:T(8,128)(2,1)}, bf16[1152,256]{1,0:T(8,128)(2,1)S(1)}, u32[]{:S(2)}) copy-start(bf16[1152,256]{1,0:T(8,128)(2,1)S(1)} %collective-permute-done.2.rest_3_.rest_5_) | copy-start | bytes 1769476
  44.3 18.9 %collective-permute-start.3 = (bf16[1216,256]{1,0:T(8,128)(2,1)S(1)}, bf16[1216,256]{1,0:T(8,128)(2,1)S(1)}, u32[]{:S(2)}, u32[]{:S(2)}) collective-permute-start(bf16[1216,256]{1,0:T(8,128)(2,1)S(1)} %shard_map.59.rest_1_), channel_id=1, source_target_pairs={{0,8},{4,12},{8,16},{12,20},{16,24},{20,28},{1,9},{5,13},{9,17},{1... | collective-permute-start | bytes 1867784 | tf_op jit(solution)/shard_map/ppermute | solution.py:444
  49.0 47.7 %copy-start.2 = (bf16[2048,256]{1,0:T(8,128)(2,1)}, bf16[2048,256]{1,0:T(8,128)(2,1)S(1)}, u32[]{:S(2)}) copy-start(bf16[2048,256]{1,0:T(8,128)(2,1)S(1)} %shard_map.64.rest_0_.own_ref) | copy-start | bytes 3145732
  49.1 47.7 %collective-permute-start.10 = (bf16[2048,256]{1,0:T(8,128)(2,1)S(1)}, bf16[2048,256]{1,0:T(8,128)(2,1)}, u32[]{:S(2)}, u32[]{:S(2)}) collective-permute-start(bf16[2048,256]{1,0:T(8,128)(2,1)S(1)} %shard_map.64.rest_0_.own_ref), channel_id=1, source_target_pairs={{0,8},{4,12},{8,16},{12,20},{16,24},{20,28},{1,9},{5,13},{9,17},{1... | collective-permute-start | bytes 3145736 | tf_op jit(solution)/shard_map/ppermute | solution.py:458
  53.5 17.3 %collective-permute-start.5 = (bf16[1216,256]{1,0:T(8,128)(2,1)}, bf16[1216,256]{1,0:T(8,128)(2,1)}, u32[]{:S(2)}, u32[]{:S(2)}) collective-permute-start(bf16[1216,256]{1,0:T(8,128)(2,1)} %shard_map.58.rest_2_), channel_id=1, source_target_pairs={{0,4},{4,0},{8,12},{12,8},{16,20},{20,16},{24,28},{28,24},{1,5},{5... | collective-permute-start | bytes 1867784 | tf_op jit(solution)/shard_map/ppermute | solution.py:451
  63.2 1.1 copy-start.5
  64.3 15.9 %collective-permute-start.6 = (bf16[1216,256]{1,0:T(8,128)(2,1)}, bf16[1216,256]{1,0:T(8,128)(2,1)S(1)}, u32[]{:S(2)}, u32[]{:S(2)}) collective-permute-start(bf16[1216,256]{1,0:T(8,128)(2,1)} %shard_map.60), channel_id=1, source_target_pairs={{0,4},{4,0},{8,12},{12,8},{16,20},{20,16},{24,28},{28,24},{1,5},{5... | collective-permute-start | bytes 1867784 | tf_op jit(solution)/shard_map/ppermute | solution.py:451
  80.2 1.1 copy-start.6
  81.3 1.1 copy-start.8
  82.3 3.6 %copy-start.13 = (bf16[1216,256]{1,0:T(8,128)(2,1)}, bf16[1216,256]{1,0:T(8,128)(2,1)S(1)}, u32[]{:S(2)}) copy-start(bf16[1216,256]{1,0:T(8,128)(2,1)S(1)} %collective-permute-done.6.rest_7_.rest_5_) | copy-start | bytes 1867780
  84.9 1.0 copy-start.1
  96.7 1.0 copy-start.14
  98.1 27.6 %collective-permute-start.11 = (bf16[2048,256]{1,0:T(8,128)(2,1)S(1)}, bf16[2048,256]{1,0:T(8,128)(2,1)S(1)}, u32[]{:S(2)}, u32[]{:S(2)}) collective-permute-start(bf16[2048,256]{1,0:T(8,128)(2,1)S(1)} %shard_map.65), channel_id=1, source_target_pairs={{0,4},{4,0},{8,12},{12,8},{16,20},{20,16},{24,28},{28,24},{1,5},{5... | collective-permute-start | bytes 3145736 | tf_op jit(solution)/shard_map/ppermute | solution.py:481
  100.0 25.0 %collective-permute-start.7 = (bf16[512,512]{1,0:T(8,128)(2,1)}, bf16[512,512]{1,0:T(8,128)(2,1)S(1)}, u32[]{:S(2)}, u32[]{:S(2)}) collective-permute-start(bf16[512,512]{1,0:T(8,128)(2,1)} %shard_map.62.rest_6_.rest_2_), channel_id=1, source_target_pairs={{0,3},{1,2},{2,1},{3,0},{4,7},{5,6},{6,5},{7,4},{8,11},{9,10},{10,... | collective-permute-start | bytes 1572872 | tf_op jit(solution)/shard_map/ppermute | solution.py:485
  123.1 43.7 %collective-permute-start.8 = (bf16[512,512]{1,0:T(8,128)(2,1)}, bf16[512,512]{1,0:T(8,128)(2,1)S(1)}, u32[]{:S(2)}, u32[]{:S(2)}) collective-permute-start(bf16[512,512]{1,0:T(8,128)(2,1)} %get-tuple-element.16), channel_id=1, source_target_pairs={{0,2},{1,3},{2,0},{3,1},{4,6},{5,7},{6,4},{7,5},{8,10},{9,11},{10,... | collective-permute-start | bytes 1572872 | tf_op jit(solution)/shard_map/ppermute | solution.py:485
  124.8 42.1 %collective-permute-start.9 = (bf16[512,512]{1,0:T(8,128)(2,1)}, bf16[512,512]{1,0:T(8,128)(2,1)S(1)}, u32[]{:S(2)}, u32[]{:S(2)}) collective-permute-start(bf16[512,512]{1,0:T(8,128)(2,1)} %get-tuple-element.17), channel_id=1, source_target_pairs={{0,1},{1,0},{2,3},{3,2},{4,5},{5,4},{6,7},{7,6},{8,9},{9,8},{10,11... | collective-permute-start | bytes 1572872 | tf_op jit(solution)/shard_map/ppermute | solution.py:485
  125.6 1.0 copy-start.16
  137.4 29.7 %collective-permute-start.12 = (bf16[512,512]{1,0:T(8,128)(2,1)}, bf16[512,512]{1,0:T(8,128)(2,1)S(1)}, u32[]{:S(2)}, u32[]{:S(2)}) collective-permute-start(bf16[512,512]{1,0:T(8,128)(2,1)} %shard_map.66.rest_2_), channel_id=1, source_target_pairs={{0,3},{1,2},{2,1},{3,0},{4,7},{5,6},{6,5},{7,4},{8,11},{9,10},{10,... | collective-permute-start | bytes 1572872 | tf_op jit(solution)/shard_map/ppermute | solution.py:485
  149.4 17.6 %copy-start.17 = (bf16[512,512]{1,0:T(8,128)(2,1)S(1)}, bf16[512,512]{1,0:T(8,128)(2,1)}, u32[]{:S(2)}) copy-start(bf16[512,512]{1,0:T(8,128)(2,1)} %get-tuple-element.18.rest_2_) | copy-start | bytes 1572868
  149.4 17.7 %collective-permute-start.13 = (bf16[512,512]{1,0:T(8,128)(2,1)}, bf16[512,512]{1,0:T(8,128)(2,1)S(1)}, u32[]{:S(2)}, u32[]{:S(2)}) collective-permute-start(bf16[512,512]{1,0:T(8,128)(2,1)} %shard_map.67.rest_2_), channel_id=1, source_target_pairs={{0,2},{1,3},{2,0},{3,1},{4,6},{5,7},{6,4},{7,5},{8,10},{9,11},{10,... | collective-permute-start | bytes 1572872 | tf_op jit(solution)/shard_map/ppermute | solution.py:485
  166.7 4.3 %copy-start.18 = (bf16[512,512]{1,0:T(8,128)(2,1)S(1)}, bf16[512,512]{1,0:T(8,128)(2,1)}, u32[]{:S(2)}) copy-start(bf16[512,512]{1,0:T(8,128)(2,1)} %get-tuple-element.20) | copy-start | bytes 1572868
  166.8 2.2 %collective-permute-start.14 = (bf16[512,512]{1,0:T(8,128)(2,1)}, bf16[512,512]{1,0:T(8,128)(2,1)S(1)}, u32[]{:S(2)}, u32[]{:S(2)}) collective-permute-start(bf16[512,512]{1,0:T(8,128)(2,1)} %get-tuple-element.19), channel_id=1, source_target_pairs={{0,1},{1,0},{2,3},{3,2},{4,5},{5,4},{6,7},{7,6},{8,9},{9,8},{10,11... | collective-permute-start | bytes 1572872 | tf_op jit(solution)/shard_map/ppermute | solution.py:485
  169.0 2.0 %copy-start.15 = (bf16[512,4096]{1,0:T(8,128)(2,1)}, bf16[512,4096]{1,0:T(8,128)(2,1)S(1)}, u32[]{:S(2)}) copy-start(bf16[512,4096]{1,0:T(8,128)(2,1)S(1)} %constant_dynamic-update-slice_fusion.1) | copy-start | bytes 12582916

commit v9 on v8

--- a/solution.py
+++ b/solution.py
@@ -365,7 +365,7 @@
             ],
         ),
         compiler_params=pltpu.CompilerParams(
-            dimension_semantics=("arbitrary",), vmem_limit_bytes=56 << 20
+            dimension_semantics=("arbitrary",), vmem_limit_bytes=18 << 20
         ),
         cost_estimate=pl.CostEstimate(
             flops=4 * parts * part_rows * group_heads * keys_seen * HD,
@@ -386,7 +386,7 @@
     blocks_dev = tok_rows // BLK
     part_rows = tok_rows // head_count
     partner = shard_index ^ 1
-    two_pairs = [(i, i + 2) for i in range(shard_count - 2)]
+    two_pairs = [(i, (i + 2) % shard_count) for i in range(shard_count)]
     across_pairs = [(i, i ^ 1) for i in range(shard_count)]
     parity = (shard_index % 2).reshape(1).astype(jnp.int32)
 
@@ -443,8 +443,7 @@
             )
         come = lax.ppermute(send, "ctx", two_pairs)
         if step == 0:
-            pairs = [(i, i + 1) for i in range(0, shard_count, 2)]
-            across.append((lax.ppermute(slots_own, "ctx", pairs), 0))
+            across.append((lax.ppermute(slots_own, "ctx", across_pairs), 0))
         two_back.append(come)
         behind.append((come, rows))
         cross = joined(parity, [(rows, here, (come, 0)), (slot_rows, behind[-1], behind[-1])])

time: 173 us -> 171 us (0.988)
  local copies, waits for them, and re-layouts: 12.4 us -> 29.8 us
  starting transfers between devices: 30.4 us -> 15 us
  Pallas kernels: 79.9 us -> 67.9 us
  waiting for transfers between devices: 41.6 us -> 51.1 us
    unnamed x44 -> x64, local copies, waits for them, and re-layouts: 9.79 us -> 27.2 us
    ppermute x3, waiting for transfers between devices: 25.9 us -> 41.3 us  [local(): come = lax.ppermute(send, 'ctx', two_pairs)]
    pallas_call x5, Pallas kernels: 71.3 us -> 58.5 us  [attend(): pl.pallas_call(functools.partial(attend_kernel, head, parts, bounds, len(...]
    ppermute x3, starting transfers between devices: 13.8 us -> 3.19 us  [local(): come = lax.ppermute(send, 'ctx', two_pairs)]
    ppermute x3, waiting for transfers between devices: 13.9 us -> 8.25 us  [local(): one_back.append(lax.ppermute(cross, 'ctx', across_pairs))]
    ppermute x1, starting transfers between devices: 4.42 us -> 0.06 us  [local(): come = lax.ppermute(own, 'ctx', two_pairs)]
    ppermute x1, starting transfers between devices: 4.09 us -> 1.49 us  [local(): across.append((lax.ppermute(slots_own, 'ctx', across_pairs), 0))]
  transfers between devices with their start and end apart: 15 -> 15, of which waited for: 6 -> 6; matrix products, arithmetic and copies ran while one was open for 4% -> 3% of each run, Pallas kernels for 45% -> 38%
where the time goes in v9:
time: 171 us; the launch traced here: 170 us
  Pallas kernels  67.9 us (40%)
  waiting for transfers between devices  51.1 us (30%)
  local copies, waits for them, and re-layouts  29.8 us (17%)
  starting transfers between devices  15 us (9%)
  other arithmetic  4.96 us (3%)
    pallas_call x5, Pallas kernels, attend(): pl.pallas_call(functools.partial(attend_kernel, head, parts, bounds, len(...  58.5 us
    ppermute x3, waiting for transfers between devices, local(): come = lax.ppermute(send, 'ctx', two_pairs)  41.3 us
    unnamed x64, local copies, waits for them, and re-layouts  27.2 us
    ppermute x3, waiting for transfers between devices, local(): one_back.append(lax.ppermute(cross, 'ctx', across_pairs))  8.25 us
    ppermute x6, starting transfers between devices, local(): lax.ppermute(piece, 'head', [(i, i ^ flip) for i in range(head_count)])  5.02 us
    pallas_call x6, Pallas kernels, joined(): pl.pallas_call(functools.partial(joined_kernel, plan), out_shape=jax.Shap...  4.68 us
  transfers between devices with their start and end apart: 15, of which 6 were waited for; matrix products, arithmetic and copies ran while one was open for 3% of the time, Pallas kernels for 38%

profile of v9, /device:TPU:0, one launch (start us, length us, event | category | flops | bytes accessed | tf_op | source)
XLA Modules:
  0.0 169.5 jit_solution(10418815125358799434)
XLA Ops:
  1.8 1.2 copy-done.19
  3.0 1.2 copy-done.21
  4.2 2.0 %shard_map.55 = (bf16[2048,256]{1,0:T(8,128)(2,1)S(1)}, bf16[1152,256]{1,0:T(8,128)(2,1)S(1)}, bf16[512,256]{1,0:T(8,128)(2,1)}) custom-call(s32[2,4]{1,0:T(2,128)S(1)} %select_reduce_fusion.2.local_ref, bf16[2048,256]{1,0:T(8,128)(2,1)S(1)} %copy-done.19, bf16[2048,256]{1,0:T(8,128)(2,1)S(1)} %copy-done.21), custom_call_target="tpu_custom_call" | custom-call | bytes 4194304 | tf_op jit(solution)/shard_map/pallas_call | solution.py:58
  6.2 3.1 %collective-permute-start = (bf16[1152,256]{1,0:T(8,128)(2,1)S(1)}, bf16[1152,256]{1,0:T(8,128)(2,1)S(1)}, u32[]{:S(2)}, u32[]{:S(2)}) collective-permute-start(bf16[1152,256]{1,0:T(8,128)(2,1)S(1)} %get-tuple-element.14), channel_id=1, source_target_pairs={{0,8},{4,12},{8,16},{12,20},{16,24},{20,28},{24,0},{28,4},{1,9},{5... | collective-permute-start | bytes 1769480 | tf_op jit(solution)/shard_map/ppermute | solution.py:444
  9.3 1.5 collective-permute-start.4
  10.8 1.0 convert_reduce_fusion.1
  13.4 11.2 %collective-permute-done.rest_1_.rest_0_ = bf16[1152,256]{1,0:T(8,128)(2,1)S(1)} collective-permute-done((bf16[1152,256]{1,0:T(8,128)(2,1)S(1)}, bf16[1152,256]{1,0:T(8,128)(2,1)S(1)}, u32[]{:S(2)}, u32[]{:S(2)}) %collective-permute-start) | collective-permute-done | bytes 589856 | tf_op jit(solution)/shard_map/ppermute | solution.py:444
  24.8 1.5 collective-permute-start.2
  26.4 1.0 shard_map.57
  28.6 15.6 %collective-permute-done.1.rest_1_.rest_2_.rest_0_ = bf16[1216,256]{1,0:T(8,128)(2,1)S(1)} collective-permute-done((bf16[1216,256]{1,0:T(8,128)(2,1)}, bf16[1216,256]{1,0:T(8,128)(2,1)S(1)}, u32[]{:S(2)}, u32[]{:S(2)}) %collective-permute-start.1) | collective-permute-done | bytes 622624 | tf_op jit(solution)/shard_map/ppermute | solution.py:444
  44.1 1.0 shard_map.58.rest_2_
  46.0 1.2 copy-done.20
  47.3 1.2 copy-done.22
  48.8 0.9 collective-permute-start.5
  49.7 14.5 %collective-permute-done.3.rest_1_.rest_3_.rest_2_ = bf16[1216,256]{1,0:T(8,128)(2,1)S(1)} collective-permute-done((bf16[1216,256]{1,0:T(8,128)(2,1)S(1)}, bf16[1216,256]{1,0:T(8,128)(2,1)S(1)}, u32[]{:S(2)}, u32[]{:S(2)}) %collective-permute-start.3) | collective-permute-done | bytes 622624 | tf_op jit(solution)/shard_map/ppermute | solution.py:444
  64.2 1.0 shard_map.60
  66.1 0.9 collective-permute-start.6
  67.6 0.8 copy-done.23
  68.4 8.2 %collective-permute-done.6.rest_7_.rest_5_ = bf16[1216,256]{1,0:T(8,128)(2,1)} collective-permute-done((bf16[1216,256]{1,0:T(8,128)(2,1)}, bf16[1216,256]{1,0:T(8,128)(2,1)}, u32[]{:S(2)}, u32[]{:S(2)}) %collective-permute-start.6) | collective-permute-done | bytes 622624 | tf_op jit(solution)/shard_map/ppermute | solution.py:450
  76.7 1.1 copy-done.4
  77.7 1.1 copy-done.8
  78.8 1.1 copy-done.12
  79.9 1.1 copy-done.16
  80.9 1.1 copy-done.24
  82.0 2.6 %shard_map.61.vert_ref = bf16[2,1024,256]{2,1,0:T(8,128)(2,1)S(1)} custom-call(s32[8,2,4]{2,1,0:T(2,128)S(1)} %broadcast_add_fusion.place_ref, s32[2,16]{1,0:T(2,128)S(1)} %compare_select_fusion.1.source_ref, bf16[512,256]{1,0:T(8,128)(2,1)} %get-tuple-element.13.rest_0_, bf16[1152,256]{1,0:T(8,128)(2,1)S(1)} %copy-done.8, bf16[1216,256]{1,0:T(8,128)(2,1)S(1)} %copy-done.4, ...), custom_call_target="tpu_custom_call" | custom-call | bytes 2097152 | tf_op jit(solution)/shard_map/pallas_call | solution.py:162
  84.7 1.1 copy-done.9
  85.7 1.1 copy-done.17
  86.8 1.1 copy-done.25
  87.8 8.4 %shard_map.62.rest_6_.rest_2_ = bf16[512,512]{1,0:T(8,128)(2,1)S(1)} custom-call(s32[1]{0:T(128)} %bitcast.part_ref, s32[2,8]{1,0:T(2,128)S(1)} %select_reduce_fusion.1.slash_ref, f32[64,1536]{1,0:T(8,128)S(1)} %fusion.bias_ref, bf16[2048,1024]{1,0:T(8,128)(2,1)S(1)} %copy-done, bf16[2,1024,256]{2,1,0:T(8,128)(2,1)S(1)} %shard_map.61.vert_ref, ...), custom_call_target="tpu_custom_call" | custom-call | flops 1610612736 | bytes 4194304 | tf_op jit(solution)/shard_map/pallas_call | solution.py:338
  96.3 1.2 shard_map.65
  98.4 1.9 %collective-permute-start.11 = (bf16[2048,256]{1,0:T(8,128)(2,1)}, bf16[2048,256]{1,0:T(8,128)(2,1)}, u32[]{:S(2)}, u32[]{:S(2)}) collective-permute-start(bf16[2048,256]{1,0:T(8,128)(2,1)} %shard_map.65), channel_id=1, source_target_pairs={{0,4},{4,0},{8,12},{12,8},{16,20},{20,16},{24,28},{28,24},{1,5},{5... | collective-permute-start | bytes 3145736 | tf_op jit(solution)/shard_map/ppermute | solution.py:480
  100.4 2.2 %copy-done.1 = bf16[2048,1024]{1,0:T(8,128)(2,1)S(1)} copy-done((bf16[2048,1024]{1,0:T(8,128)(2,1)S(1)}, bf16[2048,1024]{1,0:T(8,128)(2,1)}, u32[]{:S(2)}) %copy-start.1) | copy-done | bytes 4194328
  102.6 1.1 copy-done.6
  103.7 1.1 copy-done.10
  104.8 1.1 copy-done.14
  105.8 1.1 copy-done.18
  106.9 1.1 copy-done.26
  108.0 1.0 copy-done.28
  109.0 19.6 %shard_map.63 = (bf16[512,512]{1,0:T(8,128)(2,1)S(1)}, bf16[512,512]{1,0:T(8,128)(2,1)S(1)}, bf16[512,512]{1,0:T(8,128)(2,1)S(1)}) custom-call(s32[3]{0:T(128)S(1)} %pad_add_fusion.part_ref, s32[2,8]{1,0:T(2,128)S(1)} %select_reduce_fusion.1.slash_ref, f32[64,1536]{1,0:T(8,128)S(1)} %fusion.bias_ref, bf16[2048,1024]{1,0:T(8,128)(2,1)S(1)} %copy-done.1, ...), custom_call_target="tpu_custom_call" | custom-call | flops 4831838208 | bytes 6291456 | tf_op jit(solution)/shard_map/pallas_call | solution.py:338
  128.6 1.6 collective-permute-start.8
  131.2 8.3 %shard_map.66.rest_2_ = bf16[512,512]{1,0:T(8,128)(2,1)S(1)} custom-call(s32[1]{0:T(128)} %bitcast.part_ref, s32[2,8]{1,0:T(2,128)S(1)} %select_reduce_fusion.1.slash_ref, f32[64,1536]{1,0:T(8,128)S(1)} %fusion.bias_ref, bf16[2048,1024]{1,0:T(8,128)(2,1)S(1)} %copy-done.2, bf16[2,1024,256]{2,1,0:T(8,128)(2,1)S(1)} %shard_map.61.vert_ref, ...), custom_call_target="tpu_custom_call" | custom-call | flops 1610612736 | bytes 4194304 | tf_op jit(solution)/shard_map/pallas_call | solution.py:338
  139.5 1.5 collective-permute-start.12
  140.9 8.3 %shard_map.67.rest_2_ = bf16[512,512]{1,0:T(8,128)(2,1)S(1)} custom-call(s32[1]{0:T(128)} %bitcast.2.part_ref, s32[2,8]{1,0:T(2,128)S(1)} %select_reduce_fusion.1.slash_ref, f32[64,1536]{1,0:T(8,128)S(1)} %fusion.bias_ref, bf16[2048,1024]{1,0:T(8,128)(2,1)S(1)} %copy-done.2, bf16[2,1024,256]{2,1,0:T(8,128)(2,1)S(1)} %shard_map.61.vert_ref, ...), custom_call_target="tpu_custom_call" | custom-call | flops 1610612736 | bytes 4194304 | tf_op jit(solution)/shard_map/pallas_call | solution.py:338
  149.3 1.6 collective-permute-start.13
  150.8 13.8 %shard_map.68 = (bf16[512,512]{1,0:T(8,128)(2,1)S(1)}, bf16[512,512]{1,0:T(8,128)(2,1)S(1)}) custom-call(s32[2]{0:T(128)S(1)} %pad_add_fusion.1.part_ref, s32[2,8]{1,0:T(2,128)S(1)} %select_reduce_fusion.1.slash_ref, f32[64,1536]{1,0:T(8,128)S(1)} %fusion.bias_ref, bf16[2048,1024]{1,0:T(8,128)(2,1)S(1)} %copy-done.2, ...), custom_call_target="tpu_custom_call" | custom-call | flops 3221225472 | bytes 5242880 | tf_op jit(solution)/shard_map/pallas_call | solution.py:338
  165.1 0.9 collective-permute-done.13
  166.7 2.0 %copy-done.29 = bf16[512,4096]{1,0:T(8,128)(2,1)} copy-done((bf16[512,4096]{1,0:T(8,128)(2,1)}, bf16[512,4096]{1,0:T(8,128)(2,1)S(1)}, u32[]{:S(2)}) %copy-start.29) | copy-done | bytes 4194328
  168.7 0.8 constant_dynamic-update-slice_fusion
  (107 shorter events, 10.2 us)
Async XLA Ops:
  0.0 27.6 %copy-start.30 = (s32[2,16]{1,0:T(2,128)S(1)}, s32[2,16]{1,0:T(2,128)}, u32[]{:S(2)}) copy-start(s32[2,16]{1,0:T(2,128)} %param.8) | copy-start | bytes 388
  1.8 1.2 copy-start.19
  3.0 1.2 copy-start.21
  6.2 18.4 %collective-permute-start = (bf16[1152,256]{1,0:T(8,128)(2,1)S(1)}, bf16[1152,256]{1,0:T(8,128)(2,1)S(1)}, u32[]{:S(2)}, u32[]{:S(2)}) collective-permute-start(bf16[1152,256]{1,0:T(8,128)(2,1)S(1)} %get-tuple-element.14), channel_id=1, source_target_pairs={{0,8},{4,12},{8,16},{12,20},{16,24},{20,28},{24,0},{28,4},{1,9},{5... | collective-permute-start | bytes 1769480 | tf_op jit(solution)/shard_map/ppermute | solution.py:444
  9.3 58.3 %collective-permute-start.4 = (bf16[512,256]{1,0:T(8,128)(2,1)}, bf16[512,256]{1,0:T(8,128)(2,1)}, u32[]{:S(2)}, u32[]{:S(2)}) collective-permute-start(bf16[512,256]{1,0:T(8,128)(2,1)} %get-tuple-element.13.rest_0_), channel_id=1, source_target_pairs={{0,4},{4,0},{8,12},{12,8},{16,20},{20,16},{24,28},{28,24},{1,5},{5... | collective-permute-start | bytes 786440 | tf_op jit(solution)/shard_map/ppermute | solution.py:446
  24.7 1.7 %copy-start.7 = (bf16[1152,256]{1,0:T(8,128)(2,1)}, bf16[1152,256]{1,0:T(8,128)(2,1)S(1)}, u32[]{:S(2)}) copy-start(bf16[1152,256]{1,0:T(8,128)(2,1)S(1)} %collective-permute-done.rest_1_.rest_0_) | copy-start | bytes 1769476
  24.8 20.4 %collective-permute-start.2 = (bf16[1152,256]{1,0:T(8,128)(2,1)S(1)}, bf16[1152,256]{1,0:T(8,128)(2,1)S(1)}, u32[]{:S(2)}, u32[]{:S(2)}) collective-permute-start(bf16[1152,256]{1,0:T(8,128)(2,1)S(1)} %shard_map.56.rest_2_), channel_id=1, source_target_pairs={{0,4},{4,0},{8,12},{12,8},{16,20},{20,16},{24,28},{28,24},{1,5},{5... | collective-permute-start | bytes 1769480 | tf_op jit(solution)/shard_map/ppermute | solution.py:450
  27.4 16.8 %collective-permute-start.1 = (bf16[1216,256]{1,0:T(8,128)(2,1)}, bf16[1216,256]{1,0:T(8,128)(2,1)S(1)}, u32[]{:S(2)}, u32[]{:S(2)}) collective-permute-start(bf16[1216,256]{1,0:T(8,128)(2,1)} %shard_map.57), channel_id=1, source_target_pairs={{0,8},{4,12},{8,16},{12,20},{16,24},{20,28},{24,0},{28,4},{1,9},{5... | collective-permute-start | bytes 1867784 | tf_op jit(solution)/shard_map/ppermute | solution.py:444
  44.1 4.5 %copy-start.3 = (bf16[1216,256]{1,0:T(8,128)(2,1)}, bf16[1216,256]{1,0:T(8,128)(2,1)S(1)}, u32[]{:S(2)}) copy-start(bf16[1216,256]{1,0:T(8,128)(2,1)S(1)} %collective-permute-done.1.rest_1_.rest_2_.rest_0_) | copy-start | bytes 1867780
  45.2 0.8 copy-start.15
  45.4 18.8 %collective-permute-start.3 = (bf16[1216,256]{1,0:T(8,128)(2,1)S(1)}, bf16[1216,256]{1,0:T(8,128)(2,1)S(1)}, u32[]{:S(2)}, u32[]{:S(2)}) collective-permute-start(bf16[1216,256]{1,0:T(8,128)(2,1)S(1)} %shard_map.59.rest_1_), channel_id=1, source_target_pairs={{0,8},{4,12},{8,16},{12,20},{16,24},{20,28},{24,0},{28,4},{1,9},{5... | collective-permute-start | bytes 1867784 | tf_op jit(solution)/shard_map/ppermute | solution.py:444
  46.0 1.2 copy-start.20
  47.3 1.2 copy-start.22
  48.7 47.6 %collective-permute-start.10 = (bf16[2048,256]{1,0:T(8,128)(2,1)S(1)}, bf16[2048,256]{1,0:T(8,128)(2,1)}, u32[]{:S(2)}, u32[]{:S(2)}) collective-permute-start(bf16[2048,256]{1,0:T(8,128)(2,1)S(1)} %shard_map.64.rest_0_.own_ref), channel_id=1, source_target_pairs={{0,8},{4,12},{8,16},{12,20},{16,24},{20,28},{24,0},{28,4},{1,9},{5... | collective-permute-start | bytes 3145736 | tf_op jit(solution)/shard_map/ppermute | solution.py:457
  48.8 18.8 %collective-permute-start.5 = (bf16[1216,256]{1,0:T(8,128)(2,1)}, bf16[1216,256]{1,0:T(8,128)(2,1)S(1)}, u32[]{:S(2)}, u32[]{:S(2)}) collective-permute-start(bf16[1216,256]{1,0:T(8,128)(2,1)} %shard_map.58.rest_2_), channel_id=1, source_target_pairs={{0,4},{4,0},{8,12},{12,8},{16,20},{20,16},{24,28},{28,24},{1,5},{5... | collective-permute-start | bytes 1867784 | tf_op jit(solution)/shard_map/ppermute | solution.py:450
  65.3 0.8 copy-start.11
  66.1 10.6 %collective-permute-start.6 = (bf16[1216,256]{1,0:T(8,128)(2,1)}, bf16[1216,256]{1,0:T(8,128)(2,1)}, u32[]{:S(2)}, u32[]{:S(2)}) collective-permute-start(bf16[1216,256]{1,0:T(8,128)(2,1)} %shard_map.60), channel_id=1, source_target_pairs={{0,4},{4,0},{8,12},{12,8},{16,20},{20,16},{24,28},{28,24},{1,5},{5... | collective-permute-start | bytes 1867784 | tf_op jit(solution)/shard_map/ppermute | solution.py:450
  67.3 17.3 %copy-start = (bf16[2048,1024]{1,0:T(8,128)(2,1)S(1)}, bf16[2048,1024]{1,0:T(8,128)(2,1)}, u32[]{:S(2)}) copy-start(bf16[2048,1024]{1,0:T(8,128)(2,1)} %query_ref.9) | copy-start | bytes 12582916
  67.6 0.8 copy-start.23
  76.7 1.1 copy-start.4
  77.7 1.1 copy-start.8
  78.8 1.1 copy-start.12
  79.9 1.1 copy-start.16
  80.9 1.1 copy-start.24
  82.0 2.6 %copy-start.5 = (bf16[1216,256]{1,0:T(8,128)(2,1)S(1)}, bf16[1216,256]{1,0:T(8,128)(2,1)}, u32[]{:S(2)}) copy-start(bf16[1216,256]{1,0:T(8,128)(2,1)} %copy-done.3) | copy-start | bytes 1867780
  82.0 2.6 %copy-start.13 = (bf16[1216,256]{1,0:T(8,128)(2,1)S(1)}, bf16[1216,256]{1,0:T(8,128)(2,1)}, u32[]{:S(2)}) copy-start(bf16[1216,256]{1,0:T(8,128)(2,1)} %copy-done.11) | copy-start | bytes 1867780
  84.6 1.1 copy-start.9
  85.7 1.1 copy-start.17
  86.8 1.1 copy-start.25
  97.6 0.8 copy-start.27
  98.4 32.8 %collective-permute-start.11 = (bf16[2048,256]{1,0:T(8,128)(2,1)}, bf16[2048,256]{1,0:T(8,128)(2,1)}, u32[]{:S(2)}, u32[]{:S(2)}) collective-permute-start(bf16[2048,256]{1,0:T(8,128)(2,1)} %shard_map.65), channel_id=1, source_target_pairs={{0,4},{4,0},{8,12},{12,8},{16,20},{20,16},{24,28},{28,24},{1,5},{5... | collective-permute-start | bytes 3145736 | tf_op jit(solution)/shard_map/ppermute | solution.py:480
  100.4 30.2 %collective-permute-start.7 = (bf16[512,512]{1,0:T(8,128)(2,1)}, bf16[512,512]{1,0:T(8,128)(2,1)S(1)}, u32[]{:S(2)}, u32[]{:S(2)}) collective-permute-start(bf16[512,512]{1,0:T(8,128)(2,1)} %copy-done.27), channel_id=1, source_target_pairs={{0,3},{1,2},{2,1},{3,0},{4,7},{5,6},{6,5},{7,4},{8,11},{9,10},{10,... | collective-permute-start | bytes 1572872 | tf_op jit(solution)/shard_map/ppermute | solution.py:484
  100.4 2.2 %copy-start.1 = (bf16[2048,1024]{1,0:T(8,128)(2,1)S(1)}, bf16[2048,1024]{1,0:T(8,128)(2,1)}, u32[]{:S(2)}) copy-start(bf16[2048,1024]{1,0:T(8,128)(2,1)} %query_ref.9) | copy-start | bytes 12582916
  102.6 1.1 copy-start.6
  103.7 1.1 copy-start.10
  104.8 1.1 copy-start.14
  105.8 1.1 copy-start.18
  106.9 1.1 copy-start.26
  108.0 1.0 copy-start.28
  128.6 2.5 %copy-start.2 = (bf16[2048,1024]{1,0:T(8,128)(2,1)S(1)}, bf16[2048,1024]{1,0:T(8,128)(2,1)}, u32[]{:S(2)}) copy-start(bf16[2048,1024]{1,0:T(8,128)(2,1)} %query_ref.9) | copy-start | bytes 12582916
  128.6 36.1 %collective-permute-start.8 = (bf16[512,512]{1,0:T(8,128)(2,1)S(1)}, bf16[512,512]{1,0:T(8,128)(2,1)S(1)}, u32[]{:S(2)}, u32[]{:S(2)}) collective-permute-start(bf16[512,512]{1,0:T(8,128)(2,1)S(1)} %get-tuple-element.16), channel_id=1, source_target_pairs={{0,2},{1,3},{2,0},{3,1},{4,6},{5,7},{6,4},{7,5},{8,10},{9,11},{10,... | collective-permute-start | bytes 1572872 | tf_op jit(solution)/shard_map/ppermute | solution.py:484
  130.2 34.6 %collective-permute-start.9 = (bf16[512,512]{1,0:T(8,128)(2,1)S(1)}, bf16[512,512]{1,0:T(8,128)(2,1)S(1)}, u32[]{:S(2)}, u32[]{:S(2)}) collective-permute-start(bf16[512,512]{1,0:T(8,128)(2,1)S(1)} %get-tuple-element.17), channel_id=1, source_target_pairs={{0,1},{1,0},{2,3},{3,2},{4,5},{5,4},{6,7},{7,6},{8,9},{9,8},{10,11... | collective-permute-start | bytes 1572872 | tf_op jit(solution)/shard_map/ppermute | solution.py:484
  139.5 25.5 %collective-permute-start.12 = (bf16[512,512]{1,0:T(8,128)(2,1)S(1)}, bf16[512,512]{1,0:T(8,128)(2,1)S(1)}, u32[]{:S(2)}, u32[]{:S(2)}) collective-permute-start(bf16[512,512]{1,0:T(8,128)(2,1)S(1)} %shard_map.66.rest_2_), channel_id=1, source_target_pairs={{0,3},{1,2},{2,1},{3,0},{4,7},{5,6},{6,5},{7,4},{8,11},{9,10},{10,... | collective-permute-start | bytes 1572872 | tf_op jit(solution)/shard_map/ppermute | solution.py:484
  149.3 16.7 %collective-permute-start.13 = (bf16[512,512]{1,0:T(8,128)(2,1)S(1)}, bf16[512,512]{1,0:T(8,128)(2,1)S(1)}, u32[]{:S(2)}, u32[]{:S(2)}) collective-permute-start(bf16[512,512]{1,0:T(8,128)(2,1)S(1)} %shard_map.67.rest_2_), channel_id=1, source_target_pairs={{0,2},{1,3},{2,0},{3,1},{4,6},{5,7},{6,4},{7,5},{8,10},{9,11},{10,... | collective-permute-start | bytes 1572872 | tf_op jit(solution)/shard_map/ppermute | solution.py:484
  164.7 2.0 %collective-permute-start.14 = (bf16[512,512]{1,0:T(8,128)(2,1)S(1)}, bf16[512,512]{1,0:T(8,128)(2,1)S(1)}, u32[]{:S(2)}, u32[]{:S(2)}) collective-permute-start(bf16[512,512]{1,0:T(8,128)(2,1)S(1)} %get-tuple-element.19), channel_id=1, source_target_pairs={{0,1},{1,0},{2,3},{3,2},{4,5},{5,4},{6,7},{7,6},{8,9},{9,8},{10,11... | collective-permute-start | bytes 1572872 | tf_op jit(solution)/shard_map/ppermute | solution.py:484
  166.7 2.0 %copy-start.29 = (bf16[512,4096]{1,0:T(8,128)(2,1)}, bf16[512,4096]{1,0:T(8,128)(2,1)S(1)}, u32[]{:S(2)}) copy-start(bf16[512,4096]{1,0:T(8,128)(2,1)S(1)} %constant_dynamic-update-slice_fusion.1) | copy-start | bytes 12582916

commit v10 on v9

--- a/solution.py
+++ b/solution.py
@@ -18,6 +18,7 @@
 STEP_BLOCKS = 2
 TILE = 256
 HBM = pl.BlockSpec(memory_space=pltpu.HBM)
+ANY = pl.BlockSpec(memory_space=pl.ANY)
 VMEM = pl.BlockSpec(memory_space=pltpu.VMEM)
 SMEM = pl.BlockSpec(memory_space=pltpu.SMEM)
 
@@ -343,8 +344,8 @@
         grid_spec=pltpu.PrefetchScalarGridSpec(
             num_scalar_prefetch=2,
             grid=(parts * part_blocks // STEP_BLOCKS,),
-            in_specs=[pl.BlockSpec(bias.shape, lambda s, *_: (0, 0))] + [HBM] * (3 + 2 * len(two_back) + len(after)),
-            out_specs=[HBM] * parts,
+            in_specs=[pl.BlockSpec(bias.shape, lambda s, *_: (0, 0))] + [ANY] * (3 + 2 * len(two_back) + len(after)),
+            out_specs=[ANY] * parts,
             scratch_shapes=[
                 pltpu.VMEM((parts * part_rows, group_cols), jnp.bfloat16),
                 pltpu.VMEM((parts * part_rows, group_cols), jnp.bfloat16),
@@ -365,7 +366,7 @@
             ],
         ),
         compiler_params=pltpu.CompilerParams(
-            dimension_semantics=("arbitrary",), vmem_limit_bytes=18 << 20
+            dimension_semantics=("arbitrary",), vmem_limit_bytes=32 << 20
         ),
         cost_estimate=pl.CostEstimate(
             flops=4 * parts * part_rows * group_heads * keys_seen * HD,

time: 171 us -> 171 us (level)
  no operation moved by 1% of the time
where the time goes in v10:
time: 171 us; the launch traced here: 170 us
  Pallas kernels  67.9 us (40%)
  waiting for transfers between devices  51.1 us (30%)
  local copies, waits for them, and re-layouts  29.8 us (17%)
  starting transfers between devices  15 us (9%)
  other arithmetic  4.96 us (3%)
    pallas_call x5, Pallas kernels, attend(): pl.pallas_call(functools.partial(attend_kernel, head, parts, bounds, len(...  58.5 us
    ppermute x3, waiting for transfers between devices, local(): come = lax.ppermute(send, 'ctx', two_pairs)  41.3 us
    unnamed x64, local copies, waits for them, and re-layouts  27.2 us
    ppermute x3, waiting for transfers between devices, local(): one_back.append(lax.ppermute(cross, 'ctx', across_pairs))  8.25 us
    ppermute x6, starting transfers between devices, local(): lax.ppermute(piece, 'head', [(i, i ^ flip) for i in range(head_count)])  5.03 us
    pallas_call x6, Pallas kernels, joined(): pl.pallas_call(functools.partial(joined_kernel, plan), out_shape=jax.Shap...  4.68 us
  transfers between devices with their start and end apart: 15, of which 6 were waited for; matrix products, arithmetic and copies ran while one was open for 3% of the time, Pallas kernels for 38%

profile of v10, /device:TPU:0, one launch (start us, length us, event | category | flops | bytes accessed | tf_op | source)
XLA Modules:
  0.0 169.6 jit_solution(12621563420324761523)
XLA Ops:
  1.8 1.2 copy-done.19
  3.0 1.2 copy-done.21
  4.2 2.0 %shard_map.55 = (bf16[2048,256]{1,0:T(8,128)(2,1)S(1)}, bf16[1152,256]{1,0:T(8,128)(2,1)S(1)}, bf16[512,256]{1,0:T(8,128)(2,1)}) custom-call(s32[2,4]{1,0:T(2,128)S(1)} %select_reduce_fusion.2.local_ref, bf16[2048,256]{1,0:T(8,128)(2,1)S(1)} %copy-done.19, bf16[2048,256]{1,0:T(8,128)(2,1)S(1)} %copy-done.21), custom_call_target="tpu_custom_call" | custom-call | bytes 4194304 | tf_op jit(solution)/shard_map/pallas_call | solution.py:59
  6.2 3.1 %collective-permute-start = (bf16[1152,256]{1,0:T(8,128)(2,1)S(1)}, bf16[1152,256]{1,0:T(8,128)(2,1)S(1)}, u32[]{:S(2)}, u32[]{:S(2)}) collective-permute-start(bf16[1152,256]{1,0:T(8,128)(2,1)S(1)} %get-tuple-element.14), channel_id=1, source_target_pairs={{0,8},{4,12},{8,16},{12,20},{16,24},{20,28},{24,0},{28,4},{1,9},{5... | collective-permute-start | bytes 1769480 | tf_op jit(solution)/shard_map/ppermute | solution.py:445
  9.3 1.5 collective-permute-start.4
  10.8 1.0 convert_reduce_fusion.1
  13.4 11.2 %collective-permute-done.rest_1_.rest_0_ = bf16[1152,256]{1,0:T(8,128)(2,1)S(1)} collective-permute-done((bf16[1152,256]{1,0:T(8,128)(2,1)S(1)}, bf16[1152,256]{1,0:T(8,128)(2,1)S(1)}, u32[]{:S(2)}, u32[]{:S(2)}) %collective-permute-start) | collective-permute-done | bytes 589856 | tf_op jit(solution)/shard_map/ppermute | solution.py:445
  24.8 1.5 collective-permute-start.2
  26.4 1.0 shard_map.57
  28.6 15.6 %collective-permute-done.1.rest_1_.rest_2_.rest_0_ = bf16[1216,256]{1,0:T(8,128)(2,1)S(1)} collective-permute-done((bf16[1216,256]{1,0:T(8,128)(2,1)}, bf16[1216,256]{1,0:T(8,128)(2,1)S(1)}, u32[]{:S(2)}, u32[]{:S(2)}) %collective-permute-start.1) | collective-permute-done | bytes 622624 | tf_op jit(solution)/shard_map/ppermute | solution.py:445
  44.1 1.0 shard_map.58.rest_2_
  46.0 1.2 copy-done.20
  47.3 1.2 copy-done.22
  48.8 0.9 collective-permute-start.5
  49.7 14.5 %collective-permute-done.3.rest_1_.rest_3_.rest_2_ = bf16[1216,256]{1,0:T(8,128)(2,1)S(1)} collective-permute-done((bf16[1216,256]{1,0:T(8,128)(2,1)S(1)}, bf16[1216,256]{1,0:T(8,128)(2,1)S(1)}, u32[]{:S(2)}, u32[]{:S(2)}) %collective-permute-start.3) | collective-permute-done | bytes 622624 | tf_op jit(solution)/shard_map/ppermute | solution.py:445
  64.2 1.0 shard_map.60
  66.1 0.9 collective-permute-start.6
  67.6 0.8 copy-done.23
  68.4 8.2 %collective-permute-done.6.rest_7_.rest_5_ = bf16[1216,256]{1,0:T(8,128)(2,1)} collective-permute-done((bf16[1216,256]{1,0:T(8,128)(2,1)}, bf16[1216,256]{1,0:T(8,128)(2,1)}, u32[]{:S(2)}, u32[]{:S(2)}) %collective-permute-start.6) | collective-permute-done | bytes 622624 | tf_op jit(solution)/shard_map/ppermute | solution.py:451
  76.7 1.1 copy-done.4
  77.7 1.1 copy-done.8
  78.8 1.1 copy-done.12
  79.9 1.1 copy-done.16
  80.9 1.1 copy-done.24
  82.0 2.6 %shard_map.61.vert_ref = bf16[2,1024,256]{2,1,0:T(8,128)(2,1)S(1)} custom-call(s32[8,2,4]{2,1,0:T(2,128)S(1)} %broadcast_add_fusion.place_ref, s32[2,16]{1,0:T(2,128)S(1)} %compare_select_fusion.1.source_ref, bf16[512,256]{1,0:T(8,128)(2,1)} %get-tuple-element.13.rest_0_, bf16[1152,256]{1,0:T(8,128)(2,1)S(1)} %copy-done.8, bf16[1216,256]{1,0:T(8,128)(2,1)S(1)} %copy-done.4, ...), custom_call_target="tpu_custom_call" | custom-call | bytes 2097152 | tf_op jit(solution)/shard_map/pallas_call | solution.py:163
  84.7 1.1 copy-done.9
  85.7 1.1 copy-done.17
  86.8 1.1 copy-done.25
  87.9 8.4 %shard_map.62.rest_6_.rest_2_ = bf16[512,512]{1,0:T(8,128)(2,1)S(1)} custom-call(s32[1]{0:T(128)} %bitcast.part_ref, s32[2,8]{1,0:T(2,128)S(1)} %select_reduce_fusion.1.slash_ref, f32[64,1536]{1,0:T(8,128)S(1)} %fusion.bias_ref, bf16[2048,1024]{1,0:T(8,128)(2,1)S(1)} %copy-done, bf16[2,1024,256]{2,1,0:T(8,128)(2,1)S(1)} %shard_map.61.vert_ref, ...), custom_call_target="tpu_custom_call" | custom-call | flops 1610612736 | bytes 4194304 | tf_op jit(solution)/shard_map/pallas_call | solution.py:339
  96.3 1.2 shard_map.65
  98.4 1.9 %collective-permute-start.11 = (bf16[2048,256]{1,0:T(8,128)(2,1)}, bf16[2048,256]{1,0:T(8,128)(2,1)}, u32[]{:S(2)}, u32[]{:S(2)}) collective-permute-start(bf16[2048,256]{1,0:T(8,128)(2,1)} %shard_map.65), channel_id=1, source_target_pairs={{0,4},{4,0},{8,12},{12,8},{16,20},{20,16},{24,28},{28,24},{1,5},{5... | collective-permute-start | bytes 3145736 | tf_op jit(solution)/shard_map/ppermute | solution.py:481
  100.4 2.2 %copy-done.1 = bf16[2048,1024]{1,0:T(8,128)(2,1)S(1)} copy-done((bf16[2048,1024]{1,0:T(8,128)(2,1)S(1)}, bf16[2048,1024]{1,0:T(8,128)(2,1)}, u32[]{:S(2)}) %copy-start.1) | copy-done | bytes 4194328
  102.6 1.1 copy-done.6
  103.7 1.1 copy-done.10
  104.8 1.1 copy-done.14
  105.8 1.1 copy-done.18
  106.9 1.1 copy-done.26
  108.0 1.0 copy-done.28
  109.0 19.6 %shard_map.63 = (bf16[512,512]{1,0:T(8,128)(2,1)S(1)}, bf16[512,512]{1,0:T(8,128)(2,1)S(1)}, bf16[512,512]{1,0:T(8,128)(2,1)S(1)}) custom-call(s32[3]{0:T(128)S(1)} %pad_add_fusion.part_ref, s32[2,8]{1,0:T(2,128)S(1)} %select_reduce_fusion.1.slash_ref, f32[64,1536]{1,0:T(8,128)S(1)} %fusion.bias_ref, bf16[2048,1024]{1,0:T(8,128)(2,1)S(1)} %copy-done.1, ...), custom_call_target="tpu_custom_call" | custom-call | flops 4831838208 | bytes 6291456 | tf_op jit(solution)/shard_map/pallas_call | solution.py:339
  128.6 1.6 collective-permute-start.8
  131.2 8.3 %shard_map.66.rest_2_ = bf16[512,512]{1,0:T(8,128)(2,1)S(1)} custom-call(s32[1]{0:T(128)} %bitcast.part_ref, s32[2,8]{1,0:T(2,128)S(1)} %select_reduce_fusion.1.slash_ref, f32[64,1536]{1,0:T(8,128)S(1)} %fusion.bias_ref, bf16[2048,1024]{1,0:T(8,128)(2,1)S(1)} %copy-done.2, bf16[2,1024,256]{2,1,0:T(8,128)(2,1)S(1)} %shard_map.61.vert_ref, ...), custom_call_target="tpu_custom_call" | custom-call | flops 1610612736 | bytes 4194304 | tf_op jit(solution)/shard_map/pallas_call | solution.py:339
  139.5 1.5 collective-permute-start.12
  140.9 8.3 %shard_map.67.rest_2_ = bf16[512,512]{1,0:T(8,128)(2,1)S(1)} custom-call(s32[1]{0:T(128)} %bitcast.2.part_ref, s32[2,8]{1,0:T(2,128)S(1)} %select_reduce_fusion.1.slash_ref, f32[64,1536]{1,0:T(8,128)S(1)} %fusion.bias_ref, bf16[2048,1024]{1,0:T(8,128)(2,1)S(1)} %copy-done.2, bf16[2,1024,256]{2,1,0:T(8,128)(2,1)S(1)} %shard_map.61.vert_ref, ...), custom_call_target="tpu_custom_call" | custom-call | flops 1610612736 | bytes 4194304 | tf_op jit(solution)/shard_map/pallas_call | solution.py:339
  149.2 1.6 collective-permute-start.13
  150.8 13.8 %shard_map.68 = (bf16[512,512]{1,0:T(8,128)(2,1)S(1)}, bf16[512,512]{1,0:T(8,128)(2,1)S(1)}) custom-call(s32[2]{0:T(128)S(1)} %pad_add_fusion.1.part_ref, s32[2,8]{1,0:T(2,128)S(1)} %select_reduce_fusion.1.slash_ref, f32[64,1536]{1,0:T(8,128)S(1)} %fusion.bias_ref, bf16[2048,1024]{1,0:T(8,128)(2,1)S(1)} %copy-done.2, ...), custom_call_target="tpu_custom_call" | custom-call | flops 3221225472 | bytes 5242880 | tf_op jit(solution)/shard_map/pallas_call | solution.py:339
  165.1 0.9 collective-permute-done.13
  166.7 2.0 %copy-done.29 = bf16[512,4096]{1,0:T(8,128)(2,1)} copy-done((bf16[512,4096]{1,0:T(8,128)(2,1)}, bf16[512,4096]{1,0:T(8,128)(2,1)S(1)}, u32[]{:S(2)}) %copy-start.29) | copy-done | bytes 4194328
  168.7 0.8 constant_dynamic-update-slice_fusion
  (107 shorter events, 10.2 us)
Async XLA Ops:
  0.0 27.6 %copy-start.30 = (s32[2,16]{1,0:T(2,128)S(1)}, s32[2,16]{1,0:T(2,128)}, u32[]{:S(2)}) copy-start(s32[2,16]{1,0:T(2,128)} %param.8) | copy-start | bytes 388
  1.8 1.2 copy-start.19
  3.0 1.2 copy-start.21
  6.2 18.4 %collective-permute-start = (bf16[1152,256]{1,0:T(8,128)(2,1)S(1)}, bf16[1152,256]{1,0:T(8,128)(2,1)S(1)}, u32[]{:S(2)}, u32[]{:S(2)}) collective-permute-start(bf16[1152,256]{1,0:T(8,128)(2,1)S(1)} %get-tuple-element.14), channel_id=1, source_target_pairs={{0,8},{4,12},{8,16},{12,20},{16,24},{20,28},{24,0},{28,4},{1,9},{5... | collective-permute-start | bytes 1769480 | tf_op jit(solution)/shard_map/ppermute | solution.py:445
  9.3 58.3 %collective-permute-start.4 = (bf16[512,256]{1,0:T(8,128)(2,1)}, bf16[512,256]{1,0:T(8,128)(2,1)}, u32[]{:S(2)}, u32[]{:S(2)}) collective-permute-start(bf16[512,256]{1,0:T(8,128)(2,1)} %get-tuple-element.13.rest_0_), channel_id=1, source_target_pairs={{0,4},{4,0},{8,12},{12,8},{16,20},{20,16},{24,28},{28,24},{1,5},{5... | collective-permute-start | bytes 786440 | tf_op jit(solution)/shard_map/ppermute | solution.py:447
  24.7 1.7 %copy-start.7 = (bf16[1152,256]{1,0:T(8,128)(2,1)}, bf16[1152,256]{1,0:T(8,128)(2,1)S(1)}, u32[]{:S(2)}) copy-start(bf16[1152,256]{1,0:T(8,128)(2,1)S(1)} %collective-permute-done.rest_1_.rest_0_) | copy-start | bytes 1769476
  24.8 20.4 %collective-permute-start.2 = (bf16[1152,256]{1,0:T(8,128)(2,1)S(1)}, bf16[1152,256]{1,0:T(8,128)(2,1)S(1)}, u32[]{:S(2)}, u32[]{:S(2)}) collective-permute-start(bf16[1152,256]{1,0:T(8,128)(2,1)S(1)} %shard_map.56.rest_2_), channel_id=1, source_target_pairs={{0,4},{4,0},{8,12},{12,8},{16,20},{20,16},{24,28},{28,24},{1,5},{5... | collective-permute-start | bytes 1769480 | tf_op jit(solution)/shard_map/ppermute | solution.py:451
  27.4 16.8 %collective-permute-start.1 = (bf16[1216,256]{1,0:T(8,128)(2,1)}, bf16[1216,256]{1,0:T(8,128)(2,1)S(1)}, u32[]{:S(2)}, u32[]{:S(2)}) collective-permute-start(bf16[1216,256]{1,0:T(8,128)(2,1)} %shard_map.57), channel_id=1, source_target_pairs={{0,8},{4,12},{8,16},{12,20},{16,24},{20,28},{24,0},{28,4},{1,9},{5... | collective-permute-start | bytes 1867784 | tf_op jit(solution)/shard_map/ppermute | solution.py:445
  44.1 4.5 %copy-start.3 = (bf16[1216,256]{1,0:T(8,128)(2,1)}, bf16[1216,256]{1,0:T(8,128)(2,1)S(1)}, u32[]{:S(2)}) copy-start(bf16[1216,256]{1,0:T(8,128)(2,1)S(1)} %collective-permute-done.1.rest_1_.rest_2_.rest_0_) | copy-start | bytes 1867780
  45.2 0.8 copy-start.15
  45.4 18.8 %collective-permute-start.3 = (bf16[1216,256]{1,0:T(8,128)(2,1)S(1)}, bf16[1216,256]{1,0:T(8,128)(2,1)S(1)}, u32[]{:S(2)}, u32[]{:S(2)}) collective-permute-start(bf16[1216,256]{1,0:T(8,128)(2,1)S(1)} %shard_map.59.rest_1_), channel_id=1, source_target_pairs={{0,8},{4,12},{8,16},{12,20},{16,24},{20,28},{24,0},{28,4},{1,9},{5... | collective-permute-start | bytes 1867784 | tf_op jit(solution)/shard_map/ppermute | solution.py:445
  46.0 1.2 copy-start.20
  47.3 1.2 copy-start.22
  48.7 47.6 %collective-permute-start.10 = (bf16[2048,256]{1,0:T(8,128)(2,1)S(1)}, bf16[2048,256]{1,0:T(8,128)(2,1)}, u32[]{:S(2)}, u32[]{:S(2)}) collective-permute-start(bf16[2048,256]{1,0:T(8,128)(2,1)S(1)} %shard_map.64.rest_0_.own_ref), channel_id=1, source_target_pairs={{0,8},{4,12},{8,16},{12,20},{16,24},{20,28},{24,0},{28,4},{1,9},{5... | collective-permute-start | bytes 3145736 | tf_op jit(solution)/shard_map/ppermute | solution.py:458
  48.8 18.8 %collective-permute-start.5 = (bf16[1216,256]{1,0:T(8,128)(2,1)}, bf16[1216,256]{1,0:T(8,128)(2,1)S(1)}, u32[]{:S(2)}, u32[]{:S(2)}) collective-permute-start(bf16[1216,256]{1,0:T(8,128)(2,1)} %shard_map.58.rest_2_), channel_id=1, source_target_pairs={{0,4},{4,0},{8,12},{12,8},{16,20},{20,16},{24,28},{28,24},{1,5},{5... | collective-permute-start | bytes 1867784 | tf_op jit(solution)/shard_map/ppermute | solution.py:451
  65.3 0.8 copy-start.11
  66.1 10.6 %collective-permute-start.6 = (bf16[1216,256]{1,0:T(8,128)(2,1)}, bf16[1216,256]{1,0:T(8,128)(2,1)}, u32[]{:S(2)}, u32[]{:S(2)}) collective-permute-start(bf16[1216,256]{1,0:T(8,128)(2,1)} %shard_map.60), channel_id=1, source_target_pairs={{0,4},{4,0},{8,12},{12,8},{16,20},{20,16},{24,28},{28,24},{1,5},{5... | collective-permute-start | bytes 1867784 | tf_op jit(solution)/shard_map/ppermute | solution.py:451
  67.3 17.3 %copy-start = (bf16[2048,1024]{1,0:T(8,128)(2,1)S(1)}, bf16[2048,1024]{1,0:T(8,128)(2,1)}, u32[]{:S(2)}) copy-start(bf16[2048,1024]{1,0:T(8,128)(2,1)} %query_ref.9) | copy-start | bytes 12582916
  67.6 0.8 copy-start.23
  76.7 1.1 copy-start.4
  77.7 1.1 copy-start.8
  78.8 1.1 copy-start.12
  79.9 1.1 copy-start.16
  80.9 1.1 copy-start.24
  82.0 2.6 %copy-start.5 = (bf16[1216,256]{1,0:T(8,128)(2,1)S(1)}, bf16[1216,256]{1,0:T(8,128)(2,1)}, u32[]{:S(2)}) copy-start(bf16[1216,256]{1,0:T(8,128)(2,1)} %copy-done.3) | copy-start | bytes 1867780
  82.0 2.6 %copy-start.13 = (bf16[1216,256]{1,0:T(8,128)(2,1)S(1)}, bf16[1216,256]{1,0:T(8,128)(2,1)}, u32[]{:S(2)}) copy-start(bf16[1216,256]{1,0:T(8,128)(2,1)} %copy-done.11) | copy-start | bytes 1867780
  84.7 1.1 copy-start.9
  85.7 1.1 copy-start.17
  86.8 1.1 copy-start.25
  97.6 0.8 copy-start.27
  98.4 32.8 %collective-permute-start.11 = (bf16[2048,256]{1,0:T(8,128)(2,1)}, bf16[2048,256]{1,0:T(8,128)(2,1)}, u32[]{:S(2)}, u32[]{:S(2)}) collective-permute-start(bf16[2048,256]{1,0:T(8,128)(2,1)} %shard_map.65), channel_id=1, source_target_pairs={{0,4},{4,0},{8,12},{12,8},{16,20},{20,16},{24,28},{28,24},{1,5},{5... | collective-permute-start | bytes 3145736 | tf_op jit(solution)/shard_map/ppermute | solution.py:481
  100.4 30.2 %collective-permute-start.7 = (bf16[512,512]{1,0:T(8,128)(2,1)}, bf16[512,512]{1,0:T(8,128)(2,1)S(1)}, u32[]{:S(2)}, u32[]{:S(2)}) collective-permute-start(bf16[512,512]{1,0:T(8,128)(2,1)} %copy-done.27), channel_id=1, source_target_pairs={{0,3},{1,2},{2,1},{3,0},{4,7},{5,6},{6,5},{7,4},{8,11},{9,10},{10,... | collective-permute-start | bytes 1572872 | tf_op jit(solution)/shard_map/ppermute | solution.py:485
  100.4 2.2 %copy-start.1 = (bf16[2048,1024]{1,0:T(8,128)(2,1)S(1)}, bf16[2048,1024]{1,0:T(8,128)(2,1)}, u32[]{:S(2)}) copy-start(bf16[2048,1024]{1,0:T(8,128)(2,1)} %query_ref.9) | copy-start | bytes 12582916
  102.6 1.1 copy-start.6
  103.7 1.1 copy-start.10
  104.8 1.1 copy-start.14
  105.8 1.1 copy-start.18
  106.9 1.1 copy-start.26
  108.0 1.0 copy-start.28
  128.6 2.5 %copy-start.2 = (bf16[2048,1024]{1,0:T(8,128)(2,1)S(1)}, bf16[2048,1024]{1,0:T(8,128)(2,1)}, u32[]{:S(2)}) copy-start(bf16[2048,1024]{1,0:T(8,128)(2,1)} %query_ref.9) | copy-start | bytes 12582916
  128.6 36.1 %collective-permute-start.8 = (bf16[512,512]{1,0:T(8,128)(2,1)S(1)}, bf16[512,512]{1,0:T(8,128)(2,1)S(1)}, u32[]{:S(2)}, u32[]{:S(2)}) collective-permute-start(bf16[512,512]{1,0:T(8,128)(2,1)S(1)} %get-tuple-element.16), channel_id=1, source_target_pairs={{0,2},{1,3},{2,0},{3,1},{4,6},{5,7},{6,4},{7,5},{8,10},{9,11},{10,... | collective-permute-start | bytes 1572872 | tf_op jit(solution)/shard_map/ppermute | solution.py:485
  130.2 34.6 %collective-permute-start.9 = (bf16[512,512]{1,0:T(8,128)(2,1)S(1)}, bf16[512,512]{1,0:T(8,128)(2,1)S(1)}, u32[]{:S(2)}, u32[]{:S(2)}) collective-permute-start(bf16[512,512]{1,0:T(8,128)(2,1)S(1)} %get-tuple-element.17), channel_id=1, source_target_pairs={{0,1},{1,0},{2,3},{3,2},{4,5},{5,4},{6,7},{7,6},{8,9},{9,8},{10,11... | collective-permute-start | bytes 1572872 | tf_op jit(solution)/shard_map/ppermute | solution.py:485
  139.5 25.5 %collective-permute-start.12 = (bf16[512,512]{1,0:T(8,128)(2,1)S(1)}, bf16[512,512]{1,0:T(8,128)(2,1)S(1)}, u32[]{:S(2)}, u32[]{:S(2)}) collective-permute-start(bf16[512,512]{1,0:T(8,128)(2,1)S(1)} %shard_map.66.rest_2_), channel_id=1, source_target_pairs={{0,3},{1,2},{2,1},{3,0},{4,7},{5,6},{6,5},{7,4},{8,11},{9,10},{10,... | collective-permute-start | bytes 1572872 | tf_op jit(solution)/shard_map/ppermute | solution.py:485
  149.2 16.7 %collective-permute-start.13 = (bf16[512,512]{1,0:T(8,128)(2,1)S(1)}, bf16[512,512]{1,0:T(8,128)(2,1)S(1)}, u32[]{:S(2)}, u32[]{:S(2)}) collective-permute-start(bf16[512,512]{1,0:T(8,128)(2,1)S(1)} %shard_map.67.rest_2_), channel_id=1, source_target_pairs={{0,2},{1,3},{2,0},{3,1},{4,6},{5,7},{6,4},{7,5},{8,10},{9,11},{10,... | collective-permute-start | bytes 1572872 | tf_op jit(solution)/shard_map/ppermute | solution.py:485
  164.7 2.0 %collective-permute-start.14 = (bf16[512,512]{1,0:T(8,128)(2,1)S(1)}, bf16[512,512]{1,0:T(8,128)(2,1)S(1)}, u32[]{:S(2)}, u32[]{:S(2)}) collective-permute-start(bf16[512,512]{1,0:T(8,128)(2,1)S(1)} %get-tuple-element.19), channel_id=1, source_target_pairs={{0,1},{1,0},{2,3},{3,2},{4,5},{5,4},{6,7},{7,6},{8,9},{9,8},{10,11... | collective-permute-start | bytes 1572872 | tf_op jit(solution)/shard_map/ppermute | solution.py:485
  166.7 2.0 %copy-start.29 = (bf16[512,4096]{1,0:T(8,128)(2,1)}, bf16[512,4096]{1,0:T(8,128)(2,1)S(1)}, u32[]{:S(2)}) copy-start(bf16[512,4096]{1,0:T(8,128)(2,1)S(1)} %constant_dynamic-update-slice_fusion.1) | copy-start | bytes 12582916

commit v11 on v10

--- a/solution.py
+++ b/solution.py
@@ -100,12 +100,13 @@
     to = 0
     for rows, even, odd in pieces:
         for value, (index, low) in enumerate((even, odd)):
-
-            @pl.when(parity_ref[0] == value)
-            def _():
-                pltpu.make_async_copy(
-                    refs[index].at[pl.ds(low, rows)], out_ref.at[pl.ds(to, rows)], sem
-                ).start()
+            copy = pltpu.make_async_copy(
+                refs[index].at[pl.ds(low, rows)], out_ref.at[pl.ds(to, rows)], sem
+            )
+            if even != odd:
+                pl.when(parity_ref[0] == value)(copy.start)
+            elif value:
+                copy.start()
 
         to += rows
     pltpu.make_async_copy(out_ref, out_ref, sem).wait()
@@ -174,21 +175,17 @@
 
 
 def attend_kernel(
-    head, parts, bounds, waits, part_blocks, group_heads, part_ref, slash_ref, bias_ref, query_ref,
-    vert_ref, own_ref, *rest,
+    head, parts, waits, part_blocks, group_heads, part_ref, slash_ref, bias_ref, query_ref,
+    vert_ref, window, *rest,
 ):
-    chunks = len(bounds) - 1
-    two_back = rest[:chunks]
-    one_back = rest[chunks : 2 * chunks]
-    rest = rest[2 * chunks + waits :]
+    rest = rest[waits:]
     out_refs = rest[:parts]
     (
-        queries, out, vert, vert_keys, window, scores_a, scores_b, weights_a, weights_b, max_a,
-        max_b, diagonal_ref, query_sem, vert_sem, window_sem, out_sem,
+        queries, out, vert, vert_keys, scores_a, scores_b, weights_a, weights_b, max_a,
+        max_b, diagonal_ref, query_sem, vert_sem, out_sem,
     ) = rest[parts:]
     scores, weights, maxima = (scores_a, scores_b), (weights_a, weights_b), (max_a, max_b)
-    tok_rows = own_ref.shape[0]
-    blocks_dev = tok_rows // BLK
+    blocks_dev = window.shape[0] // ((LOOK + 1) * BLK)
     part_rows = part_blocks * BLK
     group_cols = group_heads * HD
     last = parts * part_blocks - 1
@@ -244,7 +241,7 @@
         for h in range(group_heads):
             out[rows, h * HD : (h + 1) * HD] = result[h * BLK : (h + 1) * BLK]
 
-    def stage(block, at, score, weigh, combine, arrives=False):
+    def stage(block, at, score, weigh, combine):
         other = 1 - at
         if score:
             fresh = jnp.minimum(block, last)
@@ -260,8 +257,6 @@
         highest = None
         for tile in range((NV + NS) * BLK // TILE):
             low = tile * TILE
-            if arrives and low == NV * BLK:
-                pltpu.make_async_copy(window, window, window_sem).wait()
             if score:
                 found = score_tile(query, bias, rows, tile)
                 scores[at][:, low : low + TILE] = found
@@ -291,17 +286,6 @@
                 query_sem,
             ).start()
         pltpu.make_async_copy(vert_ref.at[head], vert, vert_sem).start()
-        for back, sources in enumerate((two_back, one_back)):
-            for chunk, source in enumerate(sources):
-                rows = bounds[chunk + 1] - bounds[chunk]
-                pltpu.make_async_copy(
-                    source.at[pl.ds(0, rows)],
-                    window.at[pl.ds(back * tok_rows + bounds[chunk], rows)],
-                    window_sem,
-                ).start()
-        pltpu.make_async_copy(
-            own_ref, window.at[pl.ds(LOOK * tok_rows, tok_rows)], window_sem
-        ).start()
         column = lax.broadcasted_iota(jnp.int32, (BLK, 2 * BLK), 1)
         row = lax.broadcasted_iota(jnp.int32, (BLK, 2 * BLK), 0)
         diagonal_ref[...] = jnp.where((column < BLK) & (column > row), NEG, 0.0).astype(jnp.float32)
@@ -309,7 +293,7 @@
         pltpu.make_async_copy(vert, vert, vert_sem).wait()
         vert_keys[...] = vert[:, :HD].T
         pltpu.make_async_copy(queries, queries, query_sem).wait()
-        stage(0, 0, True, False, False, True)
+        stage(0, 0, True, False, False)
 
     first = step * STEP_BLOCKS
     stage(first + 1, 1, True, True, True)
@@ -328,30 +312,27 @@
             ).wait()
 
 
-def attend(head, part, bounds, slash, bias, queries, vert, own, two_back, one_back, part_rows, after):
+def attend(head, part, slash, bias, queries, vert, window, part_rows, after):
     parts = part.shape[0]
     group_cols = queries.shape[1] // slash.shape[0]
     group_heads = group_cols // HD
     part_blocks = part_rows // BLK
-    tok_rows = own.shape[0]
     rows = group_heads * BLK
     keys_seen = (NV + NS) * BLK
     return pl.pallas_call(
-        functools.partial(
-            attend_kernel, head, parts, bounds, len(after), part_blocks, group_heads
-        ),
+        functools.partial(attend_kernel, head, parts, len(after), part_blocks, group_heads),
         out_shape=[jax.ShapeDtypeStruct((part_rows, group_cols), jnp.bfloat16)] * parts,
         grid_spec=pltpu.PrefetchScalarGridSpec(
             num_scalar_prefetch=2,
             grid=(parts * part_blocks // STEP_BLOCKS,),
-            in_specs=[pl.BlockSpec(bias.shape, lambda s, *_: (0, 0))] + [ANY] * (3 + 2 * len(two_back) + len(after)),
+            in_specs=[pl.BlockSpec(bias.shape, lambda s, *_: (0, 0))] + [ANY, ANY, VMEM]
+            + [ANY] * len(after),
             out_specs=[ANY] * parts,
             scratch_shapes=[
                 pltpu.VMEM((parts * part_rows, group_cols), jnp.bfloat16),
                 pltpu.VMEM((parts * part_rows, group_cols), jnp.bfloat16),
                 pltpu.VMEM((NV * BLK, 2 * HD), jnp.bfloat16),
                 pltpu.VMEM((HD, NV * BLK), jnp.bfloat16),
-                pltpu.VMEM(((LOOK + 1) * tok_rows, 2 * HD), jnp.bfloat16),
                 pltpu.VMEM((rows, keys_seen), jnp.float32),
                 pltpu.VMEM((rows, keys_seen), jnp.float32),
                 pltpu.VMEM((rows, keys_seen), jnp.bfloat16),
@@ -359,7 +340,6 @@
                 pltpu.VMEM((rows, HD), jnp.float32),
                 pltpu.VMEM((rows, HD), jnp.float32),
                 pltpu.VMEM((BLK, 2 * BLK), jnp.float32),
-                pltpu.SemaphoreType.DMA,
                 pltpu.SemaphoreType.DMA,
                 pltpu.SemaphoreType.DMA,
                 pltpu.SemaphoreType.DMA((parts,)),
@@ -370,10 +350,10 @@
         ),
         cost_estimate=pl.CostEstimate(
             flops=4 * parts * part_rows * group_heads * keys_seen * HD,
-            bytes_accessed=4 * parts * part_rows * group_cols + 12 * tok_rows * HD,
+            bytes_accessed=4 * parts * part_rows * group_cols + 4 * window.shape[0] * HD,
             transcendentals=parts * part_rows * group_heads * keys_seen,
         ),
-    )(part, slash, bias, queries, vert, own, *two_back, *one_back, *after)
+    )(part, slash, bias, queries, vert, window, *after)
 
 
 def local(queries, keys, values, vertical, slash):
@@ -468,11 +448,17 @@
     vert = listed_blocks(place, source, slots)
     for head in range(kv_local):
         bounds, own, two_back, one_back = windows[head]
+        pieces = []
+        for arrays in (two_back, one_back):
+            for low, high, array in zip(bounds[:-1], bounds[1:], arrays):
+                pieces.append((high - low, (array, 0), (array, 0)))
+        pieces.append((tok_rows, (own, 0), (own, 0)))
+        window = joined(parity, pieces)
         for flips in calls[head]:
             others = [head_index ^ flip for flip in flips]
             pieces = attend(
-                head, jnp.stack(others).astype(jnp.int32), bounds, slash, bias, queries, vert, own,
-                two_back, one_back, part_rows, after,
+                head, jnp.stack(others).astype(jnp.int32), slash, bias, queries, vert, window,
+                part_rows, after,
             )
             after = [pieces[-1]]
             if flips == calls[head][0] and head + 1 < kv_local:

time: 171 us -> 160 us (0.936)
  local copies, waits for them, and re-layouts: 29.8 us -> 17.4 us
  waiting for transfers between devices: 51.1 us -> 56.3 us
    unnamed x64 -> x40, local copies, waits for them, and re-layouts: 27.2 us -> 14.7 us
    pallas_call x5, Pallas kernels: 58.5 us -> 52.6 us  [attend(): pl.pallas_call(functools.partial(attend_kernel, head, parts, len(after),...]
    pallas_call x6 -> x8, Pallas kernels: 4.68 us -> 8.69 us  [joined(): pl.pallas_call(functools.partial(joined_kernel, plan), out_shape=jax.Shap...]
    ppermute x3, waiting for transfers between devices: 41.3 us -> 43.8 us  [local(): come = lax.ppermute(send, 'ctx', two_pairs)]
    ppermute x6, waiting for transfers between devices: 1.53 us -> 3.24 us  [local(): lax.ppermute(piece, 'head', [(i, i ^ flip) for i in range(head_count)])]
  transfers between devices with their start and end apart: 15 -> 15, of which waited for: 6 -> 5; matrix products, arithmetic and copies ran while one was open for 3% -> 3% of each run, Pallas kernels for 38% -> 40%
where the time goes in v11:
time: 160 us
  Pallas kernels  66.7 us (42%)
  waiting for transfers between devices  56.3 us (35%)
  local copies, waits for them, and re-layouts  17.4 us (11%)
  starting transfers between devices  13.9 us (9%)
  other arithmetic  4.97 us (3%)
    pallas_call x5, Pallas kernels, attend(): pl.pallas_call(functools.partial(attend_kernel, head, parts, len(after),...  52.6 us
    ppermute x3, waiting for transfers between devices, local(): come = lax.ppermute(send, 'ctx', two_pairs)  43.8 us
    unnamed x40, local copies, waits for them, and re-layouts  14.7 us
    ppermute x3, waiting for transfers between devices, local(): one_back.append(lax.ppermute(cross, 'ctx', across_pairs))  9.19 us
    pallas_call x8, Pallas kernels, joined(): pl.pallas_call(functools.partial(joined_kernel, plan), out_shape=jax.Shap...  8.69 us
    ppermute x6, starting transfers between devices, local(): lax.ppermute(piece, 'head', [(i, i ^ flip) for i in range(head_count)])  3.98 us
    pallas_call x1, Pallas kernels, listed_blocks(): pl.pallas_call(functools.partial(listed_kernel, [low for _, low in slots]...  3.27 us
    ppermute x6, waiting for transfers between devices, local(): lax.ppermute(piece, 'head', [(i, i ^ flip) for i in range(head_count)])  3.24 us
  transfers between devices with their start and end apart: 15, of which 5 were waited for; matrix products, arithmetic and copies ran while one was open for 3% of the time, Pallas kernels for 40%

profile of v11, /device:TPU:0, one launch (start us, length us, event | category | flops | bytes accessed | tf_op | source)
XLA Modules:
  0.0 159.9 jit_solution(10245455070480185998)
XLA Ops:
  0.0 0.8 and_select_fusion
  0.8 0.7 broadcast_compare_fusion.2
  1.8 1.2 copy-done.13
  3.0 1.2 copy-done.15
  4.2 2.0 %shard_map.55 = (bf16[2048,256]{1,0:T(8,128)(2,1)S(1)}, bf16[1152,256]{1,0:T(8,128)(2,1)S(1)}, bf16[512,256]{1,0:T(8,128)(2,1)}) custom-call(s32[2,4]{1,0:T(2,128)S(1)} %select_reduce_fusion.2.local_ref, bf16[2048,256]{1,0:T(8,128)(2,1)S(1)} %copy-done.13, bf16[2048,256]{1,0:T(8,128)(2,1)S(1)} %copy-done.15), custom_call_target="tpu_custom_call" | custom-call | bytes 4194304 | tf_op jit(solution)/shard_map/pallas_call | solution.py:59
  6.2 3.1 %collective-permute-start = (bf16[1152,256]{1,0:T(8,128)(2,1)S(1)}, bf16[1152,256]{1,0:T(8,128)(2,1)S(1)}, u32[]{:S(2)}, u32[]{:S(2)}) collective-permute-start(bf16[1152,256]{1,0:T(8,128)(2,1)S(1)} %get-tuple-element.14), channel_id=1, source_target_pairs={{0,8},{4,12},{8,16},{12,20},{16,24},{20,28},{24,0},{28,4},{1,9},{5... | collective-permute-start | bytes 1769480 | tf_op jit(solution)/shard_map/ppermute | solution.py:425
  9.3 1.5 collective-permute-start.4
  10.8 1.0 convert_reduce_fusion.1
  11.8 0.8 select_reduce_fusion.1.slash_ref
  12.6 0.8 compare_reduce_fusion
  13.4 11.2 %collective-permute-done.rest_1_.rest_0_ = bf16[1152,256]{1,0:T(8,128)(2,1)S(1)} collective-permute-done((bf16[1152,256]{1,0:T(8,128)(2,1)S(1)}, bf16[1152,256]{1,0:T(8,128)(2,1)S(1)}, u32[]{:S(2)}, u32[]{:S(2)}) %collective-permute-start) | collective-permute-done | bytes 589856 | tf_op jit(solution)/shard_map/ppermute | solution.py:425
  24.7 1.0 shard_map.56.rest_2_
  25.6 1.5 collective-permute-start.2
  27.2 1.0 shard_map.57
  29.4 15.6 %collective-permute-done.1.rest_1_.rest_2_.rest_0_ = bf16[1216,256]{1,0:T(8,128)(2,1)S(1)} collective-permute-done((bf16[1216,256]{1,0:T(8,128)(2,1)}, bf16[1216,256]{1,0:T(8,128)(2,1)S(1)}, u32[]{:S(2)}, u32[]{:S(2)}) %collective-permute-start.1) | collective-permute-done | bytes 622624 | tf_op jit(solution)/shard_map/ppermute | solution.py:425
  44.9 1.0 shard_map.58.rest_2_
  46.2 0.5 copy-done.11
  47.1 0.8 collective-permute-start.5
  47.9 17.0 %collective-permute-done.3.rest_1_.rest_3_.rest_2_ = bf16[1216,256]{1,0:T(8,128)(2,1)S(1)} collective-permute-done((bf16[1216,256]{1,0:T(8,128)(2,1)S(1)}, bf16[1216,256]{1,0:T(8,128)(2,1)S(1)}, u32[]{:S(2)}, u32[]{:S(2)}) %collective-permute-start.3) | collective-permute-done | bytes 622624 | tf_op jit(solution)/shard_map/ppermute | solution.py:425
  65.0 1.0 shard_map.60
  66.0 0.8 copy-done.8
  66.8 0.8 collective-permute-start.6
  68.2 9.2 %collective-permute-done.6.rest_7_.rest_5_ = bf16[1216,256]{1,0:T(8,128)(2,1)} collective-permute-done((bf16[1216,256]{1,0:T(8,128)(2,1)}, bf16[1216,256]{1,0:T(8,128)(2,1)}, u32[]{:S(2)}, u32[]{:S(2)}) %collective-permute-start.6) | collective-permute-done | bytes 622624 | tf_op jit(solution)/shard_map/ppermute | solution.py:431
  77.4 1.1 copy-done.9
  78.5 1.1 copy-done.12
  79.5 1.6 shard_map.62.window
  81.2 3.3 %shard_map.61.vert_ref = bf16[2,1024,256]{2,1,0:T(8,128)(2,1)S(1)} custom-call(s32[8,2,4]{2,1,0:T(2,128)S(1)} %broadcast_add_fusion.place_ref, s32[2,16]{1,0:T(2,128)S(1)} %compare_select_fusion.1.source_ref, bf16[512,256]{1,0:T(8,128)(2,1)} %get-tuple-element.13.rest_0_, bf16[1152,256]{1,0:T(8,128)(2,1)S(1)} %collective-permute-done.rest_1_.rest_0_, ...), custom_call_target="tpu_custom_call" | custom-call | bytes 2097152 | tf_op jit(solution)/shard_map/pallas_call | solution.py:164
  84.5 0.4 copy-done
  84.9 7.2 %shard_map.63.rest_0_.rest_2_ = bf16[512,512]{1,0:T(8,128)(2,1)S(1)} custom-call(s32[1]{0:T(128)} %bitcast.part_ref, s32[2,8]{1,0:T(2,128)S(1)} %select_reduce_fusion.1.slash_ref, f32[64,1536]{1,0:T(8,128)S(1)} %fusion.bias_ref, bf16[2048,1024]{1,0:T(8,128)(2,1)S(1)} %copy-done, bf16[2,1024,256]{2,1,0:T(8,128)(2,1)S(1)} %shard_map.61.vert_ref, ...), custom_call_target="tpu_custom_call" | custom-call | flops 1610612736 | bytes 4194304 | tf_op jit(solution)/shard_map/pallas_call | solution.py:322
  92.0 1.3 shard_map.66
  93.3 2.0 %collective-permute-start.11 = (bf16[2048,256]{1,0:T(8,128)(2,1)}, bf16[2048,256]{1,0:T(8,128)(2,1)}, u32[]{:S(2)}, u32[]{:S(2)}) collective-permute-start(bf16[2048,256]{1,0:T(8,128)(2,1)} %shard_map.66), channel_id=1, source_target_pairs={{0,4},{4,0},{8,12},{12,8},{16,20},{20,16},{24,28},{28,24},{1,5},{5... | collective-permute-start | bytes 3145736 | tf_op jit(solution)/shard_map/ppermute | solution.py:467
  95.5 2.2 %copy-done.1 = bf16[2048,1024]{1,0:T(8,128)(2,1)S(1)} copy-done((bf16[2048,1024]{1,0:T(8,128)(2,1)S(1)}, bf16[2048,1024]{1,0:T(8,128)(2,1)}, u32[]{:S(2)}) %copy-start.1) | copy-done | bytes 4194328
  97.6 1.9 %copy-done.4 = bf16[6144,256]{1,0:T(8,128)(2,1)S(1)} copy-done((bf16[6144,256]{1,0:T(8,128)(2,1)S(1)}, bf16[6144,256]{1,0:T(8,128)(2,1)}, u32[]{:S(2)}) %copy-start.4) | copy-done | bytes 3145752
  99.5 1.0 copy-done.6
  100.5 18.4 %shard_map.64 = (bf16[512,512]{1,0:T(8,128)(2,1)S(1)}, bf16[512,512]{1,0:T(8,128)(2,1)S(1)}, bf16[512,512]{1,0:T(8,128)(2,1)S(1)}) custom-call(s32[3]{0:T(128)S(1)} %pad_add_fusion.part_ref, s32[2,8]{1,0:T(2,128)S(1)} %select_reduce_fusion.1.slash_ref, f32[64,1536]{1,0:T(8,128)S(1)} %copy-done.6, bf16[2048,1024]{1,0:T(8,128)(2,1)S(1)} %copy-done.1, ...), custom_call_target="tpu_custom_call" | custom-call | flops 4831838208 | bytes 6291456 | tf_op jit(solution)/shard_map/pallas_call | solution.py:322
  118.9 1.3 collective-permute-start.8
  120.3 0.6 collective-permute-start.9
  120.8 0.5 broadcast_in_dim.14
  121.4 1.7 %shard_map.67.window = bf16[6144,256]{1,0:T(8,128)(2,1)S(1)} custom-call(s32[1]{0:T(128)} %bitcast.1.parity_ref, bf16[2048,256]{1,0:T(8,128)(2,1)} %collective-permute-done.10.rest_1_.rest_0_, bf16[2048,256]{1,0:T(8,128)(2,1)} %collective-permute-done.11.rest_1_, bf16[2048,256]{1,0:T(8,128)(2,1)S(1)} %shard_map.65.rest_0_.rest_2_), custom_call_target="tpu_custom_call" | custom-call | bytes 6291456 | tf_op jit(solution)/shard_map/pallas_call | solution.py:128
  123.2 1.0 copy-done.2
  124.2 7.2 %shard_map.68.rest_0_ = bf16[512,512]{1,0:T(8,128)(2,1)S(1)} custom-call(s32[1]{0:T(128)} %bitcast.part_ref, s32[2,8]{1,0:T(2,128)S(1)} %select_reduce_fusion.1.slash_ref, f32[64,1536]{1,0:T(8,128)S(1)} %copy-done.7, bf16[2048,1024]{1,0:T(8,128)(2,1)S(1)} %copy-done.2, bf16[2,1024,256]{2,1,0:T(8,128)(2,1)S(1)} %shard_map.61.vert_ref, ...), custom_call_target="tpu_custom_call" | custom-call | flops 1610612736 | bytes 4194304 | tf_op jit(solution)/shard_map/pallas_call | solution.py:322
  131.4 0.9 collective-permute-start.12
  132.4 7.2 %shard_map.69.rest_0_ = bf16[512,512]{1,0:T(8,128)(2,1)S(1)} custom-call(s32[1]{0:T(128)} %bitcast.2.part_ref, s32[2,8]{1,0:T(2,128)S(1)} %select_reduce_fusion.1.slash_ref, f32[64,1536]{1,0:T(8,128)S(1)} %copy-done.7, bf16[2048,1024]{1,0:T(8,128)(2,1)S(1)} %copy-done.2, bf16[2,1024,256]{2,1,0:T(8,128)(2,1)S(1)} %shard_map.61.vert_ref, ...), custom_call_target="tpu_custom_call" | custom-call | flops 1610612736 | bytes 4194304 | tf_op jit(solution)/shard_map/pallas_call | solution.py:322
  139.5 0.8 collective-permute-start.13
  140.3 12.7 %shard_map.70 = (bf16[512,512]{1,0:T(8,128)(2,1)S(1)}, bf16[512,512]{1,0:T(8,128)(2,1)S(1)}) custom-call(s32[2]{0:T(128)S(1)} %pad_add_fusion.1.part_ref, s32[2,8]{1,0:T(2,128)S(1)} %select_reduce_fusion.1.slash_ref, f32[64,1536]{1,0:T(8,128)S(1)} %copy-done.7, bf16[2048,1024]{1,0:T(8,128)(2,1)S(1)} %copy-done.2, ...), custom_call_target="tpu_custom_call" | custom-call | flops 3221225472 | bytes 5242880 | tf_op jit(solution)/shard_map/pallas_call | solution.py:322
  153.7 3.2 %collective-permute-done.13 = bf16[512,512]{1,0:T(8,128)(2,1)S(1)} collective-permute-done((bf16[512,512]{1,0:T(8,128)(2,1)S(1)}, bf16[512,512]{1,0:T(8,128)(2,1)S(1)}, u32[]{:S(2)}, u32[]{:S(2)}) %collective-permute-start.13) | collective-permute-done | bytes 524320 | tf_op jit(solution)/shard_map/ppermute | solution.py:471
  157.1 2.0 %copy-done.17 = bf16[512,4096]{1,0:T(8,128)(2,1)} copy-done((bf16[512,4096]{1,0:T(8,128)(2,1)}, bf16[512,4096]{1,0:T(8,128)(2,1)S(1)}, u32[]{:S(2)}) %copy-start.17) | copy-done | bytes 4194328
  159.1 0.8 constant_dynamic-update-slice_fusion
  (85 shorter events, 3.7 us)
Async XLA Ops:
  0.0 28.3 %copy-start.18 = (s32[2,16]{1,0:T(2,128)S(1)}, s32[2,16]{1,0:T(2,128)}, u32[]{:S(2)}) copy-start(s32[2,16]{1,0:T(2,128)} %param.8) | copy-start | bytes 388
  1.8 1.2 copy-start.13
  3.0 1.2 copy-start.15
  6.2 18.4 %collective-permute-start = (bf16[1152,256]{1,0:T(8,128)(2,1)S(1)}, bf16[1152,256]{1,0:T(8,128)(2,1)S(1)}, u32[]{:S(2)}, u32[]{:S(2)}) collective-permute-start(bf16[1152,256]{1,0:T(8,128)(2,1)S(1)} %get-tuple-element.14), channel_id=1, source_target_pairs={{0,8},{4,12},{8,16},{12,20},{16,24},{20,28},{24,0},{28,4},{1,9},{5... | collective-permute-start | bytes 1769480 | tf_op jit(solution)/shard_map/ppermute | solution.py:425
  9.3 71.8 %collective-permute-start.4 = (bf16[512,256]{1,0:T(8,128)(2,1)}, bf16[512,256]{1,0:T(8,128)(2,1)}, u32[]{:S(2)}, u32[]{:S(2)}) collective-permute-start(bf16[512,256]{1,0:T(8,128)(2,1)} %get-tuple-element.13.rest_0_), channel_id=1, source_target_pairs={{0,4},{4,0},{8,12},{12,8},{16,20},{20,16},{24,28},{28,24},{1,5},{5... | collective-permute-start | bytes 786440 | tf_op jit(solution)/shard_map/ppermute | solution.py:427
  25.6 20.3 %collective-permute-start.2 = (bf16[1152,256]{1,0:T(8,128)(2,1)}, bf16[1152,256]{1,0:T(8,128)(2,1)S(1)}, u32[]{:S(2)}, u32[]{:S(2)}) collective-permute-start(bf16[1152,256]{1,0:T(8,128)(2,1)} %shard_map.56.rest_2_), channel_id=1, source_target_pairs={{0,4},{4,0},{8,12},{12,8},{16,20},{20,16},{24,28},{28,24},{1,5},{5... | collective-permute-start | bytes 1769480 | tf_op jit(solution)/shard_map/ppermute | solution.py:431
  28.2 16.8 %collective-permute-start.1 = (bf16[1216,256]{1,0:T(8,128)(2,1)}, bf16[1216,256]{1,0:T(8,128)(2,1)S(1)}, u32[]{:S(2)}, u32[]{:S(2)}) collective-permute-start(bf16[1216,256]{1,0:T(8,128)(2,1)} %shard_map.57), channel_id=1, source_target_pairs={{0,8},{4,12},{8,16},{12,20},{16,24},{20,28},{24,0},{28,4},{1,9},{5... | collective-permute-start | bytes 1867784 | tf_op jit(solution)/shard_map/ppermute | solution.py:425
  29.2 17.6 %copy-start.14 = (bf16[2048,256]{1,0:T(8,128)(2,1)S(1)}, bf16[2048,256]{1,0:T(8,128)(2,1)}, u32[]{:S(2)}) copy-start(bf16[2048,256]{1,0:T(8,128)(2,1)} %keys_ref.3) | copy-start | bytes 3145732
  29.2 17.6 %copy-start.16 = (bf16[2048,256]{1,0:T(8,128)(2,1)S(1)}, bf16[2048,256]{1,0:T(8,128)(2,1)}, u32[]{:S(2)}) copy-start(bf16[2048,256]{1,0:T(8,128)(2,1)} %values_ref.3) | copy-start | bytes 3145732
  46.0 0.8 copy-start.11
  46.2 18.8 %collective-permute-start.3 = (bf16[1216,256]{1,0:T(8,128)(2,1)S(1)}, bf16[1216,256]{1,0:T(8,128)(2,1)S(1)}, u32[]{:S(2)}, u32[]{:S(2)}) collective-permute-start(bf16[1216,256]{1,0:T(8,128)(2,1)S(1)} %shard_map.59.rest_1_), channel_id=1, source_target_pairs={{0,8},{4,12},{8,16},{12,20},{16,24},{20,28},{24,0},{28,4},{1,9},{5... | collective-permute-start | bytes 1867784 | tf_op jit(solution)/shard_map/ppermute | solution.py:425
  47.0 45.0 %collective-permute-start.10 = (bf16[2048,256]{1,0:T(8,128)(2,1)S(1)}, bf16[2048,256]{1,0:T(8,128)(2,1)}, u32[]{:S(2)}, u32[]{:S(2)}) collective-permute-start(bf16[2048,256]{1,0:T(8,128)(2,1)S(1)} %shard_map.65.rest_0_.rest_2_), channel_id=1, source_target_pairs={{0,8},{4,12},{8,16},{12,20},{16,24},{20,28},{24,0},{28,4},{1,9},{5... | collective-permute-start | bytes 3145736 | tf_op jit(solution)/shard_map/ppermute | solution.py:438
  47.1 21.1 %collective-permute-start.5 = (bf16[1216,256]{1,0:T(8,128)(2,1)}, bf16[1216,256]{1,0:T(8,128)(2,1)}, u32[]{:S(2)}, u32[]{:S(2)}) collective-permute-start(bf16[1216,256]{1,0:T(8,128)(2,1)} %shard_map.58.rest_2_), channel_id=1, source_target_pairs={{0,4},{4,0},{8,12},{12,8},{16,20},{20,16},{24,28},{28,24},{1,5},{5... | collective-permute-start | bytes 1867784 | tf_op jit(solution)/shard_map/ppermute | solution.py:431
  66.0 0.8 copy-start.8
  66.8 10.6 %collective-permute-start.6 = (bf16[1216,256]{1,0:T(8,128)(2,1)}, bf16[1216,256]{1,0:T(8,128)(2,1)}, u32[]{:S(2)}, u32[]{:S(2)}) collective-permute-start(bf16[1216,256]{1,0:T(8,128)(2,1)} %shard_map.60), channel_id=1, source_target_pairs={{0,4},{4,0},{8,12},{12,8},{16,20},{20,16},{24,28},{28,24},{1,5},{5... | collective-permute-start | bytes 1867784 | tf_op jit(solution)/shard_map/ppermute | solution.py:431
  68.2 16.3 %copy-start.5 = (f32[64,1536]{1,0:T(8,128)}, f32[64,1536]{1,0:T(8,128)S(1)}, u32[]{:S(2)}) copy-start(f32[64,1536]{1,0:T(8,128)S(1)} %fusion.bias_ref) | copy-start | bytes 1179652
  77.4 1.1 copy-start.9
  78.5 1.1 copy-start.12
  79.5 1.6 %copy-start.10 = (bf16[1216,256]{1,0:T(8,128)(2,1)S(1)}, bf16[1216,256]{1,0:T(8,128)(2,1)}, u32[]{:S(2)}) copy-start(bf16[1216,256]{1,0:T(8,128)(2,1)} %copy-done.8) | copy-start | bytes 1867780
  81.1 10.9 %copy-start.3 = (bf16[6144,256]{1,0:T(8,128)(2,1)}, bf16[6144,256]{1,0:T(8,128)(2,1)S(1)}, u32[]{:S(2)}) copy-start(bf16[6144,256]{1,0:T(8,128)(2,1)S(1)} %shard_map.62.window) | copy-start | bytes 9437188
  81.1 3.7 %copy-start = (bf16[2048,1024]{1,0:T(8,128)(2,1)S(1)}, bf16[2048,1024]{1,0:T(8,128)(2,1)}, u32[]{:S(2)}) copy-start(bf16[2048,1024]{1,0:T(8,128)(2,1)} %query_ref.9) | copy-start | bytes 12582916
  93.3 28.1 %collective-permute-start.11 = (bf16[2048,256]{1,0:T(8,128)(2,1)}, bf16[2048,256]{1,0:T(8,128)(2,1)}, u32[]{:S(2)}, u32[]{:S(2)}) collective-permute-start(bf16[2048,256]{1,0:T(8,128)(2,1)} %shard_map.66), channel_id=1, source_target_pairs={{0,4},{4,0},{8,12},{12,8},{16,20},{20,16},{24,28},{28,24},{1,5},{5... | collective-permute-start | bytes 3145736 | tf_op jit(solution)/shard_map/ppermute | solution.py:467
  95.4 25.5 %collective-permute-start.7 = (bf16[512,512]{1,0:T(8,128)(2,1)S(1)}, bf16[512,512]{1,0:T(8,128)(2,1)S(1)}, u32[]{:S(2)}, u32[]{:S(2)}) collective-permute-start(bf16[512,512]{1,0:T(8,128)(2,1)S(1)} %shard_map.63.rest_0_.rest_2_), channel_id=1, source_target_pairs={{0,3},{1,2},{2,1},{3,0},{4,7},{5,6},{6,5},{7,4},{8,11},{9,10},{10,... | collective-permute-start | bytes 1572872 | tf_op jit(solution)/shard_map/ppermute | solution.py:471
  95.5 2.2 %copy-start.1 = (bf16[2048,1024]{1,0:T(8,128)(2,1)S(1)}, bf16[2048,1024]{1,0:T(8,128)(2,1)}, u32[]{:S(2)}) copy-start(bf16[2048,1024]{1,0:T(8,128)(2,1)} %query_ref.9) | copy-start | bytes 12582916
  97.6 1.9 %copy-start.4 = (bf16[6144,256]{1,0:T(8,128)(2,1)S(1)}, bf16[6144,256]{1,0:T(8,128)(2,1)}, u32[]{:S(2)}) copy-start(bf16[6144,256]{1,0:T(8,128)(2,1)} %copy-done.3) | copy-start | bytes 9437188
  99.5 1.0 copy-start.6
  118.9 34.5 %collective-permute-start.8 = (bf16[512,512]{1,0:T(8,128)(2,1)S(1)}, bf16[512,512]{1,0:T(8,128)(2,1)S(1)}, u32[]{:S(2)}, u32[]{:S(2)}) collective-permute-start(bf16[512,512]{1,0:T(8,128)(2,1)S(1)} %get-tuple-element.16), channel_id=1, source_target_pairs={{0,2},{1,3},{2,0},{3,1},{4,6},{5,7},{6,4},{7,5},{8,10},{9,11},{10,... | collective-permute-start | bytes 1572872 | tf_op jit(solution)/shard_map/ppermute | solution.py:471
  120.3 33.2 %collective-permute-start.9 = (bf16[512,512]{1,0:T(8,128)(2,1)S(1)}, bf16[512,512]{1,0:T(8,128)(2,1)S(1)}, u32[]{:S(2)}, u32[]{:S(2)}) collective-permute-start(bf16[512,512]{1,0:T(8,128)(2,1)S(1)} %get-tuple-element.17), channel_id=1, source_target_pairs={{0,1},{1,0},{2,3},{3,2},{4,5},{5,4},{6,7},{7,6},{8,9},{9,8},{10,11... | collective-permute-start | bytes 1572872 | tf_op jit(solution)/shard_map/ppermute | solution.py:471
  121.3 2.8 %copy-start.2 = (bf16[2048,1024]{1,0:T(8,128)(2,1)S(1)}, bf16[2048,1024]{1,0:T(8,128)(2,1)}, u32[]{:S(2)}) copy-start(bf16[2048,1024]{1,0:T(8,128)(2,1)} %query_ref.9) | copy-start | bytes 12582916
  121.4 2.9 %copy-start.7 = (f32[64,1536]{1,0:T(8,128)S(1)}, f32[64,1536]{1,0:T(8,128)}, u32[]{:S(2)}) copy-start(f32[64,1536]{1,0:T(8,128)} %copy-done.5) | copy-start | bytes 1179652
  131.4 22.2 %collective-permute-start.12 = (bf16[512,512]{1,0:T(8,128)(2,1)S(1)}, bf16[512,512]{1,0:T(8,128)(2,1)S(1)}, u32[]{:S(2)}, u32[]{:S(2)}) collective-permute-start(bf16[512,512]{1,0:T(8,128)(2,1)S(1)} %shard_map.68.rest_0_), channel_id=1, source_target_pairs={{0,3},{1,2},{2,1},{3,0},{4,7},{5,6},{6,5},{7,4},{8,11},{9,10},{10,... | collective-permute-start | bytes 1572872 | tf_op jit(solution)/shard_map/ppermute | solution.py:471
  139.5 17.4 %collective-permute-start.13 = (bf16[512,512]{1,0:T(8,128)(2,1)S(1)}, bf16[512,512]{1,0:T(8,128)(2,1)S(1)}, u32[]{:S(2)}, u32[]{:S(2)}) collective-permute-start(bf16[512,512]{1,0:T(8,128)(2,1)S(1)} %shard_map.69.rest_0_), channel_id=1, source_target_pairs={{0,2},{1,3},{2,0},{3,1},{4,6},{5,7},{6,4},{7,5},{8,10},{9,11},{10,... | collective-permute-start | bytes 1572872 | tf_op jit(solution)/shard_map/ppermute | solution.py:471
  153.1 3.9 %collective-permute-start.14 = (bf16[512,512]{1,0:T(8,128)(2,1)S(1)}, bf16[512,512]{1,0:T(8,128)(2,1)S(1)}, u32[]{:S(2)}, u32[]{:S(2)}) collective-permute-start(bf16[512,512]{1,0:T(8,128)(2,1)S(1)} %get-tuple-element.19), channel_id=1, source_target_pairs={{0,1},{1,0},{2,3},{3,2},{4,5},{5,4},{6,7},{7,6},{8,9},{9,8},{10,11... | collective-permute-start | bytes 1572872 | tf_op jit(solution)/shard_map/ppermute | solution.py:471
  157.1 2.0 %copy-start.17 = (bf16[512,4096]{1,0:T(8,128)(2,1)}, bf16[512,4096]{1,0:T(8,128)(2,1)S(1)}, u32[]{:S(2)}) copy-start(bf16[512,4096]{1,0:T(8,128)(2,1)S(1)} %constant_dynamic-update-slice_fusion.1) | copy-start | bytes 12582916

commit v12 on v11

--- a/solution.py
+++ b/solution.py
@@ -346,7 +346,7 @@
             ],
         ),
         compiler_params=pltpu.CompilerParams(
-            dimension_semantics=("arbitrary",), vmem_limit_bytes=32 << 20
+            dimension_semantics=("arbitrary",), vmem_limit_bytes=18 << 20
         ),
         cost_estimate=pl.CostEstimate(
             flops=4 * parts * part_rows * group_heads * keys_seen * HD,

time: 160 us -> 160 us (level)
  no operation moved by 1% of the time
where the time goes in v12:
time: 160 us
  Pallas kernels  66.7 us (42%)
  waiting for transfers between devices  56.3 us (35%)
  local copies, waits for them, and re-layouts  17.4 us (11%)
  starting transfers between devices  13.9 us (9%)
  other arithmetic  4.97 us (3%)
    pallas_call x5, Pallas kernels, attend(): pl.pallas_call(functools.partial(attend_kernel, head, parts, len(after),...  52.6 us
    ppermute x3, waiting for transfers between devices, local(): come = lax.ppermute(send, 'ctx', two_pairs)  43.8 us
    unnamed x40, local copies, waits for them, and re-layouts  14.7 us
    ppermute x3, waiting for transfers between devices, local(): one_back.append(lax.ppermute(cross, 'ctx', across_pairs))  9.19 us
    pallas_call x8, Pallas kernels, joined(): pl.pallas_call(functools.partial(joined_kernel, plan), out_shape=jax.Shap...  8.69 us
    ppermute x6, starting transfers between devices, local(): lax.ppermute(piece, 'head', [(i, i ^ flip) for i in range(head_count)])  3.98 us
    pallas_call x1, Pallas kernels, listed_blocks(): pl.pallas_call(functools.partial(listed_kernel, [low for _, low in slots]...  3.27 us
    ppermute x6, waiting for transfers between devices, local(): lax.ppermute(piece, 'head', [(i, i ^ flip) for i in range(head_count)])  3.24 us
  transfers between devices with their start and end apart: 15, of which 5 were waited for; matrix products, arithmetic and copies ran while one was open for 3% of the time, Pallas kernels for 40%

profile of v12, /device:TPU:0, one launch (start us, length us, event | category | flops | bytes accessed | tf_op | source)
XLA Modules:
  0.0 159.9 jit_solution(13289621258359135693)
XLA Ops:
  0.0 0.8 and_select_fusion
  0.8 0.7 broadcast_compare_fusion.2
  1.8 1.2 copy-done.13
  3.0 1.2 copy-done.15
  4.2 2.0 %shard_map.55 = (bf16[2048,256]{1,0:T(8,128)(2,1)S(1)}, bf16[1152,256]{1,0:T(8,128)(2,1)S(1)}, bf16[512,256]{1,0:T(8,128)(2,1)}) custom-call(s32[2,4]{1,0:T(2,128)S(1)} %select_reduce_fusion.2.local_ref, bf16[2048,256]{1,0:T(8,128)(2,1)S(1)} %copy-done.13, bf16[2048,256]{1,0:T(8,128)(2,1)S(1)} %copy-done.15), custom_call_target="tpu_custom_call" | custom-call | bytes 4194304 | tf_op jit(solution)/shard_map/pallas_call | solution.py:59
  6.2 3.1 %collective-permute-start = (bf16[1152,256]{1,0:T(8,128)(2,1)S(1)}, bf16[1152,256]{1,0:T(8,128)(2,1)S(1)}, u32[]{:S(2)}, u32[]{:S(2)}) collective-permute-start(bf16[1152,256]{1,0:T(8,128)(2,1)S(1)} %get-tuple-element.14), channel_id=1, source_target_pairs={{0,8},{4,12},{8,16},{12,20},{16,24},{20,28},{24,0},{28,4},{1,9},{5... | collective-permute-start | bytes 1769480 | tf_op jit(solution)/shard_map/ppermute | solution.py:425
  9.3 1.5 collective-permute-start.4
  10.8 1.0 convert_reduce_fusion.1
  11.8 0.8 select_reduce_fusion.1.slash_ref
  12.6 0.8 compare_reduce_fusion
  13.4 11.2 %collective-permute-done.rest_1_.rest_0_ = bf16[1152,256]{1,0:T(8,128)(2,1)S(1)} collective-permute-done((bf16[1152,256]{1,0:T(8,128)(2,1)S(1)}, bf16[1152,256]{1,0:T(8,128)(2,1)S(1)}, u32[]{:S(2)}, u32[]{:S(2)}) %collective-permute-start) | collective-permute-done | bytes 589856 | tf_op jit(solution)/shard_map/ppermute | solution.py:425
  24.7 1.0 shard_map.56.rest_2_
  25.6 1.5 collective-permute-start.2
  27.2 1.0 shard_map.57
  29.4 15.6 %collective-permute-done.1.rest_1_.rest_2_.rest_0_ = bf16[1216,256]{1,0:T(8,128)(2,1)S(1)} collective-permute-done((bf16[1216,256]{1,0:T(8,128)(2,1)}, bf16[1216,256]{1,0:T(8,128)(2,1)S(1)}, u32[]{:S(2)}, u32[]{:S(2)}) %collective-permute-start.1) | collective-permute-done | bytes 622624 | tf_op jit(solution)/shard_map/ppermute | solution.py:425
  44.9 1.0 shard_map.58.rest_2_
  46.2 0.5 copy-done.11
  47.1 0.8 collective-permute-start.5
  47.9 17.0 %collective-permute-done.3.rest_1_.rest_3_.rest_2_ = bf16[1216,256]{1,0:T(8,128)(2,1)S(1)} collective-permute-done((bf16[1216,256]{1,0:T(8,128)(2,1)S(1)}, bf16[1216,256]{1,0:T(8,128)(2,1)S(1)}, u32[]{:S(2)}, u32[]{:S(2)}) %collective-permute-start.3) | collective-permute-done | bytes 622624 | tf_op jit(solution)/shard_map/ppermute | solution.py:425
  65.0 1.0 shard_map.60
  66.0 0.8 copy-done.8
  66.8 0.8 collective-permute-start.6
  68.2 9.2 %collective-permute-done.6.rest_7_.rest_5_ = bf16[1216,256]{1,0:T(8,128)(2,1)} collective-permute-done((bf16[1216,256]{1,0:T(8,128)(2,1)}, bf16[1216,256]{1,0:T(8,128)(2,1)}, u32[]{:S(2)}, u32[]{:S(2)}) %collective-permute-start.6) | collective-permute-done | bytes 622624 | tf_op jit(solution)/shard_map/ppermute | solution.py:431
  77.4 1.1 copy-done.9
  78.5 1.1 copy-done.12
  79.5 1.6 shard_map.62.window
  81.2 3.3 %shard_map.61.vert_ref = bf16[2,1024,256]{2,1,0:T(8,128)(2,1)S(1)} custom-call(s32[8,2,4]{2,1,0:T(2,128)S(1)} %broadcast_add_fusion.place_ref, s32[2,16]{1,0:T(2,128)S(1)} %compare_select_fusion.1.source_ref, bf16[512,256]{1,0:T(8,128)(2,1)} %get-tuple-element.13.rest_0_, bf16[1152,256]{1,0:T(8,128)(2,1)S(1)} %collective-permute-done.rest_1_.rest_0_, ...), custom_call_target="tpu_custom_call" | custom-call | bytes 2097152 | tf_op jit(solution)/shard_map/pallas_call | solution.py:164
  84.5 0.4 copy-done
  84.9 7.2 %shard_map.63.rest_0_.rest_2_ = bf16[512,512]{1,0:T(8,128)(2,1)S(1)} custom-call(s32[1]{0:T(128)} %bitcast.part_ref, s32[2,8]{1,0:T(2,128)S(1)} %select_reduce_fusion.1.slash_ref, f32[64,1536]{1,0:T(8,128)S(1)} %fusion.bias_ref, bf16[2048,1024]{1,0:T(8,128)(2,1)S(1)} %copy-done, bf16[2,1024,256]{2,1,0:T(8,128)(2,1)S(1)} %shard_map.61.vert_ref, ...), custom_call_target="tpu_custom_call" | custom-call | flops 1610612736 | bytes 4194304 | tf_op jit(solution)/shard_map/pallas_call | solution.py:322
  92.0 1.3 shard_map.66
  93.3 2.0 %collective-permute-start.11 = (bf16[2048,256]{1,0:T(8,128)(2,1)}, bf16[2048,256]{1,0:T(8,128)(2,1)}, u32[]{:S(2)}, u32[]{:S(2)}) collective-permute-start(bf16[2048,256]{1,0:T(8,128)(2,1)} %shard_map.66), channel_id=1, source_target_pairs={{0,4},{4,0},{8,12},{12,8},{16,20},{20,16},{24,28},{28,24},{1,5},{5... | collective-permute-start | bytes 3145736 | tf_op jit(solution)/shard_map/ppermute | solution.py:467
  95.5 2.2 %copy-done.1 = bf16[2048,1024]{1,0:T(8,128)(2,1)S(1)} copy-done((bf16[2048,1024]{1,0:T(8,128)(2,1)S(1)}, bf16[2048,1024]{1,0:T(8,128)(2,1)}, u32[]{:S(2)}) %copy-start.1) | copy-done | bytes 4194328
  97.6 1.9 %copy-done.4 = bf16[6144,256]{1,0:T(8,128)(2,1)S(1)} copy-done((bf16[6144,256]{1,0:T(8,128)(2,1)S(1)}, bf16[6144,256]{1,0:T(8,128)(2,1)}, u32[]{:S(2)}) %copy-start.4) | copy-done | bytes 3145752
  99.5 1.0 copy-done.6
  100.5 18.4 %shard_map.64 = (bf16[512,512]{1,0:T(8,128)(2,1)S(1)}, bf16[512,512]{1,0:T(8,128)(2,1)S(1)}, bf16[512,512]{1,0:T(8,128)(2,1)S(1)}) custom-call(s32[3]{0:T(128)S(1)} %pad_add_fusion.part_ref, s32[2,8]{1,0:T(2,128)S(1)} %select_reduce_fusion.1.slash_ref, f32[64,1536]{1,0:T(8,128)S(1)} %copy-done.6, bf16[2048,1024]{1,0:T(8,128)(2,1)S(1)} %copy-done.1, ...), custom_call_target="tpu_custom_call" | custom-call | flops 4831838208 | bytes 6291456 | tf_op jit(solution)/shard_map/pallas_call | solution.py:322
  118.9 1.3 collective-permute-start.8
  120.3 0.6 collective-permute-start.9
  120.8 0.5 broadcast_in_dim.14
  121.4 1.7 %shard_map.67.window = bf16[6144,256]{1,0:T(8,128)(2,1)S(1)} custom-call(s32[1]{0:T(128)} %bitcast.1.parity_ref, bf16[2048,256]{1,0:T(8,128)(2,1)} %collective-permute-done.10.rest_1_.rest_0_, bf16[2048,256]{1,0:T(8,128)(2,1)} %collective-permute-done.11.rest_1_, bf16[2048,256]{1,0:T(8,128)(2,1)S(1)} %shard_map.65.rest_0_.rest_2_), custom_call_target="tpu_custom_call" | custom-call | bytes 6291456 | tf_op jit(solution)/shard_map/pallas_call | solution.py:128
  123.2 1.0 copy-done.2
  124.2 7.2 %shard_map.68.rest_0_ = bf16[512,512]{1,0:T(8,128)(2,1)S(1)} custom-call(s32[1]{0:T(128)} %bitcast.part_ref, s32[2,8]{1,0:T(2,128)S(1)} %select_reduce_fusion.1.slash_ref, f32[64,1536]{1,0:T(8,128)S(1)} %copy-done.7, bf16[2048,1024]{1,0:T(8,128)(2,1)S(1)} %copy-done.2, bf16[2,1024,256]{2,1,0:T(8,128)(2,1)S(1)} %shard_map.61.vert_ref, ...), custom_call_target="tpu_custom_call" | custom-call | flops 1610612736 | bytes 4194304 | tf_op jit(solution)/shard_map/pallas_call | solution.py:322
  131.4 0.9 collective-permute-start.12
  132.4 7.2 %shard_map.69.rest_0_ = bf16[512,512]{1,0:T(8,128)(2,1)S(1)} custom-call(s32[1]{0:T(128)} %bitcast.2.part_ref, s32[2,8]{1,0:T(2,128)S(1)} %select_reduce_fusion.1.slash_ref, f32[64,1536]{1,0:T(8,128)S(1)} %copy-done.7, bf16[2048,1024]{1,0:T(8,128)(2,1)S(1)} %copy-done.2, bf16[2,1024,256]{2,1,0:T(8,128)(2,1)S(1)} %shard_map.61.vert_ref, ...), custom_call_target="tpu_custom_call" | custom-call | flops 1610612736 | bytes 4194304 | tf_op jit(solution)/shard_map/pallas_call | solution.py:322
  139.5 0.8 collective-permute-start.13
  140.3 12.7 %shard_map.70 = (bf16[512,512]{1,0:T(8,128)(2,1)S(1)}, bf16[512,512]{1,0:T(8,128)(2,1)S(1)}) custom-call(s32[2]{0:T(128)S(1)} %pad_add_fusion.1.part_ref, s32[2,8]{1,0:T(2,128)S(1)} %select_reduce_fusion.1.slash_ref, f32[64,1536]{1,0:T(8,128)S(1)} %copy-done.7, bf16[2048,1024]{1,0:T(8,128)(2,1)S(1)} %copy-done.2, ...), custom_call_target="tpu_custom_call" | custom-call | flops 3221225472 | bytes 5242880 | tf_op jit(solution)/shard_map/pallas_call | solution.py:322
  153.7 3.2 %collective-permute-done.13 = bf16[512,512]{1,0:T(8,128)(2,1)S(1)} collective-permute-done((bf16[512,512]{1,0:T(8,128)(2,1)S(1)}, bf16[512,512]{1,0:T(8,128)(2,1)S(1)}, u32[]{:S(2)}, u32[]{:S(2)}) %collective-permute-start.13) | collective-permute-done | bytes 524320 | tf_op jit(solution)/shard_map/ppermute | solution.py:471
  157.1 2.0 %copy-done.17 = bf16[512,4096]{1,0:T(8,128)(2,1)} copy-done((bf16[512,4096]{1,0:T(8,128)(2,1)}, bf16[512,4096]{1,0:T(8,128)(2,1)S(1)}, u32[]{:S(2)}) %copy-start.17) | copy-done | bytes 4194328
  159.1 0.8 constant_dynamic-update-slice_fusion
  (85 shorter events, 3.7 us)
Async XLA Ops:
  0.0 28.3 %copy-start.18 = (s32[2,16]{1,0:T(2,128)S(1)}, s32[2,16]{1,0:T(2,128)}, u32[]{:S(2)}) copy-start(s32[2,16]{1,0:T(2,128)} %param.8) | copy-start | bytes 388
  1.8 1.2 copy-start.13
  3.0 1.2 copy-start.15
  6.2 18.4 %collective-permute-start = (bf16[1152,256]{1,0:T(8,128)(2,1)S(1)}, bf16[1152,256]{1,0:T(8,128)(2,1)S(1)}, u32[]{:S(2)}, u32[]{:S(2)}) collective-permute-start(bf16[1152,256]{1,0:T(8,128)(2,1)S(1)} %get-tuple-element.14), channel_id=1, source_target_pairs={{0,8},{4,12},{8,16},{12,20},{16,24},{20,28},{24,0},{28,4},{1,9},{5... | collective-permute-start | bytes 1769480 | tf_op jit(solution)/shard_map/ppermute | solution.py:425
  9.3 71.8 %collective-permute-start.4 = (bf16[512,256]{1,0:T(8,128)(2,1)}, bf16[512,256]{1,0:T(8,128)(2,1)}, u32[]{:S(2)}, u32[]{:S(2)}) collective-permute-start(bf16[512,256]{1,0:T(8,128)(2,1)} %get-tuple-element.13.rest_0_), channel_id=1, source_target_pairs={{0,4},{4,0},{8,12},{12,8},{16,20},{20,16},{24,28},{28,24},{1,5},{5... | collective-permute-start | bytes 786440 | tf_op jit(solution)/shard_map/ppermute | solution.py:427
  25.6 20.3 %collective-permute-start.2 = (bf16[1152,256]{1,0:T(8,128)(2,1)}, bf16[1152,256]{1,0:T(8,128)(2,1)S(1)}, u32[]{:S(2)}, u32[]{:S(2)}) collective-permute-start(bf16[1152,256]{1,0:T(8,128)(2,1)} %shard_map.56.rest_2_), channel_id=1, source_target_pairs={{0,4},{4,0},{8,12},{12,8},{16,20},{20,16},{24,28},{28,24},{1,5},{5... | collective-permute-start | bytes 1769480 | tf_op jit(solution)/shard_map/ppermute | solution.py:431
  28.2 16.8 %collective-permute-start.1 = (bf16[1216,256]{1,0:T(8,128)(2,1)}, bf16[1216,256]{1,0:T(8,128)(2,1)S(1)}, u32[]{:S(2)}, u32[]{:S(2)}) collective-permute-start(bf16[1216,256]{1,0:T(8,128)(2,1)} %shard_map.57), channel_id=1, source_target_pairs={{0,8},{4,12},{8,16},{12,20},{16,24},{20,28},{24,0},{28,4},{1,9},{5... | collective-permute-start | bytes 1867784 | tf_op jit(solution)/shard_map/ppermute | solution.py:425
  29.2 17.6 %copy-start.14 = (bf16[2048,256]{1,0:T(8,128)(2,1)S(1)}, bf16[2048,256]{1,0:T(8,128)(2,1)}, u32[]{:S(2)}) copy-start(bf16[2048,256]{1,0:T(8,128)(2,1)} %keys_ref.3) | copy-start | bytes 3145732
  29.2 17.6 %copy-start.16 = (bf16[2048,256]{1,0:T(8,128)(2,1)S(1)}, bf16[2048,256]{1,0:T(8,128)(2,1)}, u32[]{:S(2)}) copy-start(bf16[2048,256]{1,0:T(8,128)(2,1)} %values_ref.3) | copy-start | bytes 3145732
  46.0 0.8 copy-start.11
  46.2 18.8 %collective-permute-start.3 = (bf16[1216,256]{1,0:T(8,128)(2,1)S(1)}, bf16[1216,256]{1,0:T(8,128)(2,1)S(1)}, u32[]{:S(2)}, u32[]{:S(2)}) collective-permute-start(bf16[1216,256]{1,0:T(8,128)(2,1)S(1)} %shard_map.59.rest_1_), channel_id=1, source_target_pairs={{0,8},{4,12},{8,16},{12,20},{16,24},{20,28},{24,0},{28,4},{1,9},{5... | collective-permute-start | bytes 1867784 | tf_op jit(solution)/shard_map/ppermute | solution.py:425
  47.0 45.0 %collective-permute-start.10 = (bf16[2048,256]{1,0:T(8,128)(2,1)S(1)}, bf16[2048,256]{1,0:T(8,128)(2,1)}, u32[]{:S(2)}, u32[]{:S(2)}) collective-permute-start(bf16[2048,256]{1,0:T(8,128)(2,1)S(1)} %shard_map.65.rest_0_.rest_2_), channel_id=1, source_target_pairs={{0,8},{4,12},{8,16},{12,20},{16,24},{20,28},{24,0},{28,4},{1,9},{5... | collective-permute-start | bytes 3145736 | tf_op jit(solution)/shard_map/ppermute | solution.py:438
  47.1 21.1 %collective-permute-start.5 = (bf16[1216,256]{1,0:T(8,128)(2,1)}, bf16[1216,256]{1,0:T(8,128)(2,1)}, u32[]{:S(2)}, u32[]{:S(2)}) collective-permute-start(bf16[1216,256]{1,0:T(8,128)(2,1)} %shard_map.58.rest_2_), channel_id=1, source_target_pairs={{0,4},{4,0},{8,12},{12,8},{16,20},{20,16},{24,28},{28,24},{1,5},{5... | collective-permute-start | bytes 1867784 | tf_op jit(solution)/shard_map/ppermute | solution.py:431
  66.0 0.8 copy-start.8
  66.8 10.6 %collective-permute-start.6 = (bf16[1216,256]{1,0:T(8,128)(2,1)}, bf16[1216,256]{1,0:T(8,128)(2,1)}, u32[]{:S(2)}, u32[]{:S(2)}) collective-permute-start(bf16[1216,256]{1,0:T(8,128)(2,1)} %shard_map.60), channel_id=1, source_target_pairs={{0,4},{4,0},{8,12},{12,8},{16,20},{20,16},{24,28},{28,24},{1,5},{5... | collective-permute-start | bytes 1867784 | tf_op jit(solution)/shard_map/ppermute | solution.py:431
  68.2 16.3 %copy-start.5 = (f32[64,1536]{1,0:T(8,128)}, f32[64,1536]{1,0:T(8,128)S(1)}, u32[]{:S(2)}) copy-start(f32[64,1536]{1,0:T(8,128)S(1)} %fusion.bias_ref) | copy-start | bytes 1179652
  77.4 1.1 copy-start.9
  78.5 1.1 copy-start.12
  79.5 1.6 %copy-start.10 = (bf16[1216,256]{1,0:T(8,128)(2,1)S(1)}, bf16[1216,256]{1,0:T(8,128)(2,1)}, u32[]{:S(2)}) copy-start(bf16[1216,256]{1,0:T(8,128)(2,1)} %copy-done.8) | copy-start | bytes 1867780
  81.1 10.9 %copy-start.3 = (bf16[6144,256]{1,0:T(8,128)(2,1)}, bf16[6144,256]{1,0:T(8,128)(2,1)S(1)}, u32[]{:S(2)}) copy-start(bf16[6144,256]{1,0:T(8,128)(2,1)S(1)} %shard_map.62.window) | copy-start | bytes 9437188
  81.1 3.7 %copy-start = (bf16[2048,1024]{1,0:T(8,128)(2,1)S(1)}, bf16[2048,1024]{1,0:T(8,128)(2,1)}, u32[]{:S(2)}) copy-start(bf16[2048,1024]{1,0:T(8,128)(2,1)} %query_ref.9) | copy-start | bytes 12582916
  93.3 28.1 %collective-permute-start.11 = (bf16[2048,256]{1,0:T(8,128)(2,1)}, bf16[2048,256]{1,0:T(8,128)(2,1)}, u32[]{:S(2)}, u32[]{:S(2)}) collective-permute-start(bf16[2048,256]{1,0:T(8,128)(2,1)} %shard_map.66), channel_id=1, source_target_pairs={{0,4},{4,0},{8,12},{12,8},{16,20},{20,16},{24,28},{28,24},{1,5},{5... | collective-permute-start | bytes 3145736 | tf_op jit(solution)/shard_map/ppermute | solution.py:467
  95.4 25.5 %collective-permute-start.7 = (bf16[512,512]{1,0:T(8,128)(2,1)S(1)}, bf16[512,512]{1,0:T(8,128)(2,1)S(1)}, u32[]{:S(2)}, u32[]{:S(2)}) collective-permute-start(bf16[512,512]{1,0:T(8,128)(2,1)S(1)} %shard_map.63.rest_0_.rest_2_), channel_id=1, source_target_pairs={{0,3},{1,2},{2,1},{3,0},{4,7},{5,6},{6,5},{7,4},{8,11},{9,10},{10,... | collective-permute-start | bytes 1572872 | tf_op jit(solution)/shard_map/ppermute | solution.py:471
  95.5 2.2 %copy-start.1 = (bf16[2048,1024]{1,0:T(8,128)(2,1)S(1)}, bf16[2048,1024]{1,0:T(8,128)(2,1)}, u32[]{:S(2)}) copy-start(bf16[2048,1024]{1,0:T(8,128)(2,1)} %query_ref.9) | copy-start | bytes 12582916
  97.6 1.9 %copy-start.4 = (bf16[6144,256]{1,0:T(8,128)(2,1)S(1)}, bf16[6144,256]{1,0:T(8,128)(2,1)}, u32[]{:S(2)}) copy-start(bf16[6144,256]{1,0:T(8,128)(2,1)} %copy-done.3) | copy-start | bytes 9437188
  99.5 1.0 copy-start.6
  118.9 34.5 %collective-permute-start.8 = (bf16[512,512]{1,0:T(8,128)(2,1)S(1)}, bf16[512,512]{1,0:T(8,128)(2,1)S(1)}, u32[]{:S(2)}, u32[]{:S(2)}) collective-permute-start(bf16[512,512]{1,0:T(8,128)(2,1)S(1)} %get-tuple-element.16), channel_id=1, source_target_pairs={{0,2},{1,3},{2,0},{3,1},{4,6},{5,7},{6,4},{7,5},{8,10},{9,11},{10,... | collective-permute-start | bytes 1572872 | tf_op jit(solution)/shard_map/ppermute | solution.py:471
  120.3 33.2 %collective-permute-start.9 = (bf16[512,512]{1,0:T(8,128)(2,1)S(1)}, bf16[512,512]{1,0:T(8,128)(2,1)S(1)}, u32[]{:S(2)}, u32[]{:S(2)}) collective-permute-start(bf16[512,512]{1,0:T(8,128)(2,1)S(1)} %get-tuple-element.17), channel_id=1, source_target_pairs={{0,1},{1,0},{2,3},{3,2},{4,5},{5,4},{6,7},{7,6},{8,9},{9,8},{10,11... | collective-permute-start | bytes 1572872 | tf_op jit(solution)/shard_map/ppermute | solution.py:471
  121.3 2.8 %copy-start.2 = (bf16[2048,1024]{1,0:T(8,128)(2,1)S(1)}, bf16[2048,1024]{1,0:T(8,128)(2,1)}, u32[]{:S(2)}) copy-start(bf16[2048,1024]{1,0:T(8,128)(2,1)} %query_ref.9) | copy-start | bytes 12582916
  121.4 2.9 %copy-start.7 = (f32[64,1536]{1,0:T(8,128)S(1)}, f32[64,1536]{1,0:T(8,128)}, u32[]{:S(2)}) copy-start(f32[64,1536]{1,0:T(8,128)} %copy-done.5) | copy-start | bytes 1179652
  131.4 22.2 %collective-permute-start.12 = (bf16[512,512]{1,0:T(8,128)(2,1)S(1)}, bf16[512,512]{1,0:T(8,128)(2,1)S(1)}, u32[]{:S(2)}, u32[]{:S(2)}) collective-permute-start(bf16[512,512]{1,0:T(8,128)(2,1)S(1)} %shard_map.68.rest_0_), channel_id=1, source_target_pairs={{0,3},{1,2},{2,1},{3,0},{4,7},{5,6},{6,5},{7,4},{8,11},{9,10},{10,... | collective-permute-start | bytes 1572872 | tf_op jit(solution)/shard_map/ppermute | solution.py:471
  139.5 17.4 %collective-permute-start.13 = (bf16[512,512]{1,0:T(8,128)(2,1)S(1)}, bf16[512,512]{1,0:T(8,128)(2,1)S(1)}, u32[]{:S(2)}, u32[]{:S(2)}) collective-permute-start(bf16[512,512]{1,0:T(8,128)(2,1)S(1)} %shard_map.69.rest_0_), channel_id=1, source_target_pairs={{0,2},{1,3},{2,0},{3,1},{4,6},{5,7},{6,4},{7,5},{8,10},{9,11},{10,... | collective-permute-start | bytes 1572872 | tf_op jit(solution)/shard_map/ppermute | solution.py:471
  153.1 3.9 %collective-permute-start.14 = (bf16[512,512]{1,0:T(8,128)(2,1)S(1)}, bf16[512,512]{1,0:T(8,128)(2,1)S(1)}, u32[]{:S(2)}, u32[]{:S(2)}) collective-permute-start(bf16[512,512]{1,0:T(8,128)(2,1)S(1)} %get-tuple-element.19), channel_id=1, source_target_pairs={{0,1},{1,0},{2,3},{3,2},{4,5},{5,4},{6,7},{7,6},{8,9},{9,8},{10,11... | collective-permute-start | bytes 1572872 | tf_op jit(solution)/shard_map/ppermute | solution.py:471
  157.1 2.0 %copy-start.17 = (bf16[512,4096]{1,0:T(8,128)(2,1)}, bf16[512,4096]{1,0:T(8,128)(2,1)S(1)}, u32[]{:S(2)}) copy-start(bf16[512,4096]{1,0:T(8,128)(2,1)S(1)} %constant_dynamic-update-slice_fusion.1) | copy-start | bytes 12582916

commit v13 on v12

--- a/solution.py
+++ b/solution.py
@@ -16,7 +16,7 @@
 LOOK = 2
 NEG = -1e30
 STEP_BLOCKS = 2
-TILE = 256
+TILE = 512
 HBM = pl.BlockSpec(memory_space=pltpu.HBM)
 ANY = pl.BlockSpec(memory_space=pl.ANY)
 VMEM = pl.BlockSpec(memory_space=pltpu.VMEM)

time: 160 us -> 160 us (level)
  no operation moved by 1% of the time
where the time goes in v13:
time: 160 us
  Pallas kernels  66.5 us (42%)
  waiting for transfers between devices  56.3 us (35%)
  local copies, waits for them, and re-layouts  17.4 us (11%)
  starting transfers between devices  13.9 us (9%)
  other arithmetic  4.97 us (3%)
    pallas_call x5, Pallas kernels, attend(): pl.pallas_call(functools.partial(attend_kernel, head, parts, len(after),...  52.3 us
    ppermute x3, waiting for transfers between devices, local(): come = lax.ppermute(send, 'ctx', two_pairs)  43.8 us
    unnamed x40, local copies, waits for them, and re-layouts  14.7 us
    ppermute x3, waiting for transfers between devices, local(): one_back.append(lax.ppermute(cross, 'ctx', across_pairs))  9.19 us
    pallas_call x8, Pallas kernels, joined(): pl.pallas_call(functools.partial(joined_kernel, plan), out_shape=jax.Shap...  8.69 us
    ppermute x6, starting transfers between devices, local(): lax.ppermute(piece, 'head', [(i, i ^ flip) for i in range(head_count)])  3.97 us
    ppermute x6, waiting for transfers between devices, local(): lax.ppermute(piece, 'head', [(i, i ^ flip) for i in range(head_count)])  3.32 us
    pallas_call x1, Pallas kernels, listed_blocks(): pl.pallas_call(functools.partial(listed_kernel, [low for _, low in slots]...  3.27 us
  transfers between devices with their start and end apart: 15, of which 5 were waited for; matrix products, arithmetic and copies ran while one was open for 3% of the time, Pallas kernels for 40%

profile of v13, /device:TPU:0, one launch (start us, length us, event | category | flops | bytes accessed | tf_op | source)
XLA Modules:
  0.0 159.7 jit_solution(7771080586689195706)
XLA Ops:
  0.0 0.8 and_select_fusion
  0.8 0.7 broadcast_compare_fusion.2
  1.8 1.2 copy-done.13
  3.0 1.2 copy-done.15
  4.2 2.0 %shard_map.55 = (bf16[2048,256]{1,0:T(8,128)(2,1)S(1)}, bf16[1152,256]{1,0:T(8,128)(2,1)S(1)}, bf16[512,256]{1,0:T(8,128)(2,1)}) custom-call(s32[2,4]{1,0:T(2,128)S(1)} %select_reduce_fusion.2.local_ref, bf16[2048,256]{1,0:T(8,128)(2,1)S(1)} %copy-done.13, bf16[2048,256]{1,0:T(8,128)(2,1)S(1)} %copy-done.15), custom_call_target="tpu_custom_call" | custom-call | bytes 4194304 | tf_op jit(solution)/shard_map/pallas_call | solution.py:59
  6.2 3.1 %collective-permute-start = (bf16[1152,256]{1,0:T(8,128)(2,1)S(1)}, bf16[1152,256]{1,0:T(8,128)(2,1)S(1)}, u32[]{:S(2)}, u32[]{:S(2)}) collective-permute-start(bf16[1152,256]{1,0:T(8,128)(2,1)S(1)} %get-tuple-element.14), channel_id=1, source_target_pairs={{0,8},{4,12},{8,16},{12,20},{16,24},{20,28},{24,0},{28,4},{1,9},{5... | collective-permute-start | bytes 1769480 | tf_op jit(solution)/shard_map/ppermute | solution.py:425
  9.3 1.5 collective-permute-start.4
  10.8 1.0 convert_reduce_fusion.1
  11.8 0.8 select_reduce_fusion.1.slash_ref
  12.6 0.8 compare_reduce_fusion
  13.4 11.2 %collective-permute-done.rest_1_.rest_0_ = bf16[1152,256]{1,0:T(8,128)(2,1)S(1)} collective-permute-done((bf16[1152,256]{1,0:T(8,128)(2,1)S(1)}, bf16[1152,256]{1,0:T(8,128)(2,1)S(1)}, u32[]{:S(2)}, u32[]{:S(2)}) %collective-permute-start) | collective-permute-done | bytes 589856 | tf_op jit(solution)/shard_map/ppermute | solution.py:425
  24.7 1.0 shard_map.56.rest_2_
  25.6 1.5 collective-permute-start.2
  27.2 1.0 shard_map.57
  29.4 15.6 %collective-permute-done.1.rest_1_.rest_2_.rest_0_ = bf16[1216,256]{1,0:T(8,128)(2,1)S(1)} collective-permute-done((bf16[1216,256]{1,0:T(8,128)(2,1)}, bf16[1216,256]{1,0:T(8,128)(2,1)S(1)}, u32[]{:S(2)}, u32[]{:S(2)}) %collective-permute-start.1) | collective-permute-done | bytes 622624 | tf_op jit(solution)/shard_map/ppermute | solution.py:425
  44.9 1.0 shard_map.58.rest_2_
  46.2 0.5 copy-done.11
  47.1 0.8 collective-permute-start.5
  47.9 17.0 %collective-permute-done.3.rest_1_.rest_3_.rest_2_ = bf16[1216,256]{1,0:T(8,128)(2,1)S(1)} collective-permute-done((bf16[1216,256]{1,0:T(8,128)(2,1)S(1)}, bf16[1216,256]{1,0:T(8,128)(2,1)S(1)}, u32[]{:S(2)}, u32[]{:S(2)}) %collective-permute-start.3) | collective-permute-done | bytes 622624 | tf_op jit(solution)/shard_map/ppermute | solution.py:425
  65.0 1.0 shard_map.60
  66.0 0.8 copy-done.8
  66.8 0.8 collective-permute-start.6
  68.2 9.2 %collective-permute-done.6.rest_7_.rest_5_ = bf16[1216,256]{1,0:T(8,128)(2,1)} collective-permute-done((bf16[1216,256]{1,0:T(8,128)(2,1)}, bf16[1216,256]{1,0:T(8,128)(2,1)}, u32[]{:S(2)}, u32[]{:S(2)}) %collective-permute-start.6) | collective-permute-done | bytes 622624 | tf_op jit(solution)/shard_map/ppermute | solution.py:431
  77.4 1.1 copy-done.9
  78.5 1.1 copy-done.12
  79.5 1.6 shard_map.62.window
  81.2 3.3 %shard_map.61.vert_ref = bf16[2,1024,256]{2,1,0:T(8,128)(2,1)S(1)} custom-call(s32[8,2,4]{2,1,0:T(2,128)S(1)} %broadcast_add_fusion.place_ref, s32[2,16]{1,0:T(2,128)S(1)} %compare_select_fusion.1.source_ref, bf16[512,256]{1,0:T(8,128)(2,1)} %get-tuple-element.13.rest_0_, bf16[1152,256]{1,0:T(8,128)(2,1)S(1)} %collective-permute-done.rest_1_.rest_0_, ...), custom_call_target="tpu_custom_call" | custom-call | bytes 2097152 | tf_op jit(solution)/shard_map/pallas_call | solution.py:164
  84.5 0.4 copy-done
  84.9 7.1 %shard_map.63.rest_0_.rest_2_ = bf16[512,512]{1,0:T(8,128)(2,1)S(1)} custom-call(s32[1]{0:T(128)} %bitcast.part_ref, s32[2,8]{1,0:T(2,128)S(1)} %select_reduce_fusion.1.slash_ref, f32[64,1536]{1,0:T(8,128)S(1)} %fusion.bias_ref, bf16[2048,1024]{1,0:T(8,128)(2,1)S(1)} %copy-done, bf16[2,1024,256]{2,1,0:T(8,128)(2,1)S(1)} %shard_map.61.vert_ref, ...), custom_call_target="tpu_custom_call" | custom-call | flops 1610612736 | bytes 4194304 | tf_op jit(solution)/shard_map/pallas_call | solution.py:322
  92.0 1.3 shard_map.66
  93.3 2.0 %collective-permute-start.11 = (bf16[2048,256]{1,0:T(8,128)(2,1)}, bf16[2048,256]{1,0:T(8,128)(2,1)}, u32[]{:S(2)}, u32[]{:S(2)}) collective-permute-start(bf16[2048,256]{1,0:T(8,128)(2,1)} %shard_map.66), channel_id=1, source_target_pairs={{0,4},{4,0},{8,12},{12,8},{16,20},{20,16},{24,28},{28,24},{1,5},{5... | collective-permute-start | bytes 3145736 | tf_op jit(solution)/shard_map/ppermute | solution.py:467
  95.4 2.2 %copy-done.1 = bf16[2048,1024]{1,0:T(8,128)(2,1)S(1)} copy-done((bf16[2048,1024]{1,0:T(8,128)(2,1)S(1)}, bf16[2048,1024]{1,0:T(8,128)(2,1)}, u32[]{:S(2)}) %copy-start.1) | copy-done | bytes 4194328
  97.6 1.9 %copy-done.4 = bf16[6144,256]{1,0:T(8,128)(2,1)S(1)} copy-done((bf16[6144,256]{1,0:T(8,128)(2,1)S(1)}, bf16[6144,256]{1,0:T(8,128)(2,1)}, u32[]{:S(2)}) %copy-start.4) | copy-done | bytes 3145752
  99.5 1.0 copy-done.6
  100.5 18.3 %shard_map.64 = (bf16[512,512]{1,0:T(8,128)(2,1)S(1)}, bf16[512,512]{1,0:T(8,128)(2,1)S(1)}, bf16[512,512]{1,0:T(8,128)(2,1)S(1)}) custom-call(s32[3]{0:T(128)S(1)} %pad_add_fusion.part_ref, s32[2,8]{1,0:T(2,128)S(1)} %select_reduce_fusion.1.slash_ref, f32[64,1536]{1,0:T(8,128)S(1)} %copy-done.6, bf16[2048,1024]{1,0:T(8,128)(2,1)S(1)} %copy-done.1, ...), custom_call_target="tpu_custom_call" | custom-call | flops 4831838208 | bytes 6291456 | tf_op jit(solution)/shard_map/pallas_call | solution.py:322
  118.8 1.3 collective-permute-start.8
  120.1 0.6 collective-permute-start.9
  120.7 0.5 broadcast_in_dim.14
  121.3 1.7 %shard_map.67.window = bf16[6144,256]{1,0:T(8,128)(2,1)S(1)} custom-call(s32[1]{0:T(128)} %bitcast.1.parity_ref, bf16[2048,256]{1,0:T(8,128)(2,1)} %collective-permute-done.10.rest_1_.rest_0_, bf16[2048,256]{1,0:T(8,128)(2,1)} %collective-permute-done.11.rest_1_, bf16[2048,256]{1,0:T(8,128)(2,1)S(1)} %shard_map.65.rest_0_.rest_2_), custom_call_target="tpu_custom_call" | custom-call | bytes 6291456 | tf_op jit(solution)/shard_map/pallas_call | solution.py:128
  123.0 1.0 copy-done.2
  124.1 7.1 %shard_map.68.rest_0_ = bf16[512,512]{1,0:T(8,128)(2,1)S(1)} custom-call(s32[1]{0:T(128)} %bitcast.part_ref, s32[2,8]{1,0:T(2,128)S(1)} %select_reduce_fusion.1.slash_ref, f32[64,1536]{1,0:T(8,128)S(1)} %copy-done.7, bf16[2048,1024]{1,0:T(8,128)(2,1)S(1)} %copy-done.2, bf16[2,1024,256]{2,1,0:T(8,128)(2,1)S(1)} %shard_map.61.vert_ref, ...), custom_call_target="tpu_custom_call" | custom-call | flops 1610612736 | bytes 4194304 | tf_op jit(solution)/shard_map/pallas_call | solution.py:322
  131.2 0.9 collective-permute-start.12
  132.2 7.1 %shard_map.69.rest_0_ = bf16[512,512]{1,0:T(8,128)(2,1)S(1)} custom-call(s32[1]{0:T(128)} %bitcast.2.part_ref, s32[2,8]{1,0:T(2,128)S(1)} %select_reduce_fusion.1.slash_ref, f32[64,1536]{1,0:T(8,128)S(1)} %copy-done.7, bf16[2048,1024]{1,0:T(8,128)(2,1)S(1)} %copy-done.2, bf16[2,1024,256]{2,1,0:T(8,128)(2,1)S(1)} %shard_map.61.vert_ref, ...), custom_call_target="tpu_custom_call" | custom-call | flops 1610612736 | bytes 4194304 | tf_op jit(solution)/shard_map/pallas_call | solution.py:322
  139.3 0.8 collective-permute-start.13
  140.1 12.7 %shard_map.70 = (bf16[512,512]{1,0:T(8,128)(2,1)S(1)}, bf16[512,512]{1,0:T(8,128)(2,1)S(1)}) custom-call(s32[2]{0:T(128)S(1)} %pad_add_fusion.1.part_ref, s32[2,8]{1,0:T(2,128)S(1)} %select_reduce_fusion.1.slash_ref, f32[64,1536]{1,0:T(8,128)S(1)} %copy-done.7, bf16[2048,1024]{1,0:T(8,128)(2,1)S(1)} %copy-done.2, ...), custom_call_target="tpu_custom_call" | custom-call | flops 3221225472 | bytes 5242880 | tf_op jit(solution)/shard_map/pallas_call | solution.py:322
  153.4 3.3 %collective-permute-done.13 = bf16[512,512]{1,0:T(8,128)(2,1)S(1)} collective-permute-done((bf16[512,512]{1,0:T(8,128)(2,1)S(1)}, bf16[512,512]{1,0:T(8,128)(2,1)S(1)}, u32[]{:S(2)}, u32[]{:S(2)}) %collective-permute-start.13) | collective-permute-done | bytes 524320 | tf_op jit(solution)/shard_map/ppermute | solution.py:471
  156.9 2.0 %copy-done.17 = bf16[512,4096]{1,0:T(8,128)(2,1)} copy-done((bf16[512,4096]{1,0:T(8,128)(2,1)}, bf16[512,4096]{1,0:T(8,128)(2,1)S(1)}, u32[]{:S(2)}) %copy-start.17) | copy-done | bytes 4194328
  158.9 0.8 constant_dynamic-update-slice_fusion
  (85 shorter events, 3.7 us)
Async XLA Ops:
  0.0 28.3 %copy-start.18 = (s32[2,16]{1,0:T(2,128)S(1)}, s32[2,16]{1,0:T(2,128)}, u32[]{:S(2)}) copy-start(s32[2,16]{1,0:T(2,128)} %param.8) | copy-start | bytes 388
  1.8 1.2 copy-start.13
  3.0 1.2 copy-start.15
  6.2 18.4 %collective-permute-start = (bf16[1152,256]{1,0:T(8,128)(2,1)S(1)}, bf16[1152,256]{1,0:T(8,128)(2,1)S(1)}, u32[]{:S(2)}, u32[]{:S(2)}) collective-permute-start(bf16[1152,256]{1,0:T(8,128)(2,1)S(1)} %get-tuple-element.14), channel_id=1, source_target_pairs={{0,8},{4,12},{8,16},{12,20},{16,24},{20,28},{24,0},{28,4},{1,9},{5... | collective-permute-start | bytes 1769480 | tf_op jit(solution)/shard_map/ppermute | solution.py:425
  9.3 71.8 %collective-permute-start.4 = (bf16[512,256]{1,0:T(8,128)(2,1)}, bf16[512,256]{1,0:T(8,128)(2,1)}, u32[]{:S(2)}, u32[]{:S(2)}) collective-permute-start(bf16[512,256]{1,0:T(8,128)(2,1)} %get-tuple-element.13.rest_0_), channel_id=1, source_target_pairs={{0,4},{4,0},{8,12},{12,8},{16,20},{20,16},{24,28},{28,24},{1,5},{5... | collective-permute-start | bytes 786440 | tf_op jit(solution)/shard_map/ppermute | solution.py:427
  25.6 20.3 %collective-permute-start.2 = (bf16[1152,256]{1,0:T(8,128)(2,1)}, bf16[1152,256]{1,0:T(8,128)(2,1)S(1)}, u32[]{:S(2)}, u32[]{:S(2)}) collective-permute-start(bf16[1152,256]{1,0:T(8,128)(2,1)} %shard_map.56.rest_2_), channel_id=1, source_target_pairs={{0,4},{4,0},{8,12},{12,8},{16,20},{20,16},{24,28},{28,24},{1,5},{5... | collective-permute-start | bytes 1769480 | tf_op jit(solution)/shard_map/ppermute | solution.py:431
  28.2 16.8 %collective-permute-start.1 = (bf16[1216,256]{1,0:T(8,128)(2,1)}, bf16[1216,256]{1,0:T(8,128)(2,1)S(1)}, u32[]{:S(2)}, u32[]{:S(2)}) collective-permute-start(bf16[1216,256]{1,0:T(8,128)(2,1)} %shard_map.57), channel_id=1, source_target_pairs={{0,8},{4,12},{8,16},{12,20},{16,24},{20,28},{24,0},{28,4},{1,9},{5... | collective-permute-start | bytes 1867784 | tf_op jit(solution)/shard_map/ppermute | solution.py:425
  29.2 17.6 %copy-start.14 = (bf16[2048,256]{1,0:T(8,128)(2,1)S(1)}, bf16[2048,256]{1,0:T(8,128)(2,1)}, u32[]{:S(2)}) copy-start(bf16[2048,256]{1,0:T(8,128)(2,1)} %keys_ref.3) | copy-start | bytes 3145732
  29.2 17.6 %copy-start.16 = (bf16[2048,256]{1,0:T(8,128)(2,1)S(1)}, bf16[2048,256]{1,0:T(8,128)(2,1)}, u32[]{:S(2)}) copy-start(bf16[2048,256]{1,0:T(8,128)(2,1)} %values_ref.3) | copy-start | bytes 3145732
  46.0 0.8 copy-start.11
  46.2 18.8 %collective-permute-start.3 = (bf16[1216,256]{1,0:T(8,128)(2,1)S(1)}, bf16[1216,256]{1,0:T(8,128)(2,1)S(1)}, u32[]{:S(2)}, u32[]{:S(2)}) collective-permute-start(bf16[1216,256]{1,0:T(8,128)(2,1)S(1)} %shard_map.59.rest_1_), channel_id=1, source_target_pairs={{0,8},{4,12},{8,16},{12,20},{16,24},{20,28},{24,0},{28,4},{1,9},{5... | collective-permute-start | bytes 1867784 | tf_op jit(solution)/shard_map/ppermute | solution.py:425
  47.0 45.0 %collective-permute-start.10 = (bf16[2048,256]{1,0:T(8,128)(2,1)S(1)}, bf16[2048,256]{1,0:T(8,128)(2,1)}, u32[]{:S(2)}, u32[]{:S(2)}) collective-permute-start(bf16[2048,256]{1,0:T(8,128)(2,1)S(1)} %shard_map.65.rest_0_.rest_2_), channel_id=1, source_target_pairs={{0,8},{4,12},{8,16},{12,20},{16,24},{20,28},{24,0},{28,4},{1,9},{5... | collective-permute-start | bytes 3145736 | tf_op jit(solution)/shard_map/ppermute | solution.py:438
  47.1 21.1 %collective-permute-start.5 = (bf16[1216,256]{1,0:T(8,128)(2,1)}, bf16[1216,256]{1,0:T(8,128)(2,1)}, u32[]{:S(2)}, u32[]{:S(2)}) collective-permute-start(bf16[1216,256]{1,0:T(8,128)(2,1)} %shard_map.58.rest_2_), channel_id=1, source_target_pairs={{0,4},{4,0},{8,12},{12,8},{16,20},{20,16},{24,28},{28,24},{1,5},{5... | collective-permute-start | bytes 1867784 | tf_op jit(solution)/shard_map/ppermute | solution.py:431
  66.0 0.8 copy-start.8
  66.8 10.6 %collective-permute-start.6 = (bf16[1216,256]{1,0:T(8,128)(2,1)}, bf16[1216,256]{1,0:T(8,128)(2,1)}, u32[]{:S(2)}, u32[]{:S(2)}) collective-permute-start(bf16[1216,256]{1,0:T(8,128)(2,1)} %shard_map.60), channel_id=1, source_target_pairs={{0,4},{4,0},{8,12},{12,8},{16,20},{20,16},{24,28},{28,24},{1,5},{5... | collective-permute-start | bytes 1867784 | tf_op jit(solution)/shard_map/ppermute | solution.py:431
  68.2 16.3 %copy-start.5 = (f32[64,1536]{1,0:T(8,128)}, f32[64,1536]{1,0:T(8,128)S(1)}, u32[]{:S(2)}) copy-start(f32[64,1536]{1,0:T(8,128)S(1)} %fusion.bias_ref) | copy-start | bytes 1179652
  77.4 1.1 copy-start.9
  78.5 1.1 copy-start.12
  79.5 1.6 %copy-start.10 = (bf16[1216,256]{1,0:T(8,128)(2,1)S(1)}, bf16[1216,256]{1,0:T(8,128)(2,1)}, u32[]{:S(2)}) copy-start(bf16[1216,256]{1,0:T(8,128)(2,1)} %copy-done.8) | copy-start | bytes 1867780
  81.1 10.9 %copy-start.3 = (bf16[6144,256]{1,0:T(8,128)(2,1)}, bf16[6144,256]{1,0:T(8,128)(2,1)S(1)}, u32[]{:S(2)}) copy-start(bf16[6144,256]{1,0:T(8,128)(2,1)S(1)} %shard_map.62.window) | copy-start | bytes 9437188
  81.1 3.7 %copy-start = (bf16[2048,1024]{1,0:T(8,128)(2,1)S(1)}, bf16[2048,1024]{1,0:T(8,128)(2,1)}, u32[]{:S(2)}) copy-start(bf16[2048,1024]{1,0:T(8,128)(2,1)} %query_ref.9) | copy-start | bytes 12582916
  93.3 28.0 %collective-permute-start.11 = (bf16[2048,256]{1,0:T(8,128)(2,1)}, bf16[2048,256]{1,0:T(8,128)(2,1)}, u32[]{:S(2)}, u32[]{:S(2)}) collective-permute-start(bf16[2048,256]{1,0:T(8,128)(2,1)} %shard_map.66), channel_id=1, source_target_pairs={{0,4},{4,0},{8,12},{12,8},{16,20},{20,16},{24,28},{28,24},{1,5},{5... | collective-permute-start | bytes 3145736 | tf_op jit(solution)/shard_map/ppermute | solution.py:467
  95.3 25.4 %collective-permute-start.7 = (bf16[512,512]{1,0:T(8,128)(2,1)S(1)}, bf16[512,512]{1,0:T(8,128)(2,1)S(1)}, u32[]{:S(2)}, u32[]{:S(2)}) collective-permute-start(bf16[512,512]{1,0:T(8,128)(2,1)S(1)} %shard_map.63.rest_0_.rest_2_), channel_id=1, source_target_pairs={{0,3},{1,2},{2,1},{3,0},{4,7},{5,6},{6,5},{7,4},{8,11},{9,10},{10,... | collective-permute-start | bytes 1572872 | tf_op jit(solution)/shard_map/ppermute | solution.py:471
  95.4 2.2 %copy-start.1 = (bf16[2048,1024]{1,0:T(8,128)(2,1)S(1)}, bf16[2048,1024]{1,0:T(8,128)(2,1)}, u32[]{:S(2)}) copy-start(bf16[2048,1024]{1,0:T(8,128)(2,1)} %query_ref.9) | copy-start | bytes 12582916
  97.6 1.9 %copy-start.4 = (bf16[6144,256]{1,0:T(8,128)(2,1)S(1)}, bf16[6144,256]{1,0:T(8,128)(2,1)}, u32[]{:S(2)}) copy-start(bf16[6144,256]{1,0:T(8,128)(2,1)} %copy-done.3) | copy-start | bytes 9437188
  99.5 1.0 copy-start.6
  118.8 34.4 %collective-permute-start.8 = (bf16[512,512]{1,0:T(8,128)(2,1)S(1)}, bf16[512,512]{1,0:T(8,128)(2,1)S(1)}, u32[]{:S(2)}, u32[]{:S(2)}) collective-permute-start(bf16[512,512]{1,0:T(8,128)(2,1)S(1)} %get-tuple-element.16), channel_id=1, source_target_pairs={{0,2},{1,3},{2,0},{3,1},{4,6},{5,7},{6,4},{7,5},{8,10},{9,11},{10,... | collective-permute-start | bytes 1572872 | tf_op jit(solution)/shard_map/ppermute | solution.py:471
  120.1 33.1 %collective-permute-start.9 = (bf16[512,512]{1,0:T(8,128)(2,1)S(1)}, bf16[512,512]{1,0:T(8,128)(2,1)S(1)}, u32[]{:S(2)}, u32[]{:S(2)}) collective-permute-start(bf16[512,512]{1,0:T(8,128)(2,1)S(1)} %get-tuple-element.17), channel_id=1, source_target_pairs={{0,1},{1,0},{2,3},{3,2},{4,5},{5,4},{6,7},{7,6},{8,9},{9,8},{10,11... | collective-permute-start | bytes 1572872 | tf_op jit(solution)/shard_map/ppermute | solution.py:471
  121.2 2.8 %copy-start.2 = (bf16[2048,1024]{1,0:T(8,128)(2,1)S(1)}, bf16[2048,1024]{1,0:T(8,128)(2,1)}, u32[]{:S(2)}) copy-start(bf16[2048,1024]{1,0:T(8,128)(2,1)} %query_ref.9) | copy-start | bytes 12582916
  121.2 2.9 %copy-start.7 = (f32[64,1536]{1,0:T(8,128)S(1)}, f32[64,1536]{1,0:T(8,128)}, u32[]{:S(2)}) copy-start(f32[64,1536]{1,0:T(8,128)} %copy-done.5) | copy-start | bytes 1179652
  131.2 22.1 %collective-permute-start.12 = (bf16[512,512]{1,0:T(8,128)(2,1)S(1)}, bf16[512,512]{1,0:T(8,128)(2,1)S(1)}, u32[]{:S(2)}, u32[]{:S(2)}) collective-permute-start(bf16[512,512]{1,0:T(8,128)(2,1)S(1)} %shard_map.68.rest_0_), channel_id=1, source_target_pairs={{0,3},{1,2},{2,1},{3,0},{4,7},{5,6},{6,5},{7,4},{8,11},{9,10},{10,... | collective-permute-start | bytes 1572872 | tf_op jit(solution)/shard_map/ppermute | solution.py:471
  139.3 17.4 %collective-permute-start.13 = (bf16[512,512]{1,0:T(8,128)(2,1)S(1)}, bf16[512,512]{1,0:T(8,128)(2,1)S(1)}, u32[]{:S(2)}, u32[]{:S(2)}) collective-permute-start(bf16[512,512]{1,0:T(8,128)(2,1)S(1)} %shard_map.69.rest_0_), channel_id=1, source_target_pairs={{0,2},{1,3},{2,0},{3,1},{4,6},{5,7},{6,4},{7,5},{8,10},{9,11},{10,... | collective-permute-start | bytes 1572872 | tf_op jit(solution)/shard_map/ppermute | solution.py:471
  152.8 4.0 %collective-permute-start.14 = (bf16[512,512]{1,0:T(8,128)(2,1)S(1)}, bf16[512,512]{1,0:T(8,128)(2,1)S(1)}, u32[]{:S(2)}, u32[]{:S(2)}) collective-permute-start(bf16[512,512]{1,0:T(8,128)(2,1)S(1)} %get-tuple-element.19), channel_id=1, source_target_pairs={{0,1},{1,0},{2,3},{3,2},{4,5},{5,4},{6,7},{7,6},{8,9},{9,8},{10,11... | collective-permute-start | bytes 1572872 | tf_op jit(solution)/shard_map/ppermute | solution.py:471
  156.9 2.0 %copy-start.17 = (bf16[512,4096]{1,0:T(8,128)(2,1)}, bf16[512,4096]{1,0:T(8,128)(2,1)S(1)}, u32[]{:S(2)}) copy-start(bf16[512,4096]{1,0:T(8,128)(2,1)S(1)} %constant_dynamic-update-slice_fusion.1) | copy-start | bytes 12582916
